TPU v7x, 32 devices: a whole 2x2x4 slice. The times are simulated.
32 devices in a mesh: cam: 4 (over y, core), ex: 2 (over x), ey: 4 (over z).
Axes of the slice: x: 2, y: 2, z: 4, core: 2. Of those that a mesh axis runs over, the one named last changes fastest.
Arguments:
- scalar: float32 [8, 8, 32, 8, 512], P('ex', None, 'ey', None, 'cam'), may hold values from -3 to 3
- velocity: float32 [3, 8, 8, 32, 8, 512], P(None, 'ex', None, 'ey', None, 'cam'), may hold values from -6 to 6
- lumped_mass: float32 [8, 8, 32, 8, 512], P('ex', None, 'ey', None, 'cam'), may hold values from 0.3 to 3
- pixel_weights: bfloat16 [8, 512, 128], replicated, may hold values from -0.25 to 0.25
- cut_element: int32 [8, 4096], P(None, ('cam', 'ex', 'ey')), may hold values from 0 to 511
- pixel_block: int32 [8, 4096], P(None, ('cam', 'ex', 'ey')), may hold values from 0 to 1024, as said below
Outputs:
- advected: float32 [8, 8, 32, 8, 512], P('ex', None, 'ey', None, 'cam')
- images: float32 [8, 8192, 128], P('cam', ('ex', 'ey'))
Inputs may be any that keep to these rules, and one draw needn't show every extreme that they name: `pixel_block`: A value of 1024 marks an empty slot; in each device's 128 slots of one camera the filled ones come first. `cut_element`: A local element number of the owning device, with the radial index fastest, then the azimuthal, then the axial.
All inputs are finite; a program needn't handle non-finite values.
Results may differ from a plain program's by a relative error of at most 0.0028.
Values may be sent and summed in bfloat16 or wider, within the bound.
No kernel may reach another device: no remote copies, remote signals or barrier semaphores. Data moves between devices by JAX's collectives and lax.ppermute only.
A program may use at most 64 MiB of HBM per device.

v0:
```python
import jax
import jax.numpy as jnp
import numpy as np
from jax import lax
from jax.sharding import PartitionSpec as P

NBLK = 1024


time_step = 0.01


def padded(shard, sides, width, wrap):
    for axis, dim in sides:
        count, length = (lax.axis_size(axis), shard.shape[dim])
        up = [(i, (i + 1) % count) for i in range(count if wrap else count - 1)]
        down = [(j, i) for i, j in up]
        last = lax.slice_in_dim(shard, length - width, length, axis=dim)
        initial = lax.slice_in_dim(shard, 0, width, axis=dim)
        before = lax.ppermute(last, axis, up)
        after = lax.ppermute(initial, axis, down)
        shard = jnp.concatenate([before, shard, after], axis=dim)
    return shard


def legendre_seven(points):
    previous = points * 0.0 + 1.0
    current = points * 1.0
    for order in range(1, 7):
        following = ((2 * order + 1) * points * current - order * previous) / (order + 1)
        previous = current
        current = following
    return current


def gll_derivative():
    degree = 7
    gll_nodes = np.array(
        [
            -1.0,
            -0.8717401485096066,
            -0.5917001814331423,
            -0.2092992179024789,
            0.2092992179024789,
            0.5917001814331423,
            0.8717401485096066,
            1.0,
        ]
    )
    values = legendre_seven(gll_nodes)
    derivative = np.zeros((degree + 1, degree + 1))
    for target in range(degree + 1):
        for source in range(degree + 1):
            if target != source:
                derivative[target, source] = values[target] / (
                    values[source] * (gll_nodes[target] - gll_nodes[source])
                )
    derivative[0, 0] = -degree * (degree + 1) / 4.0
    derivative[degree, degree] = degree * (degree + 1) / 4.0
    return derivative


def pair_sum(extended, dim):
    length = extended.shape[dim] - 2
    middle = lax.slice_in_dim(extended, 1, length + 1, 1, dim)
    following = lax.slice_in_dim(extended, 2, length + 2, 1, dim)
    preceding = lax.slice_in_dim(extended, 0, length, 1, dim)
    shape = [1] * extended.ndim
    shape[dim] = length
    node = (jnp.arange(length, dtype=jnp.int32) % 8).reshape(shape)
    is_last = (node == 7).astype(jnp.float32)
    is_first = (node == 0).astype(jnp.float32)
    return middle + is_last * following + is_first * preceding


def assemble(stack):
    extended = padded(stack, (("ex", 1),), 1, True)
    summed = pair_sum(extended, 1)
    extended = padded(summed, (("ey", 2),), 1, True)
    summed = pair_sum(extended, 2)
    extended = padded(summed, (("cam", 3),), 1, False)
    return pair_sum(extended, 3)


def convect(field, velocity, derivative, radial_table):
    along_axial = jnp.einsum("pi,aibjz->apbjz", derivative, field, precision=lax.Precision.HIGHEST)
    along_azimuth = jnp.einsum(
        "qj,aibjz->aibqz", derivative, field, precision=lax.Precision.HIGHEST
    )
    along_radius = jnp.dot(field, radial_table, precision=lax.Precision.HIGHEST)
    return velocity[0] * along_axial + velocity[1] * along_azimuth + velocity[2] * along_radius


def per_device(scalar, velocity, lumped_mass, pixel_weights, cut_element, pixel_block):
    shape = scalar.shape
    depth = shape[4]
    derivative = jnp.asarray(gll_derivative(), jnp.float32)
    radial_table = jnp.kron(jnp.eye(depth // 8, dtype=jnp.float32), derivative.T)
    flat = (shape[0] * 8, shape[2] * 8, depth)
    first_stack = jnp.stack(
        [
            (lumped_mass * convect(scalar, velocity, derivative, radial_table)).reshape(flat),
            lumped_mass.reshape(flat),
        ]
    )
    first_sums = assemble(first_stack)
    assembled_mass = first_sums[1]
    rate_first = (first_sums[0] / assembled_mass).reshape(shape)
    first = scalar - time_step * rate_first
    second_stack = (lumped_mass * convect(first, velocity, derivative, radial_table)).reshape(
        (1,) + flat
    )
    rate_second = (assemble(second_stack)[0] / assembled_mass).reshape(shape)
    second = first - time_step * rate_second
    advected = 0.5 * (scalar + second)
    element_count = shape[0] * shape[2] * (depth // 8)
    elements = (
        advected.astype(jnp.bfloat16)
        .reshape(shape[0], 8, shape[2], 8, depth // 8, 8)
        .transpose(0, 2, 4, 1, 3, 5)
        .reshape(element_count, 512)
    )
    picked = jnp.take(elements, cut_element, axis=0)
    block_ids = jnp.arange(NBLK, dtype=jnp.int32)
    values = jnp.einsum("csp,cpx->csx", picked, pixel_weights, preferred_element_type=jnp.float32)
    onehot = (pixel_block[:, None, :] == block_ids[None, :, None]).astype(jnp.float32)
    images = lax.psum_scatter(
        jnp.einsum("cbs,csx->cbx", onehot, values, precision=lax.Precision.HIGHEST),
        "cam",
        scatter_dimension=0,
        tiled=True,
    )
    return (advected, images)


def solution(mesh):
    placed = (
        P("ex", None, "ey", None, "cam"),
        P(None, "ex", None, "ey", None, "cam"),
        P("ex", None, "ey", None, "cam"),
        P(),
        P(None, ("cam", "ex", "ey")),
        P(None, ("cam", "ex", "ey")),
    )
    return jax.shard_map(
        per_device,
        mesh=mesh,
        in_specs=placed,
        out_specs=(P("ex", None, "ey", None, "cam"), P("cam", ("ex", "ey"), None)),
        check_vma=False,
    )
```

profile of v0, /device:TPU:0, one launch (start us, length us, event | category | flops | bytes accessed | tf_op | source)
XLA Modules:
  0.0 185.9 jit_solution(16749758463349441166)
XLA Ops:
  7.2 3.8 %fusion.53 = (f32[1,4,8,8,8,128]{5,4,3,2,1,0:T(8,128)}, f32[1,4,8,8,8,128]{5,4,3,2,1,0:T(8,128)}, f32[1,4,8,8,8,128]{5,4,3,2,1,0:T(8,128)}) fusion(f32[3,4,8,8,8,128]{5,4,3,2,1,0:T(8,128)} %param.8), kind=kLoop, calls=%fused_computation.99 | loop fusion | bytes 6291456 | tf_op jit(solution)/shard_map/slice | solution.py:91
  11.0 0.1 broadcast_multiply_fusion
  11.2 0.5 reshape.95
  11.7 0.6 copy-done.1
  12.2 1.0 fusion.59
  13.2 0.2 copy-done.9
  13.5 0.3 copy-done.11
  13.8 3.1 %fusion.20 = f32[4,8,8,8,128]{4,1,3,2,0:T(8,128)S(1)} fusion(f32[8,8,1,1,1]{1,0,4,3,2:T(8,128)S(1)} %copy-done.13, f32[8,4,8,8,128]{4,0,3,2,1:T(8,128)S(1)} %fusion.59, f32[1,4,8,8,8,128]{5,4,3,2,1,0:T(8,128)S(1)} %copy-done.11, f32[1,4,8,8,8,128]{5,4,3,2,1,0:T(8,128)S(1)} %copy-done.9, f32[4,8,8,8,128]{4,3,2,1,0:T(8,128)S(1)} %copy-done.1), kind=kOutput, calls=%fused_computation.39 | convolution fusion | flops 25952256 | bytes 5243136 | tf_op jit(solution)/shard_map/pi,aibjz->apbjz/dot_general | solution.py:86
  16.9 2.4 %fusion.21 = f32[4,8,8,8,128]{4,1,3,2,0:T(8,128)S(1)} fusion(f32[4,8,8,8,128]{4,1,3,2,0:T(8,128)S(1)} %fusion.20, f32[1,4,8,8,8,128]{5,4,3,2,1,0:T(8,128)S(1)} %copy-done.7, f32[4,8,8,8,128]{4,3,2,1,0:T(8,128)S(1)} %copy-done.3, f32[4,8,8,8,128]{4,3,2,1,0:T(8,128)S(1)} %copy-done.1, f32[128,128,1,1,1]{1,0,2,3,4:T(8,128)S(1)} %reshape.95), kind=kOutput, calls=%fused_computation.40 | convolution fusion | flops 403439616 | bytes 5308416 | tf_op jit(solution)/shard_map/dot_general | solution.py:90
  19.3 0.2 copy.43
  19.6 3.0 %collective-permute-start.1 = (f32[2,1,64,128]{3,2,1,0:T(8,128)S(1)}, f32[2,1,64,128]{3,2,1,0:T(8,128)S(1)}, u32[]{:S(2)}, u32[]{:S(2)}) collective-permute-start(f32[2,1,64,128]{3,2,1,0:T(8,128)S(1)} %get-tuple-element.12), channel_id=1, source_target_pairs={{0,4},{4,0},{1,5},{5,1},{2,6},{6,2},{3,7},{7,3},{8,12},{12,8},{9,1... | collective-permute-start | bytes 196616 | tf_op jit(solution)/shard_map/ppermute | solution.py:20
  22.6 0.1 collective-permute-start
  22.6 2.3 %collective-permute-done.1 = f32[2,1,64,128]{3,2,1,0:T(8,128)S(1)} collective-permute-done((f32[2,1,64,128]{3,2,1,0:T(8,128)S(1)}, f32[2,1,64,128]{3,2,1,0:T(8,128)S(1)}, u32[]{:S(2)}, u32[]{:S(2)}) %collective-permute-start.1) | collective-permute-done | bytes 65568 | tf_op jit(solution)/shard_map/ppermute | solution.py:20
  24.9 1.9 %collective-permute-done = f32[2,1,64,128]{3,2,1,0:T(8,128)S(1)} collective-permute-done((f32[2,1,64,128]{3,2,1,0:T(8,128)S(1)}, f32[2,1,64,128]{3,2,1,0:T(8,128)S(1)}, u32[]{:S(2)}, u32[]{:S(2)}) %collective-permute-start) | collective-permute-done | bytes 65568 | tf_op jit(solution)/shard_map/ppermute | solution.py:21
  26.8 0.4 fusion.2
  27.3 1.6 collective-permute-start.3
  28.9 2.2 %collective-permute-start.2 = (f32[2,32,1,128]{3,2,1,0:T(1,128)S(1)}, f32[2,32,1,128]{3,2,1,0:T(1,128)S(1)}, u32[]{:S(2)}, u32[]{:S(2)}) collective-permute-start(f32[2,32,1,128]{3,2,1,0:T(1,128)S(1)} %get-tuple-element.9), channel_id=1, source_target_pairs={{1,0},{2,1},{3,2},{0,3},{5,4},{6,5},{7,6},{4,7},{9,8},{10,9},{11,1... | collective-permute-start | bytes 98312 | tf_op jit(solution)/shard_map/ppermute | solution.py:21
  31.2 2.0 %collective-permute-done.3 = f32[2,32,1,128]{3,2,1,0:T(1,128)S(1)} collective-permute-done((f32[2,32,1,128]{3,2,1,0:T(1,128)S(1)}, f32[2,32,1,128]{3,2,1,0:T(1,128)S(1)}, u32[]{:S(2)}, u32[]{:S(2)}) %collective-permute-start.3) | collective-permute-done | bytes 32800 | tf_op jit(solution)/shard_map/ppermute | solution.py:20
  33.2 0.8 fusion.8
  34.0 2.9 %fusion.54 = (f32[2,32,64,1]{3,2,1,0:T(8,128)}, f32[2,32,64,1]{3,2,1,0:T(8,128)}) fusion(f32[2,32,64,128]{3,2,1,0:T(8,128)S(1)} %fusion.8), kind=kLoop, calls=%fused_computation.100 | loop fusion | bytes 65536 | tf_op jit(solution)/shard_map/slice | solution.py:19
  36.9 2.3 %copy.46 = f32[2,32,64,1]{2,1,3,0:T(8,128)S(1)} copy(f32[2,32,64,1]{3,2,1,0:T(8,128)} %get-tuple-element.8) | data formatting | bytes 32768 | tf_op jit(solution)/shard_map/slice | solution.py:18
  39.2 1.3 collective-permute-start.5
  40.5 2.3 %copy.44 = f32[2,32,64,1]{2,1,3,0:T(8,128)S(1)} copy(f32[2,32,64,1]{3,2,1,0:T(8,128)} %get-tuple-element.7) | data formatting | bytes 32768 | tf_op jit(solution)/shard_map/slice | solution.py:19
  42.8 1.5 collective-permute-start.4
  44.3 2.1 %copy.47 = f32[2,32,64,1]{3,2,1,0:T(8,128)} copy(f32[2,32,64,1]{2,1,3,0:T(8,128)S(1)} %collective-permute-done.5) | data formatting | bytes 32768 | tf_op jit(solution)/shard_map/ppermute | solution.py:20
  46.3 1.3 collective-permute-done.4
  47.6 2.0 %copy.45 = f32[2,32,64,1]{3,2,1,0:T(8,128)} copy(f32[2,32,64,1]{2,1,3,0:T(8,128)S(1)} %collective-permute-done.4) | data formatting | bytes 32768 | tf_op jit(solution)/shard_map/ppermute | solution.py:21
  49.7 3.9 %fusion.4 = f32[2,32,64,128]{3,2,1,0:T(8,128)S(1)} fusion(f32[2,32,64,128]{3,2,1,0:T(8,128)S(1)} %fusion.8, f32[2,32,64,1]{3,2,1,0:T(8,128)} %copy.47, f32[2,32,64,1]{3,2,1,0:T(8,128)} %copy.45, f32[128]{0:T(128)S(1)} %get-tuple-element.23, f32[128]{0:T(128)S(1)} %get-tuple-element.24), kind=kLoop, calls=%fused_computation.12 | loop fusion | flops 3145728 | bytes 4228096 | tf_op jit(solution)/shard_map/add | solution.py:73
  53.6 0.2 fusion.37
  53.8 1.8 copy-done.2
  55.6 0.1 sub.6
  55.7 1.0 fusion.60
  56.8 0.3 copy-done.12
  57.1 3.2 %fusion.16 = f32[4,8,8,8,128]{4,1,3,2,0:T(8,128)S(1)} fusion(f32[8,8,1,1,1]{1,0,4,3,2:T(8,128)S(1)} %copy-done.13, f32[4,8,8,128,8]{3,4,2,1,0:T(8,128)S(1)} %fusion.60, f32[1,4,8,8,8,128]{5,4,3,2,1,0:T(8,128)S(1)} %copy-done.12, f32[1,4,8,8,8,128]{5,4,3,2,1,0:T(8,128)S(1)} %copy-done.10, f32[4,8,8,8,128]{4,3,2,1,0:T(8,128)S(1)} %sub.6), kind=kOutput, calls=%fused_computation.33 | convolution fusion | flops 25952256 | bytes 5243136 | tf_op jit(solution)/shard_map/pi,aibjz->apbjz/dot_general | solution.py:86
  60.4 2.4 %fusion.22 = f32[4,8,8,8,128]{4,1,3,2,0:T(8,128)S(1)} fusion(f32[4,8,8,8,128]{4,1,3,2,0:T(8,128)S(1)} %fusion.16, f32[1,4,8,8,8,128]{5,4,3,2,1,0:T(8,128)S(1)} %copy-done.8, f32[4,8,8,8,128]{4,3,2,1,0:T(8,128)S(1)} %sub.6, f32[4,8,8,8,128]{4,3,2,1,0:T(8,128)S(1)} %copy-done.4, f32[128,128,1,1,1]{1,0,2,3,4:T(8,128)S(1)} %reshape.95), kind=kOutput, calls=%fused_computation.41 | convolution fusion | flops 403439616 | bytes 5308416 | tf_op jit(solution)/shard_map/dot_general | solution.py:90
  62.8 0.2 copy.52
  63.0 1.0 collective-permute-start.7
  64.0 1.1 collective-permute-start.6
  65.1 1.9 %collective-permute-done.7 = f32[1,1,64,128]{3,2,1,0:T(8,128)S(1)} collective-permute-done((f32[1,1,64,128]{3,2,1,0:T(8,128)S(1)}, f32[1,1,64,128]{3,2,1,0:T(8,128)S(1)}, u32[]{:S(2)}, u32[]{:S(2)}) %collective-permute-start.7) | collective-permute-done | bytes 32800 | tf_op jit(solution)/shard_map/ppermute | solution.py:20
  67.0 0.9 collective-permute-done.6
  68.0 0.2 fusion.34
  68.2 1.3 collective-permute-start.9
  69.5 2.6 %collective-permute-start.8 = (f32[1,32,1,128]{3,2,1,0:T(1,128)S(1)}, f32[1,32,1,128]{3,2,1,0:T(1,128)S(1)}, u32[]{:S(2)}, u32[]{:S(2)}) collective-permute-start(f32[1,32,1,128]{3,2,1,0:T(1,128)S(1)} %get-tuple-element.15), channel_id=1, source_target_pairs={{1,0},{2,1},{3,2},{0,3},{5,4},{6,5},{7,6},{4,7},{9,8},{10,9},{11,1... | collective-permute-start | bytes 49160 | tf_op jit(solution)/shard_map/ppermute | solution.py:21
  72.1 1.7 collective-permute-done.9
  73.8 0.4 fusion.30
  74.2 1.7 fusion.56
  75.9 1.6 copy.55
  77.5 2.1 %collective-permute-start.11 = (f32[1,32,64,1]{2,1,3,0:T(8,128)S(1)}, f32[1,32,64,1]{2,1,3,0:T(8,128)S(1)}, u32[]{:S(2)}, u32[]{:S(2)}) collective-permute-start(f32[1,32,64,1]{2,1,3,0:T(8,128)S(1)} %copy.55), channel_id=1, source_target_pairs={{0,8},{8,16},{16,24},{1,9},{9,17},{17,25},{2,10},{10,18},{18,26},{... | collective-permute-start | bytes 24584 | tf_op jit(solution)/shard_map/ppermute | solution.py:20
  79.6 1.6 copy.53
  81.2 1.5 collective-permute-start.10
  82.8 1.4 copy.56
  84.2 2.8 %collective-permute-done.10 = f32[1,32,64,1]{2,1,3,0:T(8,128)S(1)} collective-permute-done((f32[1,32,64,1]{2,1,3,0:T(8,128)S(1)}, f32[1,32,64,1]{2,1,3,0:T(8,128)S(1)}, u32[]{:S(2)}, u32[]{:S(2)}) %collective-permute-start.10) | collective-permute-done | bytes 8224 | tf_op jit(solution)/shard_map/ppermute | solution.py:21
  86.9 1.4 copy.54
  88.3 3.8 %fusion.26 = f32[1,32,64,128]{3,2,1,0:T(8,128)S(1)} fusion(f32[1,32,64,128]{3,2,1,0:T(8,128)} %copy-done.5, f32[1,32,64,1]{3,2,1,0:T(8,128)} %copy.56, f32[1,32,64,1]{3,2,1,0:T(8,128)} %copy.54, f32[2,32,64,128]{3,2,1,0:T(8,128)} %copy-done.6, f32[128]{0:T(128)S(1)} %get-tuple-element.23, f32[128]{0:T(128)S(1)} %get-tuple-element.24), kind=kLoop, calls=%fused_computation.46 | loop fusion | flops 2097152 | bytes 3163136 | tf_op jit(solution)/shard_map/mul | solution.py:114
  92.1 1.5 fusion.52
  93.6 11.9 %reshape.82 = bf16[4,8,8,8,16,8]{5,4,3,2,1,0:T(8,128)(2,1)} reshape(bf16[4,8,8,8,128]{4,3,2,1,0:T(8,128)(2,1)} %get-tuple-element.2) | data formatting | bytes 1048576 | tf_op jit(solution)/shard_map/reshape | solution.py:119
  105.6 10.5 %copy.57 = bf16[4,8,16,8,8,8]{2,1,0,5,4,3:T(8,128)(2,1)} copy(bf16[4,8,16,8,8,8]{5,2,4,1,3,0:T(8,128)(2,1)} %bitcast.79) | data formatting | bytes 1048576 | tf_op jit(solution)/shard_map/transpose | solution.py:120
  116.0 7.8 %reshape.83 = bf16[512,512]{0,1:T(8,128)(2,1)S(1)} reshape(bf16[4,8,16,8,8,8]{2,1,0,5,4,3:T(8,128)(2,1)} %copy.57) | data formatting | bytes 1048576 | tf_op jit(solution)/shard_map/reshape | solution.py:121
  123.8 0.2 copy.58
  124.0 4.0 %gather_fusion = bf16[1024,512]{1,0:T(8,128)(2,1)S(1)} fusion(bf16[512,512]{1,0:T(8,128)(2,1)S(1)} %copy.58, s32[1024]{0:T(1024)S(1)} %bitcast_clamp_fusion), kind=kCustom, calls=%fused_computation | custom fusion | bytes 2101248 | tf_op jit(solution)/shard_map/jit(_take)/gather | solution.py:123
  128.0 0.5 fusion.38
  128.5 0.2 copy-done.16
  128.7 3.5 %fusion = f32[8,1024,128]{2,1,0:T(8,128)} fusion(f32[8,128,128]{2,1,0:T(8,128)S(1)} %fusion.38, s32[8,128]{1,0:T(8,128)S(1)} %copy-done.16), kind=kOutput, calls=%fused_computation.2 | convolution fusion | flops 1611661312 | bytes 4722688 | tf_op jit(solution)/shard_map/cbs,csx->cbx/dot_general | solution.py:128
  132.2 46.9 %reduce-scatter.2.cloned.1.call-done = f32[2,1024,128]{2,1,0:T(8,128)} async-done(((f32[8,1024,128]{2,1,0:T(8,128)}), f32[2,1024,128]{2,1,0:T(8,128)}) %reduce-scatter.2.cloned.1.call-update) | async-done | bytes 1048592 | tf_op jit(solution)/shard_map/reduce_scatter | solution.py:127
  (44 shorter events, 0.3 us)
Async XLA Ops:
  7.2 120.8 %copy-start = (bf16[8,512,128]{2,1,0:T(8,128)(2,1)S(1)}, bf16[8,512,128]{2,1,0:T(8,128)(2,1)}, u32[]{:S(2)}) copy-start(bf16[8,512,128]{2,1,0:T(8,128)(2,1)} %param.10) | copy-start | bytes 3145732
  7.2 171.9 %reduce-scatter.2.cloned.1.call-start = ((), (), s32[]{:S(2)}) async-start(), calls=%async_computation.1 | async-start | bytes 5242880 | tf_op jit(solution)/shard_map/reduce_scatter | solution.py:127
  7.2 3.8 %copy-start.15 = (f32[8,8]{1,0:T(8,128)S(1)}, f32[8,8]{1,0:T(8,128)}, u32[]{:S(2)}) copy-start(f32[8,8]{1,0:T(8,128)} %constant.71) | copy-start | bytes 772
  11.0 1.2 copy-start.1
  11.0 1.2 copy-start.13
  12.2 1.2 copy-start.9
  12.2 1.5 copy-start.11
  13.8 3.1 %copy-start.3 = (f32[4,8,8,8,128]{4,3,2,1,0:T(8,128)S(1)}, f32[4,8,8,8,128]{4,3,2,1,0:T(8,128)}, u32[]{:S(2)}) copy-start(f32[4,8,8,8,128]{4,3,2,1,0:T(8,128)} %param.9) | copy-start | bytes 3145732
  13.8 3.1 %copy-start.7 = (f32[1,4,8,8,8,128]{5,4,3,2,1,0:T(8,128)S(1)}, f32[1,4,8,8,8,128]{5,4,3,2,1,0:T(8,128)}, u32[]{:S(2)}) copy-start(f32[1,4,8,8,8,128]{5,4,3,2,1,0:T(8,128)} %get-tuple-element.4) | copy-start | bytes 3145732
  19.6 5.4 %collective-permute-start.1 = (f32[2,1,64,128]{3,2,1,0:T(8,128)S(1)}, f32[2,1,64,128]{3,2,1,0:T(8,128)S(1)}, u32[]{:S(2)}, u32[]{:S(2)}) collective-permute-start(f32[2,1,64,128]{3,2,1,0:T(8,128)S(1)} %get-tuple-element.12), channel_id=1, source_target_pairs={{0,4},{4,0},{1,5},{5,1},{2,6},{6,2},{3,7},{7,3},{8,12},{12,8},{9,1... | collective-permute-start | bytes 196616 | tf_op jit(solution)/shard_map/ppermute | solution.py:20
  22.6 4.3 %collective-permute-start = (f32[2,1,64,128]{3,2,1,0:T(8,128)S(1)}, f32[2,1,64,128]{3,2,1,0:T(8,128)S(1)}, u32[]{:S(2)}, u32[]{:S(2)}) collective-permute-start(f32[2,1,64,128]{3,2,1,0:T(8,128)S(1)} %get-tuple-element.11), channel_id=1, source_target_pairs={{4,0},{0,4},{5,1},{1,5},{6,2},{2,6},{7,3},{3,7},{12,8},{8,12},{13,... | collective-permute-start | bytes 196616 | tf_op jit(solution)/shard_map/ppermute | solution.py:21
  27.3 5.9 %collective-permute-start.3 = (f32[2,32,1,128]{3,2,1,0:T(1,128)S(1)}, f32[2,32,1,128]{3,2,1,0:T(1,128)S(1)}, u32[]{:S(2)}, u32[]{:S(2)}) collective-permute-start(f32[2,32,1,128]{3,2,1,0:T(1,128)S(1)} %get-tuple-element.10), channel_id=1, source_target_pairs={{0,1},{1,2},{2,3},{3,0},{4,5},{5,6},{6,7},{7,4},{8,9},{9,10},{10,1... | collective-permute-start | bytes 98312 | tf_op jit(solution)/shard_map/ppermute | solution.py:20
  28.9 4.3 %collective-permute-start.2 = (f32[2,32,1,128]{3,2,1,0:T(1,128)S(1)}, f32[2,32,1,128]{3,2,1,0:T(1,128)S(1)}, u32[]{:S(2)}, u32[]{:S(2)}) collective-permute-start(f32[2,32,1,128]{3,2,1,0:T(1,128)S(1)} %get-tuple-element.9), channel_id=1, source_target_pairs={{1,0},{2,1},{3,2},{0,3},{5,4},{6,5},{7,6},{4,7},{9,8},{10,9},{11,1... | collective-permute-start | bytes 98312 | tf_op jit(solution)/shard_map/ppermute | solution.py:21
  39.2 5.1 %collective-permute-start.5 = (f32[2,32,64,1]{2,1,3,0:T(8,128)S(1)}, f32[2,32,64,1]{2,1,3,0:T(8,128)S(1)}, u32[]{:S(2)}, u32[]{:S(2)}) collective-permute-start(f32[2,32,64,1]{2,1,3,0:T(8,128)S(1)} %copy.46), channel_id=1, source_target_pairs={{0,8},{8,16},{16,24},{1,9},{9,17},{17,25},{2,10},{10,18},{18,26},{... | collective-permute-start | bytes 49160 | tf_op jit(solution)/shard_map/ppermute | solution.py:20
  42.8 4.9 %collective-permute-start.4 = (f32[2,32,64,1]{2,1,3,0:T(8,128)S(1)}, f32[2,32,64,1]{2,1,3,0:T(8,128)S(1)}, u32[]{:S(2)}, u32[]{:S(2)}) collective-permute-start(f32[2,32,64,1]{2,1,3,0:T(8,128)S(1)} %copy.44), channel_id=1, source_target_pairs={{8,0},{16,8},{24,16},{9,1},{17,9},{25,17},{10,2},{18,10},{26,18},{... | collective-permute-start | bytes 49160 | tf_op jit(solution)/shard_map/ppermute | solution.py:21
  53.6 2.1 %copy-start.6 = (f32[2,32,64,128]{3,2,1,0:T(8,128)}, f32[2,32,64,128]{3,2,1,0:T(8,128)S(1)}, u32[]{:S(2)}) copy-start(f32[2,32,64,128]{3,2,1,0:T(8,128)S(1)} %fusion.4) | copy-start | bytes 6291460
  53.6 2.0 %copy-start.2 = (f32[4,8,8,8,128]{4,3,2,1,0:T(8,128)S(1)}, f32[4,8,8,8,128]{4,3,2,1,0:T(8,128)}, u32[]{:S(2)}) copy-start(f32[4,8,8,8,128]{4,3,2,1,0:T(8,128)} %param.7) | copy-start | bytes 3145732
  55.6 1.2 copy-start.10
  55.6 1.5 copy-start.12
  57.1 3.2 %copy-start.4 = (f32[4,8,8,8,128]{4,3,2,1,0:T(8,128)S(1)}, f32[4,8,8,8,128]{4,3,2,1,0:T(8,128)}, u32[]{:S(2)}) copy-start(f32[4,8,8,8,128]{4,3,2,1,0:T(8,128)} %param.9) | copy-start | bytes 3145732
  57.1 3.3 %copy-start.8 = (f32[1,4,8,8,8,128]{5,4,3,2,1,0:T(8,128)S(1)}, f32[1,4,8,8,8,128]{5,4,3,2,1,0:T(8,128)}, u32[]{:S(2)}) copy-start(f32[1,4,8,8,8,128]{5,4,3,2,1,0:T(8,128)} %get-tuple-element.4) | copy-start | bytes 3145732
  62.8 9.3 %copy-start.14 = (s32[8,128]{1,0:T(8,128)S(1)}, s32[8,128]{1,0:T(8,128)}, u32[]{:S(2)}) copy-start(s32[8,128]{1,0:T(8,128)} %param.11) | copy-start | bytes 12292
  63.0 4.0 %collective-permute-start.7 = (f32[1,1,64,128]{3,2,1,0:T(8,128)S(1)}, f32[1,1,64,128]{3,2,1,0:T(8,128)S(1)}, u32[]{:S(2)}, u32[]{:S(2)}) collective-permute-start(f32[1,1,64,128]{3,2,1,0:T(8,128)S(1)} %get-tuple-element.18), channel_id=1, source_target_pairs={{0,4},{4,0},{1,5},{5,1},{2,6},{6,2},{3,7},{7,3},{8,12},{12,8},{9,1... | collective-permute-start | bytes 98312 | tf_op jit(solution)/shard_map/ppermute | solution.py:20
  64.0 3.9 %collective-permute-start.6 = (f32[1,1,64,128]{3,2,1,0:T(8,128)S(1)}, f32[1,1,64,128]{3,2,1,0:T(8,128)S(1)}, u32[]{:S(2)}, u32[]{:S(2)}) collective-permute-start(f32[1,1,64,128]{3,2,1,0:T(8,128)S(1)} %get-tuple-element.17), channel_id=1, source_target_pairs={{4,0},{0,4},{5,1},{1,5},{6,2},{2,6},{7,3},{3,7},{12,8},{8,12},{13,... | collective-permute-start | bytes 98312 | tf_op jit(solution)/shard_map/ppermute | solution.py:21
  68.2 5.6 %collective-permute-start.9 = (f32[1,32,1,128]{3,2,1,0:T(1,128)S(1)}, f32[1,32,1,128]{3,2,1,0:T(1,128)S(1)}, u32[]{:S(2)}, u32[]{:S(2)}) collective-permute-start(f32[1,32,1,128]{3,2,1,0:T(1,128)S(1)} %get-tuple-element.16), channel_id=1, source_target_pairs={{0,1},{1,2},{2,3},{3,0},{4,5},{5,6},{6,7},{7,4},{8,9},{9,10},{10,1... | collective-permute-start | bytes 49160 | tf_op jit(solution)/shard_map/ppermute | solution.py:20
  69.5 4.3 %collective-permute-start.8 = (f32[1,32,1,128]{3,2,1,0:T(1,128)S(1)}, f32[1,32,1,128]{3,2,1,0:T(1,128)S(1)}, u32[]{:S(2)}, u32[]{:S(2)}) collective-permute-start(f32[1,32,1,128]{3,2,1,0:T(1,128)S(1)} %get-tuple-element.15), channel_id=1, source_target_pairs={{1,0},{2,1},{3,2},{0,3},{5,4},{6,5},{7,6},{4,7},{9,8},{10,9},{11,1... | collective-permute-start | bytes 49160 | tf_op jit(solution)/shard_map/ppermute | solution.py:21
  74.2 1.7 copy-start.5
  77.5 5.3 %collective-permute-start.11 = (f32[1,32,64,1]{2,1,3,0:T(8,128)S(1)}, f32[1,32,64,1]{2,1,3,0:T(8,128)S(1)}, u32[]{:S(2)}, u32[]{:S(2)}) collective-permute-start(f32[1,32,64,1]{2,1,3,0:T(8,128)S(1)} %copy.55), channel_id=1, source_target_pairs={{0,8},{8,16},{16,24},{1,9},{9,17},{17,25},{2,10},{10,18},{18,26},{... | collective-permute-start | bytes 24584 | tf_op jit(solution)/shard_map/ppermute | solution.py:20
  81.2 5.7 %collective-permute-start.10 = (f32[1,32,64,1]{2,1,3,0:T(8,128)S(1)}, f32[1,32,64,1]{2,1,3,0:T(8,128)S(1)}, u32[]{:S(2)}, u32[]{:S(2)}) collective-permute-start(f32[1,32,64,1]{2,1,3,0:T(8,128)S(1)} %copy.53), channel_id=1, source_target_pairs={{8,0},{16,8},{24,16},{9,1},{17,9},{25,17},{10,2},{18,10},{26,18},{... | collective-permute-start | bytes 24584 | tf_op jit(solution)/shard_map/ppermute | solution.py:21
  128.0 0.7 copy-start.16
Sparse Core Ops, SparseCore 0:
  132.3 46.7 reduce-scatter.1
where the time goes:
time: 187 us; the launch traced here: 186 us
  local copies, waits for them, and re-layouts  61.8 us (33%)
  waiting for transfers between devices  61.7 us (33%)
  starting transfers between devices  19.4 us (10%)
  matrix products  17.1 us (9%)
  between operations  14.4 us (8%)
  other arithmetic  11.5 us (6%)
    reduce_scatter x1, waiting for transfers between devices, per_device(): lax.psum_scatter(jnp.einsum('cbs,csx->cbx', onehot, values, precision=lax...  46.9 us
    reshape x3, local copies, waits for them, and re-layouts, per_device(): elements = advected.astype(jnp.bfloat16).reshape(shape[0], 8, shape[2], 8...  19.9 us
    transpose x1, local copies, waits for them, and re-layouts, per_device(): elements = advected.astype(jnp.bfloat16).reshape(shape[0], 8, shape[2], 8...  10.5 us
    ppermute x6, starting transfers between devices, padded(): before = lax.ppermute(last, axis, up)  10.3 us
    ppermute x6, starting transfers between devices, padded(): after = lax.ppermute(initial, axis, down)  9 us
    slice x7, local copies, waits for them, and re-layouts, padded(): initial = lax.slice_in_dim(shard, 0, width, axis=dim)  8.54 us
    ppermute x6, waiting for transfers between devices, padded(): before = lax.ppermute(last, axis, up)  7.94 us
    ppermute x6, waiting for transfers between devices, padded(): after = lax.ppermute(initial, axis, down)  6.88 us
  transfers between devices with their start and end apart: 13, of which 9 were waited for; matrix products, arithmetic and copies ran while one was open for 4% of the time, Pallas kernels for 0%

commit v1 on v0

v1 whole, which is shorter than its diff:
```python
import functools

import jax
import jax.numpy as jnp
import numpy as np
from jax import lax
from jax.experimental import pallas as pl
from jax.experimental.pallas import tpu as pltpu
from jax.sharding import PartitionSpec as P

NBLK = 1024
F32 = jnp.float32
BF16 = jnp.bfloat16
VMEM = pl.BlockSpec(memory_space=pltpu.VMEM)
time_step = 0.01


def legendre_seven(points):
    previous = points * 0.0 + 1.0
    current = points * 1.0
    for order in range(1, 7):
        following = ((2 * order + 1) * points * current - order * previous) / (order + 1)
        previous = current
        current = following
    return current


def gll_derivative():
    degree = 7
    gll_nodes = np.array(
        [
            -1.0,
            -0.8717401485096066,
            -0.5917001814331423,
            -0.2092992179024789,
            0.2092992179024789,
            0.5917001814331423,
            0.8717401485096066,
            1.0,
        ]
    )
    values = legendre_seven(gll_nodes)
    derivative = np.zeros((degree + 1, degree + 1))
    for target in range(degree + 1):
        for source in range(degree + 1):
            if target != source:
                derivative[target, source] = values[target] / (
                    values[source] * (gll_nodes[target] - gll_nodes[source])
                )
    derivative[0, 0] = -degree * (degree + 1) / 4.0
    derivative[degree, degree] = degree * (degree + 1) / 4.0
    return derivative


def split_two(table):
    high = table.astype(np.float32).astype(BF16)
    low = (table - high.astype(np.float64)).astype(np.float32).astype(BF16)
    return high, low


def derivative_tables():
    derivative = gll_derivative()
    eye = np.eye(8)
    rows = np.concatenate([np.kron(derivative, eye), np.kron(eye, derivative)], axis=0)
    high, low = split_two(rows)
    row_table = np.concatenate([high, high, low], axis=1)
    lanes = np.kron(np.eye(16), derivative.T)
    high, low = split_two(lanes)
    lane_table = np.concatenate(
        [
            np.concatenate([high, low], axis=1),
            np.concatenate([high, np.zeros_like(high)], axis=1),
        ],
        axis=0,
    )
    return jnp.asarray(row_table), jnp.asarray(lane_table)


def lane_ids(shape):
    return lax.broadcasted_iota(jnp.int32, shape, len(shape) - 1)


def convect_pair(fields, row_table, lane_table):
    highs = [f.astype(BF16) for f in fields]
    lows = [(f - h.astype(F32)).astype(BF16) for f, h in zip(fields, highs)]
    high = jnp.concatenate(highs, axis=1)
    low = jnp.concatenate(lows, axis=1)
    stacked = jnp.concatenate([high, low, high], axis=0)
    by_rows = jnp.dot(row_table, stacked, preferred_element_type=F32)
    out = []
    for n in range(2):
        both = jnp.concatenate([highs[n], lows[n]], axis=1)
        by_lanes = jnp.dot(both, lane_table, preferred_element_type=F32)
        out.append(
            (
                by_rows[:64, 128 * n : 128 * n + 128],
                by_rows[64:, 128 * n : 128 * n + 128],
                by_lanes[:, :128] + by_lanes[:, 128:],
            )
        )
    return out


def join_lanes(g):
    lane = lane_ids(g.shape)
    node = lane & 7
    last = (node == 7) & (lane != 127)
    first = (node == 0) & (lane != 0)
    other = jnp.where(
        last, pltpu.roll(g, 127, 1), jnp.where(first, pltpu.roll(g, 1, 1), 0.0)
    )
    return g + other


def join_local(s_ref, count):
    for b in range(7):
        total = s_ref[:, 8 * b + 7, :] + s_ref[:, 8 * b + 8, :]
        s_ref[:, 8 * b + 7, :] = total
        s_ref[:, 8 * b + 8, :] = total
    for f in range(count):
        for a in range(3):
            at = 32 * f + 8 * a + 7
            total = s_ref[at] + s_ref[at + 1]
            s_ref[at] = total
            s_ref[at + 1] = total


def axial_faces(s_ref, x_ref, count):
    for f in range(count):
        x_ref[0, f] = s_ref[32 * f + 31]
        x_ref[1, f] = s_ref[32 * f]


def first_kernel(scalar_ref, velocity_ref, mass_ref, row_ref, lane_ref, s_ref, x_ref):
    row_table = row_ref[...]
    lane_table = lane_ref[...]

    def body(a, carry):
        at = pl.ds(pl.multiple_of(a * 8, 8), 8)
        for pair in range(4):
            spans = [slice(16 * pair + 8 * n, 16 * pair + 8 * n + 8) for n in range(2)]
            fields = [scalar_ref[at, s, :].reshape(64, 128) for s in spans]
            slopes = convect_pair(fields, row_table, lane_table)
            for s, (axial, azimuth, radius) in zip(spans, slopes):
                v = [velocity_ref[n, at, s, :].reshape(64, 128) for n in range(3)]
                mass = mass_ref[at, s, :].reshape(64, 128)
                g = mass * (v[0] * axial + v[1] * azimuth + v[2] * radius)
                s_ref[at, s, :] = join_lanes(g).reshape(8, 8, 128)
                s_ref[pl.ds(pl.multiple_of(a * 8 + 32, 8), 8), s, :] = join_lanes(mass).reshape(
                    8, 8, 128
                )
        return carry

    lax.fori_loop(0, 4, body, 0)
    join_local(s_ref, 2)
    axial_faces(s_ref, x_ref, 2)


def axial_kernel(count, s_in, x_ref, s_ref, up_ref, down_ref):
    for f in range(count):
        s_ref[32 * f] = s_in[32 * f] + x_ref[0, f]
        s_ref[32 * f + 31] = s_in[32 * f + 31] + x_ref[1, f]
    up_ref[...] = s_ref[:, 63, :]
    down_ref[...] = s_ref[:, 0, :]


def azimuth_kernel(count, s_in, first_ref, last_ref, s_ref, z_ref):
    s_ref[:, 0, :] = s_in[:, 0, :] + first_ref[...]
    s_ref[:, 63, :] = s_in[:, 63, :] + last_ref[...]
    slot = ((lane_ids((8, 128)) + 1) >> 1) & 63

    def body(q, carry):
        packed = jnp.zeros((8, 128), F32)
        for i in range(8):
            for b in range(8):
                u = 8 * i + b
                block = s_ref[8 * q + i, 8 * b : 8 * b + 8, :]
                if u:
                    block = pltpu.roll(block, 2 * u, 1)
                packed = jnp.where(slot == u, block, packed)
        z_ref[q] = packed
        return carry

    lax.fori_loop(0, 4 * count, body, 0)


def merged(left, right):
    lane = lane_ids(left.shape)
    return jnp.where((lane & 1) == 0, pltpu.roll(left, 1, 1), pltpu.roll(right, 127, 1))


def unpacked(packed, b):
    lane = lane_ids((8, 128))
    ends = (lane == 0) | (lane == 127)
    rows = []
    for i in range(8):
        u = 8 * i + b
        moved = pltpu.roll(packed, (128 - 2 * u) % 128, 1) if u else packed
        rows.append(jnp.where(ends, moved, 0.0))
    return jnp.concatenate(rows, axis=0)


def second_kernel(
    s_ref, left_ref, right_ref, scalar_ref, velocity_ref, mass_ref, row_ref, lane_ref,
    g_ref, x_ref, base_ref, half_ref,
):
    row_table = row_ref[...]
    lane_table = lane_ref[...]

    def body(a, carry):
        at = pl.ds(pl.multiple_of(a * 8, 8), 8)
        at_mass = pl.ds(pl.multiple_of(a * 8 + 32, 8), 8)
        radial_g = merged(left_ref[a], right_ref[a])
        radial_m = merged(left_ref[a + 4], right_ref[a + 4])
        for pair in range(4):
            spans = [slice(16 * pair + 8 * n, 16 * pair + 8 * n + 8) for n in range(2)]
            fields = []
            for n, s in enumerate(spans):
                b = 2 * pair + n
                g = s_ref[at, s, :].reshape(64, 128) + unpacked(radial_g, b)
                m = s_ref[at_mass, s, :].reshape(64, 128) + unpacked(radial_m, b)
                scale = time_step / m
                scalar = scalar_ref[at, s, :].reshape(64, 128)
                first = scalar - scale * g
                base_ref[at, s, :] = (0.5 * (scalar + first)).reshape(8, 8, 128)
                half_ref[at, s, :] = (0.5 * scale).reshape(8, 8, 128)
                fields.append(first)
            slopes = convect_pair(fields, row_table, lane_table)
            for s, (axial, azimuth, radius) in zip(spans, slopes):
                v = [velocity_ref[n, at, s, :].reshape(64, 128) for n in range(3)]
                mass = mass_ref[at, s, :].reshape(64, 128)
                g = mass * (v[0] * axial + v[1] * azimuth + v[2] * radius)
                g_ref[at, s, :] = join_lanes(g).reshape(8, 8, 128)
        return carry

    lax.fori_loop(0, 4, body, 0)
    join_local(g_ref, 1)
    axial_faces(g_ref, x_ref, 1)


def weight_kernel(weight_ref, out_ref):
    row = lax.broadcasted_iota(jnp.int32, (512, 512), 0)
    col = lax.broadcasted_iota(jnp.int32, (512, 512), 1)
    source = (row & 63) * 8 + (row >> 6)
    order = jnp.where(col == source, 1.0, 0.0).astype(BF16)
    for m in range(8):
        out_ref[m] = jnp.dot(order, weight_ref[m], preferred_element_type=F32).astype(BF16)


def render_kernel(
    g_ref, left_ref, right_ref, base_ref, half_ref, weight_ref, cut_ref, block_ref,
    advected_ref, payload_ref, turned_ref, element_ref,
):
    def body(a, carry):
        at = pl.ds(pl.multiple_of(a * 8, 8), 8)
        radial = merged(left_ref[a], right_ref[a])
        for pair in range(4):
            blocks = []
            for n in range(2):
                b = 2 * pair + n
                s = slice(8 * b, 8 * b + 8)
                g = g_ref[at, s, :].reshape(64, 128) + unpacked(radial, b)
                advected = base_ref[at, s, :].reshape(64, 128) - half_ref[at, s, :].reshape(
                    64, 128
                ) * g
                advected_ref[at, s, :] = advected.reshape(8, 8, 128)
                blocks.append(advected.astype(BF16).astype(F32))
            p = 4 * a + pair
            turned_ref[p] = jnp.concatenate(blocks, axis=0).T
            low_half = lane_ids((16, 128)) < 64
            top = pl.ds(pl.multiple_of(p * 32, 32), 16)
            bottom = pl.ds(pl.multiple_of(p * 32 + 16, 16), 16)
            for k in range(0, 8, 2):
                even = turned_ref[p, pl.ds(k, 16, stride=8), :]
                odd = turned_ref[p, pl.ds(k + 1, 16, stride=8), :]
                columns = slice(64 * k, 64 * k + 128)
                element_ref[top, columns] = jnp.where(
                    low_half, even, pltpu.roll(odd, 64, 1)
                ).astype(BF16)
                element_ref[bottom, columns] = jnp.where(
                    low_half, pltpu.roll(even, 64, 1), odd
                ).astype(BF16)
        return carry

    lax.fori_loop(0, 4, body, 0)
    cut = cut_ref[...].astype(F32).T
    lane = lane_ids((128, 512))
    blocks = block_ref[...]
    sub = lax.broadcasted_iota(jnp.int32, (16, 128), 0)
    for m in range(8):
        onehot = jnp.where(lane == cut[:, m : m + 1].astype(jnp.int32), 1.0, 0.0).astype(BF16)
        picked = jnp.dot(onehot, element_ref[...], preferred_element_type=F32).astype(BF16)
        values = jnp.dot(picked, weight_ref[m], preferred_element_type=F32)
        payload_ref[m // 2, m % 2, :128, :] = values.astype(BF16)
        ids = blocks[m : m + 1, :]
        tail = jnp.where(sub == 0, ids >> 5, jnp.where(sub == 1, ids & 31, 0))
        payload_ref[m // 2, m % 2, 128:, :] = tail.astype(F32).astype(BF16)


def image_kernel(payload_ref, image_ref):
    sources = payload_ref.shape[0]
    for m in range(2):
        ids, values = [], []
        for d in range(sources):
            tail = payload_ref[d, m, 128:, :].astype(F32).astype(jnp.int32)
            ids.append(tail[0:1, :] * 32 + tail[1:2, :])
            values.append(payload_ref[d, m, :128, :])
        ids = jnp.concatenate(ids, axis=1)
        values = jnp.concatenate(values, axis=0)
        for chunk in range(4):
            row = lax.broadcasted_iota(jnp.int32, (256, 128 * sources), 0) + 256 * chunk
            onehot = jnp.where(row == ids, 1.0, 0.0).astype(BF16)
            image_ref[m, 256 * chunk : 256 * chunk + 256, :] = jnp.dot(
                onehot, values, preferred_element_type=F32
            )


def call(kernel, out_shape, flops=10**7, size=10**6, **options):
    return pl.pallas_call(
        kernel,
        out_shape=out_shape,
        compiler_params=pltpu.CompilerParams(vmem_limit_bytes=24 * 2**20),
        cost_estimate=pl.CostEstimate(flops=flops, bytes_accessed=size, transcendentals=0),
        **options,
    )


def shape_of(*shape, dtype=F32):
    return jax.ShapeDtypeStruct(shape, dtype)


def ring(axis, wrap):
    count = lax.axis_size(axis)
    up = [(i, (i + 1) % count) for i in range(count if wrap else count - 1)]
    return up, [(j, i) for i, j in up]


def exchange(s, x, count):
    up, down = ring("ex", True)
    if lax.axis_size("ex") == 2:
        received = lax.ppermute(x, "ex", up)
    else:
        received = jnp.stack([lax.ppermute(x[0], "ex", up), lax.ppermute(x[1], "ex", down)])
    rows = 32 * count
    s, to_up, to_down = call(
        functools.partial(axial_kernel, count),
        (shape_of(*s.shape), shape_of(rows, 128), shape_of(rows, 128)),
        input_output_aliases={0: 0},
    )(s, received)
    up, down = ring("ey", True)
    first = lax.ppermute(to_up, "ey", up)
    last = lax.ppermute(to_down, "ey", down)
    s, z = call(
        functools.partial(azimuth_kernel, count),
        (shape_of(*s.shape), shape_of(4 * count, 8, 128)),
        input_output_aliases={0: 0},
    )(s, first, last)
    up, down = ring("cam", False)
    return s, lax.ppermute(z, "cam", up), lax.ppermute(z, "cam", down)


def per_device(scalar, velocity, lumped_mass, pixel_weights, cut_element, pixel_block):
    shape = scalar.shape
    flat = (32, 64, 128)
    scalar = scalar.reshape(flat)
    velocity = velocity.reshape((3,) + flat)
    mass = lumped_mass.reshape(flat)
    row_table, lane_table = derivative_tables()
    n_cam = lax.axis_size("cam")

    weights = call(weight_kernel, shape_of(8, 512, 128, dtype=BF16))(pixel_weights)
    s, x = call(first_kernel, (shape_of(64, 64, 128), shape_of(2, 2, 64, 128)))(
        scalar, velocity, mass, row_table, lane_table
    )
    s, left, right = exchange(s, x, 2)
    g, x, base, half = call(
        second_kernel,
        (shape_of(*flat), shape_of(2, 1, 64, 128), shape_of(*flat), shape_of(*flat)),
    )(s, left, right, scalar, velocity, mass, row_table, lane_table)
    g, left, right = exchange(g, x, 1)
    advected, payload = call(
        render_kernel,
        (shape_of(*flat), shape_of(n_cam, 2, 144, 128, dtype=BF16)),
        scratch_shapes=[pltpu.VMEM((16, 128, 128), F32), pltpu.VMEM((512, 512), BF16)],
    )(g, left, right, base, half, weights, cut_element, pixel_block)
    payload = lax.all_to_all(payload, "cam", 0, 0)
    images = call(image_kernel, shape_of(2, NBLK, 128))(payload)
    return (advected.reshape(shape), images)


def solution(mesh):
    placed = (
        P("ex", None, "ey", None, "cam"),
        P(None, "ex", None, "ey", None, "cam"),
        P("ex", None, "ey", None, "cam"),
        P(),
        P(None, ("cam", "ex", "ey")),
        P(None, ("cam", "ex", "ey")),
    )
    return jax.shard_map(
        per_device,
        mesh=mesh,
        in_specs=placed,
        out_specs=(P("ex", None, "ey", None, "cam"), P("cam", ("ex", "ey"), None)),
        check_vma=False,
    )
```

time: 187 us -> 65.8 us (0.35)
  local copies, waits for them, and re-layouts: 61.8 us -> 6.09 us
  waiting for transfers between devices: 61.7 us -> 15.9 us
  matrix products: 17.1 us -> 0 us
  Pallas kernels: 0 us -> 14.1 us
  between operations: 14.4 us -> 0.77 us
  other arithmetic: 11.5 us -> 0 us
  blocking collectives: 0 us -> 9.93 us
    reduce_scatter x1 -> x0, waiting for transfers between devices: 46.9 us -> none  [per_device(): lax.psum_scatter(jnp.einsum('cbs,csx->cbx', onehot, values, precision=lax...]
    reshape x3 -> x0, local copies, waits for them, and re-layouts: 19.9 us -> none  [per_device(): elements = advected.astype(jnp.bfloat16).reshape(shape[0], 8, shape[2], 8...]
    dot_general x8 -> x0, matrix products: 17.1 us -> none  [the longest x2 6.32 us: convect(): jnp.einsum('pi,aibjz->apbjz', derivative, field, precision=lax.Precision....]
    slice x10 -> x0, local copies, waits for them, and re-layouts: 16.1 us -> none  [the longest x7 8.54 us: padded(): initial = lax.slice_in_dim(shard, 0, width, axis=dim)]
    pallas_call x0 -> x9, Pallas kernels: none -> 14.1 us  [the longest x1 4.09 us: per_device(): call(render_kernel, (shape_of(*flat), shape_of(n_cam, 2, 144, 128, dtype=...]
    transpose x1 -> x0, local copies, waits for them, and re-layouts: 10.5 us -> none  [per_device(): elements = advected.astype(jnp.bfloat16).reshape(shape[0], 8, shape[2], 8...]
    all_to_all x0 -> x1, blocking collectives: none -> 9.93 us  [per_device(): payload = lax.all_to_all(payload, 'cam', 0, 0)]
    ppermute x4 -> x0, local copies, waits for them, and re-layouts: 6.85 us -> none  [the longest x2 3.43 us: padded(): before = lax.ppermute(last, axis, up)]
  transfers between devices with their start and end apart: 13 -> 10, of which waited for: 9 -> 7; matrix products, arithmetic and copies ran while one was open for 4% -> 0% of each run, Pallas kernels for 0% -> 2%
where the time goes in v1:
time: 65.8 us; the launch traced here: 65.4 us
  starting transfers between devices  18.7 us (28%)
  waiting for transfers between devices  15.9 us (24%)
  Pallas kernels  14.1 us (21%)
  blocking collectives  9.93 us (15%)
  local copies, waits for them, and re-layouts  6.09 us (9%)
  between operations  0.77 us (1%)
    all_to_all x1, blocking collectives, per_device(): payload = lax.all_to_all(payload, 'cam', 0, 0)  9.93 us
    ppermute x2, waiting for transfers between devices, exchange(): received = lax.ppermute(x, 'ex', up)  6.27 us
    ppermute x4, starting transfers between devices, exchange(): return (s, lax.ppermute(z, 'cam', up), lax.ppermute(z, 'cam', down))  6.26 us
    unnamed x18, local copies, waits for them, and re-layouts  6.09 us
    ppermute x4, waiting for transfers between devices, exchange(): return (s, lax.ppermute(z, 'cam', up), lax.ppermute(z, 'cam', down))  5.69 us
    ppermute x2, starting transfers between devices, exchange(): last = lax.ppermute(to_down, 'ey', down)  4.69 us
    ppermute x2, starting transfers between devices, exchange(): received = lax.ppermute(x, 'ex', up)  4.56 us
    pallas_call x1, Pallas kernels, per_device(): call(render_kernel, (shape_of(*flat), shape_of(n_cam, 2, 144, 128, dtype=...  4.09 us
  transfers between devices with their start and end apart: 10, of which 7 were waited for; matrix products, arithmetic and copies ran while one was open for 0% of the time, Pallas kernels for 2%

profile of v1, /device:TPU:0, one launch (start us, length us, event | category | flops | bytes accessed | tf_op | source)
XLA Modules:
  0.0 65.4 jit_solution(15335027344950918746)
XLA Ops:
  0.6 0.0 copy-start
  0.6 1.9 %copy-done = f32[3,4,8,8,8,128]{5,4,3,2,1,0:T(8,128)S(1)} copy-done((f32[3,4,8,8,8,128]{5,4,3,2,1,0:T(8,128)S(1)}, f32[3,4,8,8,8,128]{5,4,3,2,1,0:T(8,128)}, u32[]{:S(2)}) %copy-start) | copy-done | bytes 3145752
  2.5 0.0 copy-start.2
  2.5 1.2 %copy-done.2 = f32[4,8,8,8,128]{4,3,2,1,0:T(8,128)S(1)} copy-done((f32[4,8,8,8,128]{4,3,2,1,0:T(8,128)S(1)}, f32[4,8,8,8,128]{4,3,2,1,0:T(8,128)}, u32[]{:S(2)}) %copy-start.2) | copy-done | bytes 1048600
  3.7 0.0 copy-start.3
  3.7 1.2 %copy-done.3 = f32[4,8,8,8,128]{4,3,2,1,0:T(8,128)S(1)} copy-done((f32[4,8,8,8,128]{4,3,2,1,0:T(8,128)S(1)}, f32[4,8,8,8,128]{4,3,2,1,0:T(8,128)}, u32[]{:S(2)}) %copy-start.3) | copy-done | bytes 1048600
  5.0 0.0 copy-start.5
  5.0 0.9 %copy-done.5 = bf16[256,256]{1,0:T(8,128)(2,1)S(1)} copy-done((bf16[256,256]{1,0:T(8,128)(2,1)S(1)}, bf16[256,256]{1,0:T(8,128)(2,1)}, u32[]{:S(2)}) %copy-start.5) | copy-done | bytes 131096
  5.9 0.0 copy-start.6
  5.9 0.8 %copy-done.6 = bf16[128,192]{1,0:T(8,128)(2,1)S(1)} copy-done((bf16[128,192]{1,0:T(8,128)(2,1)S(1)}, bf16[128,192]{1,0:T(8,128)(2,1)}, u32[]{:S(2)}) %copy-start.6) | copy-done | bytes 49176
  6.7 2.3 %shard_map.95 = (f32[64,64,128]{2,1,0:T(8,128)S(1)}, f32[2,2,64,128]{3,2,1,0:T(8,128)S(1)}) custom-call(f32[32,64,128]{2,1,0:T(8,128)S(1)} %bitcast.6, f32[3,32,64,128]{3,2,1,0:T(8,128)S(1)} %bitcast.4, f32[32,64,128]{2,1,0:T(8,128)S(1)} %bitcast.8, bf16[128,192]{1,0:T(8,128)(2,1)S(1)} %copy-done.6, bf16[256,256]{1,0:T(8,128)(2,1)S(1)} %copy-done.5), custom_call_target="tpu_custom_call" | custom-call | flops 10000000 | bytes 1000000 | tf_op jit(solution)/shard_map/pallas_call | solution.py:372
  9.0 3.0 %collective-permute-start = (f32[2,2,64,128]{3,2,1,0:T(8,128)S(1)}, f32[2,2,64,128]{3,2,1,0:T(8,128)S(1)}, u32[]{:S(2)}, u32[]{:S(2)}) collective-permute-start(f32[2,2,64,128]{3,2,1,0:T(8,128)S(1)} %get-tuple-element.21), channel_id=1, source_target_pairs={{0,4},{4,0},{1,5},{5,1},{2,6},{6,2},{3,7},{7,3},{8,12},{12,8},{9,1... | collective-permute-start | bytes 393224 | tf_op jit(solution)/shard_map/ppermute | solution.py:341
  12.0 3.5 %collective-permute-done.x_ref = f32[2,2,64,128]{3,2,1,0:T(8,128)S(1)} collective-permute-done((f32[2,2,64,128]{3,2,1,0:T(8,128)S(1)}, f32[2,2,64,128]{3,2,1,0:T(8,128)S(1)}, u32[]{:S(2)}, u32[]{:S(2)}) %collective-permute-start) | collective-permute-done | bytes 131104 | tf_op jit(solution)/shard_map/ppermute | solution.py:341
  15.5 0.0 copy-start.1
  15.5 0.1 shard_map.96
  15.6 1.9 %collective-permute-start.1 = (f32[64,128]{1,0:T(8,128)S(1)}, f32[64,128]{1,0:T(8,128)S(1)}, u32[]{:S(2)}, u32[]{:S(2)}) collective-permute-start(f32[64,128]{1,0:T(8,128)S(1)} %get-tuple-element.23), channel_id=1, source_target_pairs={{0,1},{1,2},{2,3},{3,0},{4,5},{5,6},{6,7},{7,4},{8,9},{9,10},{10,1... | collective-permute-start | bytes 98312 | tf_op jit(solution)/shard_map/ppermute | solution.py:351
  17.5 2.1 %collective-permute-start.2 = (f32[64,128]{1,0:T(8,128)S(1)}, f32[64,128]{1,0:T(8,128)S(1)}, u32[]{:S(2)}, u32[]{:S(2)}) collective-permute-start(f32[64,128]{1,0:T(8,128)S(1)} %get-tuple-element.24), channel_id=1, source_target_pairs={{1,0},{2,1},{3,2},{0,3},{5,4},{6,5},{7,6},{4,7},{9,8},{10,9},{11,1... | collective-permute-start | bytes 98312 | tf_op jit(solution)/shard_map/ppermute | solution.py:352
  19.6 2.0 %collective-permute-done.1.first_ref = f32[64,128]{1,0:T(8,128)S(1)} collective-permute-done((f32[64,128]{1,0:T(8,128)S(1)}, f32[64,128]{1,0:T(8,128)S(1)}, u32[]{:S(2)}, u32[]{:S(2)}) %collective-permute-start.1) | collective-permute-done | bytes 32800 | tf_op jit(solution)/shard_map/ppermute | solution.py:351
  21.6 0.2 collective-permute-done.2.last_ref
  21.8 1.3 %shard_map.97 = (f32[64,64,128]{2,1,0:T(8,128)S(1)}, f32[8,8,128]{2,1,0:T(8,128)S(1)}) custom-call(f32[64,64,128]{2,1,0:T(8,128)S(1)} %get-tuple-element.22.s_in, f32[64,128]{1,0:T(8,128)S(1)} %collective-permute-done.1.first_ref, f32[64,128]{1,0:T(8,128)S(1)} %collective-permute-done.2.last_ref), custom_call_target="tpu_custom_call", output_to_operand_aliasing={{0}: (0, {})} | custom-call | flops 10000000 | bytes 1000000 | tf_op jit(solution)/shard_map/pallas_call | solution.py:353
  23.1 1.3 %collective-permute-start.3 = (f32[8,8,128]{2,1,0:T(8,128)S(1)}, f32[8,8,128]{2,1,0:T(8,128)S(1)}, u32[]{:S(2)}, u32[]{:S(2)}) collective-permute-start(f32[8,8,128]{2,1,0:T(8,128)S(1)} %get-tuple-element.26), channel_id=1, source_target_pairs={{0,8},{8,16},{16,24},{1,9},{9,17},{17,25},{2,10},{10,18},{18,26},{... | collective-permute-start | bytes 98312 | tf_op jit(solution)/shard_map/ppermute | solution.py:359
  24.4 1.3 %collective-permute-start.4 = (f32[8,8,128]{2,1,0:T(8,128)S(1)}, f32[8,8,128]{2,1,0:T(8,128)S(1)}, u32[]{:S(2)}, u32[]{:S(2)}) collective-permute-start(f32[8,8,128]{2,1,0:T(8,128)S(1)} %get-tuple-element.26), channel_id=1, source_target_pairs={{8,0},{16,8},{24,16},{9,1},{17,9},{25,17},{10,2},{18,10},{26,18},{... | collective-permute-start | bytes 98312 | tf_op jit(solution)/shard_map/ppermute | solution.py:359
  25.7 0.0 collective-permute-done.3.left_ref
  25.7 3.5 %collective-permute-done.4.right_ref = f32[8,8,128]{2,1,0:T(8,128)S(1)} collective-permute-done((f32[8,8,128]{2,1,0:T(8,128)S(1)}, f32[8,8,128]{2,1,0:T(8,128)S(1)}, u32[]{:S(2)}, u32[]{:S(2)}) %collective-permute-start.4) | collective-permute-done | bytes 32800 | tf_op jit(solution)/shard_map/ppermute | solution.py:359
  29.2 0.0 copy-done.1
  29.2 2.8 %shard_map.98 = (f32[32,64,128]{2,1,0:T(8,128)S(1)}, f32[2,1,64,128]{3,2,1,0:T(8,128)S(1)}, f32[32,64,128]{2,1,0:T(8,128)S(1)}, f32[32,64,128]{2,1,0:T(8,128)S(1)}) custom-call(f32[64,64,128]{2,1,0:T(8,128)S(1)} %get-tuple-element.25.s_ref, f32[8,8,128]{2,1,0:T(8,128)S(1)} %collective-permute-done.3.left_ref, ...), custom_call_target="tpu_custom_call" | custom-call | flops 10000000 | bytes 1000000 | tf_op jit(solution)/shard_map/pallas_call | solution.py:376
  32.0 0.0 copy-start.4
  32.0 1.6 %collective-permute-start.5 = (f32[2,1,64,128]{3,2,1,0:T(8,128)S(1)}, f32[2,1,64,128]{3,2,1,0:T(8,128)S(1)}, u32[]{:S(2)}, u32[]{:S(2)}) collective-permute-start(f32[2,1,64,128]{3,2,1,0:T(8,128)S(1)} %get-tuple-element.28), channel_id=1, source_target_pairs={{0,4},{4,0},{1,5},{5,1},{2,6},{6,2},{3,7},{7,3},{8,12},{12,8},{9,1... | collective-permute-start | bytes 196616 | tf_op jit(solution)/shard_map/ppermute | solution.py:341
  33.5 2.8 %collective-permute-done.5.x_ref = f32[2,1,64,128]{3,2,1,0:T(8,128)S(1)} collective-permute-done((f32[2,1,64,128]{3,2,1,0:T(8,128)S(1)}, f32[2,1,64,128]{3,2,1,0:T(8,128)S(1)}, u32[]{:S(2)}, u32[]{:S(2)}) %collective-permute-start.5) | collective-permute-done | bytes 65568 | tf_op jit(solution)/shard_map/ppermute | solution.py:341
  36.3 0.0 copy-start.7
  36.3 0.0 copy-start.8
  36.4 1.3 %collective-permute-start.6 = (f32[32,128]{1,0:T(8,128)S(1)}, f32[32,128]{1,0:T(8,128)S(1)}, u32[]{:S(2)}, u32[]{:S(2)}) collective-permute-start(f32[32,128]{1,0:T(8,128)S(1)} %get-tuple-element.30), channel_id=1, source_target_pairs={{0,1},{1,2},{2,3},{3,0},{4,5},{5,6},{6,7},{7,4},{8,9},{9,10},{10,1... | collective-permute-start | bytes 49160 | tf_op jit(solution)/shard_map/ppermute | solution.py:351
  37.6 2.6 %collective-permute-start.7 = (f32[32,128]{1,0:T(8,128)S(1)}, f32[32,128]{1,0:T(8,128)S(1)}, u32[]{:S(2)}, u32[]{:S(2)}) collective-permute-start(f32[32,128]{1,0:T(8,128)S(1)} %get-tuple-element.31), channel_id=1, source_target_pairs={{1,0},{2,1},{3,2},{0,3},{5,4},{6,5},{7,6},{4,7},{9,8},{10,9},{11,1... | collective-permute-start | bytes 49160 | tf_op jit(solution)/shard_map/ppermute | solution.py:352
  40.2 1.7 %collective-permute-done.6.first_ref = f32[32,128]{1,0:T(8,128)S(1)} collective-permute-done((f32[32,128]{1,0:T(8,128)S(1)}, f32[32,128]{1,0:T(8,128)S(1)}, u32[]{:S(2)}, u32[]{:S(2)}) %collective-permute-start.6) | collective-permute-done | bytes 16416 | tf_op jit(solution)/shard_map/ppermute | solution.py:351
  42.0 0.0 collective-permute-done.7.last_ref
  42.0 0.6 shard_map.100
  42.6 2.4 %collective-permute-start.8 = (f32[4,8,128]{2,1,0:T(8,128)S(1)}, f32[4,8,128]{2,1,0:T(8,128)S(1)}, u32[]{:S(2)}, u32[]{:S(2)}) collective-permute-start(f32[4,8,128]{2,1,0:T(8,128)S(1)} %get-tuple-element.33), channel_id=1, source_target_pairs={{0,8},{8,16},{16,24},{1,9},{9,17},{17,25},{2,10},{10,18},{18,26},{... | collective-permute-start | bytes 49160 | tf_op jit(solution)/shard_map/ppermute | solution.py:359
  45.0 1.3 %collective-permute-start.9 = (f32[4,8,128]{2,1,0:T(8,128)S(1)}, f32[4,8,128]{2,1,0:T(8,128)S(1)}, u32[]{:S(2)}, u32[]{:S(2)}) collective-permute-start(f32[4,8,128]{2,1,0:T(8,128)S(1)} %get-tuple-element.33), channel_id=1, source_target_pairs={{8,0},{16,8},{24,16},{9,1},{17,9},{25,17},{10,2},{18,10},{26,18},{... | collective-permute-start | bytes 49160 | tf_op jit(solution)/shard_map/ppermute | solution.py:359
  46.3 0.0 copy-done.4
  46.3 1.3 %shard_map.101.weight_ref = bf16[8,512,128]{2,1,0:T(8,128)(2,1)S(1)} custom-call(bf16[8,512,128]{2,1,0:T(8,128)(2,1)S(1)} %copy-done.4), custom_call_target="tpu_custom_call" | custom-call | flops 10000000 | bytes 1000000 | tf_op jit(solution)/shard_map/pallas_call | solution.py:371
  47.6 0.0 collective-permute-done.8.left_ref
  47.6 2.1 %collective-permute-done.9.right_ref = f32[4,8,128]{2,1,0:T(8,128)S(1)} collective-permute-done((f32[4,8,128]{2,1,0:T(8,128)S(1)}, f32[4,8,128]{2,1,0:T(8,128)S(1)}, u32[]{:S(2)}, u32[]{:S(2)}) %collective-permute-start.9) | collective-permute-done | bytes 16416 | tf_op jit(solution)/shard_map/ppermute | solution.py:359
  49.7 0.0 copy-done.7
  49.7 0.0 copy-done.8
  49.7 4.1 %shard_map.102 = (f32[32,64,128]{2,1,0:T(8,128)}, bf16[4,2,144,128]{3,2,1,0:T(8,128)(2,1)S(1)}) custom-call(f32[32,64,128]{2,1,0:T(8,128)S(1)} %get-tuple-element.32.g_ref, f32[4,8,128]{2,1,0:T(8,128)S(1)} %collective-permute-done.8.left_ref, f32[4,8,128]{2,1,0:T(8,128)S(1)} %collective-permute-done.9.right_ref, ...), custom_call_target="tpu_custom_call" | custom-call | flops 10000000 | bytes 1000000 | tf_op jit(solution)/shard_map/pallas_call | solution.py:381
  53.8 9.9 %all_to_all.5.payload_ref = bf16[4,2,144,128]{3,2,1,0:T(8,128)(2,1)S(1)} all-to-all(bf16[4,2,144,128]{3,2,1,0:T(8,128)(2,1)S(1)} %get-tuple-element.37), channel_id=1, replica_groups=mesh['cam'=4,'ex'=2,'ey'=4] {'cam'}, dimensions={0} | all-to-all | bytes 589824 | tf_op jit(solution)/shard_map/all_to_all | solution.py:386
  63.8 1.7 %shard_map.103 = f32[2,1024,128]{2,1,0:T(8,128)} custom-call(bf16[4,2,144,128]{3,2,1,0:T(8,128)(2,1)S(1)} %all_to_all.5.payload_ref), custom_call_target="tpu_custom_call" | custom-call | flops 10000000 | bytes 1000000 | tf_op jit(solution)/shard_map/pallas_call | solution.py:387
  (1 shorter events, 0.0 us)
Async XLA Ops:
  0.6 1.9 %copy-start = (f32[3,4,8,8,8,128]{5,4,3,2,1,0:T(8,128)S(1)}, f32[3,4,8,8,8,128]{5,4,3,2,1,0:T(8,128)}, u32[]{:S(2)}) copy-start(f32[3,4,8,8,8,128]{5,4,3,2,1,0:T(8,128)} %param.9) | copy-start | bytes 9437188
  2.5 1.2 %copy-start.2 = (f32[4,8,8,8,128]{4,3,2,1,0:T(8,128)S(1)}, f32[4,8,8,8,128]{4,3,2,1,0:T(8,128)}, u32[]{:S(2)}) copy-start(f32[4,8,8,8,128]{4,3,2,1,0:T(8,128)} %param.8) | copy-start | bytes 3145732
  3.7 1.2 %copy-start.3 = (f32[4,8,8,8,128]{4,3,2,1,0:T(8,128)S(1)}, f32[4,8,8,8,128]{4,3,2,1,0:T(8,128)}, u32[]{:S(2)}) copy-start(f32[4,8,8,8,128]{4,3,2,1,0:T(8,128)} %param.10) | copy-start | bytes 3145732
  5.0 0.9 %copy-start.5 = (bf16[256,256]{1,0:T(8,128)(2,1)S(1)}, bf16[256,256]{1,0:T(8,128)(2,1)}, u32[]{:S(2)}) copy-start(bf16[256,256]{1,0:T(8,128)(2,1)} %constant.5.clone.lane_ref) | copy-start | bytes 393220
  5.9 0.8 %copy-start.6 = (bf16[128,192]{1,0:T(8,128)(2,1)S(1)}, bf16[128,192]{1,0:T(8,128)(2,1)}, u32[]{:S(2)}) copy-start(bf16[128,192]{1,0:T(8,128)(2,1)} %constant.4.clone.row_ref) | copy-start | bytes 147460
  9.0 6.5 %collective-permute-start = (f32[2,2,64,128]{3,2,1,0:T(8,128)S(1)}, f32[2,2,64,128]{3,2,1,0:T(8,128)S(1)}, u32[]{:S(2)}, u32[]{:S(2)}) collective-permute-start(f32[2,2,64,128]{3,2,1,0:T(8,128)S(1)} %get-tuple-element.21), channel_id=1, source_target_pairs={{0,4},{4,0},{1,5},{5,1},{2,6},{6,2},{3,7},{7,3},{8,12},{12,8},{9,1... | collective-permute-start | bytes 393224 | tf_op jit(solution)/shard_map/ppermute | solution.py:341
  15.5 13.7 %copy-start.1 = (f32[3,4,8,8,8,128]{5,4,3,2,1,0:T(8,128)S(1)}, f32[3,4,8,8,8,128]{5,4,3,2,1,0:T(8,128)}, u32[]{:S(2)}) copy-start(f32[3,4,8,8,8,128]{5,4,3,2,1,0:T(8,128)} %param.9) | copy-start | bytes 9437188
  15.6 6.0 %collective-permute-start.1 = (f32[64,128]{1,0:T(8,128)S(1)}, f32[64,128]{1,0:T(8,128)S(1)}, u32[]{:S(2)}, u32[]{:S(2)}) collective-permute-start(f32[64,128]{1,0:T(8,128)S(1)} %get-tuple-element.23), channel_id=1, source_target_pairs={{0,1},{1,2},{2,3},{3,0},{4,5},{5,6},{6,7},{7,4},{8,9},{9,10},{10,1... | collective-permute-start | bytes 98312 | tf_op jit(solution)/shard_map/ppermute | solution.py:351
  17.5 4.3 %collective-permute-start.2 = (f32[64,128]{1,0:T(8,128)S(1)}, f32[64,128]{1,0:T(8,128)S(1)}, u32[]{:S(2)}, u32[]{:S(2)}) collective-permute-start(f32[64,128]{1,0:T(8,128)S(1)} %get-tuple-element.24), channel_id=1, source_target_pairs={{1,0},{2,1},{3,2},{0,3},{5,4},{6,5},{7,6},{4,7},{9,8},{10,9},{11,1... | collective-permute-start | bytes 98312 | tf_op jit(solution)/shard_map/ppermute | solution.py:352
  23.1 2.6 %collective-permute-start.3 = (f32[8,8,128]{2,1,0:T(8,128)S(1)}, f32[8,8,128]{2,1,0:T(8,128)S(1)}, u32[]{:S(2)}, u32[]{:S(2)}) collective-permute-start(f32[8,8,128]{2,1,0:T(8,128)S(1)} %get-tuple-element.26), channel_id=1, source_target_pairs={{0,8},{8,16},{16,24},{1,9},{9,17},{17,25},{2,10},{10,18},{18,26},{... | collective-permute-start | bytes 98312 | tf_op jit(solution)/shard_map/ppermute | solution.py:359
  24.4 4.9 %collective-permute-start.4 = (f32[8,8,128]{2,1,0:T(8,128)S(1)}, f32[8,8,128]{2,1,0:T(8,128)S(1)}, u32[]{:S(2)}, u32[]{:S(2)}) collective-permute-start(f32[8,8,128]{2,1,0:T(8,128)S(1)} %get-tuple-element.26), channel_id=1, source_target_pairs={{8,0},{16,8},{24,16},{9,1},{17,9},{25,17},{10,2},{18,10},{26,18},{... | collective-permute-start | bytes 98312 | tf_op jit(solution)/shard_map/ppermute | solution.py:359
  32.0 14.3 %copy-start.4 = (bf16[8,512,128]{2,1,0:T(8,128)(2,1)S(1)}, bf16[8,512,128]{2,1,0:T(8,128)(2,1)}, u32[]{:S(2)}) copy-start(bf16[8,512,128]{2,1,0:T(8,128)(2,1)} %weight_ref.1) | copy-start | bytes 3145732
  32.0 4.3 %collective-permute-start.5 = (f32[2,1,64,128]{3,2,1,0:T(8,128)S(1)}, f32[2,1,64,128]{3,2,1,0:T(8,128)S(1)}, u32[]{:S(2)}, u32[]{:S(2)}) collective-permute-start(f32[2,1,64,128]{3,2,1,0:T(8,128)S(1)} %get-tuple-element.28), channel_id=1, source_target_pairs={{0,4},{4,0},{1,5},{5,1},{2,6},{6,2},{3,7},{7,3},{8,12},{12,8},{9,1... | collective-permute-start | bytes 196616 | tf_op jit(solution)/shard_map/ppermute | solution.py:341
  36.3 13.4 %copy-start.7 = (s32[8,128]{1,0:T(8,128)S(1)}, s32[8,128]{1,0:T(8,128)}, u32[]{:S(2)}) copy-start(s32[8,128]{1,0:T(8,128)} %cut_ref.1) | copy-start | bytes 12292
  36.3 13.4 %copy-start.8 = (s32[8,128]{1,0:T(8,128)S(1)}, s32[8,128]{1,0:T(8,128)}, u32[]{:S(2)}) copy-start(s32[8,128]{1,0:T(8,128)} %block_ref.1) | copy-start | bytes 12292
  36.4 5.6 %collective-permute-start.6 = (f32[32,128]{1,0:T(8,128)S(1)}, f32[32,128]{1,0:T(8,128)S(1)}, u32[]{:S(2)}, u32[]{:S(2)}) collective-permute-start(f32[32,128]{1,0:T(8,128)S(1)} %get-tuple-element.30), channel_id=1, source_target_pairs={{0,1},{1,2},{2,3},{3,0},{4,5},{5,6},{6,7},{7,4},{8,9},{9,10},{10,1... | collective-permute-start | bytes 49160 | tf_op jit(solution)/shard_map/ppermute | solution.py:351
  37.6 4.3 %collective-permute-start.7 = (f32[32,128]{1,0:T(8,128)S(1)}, f32[32,128]{1,0:T(8,128)S(1)}, u32[]{:S(2)}, u32[]{:S(2)}) collective-permute-start(f32[32,128]{1,0:T(8,128)S(1)} %get-tuple-element.31), channel_id=1, source_target_pairs={{1,0},{2,1},{3,2},{0,3},{5,4},{6,5},{7,6},{4,7},{9,8},{10,9},{11,1... | collective-permute-start | bytes 49160 | tf_op jit(solution)/shard_map/ppermute | solution.py:352
  42.6 5.0 %collective-permute-start.8 = (f32[4,8,128]{2,1,0:T(8,128)S(1)}, f32[4,8,128]{2,1,0:T(8,128)S(1)}, u32[]{:S(2)}, u32[]{:S(2)}) collective-permute-start(f32[4,8,128]{2,1,0:T(8,128)S(1)} %get-tuple-element.33), channel_id=1, source_target_pairs={{0,8},{8,16},{16,24},{1,9},{9,17},{17,25},{2,10},{10,18},{18,26},{... | collective-permute-start | bytes 49160 | tf_op jit(solution)/shard_map/ppermute | solution.py:359
  45.0 4.7 %collective-permute-start.9 = (f32[4,8,128]{2,1,0:T(8,128)S(1)}, f32[4,8,128]{2,1,0:T(8,128)S(1)}, u32[]{:S(2)}, u32[]{:S(2)}) collective-permute-start(f32[4,8,128]{2,1,0:T(8,128)S(1)} %get-tuple-element.33), channel_id=1, source_target_pairs={{8,0},{16,8},{24,16},{9,1},{17,9},{25,17},{10,2},{18,10},{26,18},{... | collective-permute-start | bytes 49160 | tf_op jit(solution)/shard_map/ppermute | solution.py:359

commit v2 on v0

v2 whole, which is shorter than its diff:
```python
import functools

import jax
import jax.numpy as jnp
import numpy as np
from jax import lax
from jax.experimental import pallas as pl
from jax.experimental.pallas import tpu as pltpu
from jax.sharding import PartitionSpec as P

NBLK = 1024
F32 = jnp.float32
BF16 = jnp.bfloat16
VMEM = pl.BlockSpec(memory_space=pltpu.VMEM)
HBM = pl.BlockSpec(memory_space=pltpu.HBM)
time_step = 0.01


def legendre_seven(points):
    previous = points * 0.0 + 1.0
    current = points * 1.0
    for order in range(1, 7):
        following = ((2 * order + 1) * points * current - order * previous) / (order + 1)
        previous = current
        current = following
    return current


def gll_derivative():
    degree = 7
    gll_nodes = np.array(
        [
            -1.0,
            -0.8717401485096066,
            -0.5917001814331423,
            -0.2092992179024789,
            0.2092992179024789,
            0.5917001814331423,
            0.8717401485096066,
            1.0,
        ]
    )
    values = legendre_seven(gll_nodes)
    derivative = np.zeros((degree + 1, degree + 1))
    for target in range(degree + 1):
        for source in range(degree + 1):
            if target != source:
                derivative[target, source] = values[target] / (
                    values[source] * (gll_nodes[target] - gll_nodes[source])
                )
    derivative[0, 0] = -degree * (degree + 1) / 4.0
    derivative[degree, degree] = degree * (degree + 1) / 4.0
    return derivative


def split_two(table):
    high = table.astype(np.float32).astype(BF16)
    low = (table - high.astype(np.float64)).astype(np.float32).astype(BF16)
    return high, low


def derivative_tables():
    derivative = gll_derivative()
    eye = np.eye(8)
    rows = np.concatenate([np.kron(derivative, eye), np.kron(eye, derivative)], axis=0)
    high, low = split_two(rows)
    row_table = np.concatenate([high, high, low, np.zeros_like(high)], axis=1)
    high, low = split_two(np.kron(np.eye(16), derivative.T))
    lane_table = np.concatenate(
        [
            np.concatenate([high, low], axis=1),
            np.concatenate([high, np.zeros_like(high)], axis=1),
        ],
        axis=0,
    )
    swap = np.zeros((128, 128))
    for c in range(15):
        swap[8 * c + 7, 8 * c + 8] = 1.0
        swap[8 * c + 8, 8 * c + 7] = 1.0
    join_table = np.concatenate([swap, swap], axis=0).astype(np.float32).astype(BF16)
    split = [row_table[:, :128], row_table[:, 128:], lane_table[:, :128], lane_table[:, 128:]]
    return jnp.asarray(np.concatenate(split + [join_table], axis=0))


def row_table(table_ref, first=0):
    high, low = table_ref[first:128], table_ref[128 + first : 256]
    return jnp.concatenate([high, low[:, :64]], axis=1)


def lane_table(table_ref):
    return jnp.concatenate([table_ref[256:512], table_ref[512:768]], axis=1)


def join_table(table_ref):
    return table_ref[768:1024]


def lane_ids(shape):
    return lax.broadcasted_iota(jnp.int32, shape, len(shape) - 1)


def row_ids(shape):
    return lax.broadcasted_iota(jnp.int32, shape, len(shape) - 2)


def halves(value):
    high = value.astype(BF16)
    return high, (value - high.astype(F32)).astype(BF16)


def dot(a, b):
    return jnp.dot(a, b, preferred_element_type=F32)


def by_lanes(pairs, table_ref):
    rows = jnp.concatenate([jnp.concatenate(p, axis=1) for p in pairs], axis=0)
    both = dot(rows, lane_table(table_ref))
    return both[:, :128] + both[:, 128:]


def join_lanes(values, table_ref):
    rows = jnp.concatenate([jnp.concatenate(halves(v), axis=1) for v in values], axis=0)
    other = dot(rows, join_table(table_ref))
    out, at = [], 0
    for v in values:
        out.append(v + other[at : at + v.shape[0]])
        at += v.shape[0]
    return out


def join_rows(value):
    row = row_ids(value.shape)
    last = ((row & 7) == 7) & (row != 63)
    first = ((row & 7) == 0) & (row != 0)
    other = jnp.where(
        last, pltpu.roll(value, 63, 0), jnp.where(first, pltpu.roll(value, 1, 0), 0.0)
    )
    return value + other


def convect_pair(fields, velocities, masses, table_ref):
    pairs = [halves(f) for f in fields]
    high = jnp.concatenate([p[0] for p in pairs], axis=1)
    low = jnp.concatenate([p[1] for p in pairs], axis=1)
    stacked = jnp.concatenate([high, low, high], axis=0)
    rows = dot(row_table(table_ref), stacked)
    radius = by_lanes(pairs, table_ref)
    out = []
    for n in range(2):
        lanes = slice(128 * n, 128 * n + 128)
        v = velocities[n]
        slope = v[0] * rows[:64, lanes] + v[1] * rows[64:, lanes]
        out.append(masses[n] * (slope + v[2] * radius[64 * n : 64 * n + 64]))
    return out


def face_kernel(
    scalar_hbm, velocity_hbm, mass_hbm, table_hbm, x_ref, table_ref, f_ref, v_ref, m_ref, sems,
):
    copies = []

    def start(source, target):
        copy = pltpu.make_async_copy(source, target, sems.at[len(copies)])
        copy.start()
        copies.append(copy)

    last = scalar_hbm.shape[0] - 1
    start(scalar_hbm.at[pl.ds(last - 7, 8)], f_ref.at[0])
    start(scalar_hbm.at[pl.ds(0, 8)], f_ref.at[1])
    start(velocity_hbm.at[:, last], v_ref.at[0])
    start(velocity_hbm.at[:, 0], v_ref.at[1])
    start(mass_hbm.at[last], m_ref.at[0])
    start(mass_hbm.at[0], m_ref.at[1])
    start(table_hbm, table_ref)
    for copy in copies:
        copy.wait()
    derivative = gll_derivative()
    fields = [f_ref[0, 7], f_ref[1, 0]]
    pairs = [halves(f) for f in fields]
    high = jnp.concatenate([p[0] for p in pairs], axis=1)
    low = jnp.concatenate([p[1] for p in pairs], axis=1)
    azimuth = dot(row_table(table_ref, 64), jnp.concatenate([high, low, high], axis=0))
    radius = by_lanes(pairs, table_ref)
    values = []
    for n, node in enumerate((7, 0)):
        axial = f_ref[n, 0] * float(derivative[node, 0])
        for p in range(1, 8):
            axial = axial + f_ref[n, p] * float(derivative[node, p])
        slope = v_ref[n, 0] * axial + v_ref[n, 1] * azimuth[:, 128 * n : 128 * n + 128]
        values.append(m_ref[n] * (slope + v_ref[n, 2] * radius[64 * n : 64 * n + 64]))
        values.append(m_ref[n])
    for n, value in enumerate(join_lanes(values, table_ref)):
        x_ref[n // 2, n % 2] = join_rows(value)


def join_block(s_ref):
    for b in range(s_ref.shape[1] // 8 - 1):
        total = s_ref[:, 8 * b + 7, :] + s_ref[:, 8 * b + 8, :]
        s_ref[:, 8 * b + 7, :] = total
        s_ref[:, 8 * b + 8, :] = total
    join_axial(s_ref)


def join_axial(s_ref):
    for f in range(s_ref.shape[0] // 32):
        for a in range(3):
            at = 32 * f + 8 * a + 7
            total = s_ref[at] + s_ref[at + 1]
            s_ref[at] = total
            s_ref[at + 1] = total


def pack_blocks(blocks):
    slot = ((lane_ids((8, 128)) + 1) >> 1) & 63
    parts = [jnp.zeros((8, 128), F32) for _ in range(4)]
    for n, (u, block) in enumerate(blocks):
        if u:
            block = pltpu.roll(block, 2 * u, 1)
        parts[n % 4] = jnp.where(slot == u, block, parts[n % 4])
    return (parts[0] + parts[1]) + (parts[2] + parts[3])


def pack_all(s_ref, z_ref):
    def body(q, carry):
        z_ref[q] = pack_blocks(
            [
                (56 - 8 * i + b, s_ref[8 * q + i, 8 * b : 8 * b + 8, :])
                for i in range(8)
                for b in range(8)
            ]
        )
        return carry

    lax.fori_loop(0, z_ref.shape[0], body, 0)


def first_kernel(
    scalar_hbm, velocity_hbm, mass_hbm, table_ref,
    s_ref, z_ref, scalar_ref, velocity_ref, mass_ref, sems,
):
    def copies(a):
        at = pl.ds(pl.multiple_of(a * 8, 8), 8)
        return [
            pltpu.make_async_copy(scalar_hbm.at[at], scalar_ref.at[at], sems.at[0, a]),
            pltpu.make_async_copy(velocity_hbm.at[:, at], velocity_ref.at[:, at], sems.at[1, a]),
            pltpu.make_async_copy(mass_hbm.at[at], mass_ref.at[at], sems.at[2, a]),
        ]

    for a in range(4):
        for copy in copies(a):
            copy.start()

    def body(a, carry):
        for copy in copies(a):
            copy.wait()
        at = pl.ds(pl.multiple_of(a * 8, 8), 8)
        at_mass = pl.ds(pl.multiple_of(a * 8 + 32, 8), 8)
        for pair in range(4):
            spans = [slice(16 * pair + 8 * n, 16 * pair + 8 * n + 8) for n in range(2)]
            fields = [scalar_ref[at, s, :].reshape(64, 128) for s in spans]
            velocities = [
                [velocity_ref[d, at, s, :].reshape(64, 128) for d in range(3)] for s in spans
            ]
            masses = [mass_ref[at, s, :].reshape(64, 128) for s in spans]
            values = convect_pair(fields, velocities, masses, table_ref)
            joined = join_lanes(values + masses, table_ref)
            for n, s in enumerate(spans):
                s_ref[at, s, :] = joined[n].reshape(8, 8, 128)
                s_ref[at_mass, s, :] = joined[n + 2].reshape(8, 8, 128)
        return carry

    lax.fori_loop(0, 4, body, 0)
    join_block(s_ref)
    pack_all(s_ref, z_ref)


def pack_kernel(s_ref, z_ref):
    pack_all(s_ref, z_ref)


def radial_kernel(count, z_in, x_ref, z_ref):
    for f in range(count):
        spans = [slice(8 * b, 8 * b + 8) for b in range(8)]
        z_ref[4 * f] = z_in[4 * f] + pack_blocks(
            [(56 + b, x_ref[0, f, s, :]) for b, s in enumerate(spans)]
        )
        z_ref[4 * f + 1] = z_in[4 * f + 1]
        z_ref[4 * f + 2] = z_in[4 * f + 2]
        z_ref[4 * f + 3] = z_in[4 * f + 3] + pack_blocks(
            [(b, x_ref[1, f, s, :]) for b, s in enumerate(spans)]
        )


def merged(one, two, cam_count):
    me = lax.axis_index("cam")
    even = (me & 1) == 0
    left = jnp.where(even, two, one)
    right = jnp.where(even, one, two)
    left = jnp.where(me == 0, 0.0, left)
    right = jnp.where(me == cam_count - 1, 0.0, right)
    lane = lane_ids((8, 128))
    return jnp.where((lane & 1) == 0, pltpu.roll(left, 1, 1), pltpu.roll(right, 127, 1))


def end_lanes(shape):
    lane = lane_ids(shape)
    return (lane == 0) | (lane == 127)


def azimuth_kernel(cam_count, s_ref, x_ref, one_ref, two_ref, even_ref, odd_ref):
    ends = end_lanes((8, 128))
    row = row_ids((8, 128))
    even = (lax.axis_index("ey") & 1) == 0
    for q in range(one_ref.shape[0]):
        packed = merged(one_ref[q], two_ref[q], cam_count)
        f, a = q // 4, q % 4
        at = slice(8 * q, 8 * q + 8)
        faces = []
        for line, shift in ((0, 16), (63, 2)):
            j = line & 7
            spread = jnp.broadcast_to(packed[j : j + 1, :], (8, 128))
            moved = pltpu.roll(spread, shift, 1, stride=16, stride_axis=0)
            face = s_ref[at, line, :] + jnp.where(ends, moved, 0.0)
            if a == 0:
                face = face + jnp.where(row == 0, x_ref[0, f, line : line + 1, :], 0.0)
            if a == 3:
                face = face + jnp.where(row == 7, x_ref[1, f, line : line + 1, :], 0.0)
            faces.append(face)
        even_ref[at, :] = jnp.where(even, faces[1], faces[0])
        odd_ref[at, :] = jnp.where(even, faces[0], faces[1])


def unpacked(packed, b):
    ends = end_lanes((8, 128))
    rows = []
    for i in range(8):
        u = 56 - 8 * i + b
        moved = pltpu.roll(packed, (128 - 2 * u) % 128, 1) if u else packed
        rows.append(jnp.where(ends, moved, 0.0))
    return rows


def assembled(s_ref, x_ref, packed, f, a, b, y_refs=None):
    span = slice(8 * b, 8 * b + 8)
    rows = unpacked(packed, b)
    rows[0] = rows[0] + jnp.where(a == 0, x_ref[0, f, span, :], 0.0)
    rows[7] = rows[7] + jnp.where(a == 3, x_ref[1, f, span, :], 0.0)
    block = s_ref[pl.ds(pl.multiple_of(a * 8 + 32 * f, 8), 8), span, :]
    if y_refs is not None:
        one_ref, two_ref = y_refs
        at = pl.ds(pl.multiple_of(a * 8 + 32 * f, 8), 8)
        even = (lax.axis_index("ey") & 1) == 0
        if b == 0:
            line, sublane = jnp.where(even, two_ref[at, :], one_ref[at, :]), 0
        else:
            line, sublane = jnp.where(even, one_ref[at, :], two_ref[at, :]), 7
        node = lax.broadcasted_iota(jnp.int32, (8, 8, 128), 1)
        block = block + jnp.where(node == sublane, line[:, None, :], 0.0)
    return block.reshape(64, 128) + jnp.concatenate(rows, axis=0)


def second_pairs(
    cam_count, pairs, s_ref, x_ref, one_ref, two_ref, y_refs, scalar_ref, velocity_ref, mass_ref,
    table_ref, g_ref, base_ref, half_ref,
):
    def body(a, carry):
        at = pl.ds(pl.multiple_of(a * 8, 8), 8)
        radial_g = merged(one_ref[a], two_ref[a], cam_count)
        radial_m = merged(one_ref[a + 4], two_ref[a + 4], cam_count)
        for n, pair in enumerate(pairs):
            fields, velocities, masses = [], [], []
            for h, b in enumerate(pair):
                s = slice(8 * b, 8 * b + 8)
                out = slice(16 * n + 8 * h, 16 * n + 8 * h + 8)
                g = assembled(s_ref, x_ref, radial_g, 0, a, b, y_refs)
                m = assembled(s_ref, x_ref, radial_m, 1, a, b, y_refs)
                scale = time_step / m
                scalar = scalar_ref[at, s, :].reshape(64, 128)
                first = scalar - scale * g
                base_ref[at, out, :] = (0.5 * (scalar + first)).reshape(8, 8, 128)
                half_ref[at, out, :] = (0.5 * scale).reshape(8, 8, 128)
                fields.append(first)
                velocities.append(
                    [velocity_ref[d, at, s, :].reshape(64, 128) for d in range(3)]
                )
                masses.append(mass_ref[at, s, :].reshape(64, 128))
            values = convect_pair(fields, velocities, masses, table_ref)
            joined = join_lanes(values, table_ref)
            for h in range(2):
                out = slice(16 * n + 8 * h, 16 * n + 8 * h + 8)
                g_ref[at, out, :] = joined[h].reshape(8, 8, 128)
        return carry

    lax.fori_loop(0, 4, body, 0)


def second_inner_kernel(
    cam_count, s_ref, x_ref, one_ref, two_ref, scalar_ref, velocity_ref, mass_ref,
    table_ref, g_ref, base_ref, half_ref,
):
    second_pairs(
        cam_count, ((1, 2), (3, 4), (5, 6)), s_ref, x_ref, one_ref, two_ref, None,
        scalar_ref, velocity_ref, mass_ref, table_ref, g_ref, base_ref, half_ref,
    )
    join_block(g_ref)


def second_outer_kernel(
    cam_count, s_ref, x_ref, one_ref, two_ref, y_one_ref, y_two_ref, scalar_ref, velocity_ref,
    mass_ref, table_ref, inner_ref, g_ref, x_out_ref, base_ref, half_ref, edge_ref,
):
    second_pairs(
        cam_count, ((0, 7),), s_ref, x_ref, one_ref, two_ref, (y_one_ref, y_two_ref),
        scalar_ref, velocity_ref, mass_ref, table_ref, edge_ref, base_ref, half_ref,
    )
    join_axial(edge_ref)
    g_ref[:, 0:8, :] = edge_ref[:, 0:8, :]
    g_ref[:, 8:56, :] = inner_ref[...]
    g_ref[:, 56:64, :] = edge_ref[:, 8:16, :]
    for low in (7, 55):
        total = g_ref[:, low, :] + g_ref[:, low + 1, :]
        g_ref[:, low, :] = total
        g_ref[:, low + 1, :] = total
    x_out_ref[0, 0] = g_ref[31]
    x_out_ref[1, 0] = g_ref[0]


def weight_kernel(weight_ref, out_ref):
    row = row_ids((512, 512))
    source = (row & 63) * 8 + (row >> 6)
    order = jnp.where(lane_ids((512, 512)) == source, 1.0, 0.0).astype(BF16)
    for m in range(8):
        out_ref[:, 128 * m : 128 * m + 128] = dot(order, weight_ref[m]).astype(BF16)


def pick_kernel(cut_ref, pick_ref):
    cut = cut_ref[...]
    a, b, c = cut >> 7, (cut >> 4) & 7, cut & 15
    inner = 96 * a + 16 * (b - 1) + c
    outer = 384 + 32 * a + jnp.where(b == 7, 16, 0) + c
    place = jnp.where((b == 0) | (b == 7), outer, inner)
    turned = place.astype(F32).T.astype(jnp.int32)
    lane = lane_ids((128, 512))
    for m in range(8):
        pick_ref[m] = jnp.where(lane == turned[:, m : m + 1], 1.0, 0.0).astype(BF16)


def advance(
    cam_count, pairs, g_ref, x_ref, one_ref, two_ref, y_refs, base_ref, half_ref,
    advected_ref, turned_ref, element_ref,
):
    def body(a, carry):
        at = pl.ds(pl.multiple_of(a * 8, 8), 8)
        radial = merged(one_ref[a], two_ref[a], cam_count)
        for n, pair in enumerate(pairs):
            blocks = []
            for h, b in enumerate(pair):
                g = assembled(g_ref, x_ref, radial, 0, a, b, y_refs)
                out = slice(16 * n + 8 * h, 16 * n + 8 * h + 8)
                base = base_ref[at, out, :].reshape(64, 128)
                half = half_ref[at, out, :].reshape(64, 128)
                advected = base - half * g
                advected_ref[at, out, :] = advected.reshape(8, 8, 128)
                blocks.append(advected.astype(BF16).astype(F32))
            p = len(pairs) * a + n
            turned_ref[p] = jnp.concatenate(blocks, axis=0).T
            low_half = lane_ids((16, 128)) < 64
            top = pl.ds(pl.multiple_of(p * 32, 32), 16)
            bottom = pl.ds(pl.multiple_of(p * 32 + 16, 16), 16)
            for k in range(0, 8, 2):
                even = turned_ref[p, pl.ds(k, 16, stride=8), :]
                odd = turned_ref[p, pl.ds(k + 1, 16, stride=8), :]
                columns = slice(64 * k, 64 * k + 128)
                element_ref[top, columns] = jnp.where(
                    low_half, even, pltpu.roll(odd, 64, 1)
                ).astype(BF16)
                element_ref[bottom, columns] = jnp.where(
                    low_half, pltpu.roll(even, 64, 1), odd
                ).astype(BF16)
        return carry

    lax.fori_loop(0, 4, body, 0)


def render_inner_kernel(
    cam_count, g_ref, x_ref, one_ref, two_ref, base_ref, half_ref, weight_ref, pick_ref,
    out_hbm, pixel_ref, advected_ref, turned_ref, element_ref, sem,
):
    advance(
        cam_count, ((1, 2), (3, 4), (5, 6)), g_ref, x_ref, one_ref, two_ref, None,
        base_ref, half_ref, advected_ref, turned_ref, element_ref,
    )
    copy = pltpu.make_async_copy(advected_ref, out_hbm.at[:, pl.ds(8, 48)], sem)
    copy.start()
    for m in range(8):
        values = dot(element_ref[...], weight_ref[:, 128 * m : 128 * m + 128]).astype(BF16)
        pixel_ref[m] = dot(pick_ref[m, :, :384], values)
    copy.wait()


def render_outer_kernel(
    cam_count, g_ref, x_ref, one_ref, two_ref, y_one_ref, y_two_ref, base_ref, half_ref,
    weight_ref, pick_ref, pixel_ref, block_ref, out_in,
    out_hbm, *rest,
):
    payload_refs = rest[:cam_count]
    advected_ref, turned_ref, element_ref, value_ref, sems = rest[cam_count:]
    advance(
        cam_count, ((0, 7),), g_ref, x_ref, one_ref, two_ref, (y_one_ref, y_two_ref),
        base_ref, half_ref, advected_ref, turned_ref, element_ref,
    )
    copies = [
        pltpu.make_async_copy(
            advected_ref.at[:, pl.ds(8 * n, 8)], out_hbm.at[:, pl.ds(56 * n, 8)], sems.at[n]
        )
        for n in range(2)
    ]
    for copy in copies:
        copy.start()
    cameras = pixel_ref.shape[0]
    for m in range(cameras):
        value_ref[m] = dot(element_ref[...], weight_ref[:, 128 * m : 128 * m + 128]).astype(BF16)
    me = lax.axis_index("cam")
    share = cameras // cam_count
    sub = row_ids((16, 128))
    for d in range(cam_count):
        for n in range(share):
            m = share * (me ^ d) + n
            values = dot(pick_ref[m, :, 384:], value_ref[m]) + pixel_ref[m]
            payload_refs[d][n, :128, :] = values.astype(BF16)
            ids = block_ref[pl.ds(m, 1), :]
            tail = jnp.where(sub == 0, ids >> 5, jnp.where(sub == 1, ids & 31, 0))
            payload_refs[d][n, 128:, :] = tail.astype(F32).astype(BF16)
    for copy in copies:
        copy.wait()


def image_kernel(*refs):
    payload_refs, (image_hbm, image_ref, sems) = refs[:-3], refs[-3:]
    copies = []
    for m in range(image_ref.shape[0]):
        ids, values = [], []
        for payload_ref in payload_refs:
            tail = payload_ref[m, 128:, :].astype(F32).astype(jnp.int32)
            ids.append(tail[0:1, :] * 32 + tail[1:2, :])
            values.append(payload_ref[m, :128, :])
        ids = jnp.concatenate(ids, axis=1)
        values = jnp.concatenate(values, axis=0)
        for chunk in range(4):
            at = slice(256 * chunk, 256 * chunk + 256)
            row = row_ids((256, ids.shape[1])) + 256 * chunk
            onehot = jnp.where(row == ids, 1.0, 0.0).astype(BF16)
            image_ref[m, at, :] = dot(onehot, values)
            copy = pltpu.make_async_copy(
                image_ref.at[m, at], image_hbm.at[m, at], sems.at[4 * m + chunk]
            )
            copy.start()
            copies.append(copy)
    for copy in copies:
        copy.wait()


def call(kernel, out_shape, flops=10**8, size=10**7, **options):
    return pl.pallas_call(
        kernel,
        out_shape=out_shape,
        compiler_params=pltpu.CompilerParams(vmem_limit_bytes=24 * 2**20),
        cost_estimate=pl.CostEstimate(flops=flops, bytes_accessed=size, transcendentals=0),
        **options,
    )


def shape_of(*shape, dtype=F32):
    return jax.ShapeDtypeStruct(shape, dtype)


def stay(*arrays):
    return [pltpu.with_memory_space_constraint(x, pltpu.HBM) for x in arrays]


def swaps(axis):
    count = lax.axis_size(axis)
    even = [(i, i ^ 1) for i in range(count)]
    odd = [(i, (i + 1) % count if i & 1 else (i - 1) % count) for i in range(count)]
    return even, odd


def swap_axial(x):
    count = lax.axis_size("ex")
    up = [(i, (i + 1) % count) for i in range(count)]
    if count == 2:
        return lax.ppermute(x, "ex", up)
    down = [(j, i) for i, j in up]
    return jnp.stack([lax.ppermute(x[0], "ex", up), lax.ppermute(x[1], "ex", down)])


def swap_both(one, two, axis):
    even, odd = swaps(axis)
    return lax.ppermute(one, axis, even), lax.ppermute(two, axis, odd)


def per_device(scalar, velocity, lumped_mass, pixel_weights, cut_element, pixel_block):
    shape = scalar.shape
    flat = (32, 64, 128)
    inner, outer = (32, 48, 128), (32, 16, 128)
    scalar = scalar.reshape(flat)
    velocity = velocity.reshape((3,) + flat)
    mass = lumped_mass.reshape(flat)
    tables = derivative_tables()
    n_cam = lax.axis_size("cam")
    cameras = pixel_weights.shape[0]
    share = cameras // n_cam
    part = functools.partial

    x, near = call(
        face_kernel,
        (shape_of(2, 2, 64, 128), shape_of(*tables.shape, dtype=BF16)),
        in_specs=[HBM] * 4,
        scratch_shapes=[
            pltpu.VMEM((2, 8, 64, 128), F32),
            pltpu.VMEM((2, 3, 64, 128), F32),
            pltpu.VMEM((2, 64, 128), F32),
            pltpu.SemaphoreType.DMA((7,)),
        ],
    )(*stay(scalar, velocity, mass, tables))
    x_got = swap_axial(x)
    s, z, scalar, velocity, mass = call(
        first_kernel,
        (shape_of(64, 64, 128), shape_of(8, 8, 128))
        + (shape_of(*flat), shape_of(3, *flat), shape_of(*flat)),
        in_specs=[HBM] * 3 + [VMEM],
        scratch_shapes=[pltpu.SemaphoreType.DMA((3, 4))],
    )(*stay(scalar, velocity, mass), near)
    weights = call(weight_kernel, shape_of(512, 128 * cameras, dtype=BF16))(pixel_weights)
    picks = call(pick_kernel, shape_of(cameras, 128, 512, dtype=BF16))(cut_element)

    z = call(part(radial_kernel, 2), shape_of(8, 8, 128))(z, x_got)
    z_got = swap_both(z, z, "cam")
    y = call(part(azimuth_kernel, n_cam), (shape_of(64, 128), shape_of(64, 128)))(s, x_got, *z_got)
    y_got = swap_both(*y, "ey")
    g_inner, *inner_terms = call(
        part(second_inner_kernel, n_cam), (shape_of(*inner),) * 3
    )(s, x_got, *z_got, scalar, velocity, mass, near)
    g, x, *outer_terms = call(
        part(second_outer_kernel, n_cam),
        (shape_of(*flat), shape_of(2, 1, 64, 128), shape_of(*outer), shape_of(*outer)),
        scratch_shapes=[pltpu.VMEM(outer, F32)],
    )(s, x_got, *z_got, *y_got, scalar, velocity, mass, near, g_inner)

    x_got = swap_axial(x)
    z = call(pack_kernel, shape_of(4, 8, 128))(g)
    z = call(part(radial_kernel, 1), shape_of(4, 8, 128))(z, x_got)
    z_got = swap_both(z, z, "cam")
    y = call(part(azimuth_kernel, n_cam), (shape_of(32, 128), shape_of(32, 128)))(g, x_got, *z_got)
    y_got = swap_both(*y, "ey")
    advected, pixels = call(
        part(render_inner_kernel, n_cam),
        (shape_of(*flat), shape_of(cameras, 128, 128)),
        out_specs=(HBM, VMEM),
        scratch_shapes=[
            pltpu.VMEM(inner, F32),
            pltpu.VMEM((12, 128, 128), F32),
            pltpu.VMEM((384, 512), BF16),
            pltpu.SemaphoreType.DMA,
        ],
    )(g, x_got, *z_got, *inner_terms, weights, picks)
    payload_shape = shape_of(share, 144, 128, dtype=BF16)
    advected, *payloads = call(
        part(render_outer_kernel, n_cam),
        (shape_of(*flat),) + (payload_shape,) * n_cam,
        in_specs=[VMEM] * 12 + [HBM],
        out_specs=(HBM,) + (VMEM,) * n_cam,
        input_output_aliases={12: 0},
        scratch_shapes=[
            pltpu.VMEM(outer, F32),
            pltpu.VMEM((4, 128, 128), F32),
            pltpu.VMEM((128, 512), BF16),
            pltpu.VMEM((cameras, 128, 128), BF16),
            pltpu.SemaphoreType.DMA((2,)),
        ],
    )(g, x_got, *z_got, *y_got, *outer_terms, weights, picks, pixels, pixel_block, advected)
    received = [payloads[0]]
    for d in range(1, n_cam):
        received.append(lax.ppermute(payloads[d], "cam", [(i, i ^ d) for i in range(n_cam)]))
    images = call(
        image_kernel,
        shape_of(share, NBLK, 128),
        out_specs=HBM,
        scratch_shapes=[
            pltpu.VMEM((share, NBLK, 128), F32),
            pltpu.SemaphoreType.DMA((4 * share,)),
        ],
    )(*received)
    return (advected.reshape(shape), images)


def solution(mesh):
    placed = (
        P("ex", None, "ey", None, "cam"),
        P(None, "ex", None, "ey", None, "cam"),
        P("ex", None, "ey", None, "cam"),
        P(),
        P(None, ("cam", "ex", "ey")),
        P(None, ("cam", "ex", "ey")),
    )
    return jax.shard_map(
        per_device,
        mesh=mesh,
        in_specs=placed,
        out_specs=(P("ex", None, "ey", None, "cam"), P("cam", ("ex", "ey"), None)),
        check_vma=False,
    )
```

time: 187 us -> 49.9 us (0.27)
  local copies, waits for them, and re-layouts: 61.8 us -> 0.02 us
  waiting for transfers between devices: 61.7 us -> 9.45 us
  Pallas kernels: 0 us -> 24 us
  matrix products: 17.1 us -> 0 us
  between operations: 14.4 us -> 0.82 us
  other arithmetic: 11.5 us -> 0 us
  starting transfers between devices: 19.4 us -> 15.5 us
    reduce_scatter x1 -> x0, waiting for transfers between devices: 46.9 us -> none  [per_device(): lax.psum_scatter(jnp.einsum('cbs,csx->cbx', onehot, values, precision=lax...]
    pallas_call x0 -> x14, Pallas kernels: none -> 24 us  [the longest x1 5.27 us: per_device(): call(first_kernel, (shape_of(64, 64, 128), shape_of(8, 8, 128)) + (shape_...]
    reshape x3 -> x0, local copies, waits for them, and re-layouts: 19.9 us -> none  [per_device(): elements = advected.astype(jnp.bfloat16).reshape(shape[0], 8, shape[2], 8...]
    dot_general x8 -> x0, matrix products: 17.1 us -> none  [the longest x2 6.32 us: convect(): jnp.einsum('pi,aibjz->apbjz', derivative, field, precision=lax.Precision....]
    slice x10 -> x0, local copies, waits for them, and re-layouts: 16.1 us -> none  [the longest x7 8.54 us: padded(): initial = lax.slice_in_dim(shard, 0, width, axis=dim)]
    transpose x1 -> x0, local copies, waits for them, and re-layouts: 10.5 us -> none  [per_device(): elements = advected.astype(jnp.bfloat16).reshape(shape[0], 8, shape[2], 8...]
    ppermute x4 -> x0, local copies, waits for them, and re-layouts: 6.85 us -> none  [the longest x2 3.43 us: padded(): before = lax.ppermute(last, axis, up)]
    add x5 -> x0, other arithmetic: 5.71 us -> none  [pair_sum(): return middle + is_last * following + is_first * preceding]
  transfers between devices with their start and end apart: 13 -> 13, of which waited for: 9 -> 5; matrix products, arithmetic and copies ran while one was open for 4% -> 0% of each run, Pallas kernels for 0% -> 32%
where the time goes in v2:
time: 49.9 us; the launch traced here: 49.8 us
  Pallas kernels  24 us (48%)
  starting transfers between devices  15.5 us (31%)
  waiting for transfers between devices  9.45 us (19%)
  between operations  0.82 us (2%)
    ppermute x8, starting transfers between devices, swap_both(): return (lax.ppermute(one, axis, even), lax.ppermute(two, axis, odd))  9.94 us
    pallas_call x1, Pallas kernels, per_device(): call(first_kernel, (shape_of(64, 64, 128), shape_of(8, 8, 128)) + (shape_...  5.27 us
    pallas_call x1, Pallas kernels, per_device(): call(part(render_inner_kernel, n_cam), (shape_of(*flat), shape_of(cameras...  4.98 us
    ppermute x3, waiting for transfers between devices, per_device(): lax.ppermute(payloads[d], 'cam', [(i, i ^ d) for i in range(n_cam)])  4.16 us
    ppermute x2, starting transfers between devices, swap_axial(): return lax.ppermute(x, 'ex', up)  3.6 us
    pallas_call x1, Pallas kernels, per_device(): call(part(second_inner_kernel, n_cam), (shape_of(*inner),) * 3)  3.43 us
    ppermute x2, waiting for transfers between devices, swap_axial(): return lax.ppermute(x, 'ex', up)  3.19 us
    pallas_call x1, Pallas kernels, per_device(): call(part(render_outer_kernel, n_cam), (shape_of(*flat),) + (payload_shap...  2.6 us
  transfers between devices with their start and end apart: 13, of which 5 were waited for; matrix products, arithmetic and copies ran while one was open for 0% of the time, Pallas kernels for 32%

profile of v2, /device:TPU:0, one launch (start us, length us, event | category | flops | bytes accessed | tf_op | source)
XLA Modules:
  0.0 49.8 jit_solution(8045199523513281740)
XLA Ops:
  0.6 1.6 %shard_map.86 = (f32[2,2,64,128]{3,2,1,0:T(8,128)S(1)}, bf16[1024,128]{1,0:T(8,128)(2,1)S(1)}) custom-call(f32[32,64,128]{2,1,0:T(8,128)} %bitcast.6, f32[3,32,64,128]{3,2,1,0:T(8,128)} %bitcast.4, f32[32,64,128]{2,1,0:T(8,128)} %bitcast.8, bf16[1024,128]{1,0:T(8,128)(2,1)} %constant.2.clone.table_hbm), custom_call_target="tpu_custom_call" | custom-call | flops 100000000 | bytes 10000000 | tf_op jit(solution)/shard_map/pallas_call | solution.py:615
  2.2 3.0 %collective-permute-start = (f32[2,2,64,128]{3,2,1,0:T(8,128)S(1)}, f32[2,2,64,128]{3,2,1,0:T(8,128)S(1)}, u32[]{:S(2)}, u32[]{:S(2)}) collective-permute-start(f32[2,2,64,128]{3,2,1,0:T(8,128)S(1)} %get-tuple-element.29), channel_id=1, source_target_pairs={{0,4},{4,0},{1,5},{5,1},{2,6},{6,2},{3,7},{7,3},{8,12},{12,8},{9,1... | collective-permute-start | bytes 393224 | tf_op jit(solution)/shard_map/ppermute | solution.py:592
  5.2 5.3 %shard_map.87 = (f32[64,64,128]{2,1,0:T(8,128)S(1)}, f32[8,8,128]{2,1,0:T(8,128)S(1)}, f32[32,64,128]{2,1,0:T(8,128)S(1)}, f32[3,32,64,128]{3,2,1,0:T(8,128)S(1)}, f32[32,64,128]{2,1,0:T(8,128)S(1)}) custom-call(f32[32,64,128]{2,1,0:T(8,128)} %bitcast.7, f32[3,32,64,128]{3,2,1,0:T(8,128)} %bitcast.5, f32[32,64,128]{2,1,0:T(8,128)} %bitcast.9, ...), custom_call_target="tpu_custom_call" | custom-call | flops 100000000 | bytes 10000000 | tf_op jit(solution)/shard_map/pallas_call | solution.py:627
  10.5 0.0 collective-permute-done.x_ref
  10.5 0.1 shard_map.88
  10.6 0.1 collective-permute-start.1
  10.7 1.6 %collective-permute-start.2 = (f32[8,8,128]{2,1,0:T(8,128)S(1)}, f32[8,8,128]{2,1,0:T(8,128)S(1)}, u32[]{:S(2)}, u32[]{:S(2)}) collective-permute-start(f32[8,8,128]{2,1,0:T(8,128)S(1)} %shard_map.88), channel_id=1, source_target_pairs={{0,24},{8,16},{16,8},{24,0},{1,25},{9,17},{17,9},{25,1},{2,26},{10... | collective-permute-start | bytes 98312 | tf_op jit(solution)/shard_map/ppermute | solution.py:599
  12.4 0.0 collective-permute-done.1.one_ref
  12.4 1.8 %collective-permute-done.2.two_ref = f32[8,8,128]{2,1,0:T(8,128)S(1)} collective-permute-done((f32[8,8,128]{2,1,0:T(8,128)S(1)}, f32[8,8,128]{2,1,0:T(8,128)S(1)}, u32[]{:S(2)}, u32[]{:S(2)}) %collective-permute-start.2) | collective-permute-done | bytes 32800 | tf_op jit(solution)/shard_map/ppermute | solution.py:599
  14.1 0.2 shard_map.89
  14.3 1.6 %collective-permute-start.3 = (f32[64,128]{1,0:T(8,128)S(1)}, f32[64,128]{1,0:T(8,128)S(1)}, u32[]{:S(2)}, u32[]{:S(2)}) collective-permute-start(f32[64,128]{1,0:T(8,128)S(1)} %get-tuple-element.31), channel_id=1, source_target_pairs={{0,1},{1,0},{2,3},{3,2},{4,5},{5,4},{6,7},{7,6},{8,9},{9,8},{10,11... | collective-permute-start | bytes 98312 | tf_op jit(solution)/shard_map/ppermute | solution.py:599
  15.9 2.5 %collective-permute-start.4 = (f32[64,128]{1,0:T(8,128)S(1)}, f32[64,128]{1,0:T(8,128)S(1)}, u32[]{:S(2)}, u32[]{:S(2)}) collective-permute-start(f32[64,128]{1,0:T(8,128)S(1)} %get-tuple-element.32), channel_id=1, source_target_pairs={{0,3},{1,2},{2,1},{3,0},{4,7},{5,6},{6,5},{7,4},{8,11},{9,10},{10,... | collective-permute-start | bytes 98312 | tf_op jit(solution)/shard_map/ppermute | solution.py:599
  18.4 3.4 %shard_map.90 = (f32[32,48,128]{2,1,0:T(8,128)S(1)}, f32[32,48,128]{2,1,0:T(8,128)S(1)}, f32[32,48,128]{2,1,0:T(8,128)S(1)}) custom-call(f32[64,64,128]{2,1,0:T(8,128)S(1)} %get-tuple-element.28.s_ref, f32[2,2,64,128]{3,2,1,0:T(8,128)S(1)} %collective-permute-done.x_ref, f32[8,8,128]{2,1,0:T(8,128)S(1)} %collective-permute-done.1.one_ref, ...), custom_call_target="tpu_custom_call" | custom-call | flops 100000000 | bytes 10000000 | tf_op jit(solution)/shard_map/pallas_call | solution.py:641
  21.8 0.0 collective-permute-done.3.y_one_ref
  21.9 0.0 collective-permute-done.4.y_two_ref
  21.9 0.0 copy-start
  21.9 2.1 %shard_map.91 = (f32[32,64,128]{2,1,0:T(8,128)S(1)}, f32[2,1,64,128]{3,2,1,0:T(8,128)S(1)}, f32[32,16,128]{2,1,0:T(8,128)S(1)}, f32[32,16,128]{2,1,0:T(8,128)S(1)}) custom-call(f32[64,64,128]{2,1,0:T(8,128)S(1)} %get-tuple-element.28.s_ref, f32[2,2,64,128]{3,2,1,0:T(8,128)S(1)} %collective-permute-done.x_ref, ...), custom_call_target="tpu_custom_call" | custom-call | flops 100000000 | bytes 10000000 | tf_op jit(solution)/shard_map/pallas_call | solution.py:644
  24.0 0.0 copy-start.1
  24.0 0.6 %collective-permute-start.5 = (f32[2,1,64,128]{3,2,1,0:T(8,128)S(1)}, f32[2,1,64,128]{3,2,1,0:T(8,128)S(1)}, u32[]{:S(2)}, u32[]{:S(2)}) collective-permute-start(f32[2,1,64,128]{3,2,1,0:T(8,128)S(1)} %get-tuple-element.38), channel_id=1, source_target_pairs={{0,4},{4,0},{1,5},{5,1},{2,6},{6,2},{3,7},{7,3},{8,12},{12,8},{9,1... | collective-permute-start | bytes 196616 | tf_op jit(solution)/shard_map/ppermute | solution.py:592
  24.6 0.5 %shard_map.92.z_in = f32[4,8,128]{2,1,0:T(8,128)S(1)} custom-call(f32[32,64,128]{2,1,0:T(8,128)S(1)} %get-tuple-element.37.s_ref.g_ref), custom_call_target="tpu_custom_call" | custom-call | flops 100000000 | bytes 10000000 | tf_op jit(solution)/shard_map/pallas_call | solution.py:651
  25.1 3.2 %collective-permute-done.5.x_ref = f32[2,1,64,128]{3,2,1,0:T(8,128)S(1)} collective-permute-done((f32[2,1,64,128]{3,2,1,0:T(8,128)S(1)}, f32[2,1,64,128]{3,2,1,0:T(8,128)S(1)}, u32[]{:S(2)}, u32[]{:S(2)}) %collective-permute-start.5) | collective-permute-done | bytes 65568 | tf_op jit(solution)/shard_map/ppermute | solution.py:592
  28.3 0.1 shard_map.93
  28.4 0.1 collective-permute-start.6
  28.5 1.6 %collective-permute-start.7 = (f32[4,8,128]{2,1,0:T(8,128)S(1)}, f32[4,8,128]{2,1,0:T(8,128)S(1)}, u32[]{:S(2)}, u32[]{:S(2)}) collective-permute-start(f32[4,8,128]{2,1,0:T(8,128)S(1)} %shard_map.93), channel_id=1, source_target_pairs={{0,24},{8,16},{16,8},{24,0},{1,25},{9,17},{17,9},{25,1},{2,26},{10... | collective-permute-start | bytes 49160 | tf_op jit(solution)/shard_map/ppermute | solution.py:599
  30.1 0.0 copy-done
  30.1 1.3 %shard_map.95.weight_ref = bf16[512,1024]{1,0:T(8,128)(2,1)S(1)} custom-call(bf16[8,512,128]{2,1,0:T(8,128)(2,1)S(1)} %copy-done), custom_call_target="tpu_custom_call" | custom-call | flops 100000000 | bytes 10000000 | tf_op jit(solution)/shard_map/pallas_call | solution.py:634
  31.4 0.0 collective-permute-done.6.one_ref
  31.4 0.3 collective-permute-done.7.two_ref
  31.7 0.2 shard_map.94
  31.9 0.0 copy-start.2
  31.9 0.7 %collective-permute-start.8 = (f32[32,128]{1,0:T(8,128)S(1)}, f32[32,128]{1,0:T(8,128)S(1)}, u32[]{:S(2)}, u32[]{:S(2)}) collective-permute-start(f32[32,128]{1,0:T(8,128)S(1)} %get-tuple-element.39), channel_id=1, source_target_pairs={{0,1},{1,0},{2,3},{3,2},{4,5},{5,4},{6,7},{7,6},{8,9},{9,8},{10,11... | collective-permute-start | bytes 49160 | tf_op jit(solution)/shard_map/ppermute | solution.py:599
  32.6 1.7 %collective-permute-start.9 = (f32[32,128]{1,0:T(8,128)S(1)}, f32[32,128]{1,0:T(8,128)S(1)}, u32[]{:S(2)}, u32[]{:S(2)}) collective-permute-start(f32[32,128]{1,0:T(8,128)S(1)} %get-tuple-element.40), channel_id=1, source_target_pairs={{0,3},{1,2},{2,1},{3,0},{4,7},{5,6},{6,5},{7,4},{8,11},{9,10},{10,... | collective-permute-start | bytes 49160 | tf_op jit(solution)/shard_map/ppermute | solution.py:599
  34.3 0.0 copy-done.1
  34.3 0.3 shard_map.96.pick_ref
  34.6 5.0 %shard_map.97 = (f32[32,64,128]{2,1,0:T(8,128)}, f32[8,128,128]{2,1,0:T(8,128)S(1)}) custom-call(f32[32,64,128]{2,1,0:T(8,128)S(1)} %get-tuple-element.37.s_ref.g_ref, f32[2,1,64,128]{3,2,1,0:T(8,128)S(1)} %collective-permute-done.5.x_ref, f32[4,8,128]{2,1,0:T(8,128)S(1)} %collective-permute-done.6.one_ref, f32[4,8,128]{2,1,0:T(8,128)S(1)} %collective-permute-done.7.two_ref, ...), custom_call_target="tpu_custom_call" | custom-call | flops 100000000 | bytes 10000000 | tf_op jit(solution)/shard_map/pallas_call | solution.py:656
  39.6 0.0 collective-permute-done.8.y_one_ref
  39.6 0.0 collective-permute-done.9.y_two_ref
  39.6 0.0 copy-done.2
  39.6 2.6 %shard_map.98 = (f32[32,64,128]{2,1,0:T(8,128)}, bf16[2,144,128]{2,1,0:T(8,128)(2,1)S(1)}, bf16[2,144,128]{2,1,0:T(8,128)(2,1)S(1)}, bf16[2,144,128]{2,1,0:T(8,128)(2,1)S(1)}, bf16[2,144,128]{2,1,0:T(8,128)(2,1)S(1)}) custom-call(f32[32,64,128]{2,1,0:T(8,128)S(1)} %get-tuple-element.37.s_ref.g_ref, ...), custom_call_target="tpu_custom_call", output_to_operand_aliasing={{0}: (12, {})} | custom-call | flops 100000000 | bytes 10000000 | tf_op jit(solution)/shard_map/pallas_call | solution.py:668
  42.2 0.2 collective-permute-start.10
  42.5 1.5 %collective-permute-start.11 = (bf16[2,144,128]{2,1,0:T(8,128)(2,1)S(1)}, bf16[2,144,128]{2,1,0:T(8,128)(2,1)S(1)}, u32[]{:S(2)}, u32[]{:S(2)}) collective-permute-start(bf16[2,144,128]{2,1,0:T(8,128)(2,1)S(1)} %get-tuple-element.50), channel_id=1, source_target_pairs={{0,16},{8,24},{16,0},{24,8},{1,17},{9,25},{17,1},{25,9},{2,18},{10... | collective-permute-start | bytes 221192 | tf_op jit(solution)/shard_map/ppermute | solution.py:684
  44.0 0.2 collective-permute-start.12
  44.2 0.0 collective-permute-done.10.refs_1_
  44.2 2.8 %collective-permute-done.11.refs_2_ = bf16[2,144,128]{2,1,0:T(8,128)(2,1)S(1)} collective-permute-done((bf16[2,144,128]{2,1,0:T(8,128)(2,1)S(1)}, bf16[2,144,128]{2,1,0:T(8,128)(2,1)S(1)}, u32[]{:S(2)}, u32[]{:S(2)}) %collective-permute-start.11) | collective-permute-done | bytes 73760 | tf_op jit(solution)/shard_map/ppermute | solution.py:684
  47.0 1.3 %collective-permute-done.12.refs_3_ = bf16[2,144,128]{2,1,0:T(8,128)(2,1)S(1)} collective-permute-done((bf16[2,144,128]{2,1,0:T(8,128)(2,1)S(1)}, bf16[2,144,128]{2,1,0:T(8,128)(2,1)S(1)}, u32[]{:S(2)}, u32[]{:S(2)}) %collective-permute-start.12) | collective-permute-done | bytes 73760 | tf_op jit(solution)/shard_map/ppermute | solution.py:684
  48.3 1.4 %shard_map.99 = f32[2,1024,128]{2,1,0:T(8,128)} custom-call(bf16[2,144,128]{2,1,0:T(8,128)(2,1)S(1)} %get-tuple-element.48.refs_0_, bf16[2,144,128]{2,1,0:T(8,128)(2,1)S(1)} %collective-permute-done.10.refs_1_, bf16[2,144,128]{2,1,0:T(8,128)(2,1)S(1)} %collective-permute-done.11.refs_2_, bf16[2,144,128]{2,1,0:T(8,128)(2,1)S(1)} %collective-permute-done.12.refs_3_), custom_call_target="tpu_custom_call" | custom-call | flops 100000000 | bytes 10000000 | tf_op jit(solution)/shard_map/pallas_call | solution.py:685
Async XLA Ops:
  2.2 8.3 %collective-permute-start = (f32[2,2,64,128]{3,2,1,0:T(8,128)S(1)}, f32[2,2,64,128]{3,2,1,0:T(8,128)S(1)}, u32[]{:S(2)}, u32[]{:S(2)}) collective-permute-start(f32[2,2,64,128]{3,2,1,0:T(8,128)S(1)} %get-tuple-element.29), channel_id=1, source_target_pairs={{0,4},{4,0},{1,5},{5,1},{2,6},{6,2},{3,7},{7,3},{8,12},{12,8},{9,1... | collective-permute-start | bytes 393224 | tf_op jit(solution)/shard_map/ppermute | solution.py:592
  10.6 1.7 %collective-permute-start.1 = (f32[8,8,128]{2,1,0:T(8,128)S(1)}, f32[8,8,128]{2,1,0:T(8,128)S(1)}, u32[]{:S(2)}, u32[]{:S(2)}) collective-permute-start(f32[8,8,128]{2,1,0:T(8,128)S(1)} %shard_map.88), channel_id=1, source_target_pairs={{0,8},{8,0},{16,24},{24,16},{1,9},{9,1},{17,25},{25,17},{2,10},{10... | collective-permute-start | bytes 98312 | tf_op jit(solution)/shard_map/ppermute | solution.py:599
  10.7 3.4 %collective-permute-start.2 = (f32[8,8,128]{2,1,0:T(8,128)S(1)}, f32[8,8,128]{2,1,0:T(8,128)S(1)}, u32[]{:S(2)}, u32[]{:S(2)}) collective-permute-start(f32[8,8,128]{2,1,0:T(8,128)S(1)} %shard_map.88), channel_id=1, source_target_pairs={{0,24},{8,16},{16,8},{24,0},{1,25},{9,17},{17,9},{25,1},{2,26},{10... | collective-permute-start | bytes 98312 | tf_op jit(solution)/shard_map/ppermute | solution.py:599
  14.3 7.6 %collective-permute-start.3 = (f32[64,128]{1,0:T(8,128)S(1)}, f32[64,128]{1,0:T(8,128)S(1)}, u32[]{:S(2)}, u32[]{:S(2)}) collective-permute-start(f32[64,128]{1,0:T(8,128)S(1)} %get-tuple-element.31), channel_id=1, source_target_pairs={{0,1},{1,0},{2,3},{3,2},{4,5},{5,4},{6,7},{7,6},{8,9},{9,8},{10,11... | collective-permute-start | bytes 98312 | tf_op jit(solution)/shard_map/ppermute | solution.py:599
  15.9 5.9 %collective-permute-start.4 = (f32[64,128]{1,0:T(8,128)S(1)}, f32[64,128]{1,0:T(8,128)S(1)}, u32[]{:S(2)}, u32[]{:S(2)}) collective-permute-start(f32[64,128]{1,0:T(8,128)S(1)} %get-tuple-element.32), channel_id=1, source_target_pairs={{0,3},{1,2},{2,1},{3,0},{4,7},{5,6},{6,5},{7,4},{8,11},{9,10},{10,... | collective-permute-start | bytes 98312 | tf_op jit(solution)/shard_map/ppermute | solution.py:599
  21.9 8.2 %copy-start = (bf16[8,512,128]{2,1,0:T(8,128)(2,1)S(1)}, bf16[8,512,128]{2,1,0:T(8,128)(2,1)}, u32[]{:S(2)}) copy-start(bf16[8,512,128]{2,1,0:T(8,128)(2,1)} %weight_ref.1) | copy-start | bytes 3145732
  24.0 10.3 %copy-start.1 = (s32[8,128]{1,0:T(8,128)S(1)}, s32[8,128]{1,0:T(8,128)}, u32[]{:S(2)}) copy-start(s32[8,128]{1,0:T(8,128)} %cut_ref.1) | copy-start | bytes 12292
  24.0 4.3 %collective-permute-start.5 = (f32[2,1,64,128]{3,2,1,0:T(8,128)S(1)}, f32[2,1,64,128]{3,2,1,0:T(8,128)S(1)}, u32[]{:S(2)}, u32[]{:S(2)}) collective-permute-start(f32[2,1,64,128]{3,2,1,0:T(8,128)S(1)} %get-tuple-element.38), channel_id=1, source_target_pairs={{0,4},{4,0},{1,5},{5,1},{2,6},{6,2},{3,7},{7,3},{8,12},{12,8},{9,1... | collective-permute-start | bytes 196616 | tf_op jit(solution)/shard_map/ppermute | solution.py:592
  28.4 3.0 %collective-permute-start.6 = (f32[4,8,128]{2,1,0:T(8,128)S(1)}, f32[4,8,128]{2,1,0:T(8,128)S(1)}, u32[]{:S(2)}, u32[]{:S(2)}) collective-permute-start(f32[4,8,128]{2,1,0:T(8,128)S(1)} %shard_map.93), channel_id=1, source_target_pairs={{0,8},{8,0},{16,24},{24,16},{1,9},{9,1},{17,25},{25,17},{2,10},{10... | collective-permute-start | bytes 49160 | tf_op jit(solution)/shard_map/ppermute | solution.py:599
  28.5 3.2 %collective-permute-start.7 = (f32[4,8,128]{2,1,0:T(8,128)S(1)}, f32[4,8,128]{2,1,0:T(8,128)S(1)}, u32[]{:S(2)}, u32[]{:S(2)}) collective-permute-start(f32[4,8,128]{2,1,0:T(8,128)S(1)} %shard_map.93), channel_id=1, source_target_pairs={{0,24},{8,16},{16,8},{24,0},{1,25},{9,17},{17,9},{25,1},{2,26},{10... | collective-permute-start | bytes 49160 | tf_op jit(solution)/shard_map/ppermute | solution.py:599
  31.9 7.8 %copy-start.2 = (s32[8,128]{1,0:T(8,128)S(1)}, s32[8,128]{1,0:T(8,128)}, u32[]{:S(2)}) copy-start(s32[8,128]{1,0:T(8,128)} %block_ref.1) | copy-start | bytes 12292
  31.9 7.7 %collective-permute-start.8 = (f32[32,128]{1,0:T(8,128)S(1)}, f32[32,128]{1,0:T(8,128)S(1)}, u32[]{:S(2)}, u32[]{:S(2)}) collective-permute-start(f32[32,128]{1,0:T(8,128)S(1)} %get-tuple-element.39), channel_id=1, source_target_pairs={{0,1},{1,0},{2,3},{3,2},{4,5},{5,4},{6,7},{7,6},{8,9},{9,8},{10,11... | collective-permute-start | bytes 49160 | tf_op jit(solution)/shard_map/ppermute | solution.py:599
  32.6 7.0 %collective-permute-start.9 = (f32[32,128]{1,0:T(8,128)S(1)}, f32[32,128]{1,0:T(8,128)S(1)}, u32[]{:S(2)}, u32[]{:S(2)}) collective-permute-start(f32[32,128]{1,0:T(8,128)S(1)} %get-tuple-element.40), channel_id=1, source_target_pairs={{0,3},{1,2},{2,1},{3,0},{4,7},{5,6},{6,5},{7,4},{8,11},{9,10},{10,... | collective-permute-start | bytes 49160 | tf_op jit(solution)/shard_map/ppermute | solution.py:599
  42.2 1.9 %collective-permute-start.10 = (bf16[2,144,128]{2,1,0:T(8,128)(2,1)S(1)}, bf16[2,144,128]{2,1,0:T(8,128)(2,1)S(1)}, u32[]{:S(2)}, u32[]{:S(2)}) collective-permute-start(bf16[2,144,128]{2,1,0:T(8,128)(2,1)S(1)} %get-tuple-element.49), channel_id=1, source_target_pairs={{0,8},{8,0},{16,24},{24,16},{1,9},{9,1},{17,25},{25,17},{2,10},{10... | collective-permute-start | bytes 221192 | tf_op jit(solution)/shard_map/ppermute | solution.py:684
  42.5 4.5 %collective-permute-start.11 = (bf16[2,144,128]{2,1,0:T(8,128)(2,1)S(1)}, bf16[2,144,128]{2,1,0:T(8,128)(2,1)S(1)}, u32[]{:S(2)}, u32[]{:S(2)}) collective-permute-start(bf16[2,144,128]{2,1,0:T(8,128)(2,1)S(1)} %get-tuple-element.50), channel_id=1, source_target_pairs={{0,16},{8,24},{16,0},{24,8},{1,17},{9,25},{17,1},{25,9},{2,18},{10... | collective-permute-start | bytes 221192 | tf_op jit(solution)/shard_map/ppermute | solution.py:684
  44.0 4.3 %collective-permute-start.12 = (bf16[2,144,128]{2,1,0:T(8,128)(2,1)S(1)}, bf16[2,144,128]{2,1,0:T(8,128)(2,1)S(1)}, u32[]{:S(2)}, u32[]{:S(2)}) collective-permute-start(bf16[2,144,128]{2,1,0:T(8,128)(2,1)S(1)} %get-tuple-element.51), channel_id=1, source_target_pairs={{0,24},{8,16},{16,8},{24,0},{1,25},{9,17},{17,9},{25,1},{2,26},{10... | collective-permute-start | bytes 221192 | tf_op jit(solution)/shard_map/ppermute | solution.py:684

commit v3 on v2

--- a/solution.py
+++ b/solution.py
@@ -78,8 +78,18 @@
         swap[8 * c + 7, 8 * c + 8] = 1.0
         swap[8 * c + 8, 8 * c + 7] = 1.0
     join_table = np.concatenate([swap, swap], axis=0).astype(np.float32).astype(BF16)
+    spread = np.zeros((128, 128))
+    spread[0, 0::2] = 1.0
+    spread[127, 1::2] = 1.0
+    turn = np.zeros((64, 256))
+    for k in range(4):
+        for c in range(16):
+            turn[16 * k + c, 8 * c + 2 * k] = 1.0
+            turn[16 * k + c, 128 + 8 * c + 2 * k + 1] = 1.0
+    exact = np.concatenate([spread, spread, turn[:, :128], turn[:, 128:]], axis=0)
     split = [row_table[:, :128], row_table[:, 128:], lane_table[:, :128], lane_table[:, 128:]]
-    return jnp.asarray(np.concatenate(split + [join_table], axis=0))
+    split += [join_table, exact.astype(np.float32).astype(BF16)]
+    return jnp.asarray(np.concatenate(split, axis=0))
 
 
 def row_table(table_ref, first=0):
@@ -92,7 +102,31 @@
 
 
 def join_table(table_ref):
-    return table_ref[768:1024]
+    return jnp.concatenate([table_ref[768:1024], table_ref[1024:1280]], axis=1)
+
+
+def turn_table(table_ref):
+    return jnp.concatenate([table_ref[1280:1344], table_ref[1344:1408]], axis=1)
+
+
+def span_of(a, offset=0):
+    if isinstance(a, int):
+        return slice(8 * a + offset, 8 * a + offset + 8)
+    return pl.ds(pl.multiple_of(a * 8 + offset, 8), 8)
+
+
+def sweep(body, together):
+    if together == 4:
+        for a in range(4):
+            body(a)
+        return
+
+    def step(n, carry):
+        for m in range(together):
+            body(n * together + m)
+        return carry
+
+    lax.fori_loop(0, 4 // together, step, 0)
 
 
 def lane_ids(shape):
@@ -121,11 +155,13 @@
 def join_lanes(values, table_ref):
     rows = jnp.concatenate([jnp.concatenate(halves(v), axis=1) for v in values], axis=0)
     other = dot(rows, join_table(table_ref))
-    out, at = [], 0
+    joined, spread, at = [], [], 0
     for v in values:
-        out.append(v + other[at : at + v.shape[0]])
+        span = slice(at, at + v.shape[0])
+        joined.append(v + other[span, :128])
+        spread.append(other[span, 128:])
         at += v.shape[0]
-    return out
+    return joined, spread
 
 
 def join_rows(value):
@@ -189,7 +225,7 @@
         slope = v_ref[n, 0] * axial + v_ref[n, 1] * azimuth[:, 128 * n : 128 * n + 128]
         values.append(m_ref[n] * (slope + v_ref[n, 2] * radius[64 * n : 64 * n + 64]))
         values.append(m_ref[n])
-    for n, value in enumerate(join_lanes(values, table_ref)):
+    for n, value in enumerate(join_lanes(values, table_ref)[0]):
         x_ref[n // 2, n % 2] = join_rows(value)
 
 
@@ -220,41 +256,37 @@
     return (parts[0] + parts[1]) + (parts[2] + parts[3])
 
 
-def pack_all(s_ref, z_ref):
-    def body(q, carry):
-        z_ref[q] = pack_blocks(
-            [
-                (56 - 8 * i + b, s_ref[8 * q + i, 8 * b : 8 * b + 8, :])
-                for i in range(8)
-                for b in range(8)
-            ]
-        )
-        return carry
-
-    lax.fori_loop(0, z_ref.shape[0], body, 0)
-
-
-def first_kernel(
-    scalar_hbm, velocity_hbm, mass_hbm, table_ref,
-    s_ref, z_ref, scalar_ref, velocity_ref, mass_ref, sems,
-):
-    def copies(a):
-        at = pl.ds(pl.multiple_of(a * 8, 8), 8)
-        return [
-            pltpu.make_async_copy(scalar_hbm.at[at], scalar_ref.at[at], sems.at[0, a]),
-            pltpu.make_async_copy(velocity_hbm.at[:, at], velocity_ref.at[:, at], sems.at[1, a]),
-            pltpu.make_async_copy(mass_hbm.at[at], mass_ref.at[at], sems.at[2, a]),
-        ]
-
-    for a in range(4):
-        for copy in copies(a):
-            copy.start()
-
-    def body(a, carry):
-        for copy in copies(a):
-            copy.wait()
-        at = pl.ds(pl.multiple_of(a * 8, 8), 8)
-        at_mass = pl.ds(pl.multiple_of(a * 8 + 32, 8), 8)
+def pick_spread(spreads):
+    slot = ((lane_ids((8, 128)) + 1) >> 1) & 63
+    parts = [jnp.zeros((8, 128), F32) for _ in range(2)]
+    for b, spread in spreads:
+        for i in range(8):
+            block = spread[8 * i : 8 * i + 8]
+            parts[i % 2] = jnp.where(slot == 56 - 8 * i + b, block, parts[i % 2])
+    return parts[0] + parts[1]
+
+
+def join_packed(packed):
+    lane, row = lane_ids((8, 128)), row_ids((8, 128))
+    slot = ((lane + 1) >> 1) & 63
+    b = slot & 7
+    rows = []
+    for value in packed:
+        after = pltpu.roll(pltpu.roll(value, 126, 1), 7, 0)
+        before = pltpu.roll(pltpu.roll(value, 2, 1), 1, 0)
+        value = value + jnp.where((row == 7) & (b < 7), after, 0.0)
+        rows.append(value + jnp.where((row == 0) & (b > 0), before, 0.0))
+    out = list(rows)
+    for a in range(3):
+        out[a] = out[a] + jnp.where(slot < 8, pltpu.roll(rows[a + 1], 16, 1), 0.0)
+        out[a + 1] = out[a + 1] + jnp.where(slot >= 56, pltpu.roll(rows[a], 112, 1), 0.0)
+    return out
+
+
+def first_kernel(scalar_ref, velocity_ref, mass_ref, table_ref, s_ref, z_ref):
+    def body(a):
+        at = span_of(a)
+        spreads = [[], []]
         for pair in range(4):
             spans = [slice(16 * pair + 8 * n, 16 * pair + 8 * n + 8) for n in range(2)]
             fields = [scalar_ref[at, s, :].reshape(64, 128) for s in spans]
@@ -263,19 +295,19 @@
             ]
             masses = [mass_ref[at, s, :].reshape(64, 128) for s in spans]
             values = convect_pair(fields, velocities, masses, table_ref)
-            joined = join_lanes(values + masses, table_ref)
+            joined, spread = join_lanes(values + masses, table_ref)
             for n, s in enumerate(spans):
-                s_ref[at, s, :] = joined[n].reshape(8, 8, 128)
-                s_ref[at_mass, s, :] = joined[n + 2].reshape(8, 8, 128)
-        return carry
-
-    lax.fori_loop(0, 4, body, 0)
+                for f in range(2):
+                    s_ref[span_of(a, 32 * f), s, :] = joined[n + 2 * f].reshape(8, 8, 128)
+                    spreads[f].append((2 * pair + n, spread[n + 2 * f]))
+        for f in range(2):
+            z_ref[a + 4 * f] = pick_spread(spreads[f])
+
+    sweep(body, 2)
     join_block(s_ref)
-    pack_all(s_ref, z_ref)
-
-
-def pack_kernel(s_ref, z_ref):
-    pack_all(s_ref, z_ref)
+    for f in range(2):
+        for n, value in enumerate(join_packed([z_ref[4 * f + a] for a in range(4)])):
+            z_ref[4 * f + n] = value
 
 
 def radial_kernel(count, z_in, x_ref, z_ref):
@@ -343,12 +375,17 @@
 def assembled(s_ref, x_ref, packed, f, a, b, y_refs=None):
     span = slice(8 * b, 8 * b + 8)
     rows = unpacked(packed, b)
-    rows[0] = rows[0] + jnp.where(a == 0, x_ref[0, f, span, :], 0.0)
-    rows[7] = rows[7] + jnp.where(a == 3, x_ref[1, f, span, :], 0.0)
-    block = s_ref[pl.ds(pl.multiple_of(a * 8 + 32 * f, 8), 8), span, :]
+    if not isinstance(a, int):
+        rows[0] = rows[0] + jnp.where(a == 0, x_ref[0, f, span, :], 0.0)
+        rows[7] = rows[7] + jnp.where(a == 3, x_ref[1, f, span, :], 0.0)
+    elif a == 0:
+        rows[0] = rows[0] + x_ref[0, f, span, :]
+    elif a == 3:
+        rows[7] = rows[7] + x_ref[1, f, span, :]
+    at = span_of(a, 32 * f)
+    block = s_ref[at, span, :]
     if y_refs is not None:
         one_ref, two_ref = y_refs
-        at = pl.ds(pl.multiple_of(a * 8 + 32 * f, 8), 8)
         even = (lax.axis_index("ey") & 1) == 0
         if b == 0:
             line, sublane = jnp.where(even, two_ref[at, :], one_ref[at, :]), 0
@@ -360,13 +397,14 @@
 
 
 def second_pairs(
-    cam_count, pairs, s_ref, x_ref, one_ref, two_ref, y_refs, scalar_ref, velocity_ref, mass_ref,
-    table_ref, g_ref, base_ref, half_ref,
+    cam_count, pairs, together, s_ref, x_ref, one_ref, two_ref, y_refs, scalar_ref, velocity_ref,
+    mass_ref, table_ref, g_ref, base_ref, half_ref, z_ref,
 ):
-    def body(a, carry):
-        at = pl.ds(pl.multiple_of(a * 8, 8), 8)
+    def body(a):
+        at = span_of(a)
         radial_g = merged(one_ref[a], two_ref[a], cam_count)
         radial_m = merged(one_ref[a + 4], two_ref[a + 4], cam_count)
+        spreads = []
         for n, pair in enumerate(pairs):
             fields, velocities, masses = [], [], []
             for h, b in enumerate(pair):
@@ -385,33 +423,34 @@
                 )
                 masses.append(mass_ref[at, s, :].reshape(64, 128))
             values = convect_pair(fields, velocities, masses, table_ref)
-            joined = join_lanes(values, table_ref)
-            for h in range(2):
+            joined, spread = join_lanes(values, table_ref)
+            for h, b in enumerate(pair):
                 out = slice(16 * n + 8 * h, 16 * n + 8 * h + 8)
                 g_ref[at, out, :] = joined[h].reshape(8, 8, 128)
-        return carry
-
-    lax.fori_loop(0, 4, body, 0)
+                spreads.append((b, spread[h]))
+        z_ref[a] = pick_spread(spreads)
+
+    sweep(body, together)
 
 
 def second_inner_kernel(
     cam_count, s_ref, x_ref, one_ref, two_ref, scalar_ref, velocity_ref, mass_ref,
-    table_ref, g_ref, base_ref, half_ref,
+    table_ref, g_ref, base_ref, half_ref, z_ref,
 ):
     second_pairs(
-        cam_count, ((1, 2), (3, 4), (5, 6)), s_ref, x_ref, one_ref, two_ref, None,
-        scalar_ref, velocity_ref, mass_ref, table_ref, g_ref, base_ref, half_ref,
+        cam_count, ((1, 2), (3, 4), (5, 6)), 2, s_ref, x_ref, one_ref, two_ref, None,
+        scalar_ref, velocity_ref, mass_ref, table_ref, g_ref, base_ref, half_ref, z_ref,
     )
     join_block(g_ref)
 
 
 def second_outer_kernel(
     cam_count, s_ref, x_ref, one_ref, two_ref, y_one_ref, y_two_ref, scalar_ref, velocity_ref,
-    mass_ref, table_ref, inner_ref, g_ref, x_out_ref, base_ref, half_ref, edge_ref,
+    mass_ref, table_ref, inner_ref, z_in, g_ref, x_out_ref, base_ref, half_ref, z_ref, edge_ref,
 ):
     second_pairs(
-        cam_count, ((0, 7),), s_ref, x_ref, one_ref, two_ref, (y_one_ref, y_two_ref),
-        scalar_ref, velocity_ref, mass_ref, table_ref, edge_ref, base_ref, half_ref,
+        cam_count, ((0, 7),), 4, s_ref, x_ref, one_ref, two_ref, (y_one_ref, y_two_ref),
+        scalar_ref, velocity_ref, mass_ref, table_ref, edge_ref, base_ref, half_ref, z_ref,
     )
     join_axial(edge_ref)
     g_ref[:, 0:8, :] = edge_ref[:, 0:8, :]
@@ -423,6 +462,8 @@
         g_ref[:, low + 1, :] = total
     x_out_ref[0, 0] = g_ref[31]
     x_out_ref[1, 0] = g_ref[0]
+    for n, value in enumerate(join_packed([z_ref[a] + z_in[a] for a in range(4)])):
+        z_ref[n] = value
 
 
 def weight_kernel(weight_ref, out_ref):
@@ -446,11 +487,11 @@
 
 
 def advance(
-    cam_count, pairs, g_ref, x_ref, one_ref, two_ref, y_refs, base_ref, half_ref,
-    advected_ref, turned_ref, element_ref,
+    cam_count, pairs, together, g_ref, x_ref, one_ref, two_ref, y_refs, base_ref, half_ref,
+    table_ref, advected_ref, element_ref,
 ):
-    def body(a, carry):
-        at = pl.ds(pl.multiple_of(a * 8, 8), 8)
+    def body(a):
+        at = span_of(a)
         radial = merged(one_ref[a], two_ref[a], cam_count)
         for n, pair in enumerate(pairs):
             blocks = []
@@ -461,34 +502,35 @@
                 half = half_ref[at, out, :].reshape(64, 128)
                 advected = base - half * g
                 advected_ref[at, out, :] = advected.reshape(8, 8, 128)
-                blocks.append(advected.astype(BF16).astype(F32))
-            p = len(pairs) * a + n
-            turned_ref[p] = jnp.concatenate(blocks, axis=0).T
-            low_half = lane_ids((16, 128)) < 64
-            top = pl.ds(pl.multiple_of(p * 32, 32), 16)
-            bottom = pl.ds(pl.multiple_of(p * 32 + 16, 16), 16)
-            for k in range(0, 8, 2):
-                even = turned_ref[p, pl.ds(k, 16, stride=8), :]
-                odd = turned_ref[p, pl.ds(k + 1, 16, stride=8), :]
-                columns = slice(64 * k, 64 * k + 128)
-                element_ref[top, columns] = jnp.where(
-                    low_half, even, pltpu.roll(odd, 64, 1)
-                ).astype(BF16)
-                element_ref[bottom, columns] = jnp.where(
-                    low_half, pltpu.roll(even, 64, 1), odd
-                ).astype(BF16)
-        return carry
-
-    lax.fori_loop(0, 4, body, 0)
+                value = advected.astype(BF16)
+                zero = jnp.zeros_like(value)
+                blocks.append(jnp.concatenate([value, zero], axis=1))
+                blocks.append(jnp.concatenate([zero, value], axis=1))
+            turned = lax.dot_general(
+                turn_table(table_ref),
+                jnp.concatenate(blocks, axis=0),
+                (((1,), (1,)), ((), ())),
+                preferred_element_type=F32,
+            ).astype(BF16)
+            for h in range(2):
+                place = 32 * (len(pairs) * a + n) + 16 * h
+                if not isinstance(a, int):
+                    place = pl.multiple_of(place, 16)
+                for k in range(4):
+                    element_ref[pl.ds(place, 16), 128 * k : 128 * k + 128] = turned[
+                        16 * k : 16 * k + 16, 128 * h : 128 * h + 128
+                    ]
+
+    sweep(body, together)
 
 
 def render_inner_kernel(
-    cam_count, g_ref, x_ref, one_ref, two_ref, base_ref, half_ref, weight_ref, pick_ref,
-    out_hbm, pixel_ref, advected_ref, turned_ref, element_ref, sem,
+    cam_count, g_ref, x_ref, one_ref, two_ref, base_ref, half_ref, table_ref, weight_ref, pick_ref,
+    out_hbm, pixel_ref, advected_ref, element_ref, sem,
 ):
     advance(
-        cam_count, ((1, 2), (3, 4), (5, 6)), g_ref, x_ref, one_ref, two_ref, None,
-        base_ref, half_ref, advected_ref, turned_ref, element_ref,
+        cam_count, ((1, 2), (3, 4), (5, 6)), 2, g_ref, x_ref, one_ref, two_ref, None,
+        base_ref, half_ref, table_ref, advected_ref, element_ref,
     )
     copy = pltpu.make_async_copy(advected_ref, out_hbm.at[:, pl.ds(8, 48)], sem)
     copy.start()
@@ -500,14 +542,14 @@
 
 def render_outer_kernel(
     cam_count, g_ref, x_ref, one_ref, two_ref, y_one_ref, y_two_ref, base_ref, half_ref,
-    weight_ref, pick_ref, pixel_ref, block_ref, out_in,
+    table_ref, weight_ref, pick_ref, pixel_ref, block_ref, out_in,
     out_hbm, *rest,
 ):
     payload_refs = rest[:cam_count]
-    advected_ref, turned_ref, element_ref, value_ref, sems = rest[cam_count:]
+    advected_ref, element_ref, value_ref, sems = rest[cam_count:]
     advance(
-        cam_count, ((0, 7),), g_ref, x_ref, one_ref, two_ref, (y_one_ref, y_two_ref),
-        base_ref, half_ref, advected_ref, turned_ref, element_ref,
+        cam_count, ((0, 7),), 4, g_ref, x_ref, one_ref, two_ref, (y_one_ref, y_two_ref),
+        base_ref, half_ref, table_ref, advected_ref, element_ref,
     )
     copies = [
         pltpu.make_async_copy(
@@ -535,22 +577,33 @@
         copy.wait()
 
 
-def image_kernel(*refs):
+def scatter(payload_refs, m, chunk):
+    ids, values = [], []
+    for payload_ref in payload_refs:
+        tail = payload_ref[m, 128:, :].astype(F32).astype(jnp.int32)
+        ids.append(tail[0:1, :] * 32 + tail[1:2, :])
+        values.append(payload_ref[m, :128, :])
+    ids = jnp.concatenate(ids, axis=1)
+    row = row_ids((256, ids.shape[1])) + 256 * chunk
+    onehot = jnp.where(row == ids, 1.0, 0.0).astype(BF16)
+    return dot(onehot, jnp.concatenate(values, axis=0))
+
+
+def near_image_kernel(*refs):
+    payload_refs, image_ref = refs[:-1], refs[-1]
+    for m in range(image_ref.shape[0]):
+        for chunk in range(4):
+            at = slice(256 * chunk, 256 * chunk + 256)
+            image_ref[m, at, :] = scatter(payload_refs, m, chunk)
+
+
+def far_image_kernel(near_ref, *refs):
     payload_refs, (image_hbm, image_ref, sems) = refs[:-3], refs[-3:]
     copies = []
     for m in range(image_ref.shape[0]):
-        ids, values = [], []
-        for payload_ref in payload_refs:
-            tail = payload_ref[m, 128:, :].astype(F32).astype(jnp.int32)
-            ids.append(tail[0:1, :] * 32 + tail[1:2, :])
-            values.append(payload_ref[m, :128, :])
-        ids = jnp.concatenate(ids, axis=1)
-        values = jnp.concatenate(values, axis=0)
         for chunk in range(4):
             at = slice(256 * chunk, 256 * chunk + 256)
-            row = row_ids((256, ids.shape[1])) + 256 * chunk
-            onehot = jnp.where(row == ids, 1.0, 0.0).astype(BF16)
-            image_ref[m, at, :] = dot(onehot, values)
+            image_ref[m, at, :] = near_ref[m, at, :] + scatter(payload_refs, m, chunk)
             copy = pltpu.make_async_copy(
                 image_ref.at[m, at], image_hbm.at[m, at], sems.at[4 * m + chunk]
             )
@@ -624,13 +677,9 @@
         ],
     )(*stay(scalar, velocity, mass, tables))
     x_got = swap_axial(x)
-    s, z, scalar, velocity, mass = call(
-        first_kernel,
-        (shape_of(64, 64, 128), shape_of(8, 8, 128))
-        + (shape_of(*flat), shape_of(3, *flat), shape_of(*flat)),
-        in_specs=[HBM] * 3 + [VMEM],
-        scratch_shapes=[pltpu.SemaphoreType.DMA((3, 4))],
-    )(*stay(scalar, velocity, mass), near)
+    s, z = call(first_kernel, (shape_of(64, 64, 128), shape_of(8, 8, 128)))(
+        scalar, velocity, mass, near
+    )
     weights = call(weight_kernel, shape_of(512, 128 * cameras, dtype=BF16))(pixel_weights)
     picks = call(pick_kernel, shape_of(cameras, 128, 512, dtype=BF16))(cut_element)
 
@@ -638,17 +687,17 @@
     z_got = swap_both(z, z, "cam")
     y = call(part(azimuth_kernel, n_cam), (shape_of(64, 128), shape_of(64, 128)))(s, x_got, *z_got)
     y_got = swap_both(*y, "ey")
-    g_inner, *inner_terms = call(
-        part(second_inner_kernel, n_cam), (shape_of(*inner),) * 3
+    g_inner, *inner_terms, z_inner = call(
+        part(second_inner_kernel, n_cam), (shape_of(*inner),) * 3 + (shape_of(4, 8, 128),)
     )(s, x_got, *z_got, scalar, velocity, mass, near)
-    g, x, *outer_terms = call(
+    g, x, *outer_terms, z = call(
         part(second_outer_kernel, n_cam),
-        (shape_of(*flat), shape_of(2, 1, 64, 128), shape_of(*outer), shape_of(*outer)),
+        (shape_of(*flat), shape_of(2, 1, 64, 128), shape_of(*outer), shape_of(*outer))
+        + (shape_of(4, 8, 128),),
         scratch_shapes=[pltpu.VMEM(outer, F32)],
-    )(s, x_got, *z_got, *y_got, scalar, velocity, mass, near, g_inner)
+    )(s, x_got, *z_got, *y_got, scalar, velocity, mass, near, g_inner, z_inner)
 
     x_got = swap_axial(x)
-    z = call(pack_kernel, shape_of(4, 8, 128))(g)
     z = call(part(radial_kernel, 1), shape_of(4, 8, 128))(z, x_got)
     z_got = swap_both(z, z, "cam")
     y = call(part(azimuth_kernel, n_cam), (shape_of(32, 128), shape_of(32, 128)))(g, x_got, *z_got)
@@ -659,38 +708,38 @@
         out_specs=(HBM, VMEM),
         scratch_shapes=[
             pltpu.VMEM(inner, F32),
-            pltpu.VMEM((12, 128, 128), F32),
             pltpu.VMEM((384, 512), BF16),
             pltpu.SemaphoreType.DMA,
         ],
-    )(g, x_got, *z_got, *inner_terms, weights, picks)
+    )(g, x_got, *z_got, *inner_terms, near, weights, picks)
     payload_shape = shape_of(share, 144, 128, dtype=BF16)
     advected, *payloads = call(
         part(render_outer_kernel, n_cam),
         (shape_of(*flat),) + (payload_shape,) * n_cam,
-        in_specs=[VMEM] * 12 + [HBM],
+        in_specs=[VMEM] * 13 + [HBM],
         out_specs=(HBM,) + (VMEM,) * n_cam,
-        input_output_aliases={12: 0},
+        input_output_aliases={13: 0},
         scratch_shapes=[
             pltpu.VMEM(outer, F32),
-            pltpu.VMEM((4, 128, 128), F32),
             pltpu.VMEM((128, 512), BF16),
             pltpu.VMEM((cameras, 128, 128), BF16),
             pltpu.SemaphoreType.DMA((2,)),
         ],
-    )(g, x_got, *z_got, *y_got, *outer_terms, weights, picks, pixels, pixel_block, advected)
-    received = [payloads[0]]
-    for d in range(1, n_cam):
-        received.append(lax.ppermute(payloads[d], "cam", [(i, i ^ d) for i in range(n_cam)]))
+    )(g, x_got, *z_got, *y_got, *outer_terms, near, weights, picks, pixels, pixel_block, advected)
+    received = {0: payloads[0]}
+    for d in reversed(range(1, n_cam)):
+        received[d] = lax.ppermute(payloads[d], "cam", [(i, i ^ d) for i in range(n_cam)])
+    image_shape = shape_of(share, NBLK, 128)
+    images = call(near_image_kernel, image_shape)(received[0], received[1])
     images = call(
-        image_kernel,
-        shape_of(share, NBLK, 128),
+        far_image_kernel,
+        image_shape,
         out_specs=HBM,
         scratch_shapes=[
             pltpu.VMEM((share, NBLK, 128), F32),
             pltpu.SemaphoreType.DMA((4 * share,)),
         ],
-    )(*received)
+    )(images, *[received[d] for d in range(2, n_cam)])
     return (advected.reshape(shape), images)
 
 

time: 49.9 us -> 45.5 us (0.912)
  Pallas kernels: 24 us -> 17.3 us
  starting transfers between devices: 15.5 us -> 17 us
  waiting for transfers between devices: 9.45 us -> 10.1 us
    pallas_call x4, Pallas kernels: 10.7 us -> 6.7 us  [the longest x1 2.75 us: per_device(): call(part(second_inner_kernel, n_cam), (shape_of(*inner),) * 3 + (shape_o...]
    pallas_call x1, Pallas kernels: 2.6 us -> 1.58 us  [per_device(): call(part(render_outer_kernel, n_cam), (shape_of(*flat),) + (payload_shap...]
    pallas_call x1, Pallas kernels: 4.98 us -> 4.02 us  [per_device(): call(part(render_inner_kernel, n_cam), (shape_of(*flat), shape_of(cameras...]
    ppermute x2, starting transfers between devices: 3.6 us -> 4.52 us  [swap_axial(): return lax.ppermute(x, 'ex', up)]
    pallas_call x1, Pallas kernels: 2.07 us -> 1.16 us  [per_device(): call(part(second_outer_kernel, n_cam), (shape_of(*flat), shape_of(2, 1, 6...]
    ppermute x2, waiting for transfers between devices: 3.19 us -> 3.97 us  [swap_axial(): return lax.ppermute(x, 'ex', up)]
    ppermute x8, starting transfers between devices: 9.94 us -> 10.6 us  [swap_both(): return (lax.ppermute(one, axis, even), lax.ppermute(two, axis, odd))]
  transfers between devices with their start and end apart: 13 -> 13, of which waited for: 5 -> 7; matrix products, arithmetic and copies ran while one was open for 0% -> 0% of each run, Pallas kernels for 32% -> 24%
where the time goes in v3:
time: 45.5 us; the launch traced here: 45.3 us
  Pallas kernels  17.3 us (38%)
  starting transfers between devices  17 us (37%)
  waiting for transfers between devices  10.1 us (22%)
  between operations  0.81 us (2%)
    ppermute x8, starting transfers between devices, swap_both(): return (lax.ppermute(one, axis, even), lax.ppermute(two, axis, odd))  10.6 us
    ppermute x2, starting transfers between devices, swap_axial(): return lax.ppermute(x, 'ex', up)  4.52 us
    pallas_call x1, Pallas kernels, per_device(): call(part(render_inner_kernel, n_cam), (shape_of(*flat), shape_of(cameras...  4.02 us
    ppermute x2, waiting for transfers between devices, swap_axial(): return lax.ppermute(x, 'ex', up)  3.97 us
    ppermute x3, waiting for transfers between devices, per_device(): lax.ppermute(payloads[d], 'cam', [(i, i ^ d) for i in range(n_cam)])  3.74 us
    pallas_call x1, Pallas kernels, per_device(): call(part(second_inner_kernel, n_cam), (shape_of(*inner),) * 3 + (shape_o...  2.75 us
    ppermute x8, waiting for transfers between devices, swap_both(): return (lax.ppermute(one, axis, even), lax.ppermute(two, axis, odd))  2.4 us
    pallas_call x1, Pallas kernels, per_device(): call(first_kernel, (shape_of(64, 64, 128), shape_of(8, 8, 128)))  2.29 us
  transfers between devices with their start and end apart: 13, of which 7 were waited for; matrix products, arithmetic and copies ran while one was open for 0% of the time, Pallas kernels for 24%

profile of v3, /device:TPU:0, one launch (start us, length us, event | category | flops | bytes accessed | tf_op | source)
XLA Modules:
  0.0 45.3 jit_solution(1539882187196599440)
XLA Ops:
  0.6 0.0 copy-start.1
  0.6 0.0 copy-start
  0.6 0.0 copy-start.2
  0.7 1.8 %shard_map.86 = (f32[2,2,64,128]{3,2,1,0:T(8,128)S(1)}, bf16[1408,128]{1,0:T(8,128)(2,1)S(1)}) custom-call(f32[32,64,128]{2,1,0:T(8,128)} %bitcast.8, f32[3,32,64,128]{3,2,1,0:T(8,128)} %bitcast.4, f32[32,64,128]{2,1,0:T(8,128)} %bitcast.12, bf16[1408,128]{1,0:T(8,128)(2,1)} %constant.2.clone.table_hbm), custom_call_target="tpu_custom_call" | custom-call | flops 100000000 | bytes 10000000 | tf_op jit(solution)/shard_map/pallas_call | solution.py:668
  2.5 3.0 %collective-permute-start = (f32[2,2,64,128]{3,2,1,0:T(8,128)S(1)}, f32[2,2,64,128]{3,2,1,0:T(8,128)S(1)}, u32[]{:S(2)}, u32[]{:S(2)}) collective-permute-start(f32[2,2,64,128]{3,2,1,0:T(8,128)S(1)} %get-tuple-element.28), channel_id=1, source_target_pairs={{0,4},{4,0},{1,5},{5,1},{2,6},{6,2},{3,7},{7,3},{8,12},{12,8},{9,1... | collective-permute-start | bytes 393224 | tf_op jit(solution)/shard_map/ppermute | solution.py:645
  5.5 0.0 copy-done.1
  5.5 0.0 copy-done
  5.5 0.0 copy-done.2
  5.5 2.3 %shard_map.87 = (f32[64,64,128]{2,1,0:T(8,128)S(1)}, f32[8,8,128]{2,1,0:T(8,128)S(1)}) custom-call(f32[32,64,128]{2,1,0:T(8,128)S(1)} %bitcast.9, f32[3,32,64,128]{3,2,1,0:T(8,128)S(1)} %bitcast.5, f32[32,64,128]{2,1,0:T(8,128)S(1)} %bitcast.13, bf16[1408,128]{1,0:T(8,128)(2,1)S(1)} %get-tuple-element.26.table_ref), custom_call_target="tpu_custom_call" | custom-call | flops 100000000 | bytes 10000000 | tf_op jit(solution)/shard_map/pallas_call | solution.py:680
  7.8 1.2 %collective-permute-done.x_ref = f32[2,2,64,128]{3,2,1,0:T(8,128)S(1)} collective-permute-done((f32[2,2,64,128]{3,2,1,0:T(8,128)S(1)}, f32[2,2,64,128]{3,2,1,0:T(8,128)S(1)}, u32[]{:S(2)}, u32[]{:S(2)}) %collective-permute-start) | collective-permute-done | bytes 131104 | tf_op jit(solution)/shard_map/ppermute | solution.py:645
  9.0 0.1 shard_map.88
  9.1 0.1 collective-permute-start.1
  9.1 1.9 %collective-permute-start.2 = (f32[8,8,128]{2,1,0:T(8,128)S(1)}, f32[8,8,128]{2,1,0:T(8,128)S(1)}, u32[]{:S(2)}, u32[]{:S(2)}) collective-permute-start(f32[8,8,128]{2,1,0:T(8,128)S(1)} %shard_map.88), channel_id=1, source_target_pairs={{0,24},{8,16},{16,8},{24,0},{1,25},{9,17},{17,9},{25,1},{2,26},{10... | collective-permute-start | bytes 98312 | tf_op jit(solution)/shard_map/ppermute | solution.py:652
  11.0 0.0 collective-permute-done.1.one_ref
  11.0 1.6 %collective-permute-done.2.two_ref = f32[8,8,128]{2,1,0:T(8,128)S(1)} collective-permute-done((f32[8,8,128]{2,1,0:T(8,128)S(1)}, f32[8,8,128]{2,1,0:T(8,128)S(1)}, u32[]{:S(2)}, u32[]{:S(2)}) %collective-permute-start.2) | collective-permute-done | bytes 32800 | tf_op jit(solution)/shard_map/ppermute | solution.py:652
  12.6 0.2 shard_map.89
  12.8 1.8 %collective-permute-start.3 = (f32[64,128]{1,0:T(8,128)S(1)}, f32[64,128]{1,0:T(8,128)S(1)}, u32[]{:S(2)}, u32[]{:S(2)}) collective-permute-start(f32[64,128]{1,0:T(8,128)S(1)} %get-tuple-element.30), channel_id=1, source_target_pairs={{0,1},{1,0},{2,3},{3,2},{4,5},{5,4},{6,7},{7,6},{8,9},{9,8},{10,11... | collective-permute-start | bytes 98312 | tf_op jit(solution)/shard_map/ppermute | solution.py:652
  14.6 2.5 %collective-permute-start.4 = (f32[64,128]{1,0:T(8,128)S(1)}, f32[64,128]{1,0:T(8,128)S(1)}, u32[]{:S(2)}, u32[]{:S(2)}) collective-permute-start(f32[64,128]{1,0:T(8,128)S(1)} %get-tuple-element.31), channel_id=1, source_target_pairs={{0,3},{1,2},{2,1},{3,0},{4,7},{5,6},{6,5},{7,4},{8,11},{9,10},{10,... | collective-permute-start | bytes 98312 | tf_op jit(solution)/shard_map/ppermute | solution.py:652
  17.1 2.7 %shard_map.90 = (f32[32,48,128]{2,1,0:T(8,128)S(1)}, f32[32,48,128]{2,1,0:T(8,128)S(1)}, f32[32,48,128]{2,1,0:T(8,128)S(1)}, f32[4,8,128]{2,1,0:T(8,128)S(1)}) custom-call(f32[64,64,128]{2,1,0:T(8,128)S(1)} %get-tuple-element.27.s_ref, f32[2,2,64,128]{3,2,1,0:T(8,128)S(1)} %collective-permute-done.x_ref, f32[8,8,128]{2,1,0:T(8,128)S(1)} %collective-permute-done.1.one_ref, ...), custom_call_target="tpu_custom_call" | custom-call | flops 100000000 | bytes 10000000 | tf_op jit(solution)/shard_map/pallas_call | solution.py:690
  19.8 0.0 collective-permute-done.3.y_one_ref
  19.8 0.5 %collective-permute-done.4.y_two_ref = f32[64,128]{1,0:T(8,128)S(1)} collective-permute-done((f32[64,128]{1,0:T(8,128)S(1)}, f32[64,128]{1,0:T(8,128)S(1)}, u32[]{:S(2)}, u32[]{:S(2)}) %collective-permute-start.4) | collective-permute-done | bytes 32800 | tf_op jit(solution)/shard_map/ppermute | solution.py:652
  20.3 0.0 copy-start.3
  20.3 1.2 %shard_map.91 = (f32[32,64,128]{2,1,0:T(8,128)S(1)}, f32[2,1,64,128]{3,2,1,0:T(8,128)S(1)}, f32[32,16,128]{2,1,0:T(8,128)S(1)}, f32[32,16,128]{2,1,0:T(8,128)S(1)}, f32[4,8,128]{2,1,0:T(8,128)S(1)}) custom-call(f32[64,64,128]{2,1,0:T(8,128)S(1)} %get-tuple-element.27.s_ref, f32[2,2,64,128]{3,2,1,0:T(8,128)S(1)} %collective-permute-done.x_ref, ...), custom_call_target="tpu_custom_call" | custom-call | flops 100000000 | bytes 10000000 | tf_op jit(solution)/shard_map/pallas_call | solution.py:693
  21.5 0.0 copy-start.4
  21.5 1.5 %collective-permute-start.5 = (f32[2,1,64,128]{3,2,1,0:T(8,128)S(1)}, f32[2,1,64,128]{3,2,1,0:T(8,128)S(1)}, u32[]{:S(2)}, u32[]{:S(2)}) collective-permute-start(f32[2,1,64,128]{3,2,1,0:T(8,128)S(1)} %get-tuple-element.35), channel_id=1, source_target_pairs={{0,4},{4,0},{1,5},{5,1},{2,6},{6,2},{3,7},{7,3},{8,12},{12,8},{9,1... | collective-permute-start | bytes 196616 | tf_op jit(solution)/shard_map/ppermute | solution.py:645
  23.0 2.8 %collective-permute-done.5.x_ref = f32[2,1,64,128]{3,2,1,0:T(8,128)S(1)} collective-permute-done((f32[2,1,64,128]{3,2,1,0:T(8,128)S(1)}, f32[2,1,64,128]{3,2,1,0:T(8,128)S(1)}, u32[]{:S(2)}, u32[]{:S(2)}) %collective-permute-start.5) | collective-permute-done | bytes 65568 | tf_op jit(solution)/shard_map/ppermute | solution.py:645
  25.8 0.1 shard_map.92
  25.9 0.1 collective-permute-start.6
  25.9 1.6 %collective-permute-start.7 = (f32[4,8,128]{2,1,0:T(8,128)S(1)}, f32[4,8,128]{2,1,0:T(8,128)S(1)}, u32[]{:S(2)}, u32[]{:S(2)}) collective-permute-start(f32[4,8,128]{2,1,0:T(8,128)S(1)} %shard_map.92), channel_id=1, source_target_pairs={{0,24},{8,16},{16,8},{24,0},{1,25},{9,17},{17,9},{25,1},{2,26},{10... | collective-permute-start | bytes 49160 | tf_op jit(solution)/shard_map/ppermute | solution.py:652
  27.6 0.0 copy-done.3
  27.6 1.3 %shard_map.94.weight_ref = bf16[512,1024]{1,0:T(8,128)(2,1)S(1)} custom-call(bf16[8,512,128]{2,1,0:T(8,128)(2,1)S(1)} %copy-done.3), custom_call_target="tpu_custom_call" | custom-call | flops 100000000 | bytes 10000000 | tf_op jit(solution)/shard_map/pallas_call | solution.py:683
  28.8 0.0 collective-permute-done.6.one_ref
  28.8 0.3 collective-permute-done.7.two_ref
  29.2 0.2 shard_map.93
  29.3 0.0 copy-start.5
  29.3 0.3 collective-permute-start.8
  29.6 2.4 %collective-permute-start.9 = (f32[32,128]{1,0:T(8,128)S(1)}, f32[32,128]{1,0:T(8,128)S(1)}, u32[]{:S(2)}, u32[]{:S(2)}) collective-permute-start(f32[32,128]{1,0:T(8,128)S(1)} %get-tuple-element.38), channel_id=1, source_target_pairs={{0,3},{1,2},{2,1},{3,0},{4,7},{5,6},{6,5},{7,4},{8,11},{9,10},{10,... | collective-permute-start | bytes 49160 | tf_op jit(solution)/shard_map/ppermute | solution.py:652
  32.0 0.0 copy-done.4
  32.0 0.3 shard_map.95.pick_ref
  32.3 4.0 %shard_map.96 = (f32[32,64,128]{2,1,0:T(8,128)}, f32[8,128,128]{2,1,0:T(8,128)S(1)}) custom-call(f32[32,64,128]{2,1,0:T(8,128)S(1)} %get-tuple-element.34.s_ref.g_ref, f32[2,1,64,128]{3,2,1,0:T(8,128)S(1)} %collective-permute-done.5.x_ref, f32[4,8,128]{2,1,0:T(8,128)S(1)} %collective-permute-done.6.one_ref, f32[4,8,128]{2,1,0:T(8,128)S(1)} %collective-permute-done.7.two_ref, ...), custom_call_target="tpu_custom_call" | custom-call | flops 100000000 | bytes 10000000 | tf_op jit(solution)/shard_map/pallas_call | solution.py:705
  36.3 0.0 collective-permute-done.8.y_one_ref
  36.4 0.0 collective-permute-done.9.y_two_ref
  36.4 0.0 copy-done.5
  36.4 1.6 %shard_map.97 = (f32[32,64,128]{2,1,0:T(8,128)}, bf16[2,144,128]{2,1,0:T(8,128)(2,1)S(1)}, bf16[2,144,128]{2,1,0:T(8,128)(2,1)S(1)}, bf16[2,144,128]{2,1,0:T(8,128)(2,1)S(1)}, bf16[2,144,128]{2,1,0:T(8,128)(2,1)S(1)}) custom-call(f32[32,64,128]{2,1,0:T(8,128)S(1)} %get-tuple-element.34.s_ref.g_ref, ...), custom_call_target="tpu_custom_call", output_to_operand_aliasing={{0}: (13, {})} | custom-call | flops 100000000 | bytes 10000000 | tf_op jit(solution)/shard_map/pallas_call | solution.py:716
  38.0 0.2 collective-permute-start.10
  38.2 1.5 %collective-permute-start.11 = (bf16[2,144,128]{2,1,0:T(8,128)(2,1)S(1)}, bf16[2,144,128]{2,1,0:T(8,128)(2,1)S(1)}, u32[]{:S(2)}, u32[]{:S(2)}) collective-permute-start(bf16[2,144,128]{2,1,0:T(8,128)(2,1)S(1)} %get-tuple-element.48), channel_id=1, source_target_pairs={{0,16},{8,24},{16,0},{24,8},{1,17},{9,25},{17,1},{25,9},{2,18},{10... | collective-permute-start | bytes 221192 | tf_op jit(solution)/shard_map/ppermute | solution.py:731
  39.7 0.2 collective-permute-start.12
  39.9 0.0 collective-permute-done.10.refs_1_
  39.9 0.4 shard_map.98.near_ref
  40.3 2.4 %collective-permute-done.11.refs_0_ = bf16[2,144,128]{2,1,0:T(8,128)(2,1)S(1)} collective-permute-done((bf16[2,144,128]{2,1,0:T(8,128)(2,1)S(1)}, bf16[2,144,128]{2,1,0:T(8,128)(2,1)S(1)}, u32[]{:S(2)}, u32[]{:S(2)}) %collective-permute-start.11) | collective-permute-done | bytes 73760 | tf_op jit(solution)/shard_map/ppermute | solution.py:731
  42.7 1.3 %collective-permute-done.12.refs_1_ = bf16[2,144,128]{2,1,0:T(8,128)(2,1)S(1)} collective-permute-done((bf16[2,144,128]{2,1,0:T(8,128)(2,1)S(1)}, bf16[2,144,128]{2,1,0:T(8,128)(2,1)S(1)}, u32[]{:S(2)}, u32[]{:S(2)}) %collective-permute-start.12) | collective-permute-done | bytes 73760 | tf_op jit(solution)/shard_map/ppermute | solution.py:731
  44.1 1.2 %shard_map.99 = f32[2,1024,128]{2,1,0:T(8,128)} custom-call(f32[2,1024,128]{2,1,0:T(8,128)S(1)} %shard_map.98.near_ref, bf16[2,144,128]{2,1,0:T(8,128)(2,1)S(1)} %collective-permute-done.11.refs_0_, bf16[2,144,128]{2,1,0:T(8,128)(2,1)S(1)} %collective-permute-done.12.refs_1_), custom_call_target="tpu_custom_call" | custom-call | flops 100000000 | bytes 10000000 | tf_op jit(solution)/shard_map/pallas_call | solution.py:734
Async XLA Ops:
  0.6 4.8 %copy-start.1 = (f32[4,8,8,8,128]{4,3,2,1,0:T(8,128)S(1)}, f32[4,8,8,8,128]{4,3,2,1,0:T(8,128)}, u32[]{:S(2)}) copy-start(f32[4,8,8,8,128]{4,3,2,1,0:T(8,128)} %param.7) | copy-start | bytes 3145732
  0.6 4.8 %copy-start = (f32[3,4,8,8,8,128]{5,4,3,2,1,0:T(8,128)S(1)}, f32[3,4,8,8,8,128]{5,4,3,2,1,0:T(8,128)}, u32[]{:S(2)}) copy-start(f32[3,4,8,8,8,128]{5,4,3,2,1,0:T(8,128)} %param.8) | copy-start | bytes 9437188
  0.6 4.8 %copy-start.2 = (f32[4,8,8,8,128]{4,3,2,1,0:T(8,128)S(1)}, f32[4,8,8,8,128]{4,3,2,1,0:T(8,128)}, u32[]{:S(2)}) copy-start(f32[4,8,8,8,128]{4,3,2,1,0:T(8,128)} %param.9) | copy-start | bytes 3145732
  2.5 6.5 %collective-permute-start = (f32[2,2,64,128]{3,2,1,0:T(8,128)S(1)}, f32[2,2,64,128]{3,2,1,0:T(8,128)S(1)}, u32[]{:S(2)}, u32[]{:S(2)}) collective-permute-start(f32[2,2,64,128]{3,2,1,0:T(8,128)S(1)} %get-tuple-element.28), channel_id=1, source_target_pairs={{0,4},{4,0},{1,5},{5,1},{2,6},{6,2},{3,7},{7,3},{8,12},{12,8},{9,1... | collective-permute-start | bytes 393224 | tf_op jit(solution)/shard_map/ppermute | solution.py:645
  9.1 2.0 %collective-permute-start.1 = (f32[8,8,128]{2,1,0:T(8,128)S(1)}, f32[8,8,128]{2,1,0:T(8,128)S(1)}, u32[]{:S(2)}, u32[]{:S(2)}) collective-permute-start(f32[8,8,128]{2,1,0:T(8,128)S(1)} %shard_map.88), channel_id=1, source_target_pairs={{0,8},{8,0},{16,24},{24,16},{1,9},{9,1},{17,25},{25,17},{2,10},{10... | collective-permute-start | bytes 98312 | tf_op jit(solution)/shard_map/ppermute | solution.py:652
  9.1 3.5 %collective-permute-start.2 = (f32[8,8,128]{2,1,0:T(8,128)S(1)}, f32[8,8,128]{2,1,0:T(8,128)S(1)}, u32[]{:S(2)}, u32[]{:S(2)}) collective-permute-start(f32[8,8,128]{2,1,0:T(8,128)S(1)} %shard_map.88), channel_id=1, source_target_pairs={{0,24},{8,16},{16,8},{24,0},{1,25},{9,17},{17,9},{25,1},{2,26},{10... | collective-permute-start | bytes 98312 | tf_op jit(solution)/shard_map/ppermute | solution.py:652
  12.8 7.0 %collective-permute-start.3 = (f32[64,128]{1,0:T(8,128)S(1)}, f32[64,128]{1,0:T(8,128)S(1)}, u32[]{:S(2)}, u32[]{:S(2)}) collective-permute-start(f32[64,128]{1,0:T(8,128)S(1)} %get-tuple-element.30), channel_id=1, source_target_pairs={{0,1},{1,0},{2,3},{3,2},{4,5},{5,4},{6,7},{7,6},{8,9},{9,8},{10,11... | collective-permute-start | bytes 98312 | tf_op jit(solution)/shard_map/ppermute | solution.py:652
  14.6 5.7 %collective-permute-start.4 = (f32[64,128]{1,0:T(8,128)S(1)}, f32[64,128]{1,0:T(8,128)S(1)}, u32[]{:S(2)}, u32[]{:S(2)}) collective-permute-start(f32[64,128]{1,0:T(8,128)S(1)} %get-tuple-element.31), channel_id=1, source_target_pairs={{0,3},{1,2},{2,1},{3,0},{4,7},{5,6},{6,5},{7,4},{8,11},{9,10},{10,... | collective-permute-start | bytes 98312 | tf_op jit(solution)/shard_map/ppermute | solution.py:652
  20.3 7.3 %copy-start.3 = (bf16[8,512,128]{2,1,0:T(8,128)(2,1)S(1)}, bf16[8,512,128]{2,1,0:T(8,128)(2,1)}, u32[]{:S(2)}) copy-start(bf16[8,512,128]{2,1,0:T(8,128)(2,1)} %weight_ref.1) | copy-start | bytes 3145732
  21.5 10.5 %copy-start.4 = (s32[8,128]{1,0:T(8,128)S(1)}, s32[8,128]{1,0:T(8,128)}, u32[]{:S(2)}) copy-start(s32[8,128]{1,0:T(8,128)} %cut_ref.1) | copy-start | bytes 12292
  21.5 4.3 %collective-permute-start.5 = (f32[2,1,64,128]{3,2,1,0:T(8,128)S(1)}, f32[2,1,64,128]{3,2,1,0:T(8,128)S(1)}, u32[]{:S(2)}, u32[]{:S(2)}) collective-permute-start(f32[2,1,64,128]{3,2,1,0:T(8,128)S(1)} %get-tuple-element.35), channel_id=1, source_target_pairs={{0,4},{4,0},{1,5},{5,1},{2,6},{6,2},{3,7},{7,3},{8,12},{12,8},{9,1... | collective-permute-start | bytes 196616 | tf_op jit(solution)/shard_map/ppermute | solution.py:645
  25.9 3.0 %collective-permute-start.6 = (f32[4,8,128]{2,1,0:T(8,128)S(1)}, f32[4,8,128]{2,1,0:T(8,128)S(1)}, u32[]{:S(2)}, u32[]{:S(2)}) collective-permute-start(f32[4,8,128]{2,1,0:T(8,128)S(1)} %shard_map.92), channel_id=1, source_target_pairs={{0,8},{8,0},{16,24},{24,16},{1,9},{9,1},{17,25},{25,17},{2,10},{10... | collective-permute-start | bytes 49160 | tf_op jit(solution)/shard_map/ppermute | solution.py:652
  25.9 3.2 %collective-permute-start.7 = (f32[4,8,128]{2,1,0:T(8,128)S(1)}, f32[4,8,128]{2,1,0:T(8,128)S(1)}, u32[]{:S(2)}, u32[]{:S(2)}) collective-permute-start(f32[4,8,128]{2,1,0:T(8,128)S(1)} %shard_map.92), channel_id=1, source_target_pairs={{0,24},{8,16},{16,8},{24,0},{1,25},{9,17},{17,9},{25,1},{2,26},{10... | collective-permute-start | bytes 49160 | tf_op jit(solution)/shard_map/ppermute | solution.py:652
  29.3 7.0 %copy-start.5 = (s32[8,128]{1,0:T(8,128)S(1)}, s32[8,128]{1,0:T(8,128)}, u32[]{:S(2)}) copy-start(s32[8,128]{1,0:T(8,128)} %block_ref.1) | copy-start | bytes 12292
  29.3 7.0 %collective-permute-start.8 = (f32[32,128]{1,0:T(8,128)S(1)}, f32[32,128]{1,0:T(8,128)S(1)}, u32[]{:S(2)}, u32[]{:S(2)}) collective-permute-start(f32[32,128]{1,0:T(8,128)S(1)} %get-tuple-element.37), channel_id=1, source_target_pairs={{0,1},{1,0},{2,3},{3,2},{4,5},{5,4},{6,7},{7,6},{8,9},{9,8},{10,11... | collective-permute-start | bytes 49160 | tf_op jit(solution)/shard_map/ppermute | solution.py:652
  29.6 6.7 %collective-permute-start.9 = (f32[32,128]{1,0:T(8,128)S(1)}, f32[32,128]{1,0:T(8,128)S(1)}, u32[]{:S(2)}, u32[]{:S(2)}) collective-permute-start(f32[32,128]{1,0:T(8,128)S(1)} %get-tuple-element.38), channel_id=1, source_target_pairs={{0,3},{1,2},{2,1},{3,0},{4,7},{5,6},{6,5},{7,4},{8,11},{9,10},{10,... | collective-permute-start | bytes 49160 | tf_op jit(solution)/shard_map/ppermute | solution.py:652
  38.0 1.9 %collective-permute-start.10 = (bf16[2,144,128]{2,1,0:T(8,128)(2,1)S(1)}, bf16[2,144,128]{2,1,0:T(8,128)(2,1)S(1)}, u32[]{:S(2)}, u32[]{:S(2)}) collective-permute-start(bf16[2,144,128]{2,1,0:T(8,128)(2,1)S(1)} %get-tuple-element.47), channel_id=1, source_target_pairs={{0,8},{8,0},{16,24},{24,16},{1,9},{9,1},{17,25},{25,17},{2,10},{10... | collective-permute-start | bytes 221192 | tf_op jit(solution)/shard_map/ppermute | solution.py:731
  38.2 4.5 %collective-permute-start.11 = (bf16[2,144,128]{2,1,0:T(8,128)(2,1)S(1)}, bf16[2,144,128]{2,1,0:T(8,128)(2,1)S(1)}, u32[]{:S(2)}, u32[]{:S(2)}) collective-permute-start(bf16[2,144,128]{2,1,0:T(8,128)(2,1)S(1)} %get-tuple-element.48), channel_id=1, source_target_pairs={{0,16},{8,24},{16,0},{24,8},{1,17},{9,25},{17,1},{25,9},{2,18},{10... | collective-permute-start | bytes 221192 | tf_op jit(solution)/shard_map/ppermute | solution.py:731
  39.7 4.3 %collective-permute-start.12 = (bf16[2,144,128]{2,1,0:T(8,128)(2,1)S(1)}, bf16[2,144,128]{2,1,0:T(8,128)(2,1)S(1)}, u32[]{:S(2)}, u32[]{:S(2)}) collective-permute-start(bf16[2,144,128]{2,1,0:T(8,128)(2,1)S(1)} %get-tuple-element.49), channel_id=1, source_target_pairs={{0,24},{8,16},{16,8},{24,0},{1,25},{9,17},{17,9},{25,1},{2,26},{10... | collective-permute-start | bytes 221192 | tf_op jit(solution)/shard_map/ppermute | solution.py:731

commit v4 on v3

--- a/solution.py
+++ b/solution.py
@@ -86,7 +86,10 @@
         for c in range(16):
             turn[16 * k + c, 8 * c + 2 * k] = 1.0
             turn[16 * k + c, 128 + 8 * c + 2 * k + 1] = 1.0
-    exact = np.concatenate([spread, spread, turn[:, :128], turn[:, 128:]], axis=0)
+    ends = turn.reshape(4, 16, 256)[:, ::15].reshape(8, 256)
+    ends = np.concatenate([ends, np.zeros_like(ends)], axis=0)
+    exact = [spread, spread, turn[:, :128], turn[:, 128:], ends[:, :128], ends[:, 128:]]
+    exact = np.concatenate(exact, axis=0)
     split = [row_table[:, :128], row_table[:, 128:], lane_table[:, :128], lane_table[:, 128:]]
     split += [join_table, exact.astype(np.float32).astype(BF16)]
     return jnp.asarray(np.concatenate(split, axis=0))
@@ -107,6 +110,10 @@
 
 def turn_table(table_ref):
     return jnp.concatenate([table_ref[1280:1344], table_ref[1344:1408]], axis=1)
+
+
+def end_table(table_ref):
+    return jnp.concatenate([table_ref[1408:1424], table_ref[1424:1440]], axis=1)
 
 
 def span_of(a, offset=0):
@@ -226,7 +233,7 @@
         values.append(m_ref[n] * (slope + v_ref[n, 2] * radius[64 * n : 64 * n + 64]))
         values.append(m_ref[n])
     for n, value in enumerate(join_lanes(values, table_ref)[0]):
-        x_ref[n // 2, n % 2] = join_rows(value)
+        x_ref[n // 2, n % 2] = join_rows(value).astype(BF16)
 
 
 def join_block(s_ref):
@@ -310,7 +317,8 @@
             z_ref[4 * f + n] = value
 
 
-def radial_kernel(count, z_in, x_ref, z_ref):
+def radial_kernel(count, z_in, x_in, z_ref, x_ref):
+    x_ref[...] = x_in[...].astype(F32)
     for f in range(count):
         spans = [slice(8 * b, 8 * b + 8) for b in range(8)]
         z_ref[4 * f] = z_in[4 * f] + pack_blocks(
@@ -374,7 +382,12 @@
 
 def assembled(s_ref, x_ref, packed, f, a, b, y_refs=None):
     span = slice(8 * b, 8 * b + 8)
-    rows = unpacked(packed, b)
+    at = span_of(a, 32 * f)
+    block = s_ref[at, span, :]
+    if packed is None:
+        rows = [jnp.zeros((8, 128), F32) for _ in range(8)]
+    else:
+        rows = unpacked(packed, b)
     if not isinstance(a, int):
         rows[0] = rows[0] + jnp.where(a == 0, x_ref[0, f, span, :], 0.0)
         rows[7] = rows[7] + jnp.where(a == 3, x_ref[1, f, span, :], 0.0)
@@ -382,8 +395,6 @@
         rows[0] = rows[0] + x_ref[0, f, span, :]
     elif a == 3:
         rows[7] = rows[7] + x_ref[1, f, span, :]
-    at = span_of(a, 32 * f)
-    block = s_ref[at, span, :]
     if y_refs is not None:
         one_ref, two_ref = y_refs
         even = (lax.axis_index("ey") & 1) == 0
@@ -460,8 +471,8 @@
         total = g_ref[:, low, :] + g_ref[:, low + 1, :]
         g_ref[:, low, :] = total
         g_ref[:, low + 1, :] = total
-    x_out_ref[0, 0] = g_ref[31]
-    x_out_ref[1, 0] = g_ref[0]
+    x_out_ref[0, 0] = g_ref[31].astype(BF16)
+    x_out_ref[1, 0] = g_ref[0].astype(BF16)
     for n, value in enumerate(join_packed([z_ref[a] + z_in[a] for a in range(4)])):
         z_ref[n] = value
 
@@ -477,66 +488,120 @@
 def pick_kernel(cut_ref, pick_ref):
     cut = cut_ref[...]
     a, b, c = cut >> 7, (cut >> 4) & 7, cut & 15
-    inner = 96 * a + 16 * (b - 1) + c
+    order = jnp.where(a == 0, 2, jnp.where(a == 3, 3, a - 1))
+    inner = 96 * order + 16 * (b - 1) + c
+    ends = 512 + 12 * a + 2 * (b - 1) + (c >> 3)
     outer = 384 + 32 * a + jnp.where(b == 7, 16, 0) + c
-    place = jnp.where((b == 0) | (b == 7), outer, inner)
+    place = jnp.where((c == 0) | (c == 15), ends, inner)
+    place = jnp.where((b == 0) | (b == 7), outer, place)
     turned = place.astype(F32).T.astype(jnp.int32)
-    lane = lane_ids((128, 512))
+    lane = lane_ids((128, 640))
     for m in range(8):
         pick_ref[m] = jnp.where(lane == turned[:, m : m + 1], 1.0, 0.0).astype(BF16)
 
 
-def advance(
-    cam_count, pairs, together, g_ref, x_ref, one_ref, two_ref, y_refs, base_ref, half_ref,
-    table_ref, advected_ref, element_ref,
+def turn(blocks, table):
+    rows = []
+    for block in blocks:
+        value = block.astype(BF16)
+        zero = jnp.zeros_like(value)
+        rows.append(jnp.concatenate([value, zero], axis=1))
+        rows.append(jnp.concatenate([zero, value], axis=1))
+    return lax.dot_general(
+        table,
+        jnp.concatenate(rows, axis=0),
+        (((1,), (1,)), ((), ())),
+        preferred_element_type=F32,
+    )
+
+
+def advanced(g_ref, x_ref, packed, y_refs, base_ref, half_ref, a, pair, place):
+    blocks = []
+    for h, b in enumerate(pair):
+        g = assembled(g_ref, x_ref, packed, 0, a, b, y_refs)
+        out = slice(place + 8 * h, place + 8 * h + 8)
+        base = base_ref[span_of(a), out, :].reshape(64, 128)
+        half = half_ref[span_of(a), out, :].reshape(64, 128)
+        blocks.append(base - half * g)
+    return blocks
+
+
+def store_elements(element_ref, blocks, table_ref, place):
+    turned = turn(blocks, turn_table(table_ref)).astype(BF16)
+    for h in range(2):
+        for k in range(4):
+            element_ref[place + 16 * h : place + 16 * h + 16, 128 * k : 128 * k + 128] = turned[
+                16 * k : 16 * k + 16, 128 * h : 128 * h + 128
+            ]
+
+
+def pixel_values(element_ref, weight_ref, m):
+    return dot(element_ref[...], weight_ref[:, 256 * m : 256 * m + 256]).astype(BF16)
+
+
+INNER = ((1, 2), (3, 4), (5, 6))
+
+
+def inner_elements(layers, g_ref, x_ref, base_ref, half_ref, table_ref, element_ref):
+    place = 0
+    for a in layers:
+        for n, pair in enumerate(INNER):
+            blocks = advanced(g_ref, x_ref, None, None, base_ref, half_ref, a, pair, 16 * n)
+            store_elements(element_ref, blocks, table_ref, place)
+            place += 32
+
+
+def early_kernel(g_ref, base_ref, half_ref, table_ref, weight_ref, value_ref, element_ref):
+    inner_elements((1, 2), g_ref, None, base_ref, half_ref, table_ref, element_ref)
+    for m in range(4):
+        value_ref[:, 256 * m : 256 * m + 256] = pixel_values(element_ref, weight_ref, m)
+
+
+def middle_kernel(
+    g_ref, x_ref, base_ref, half_ref, table_ref, weight_ref, pick_ref, early_ref,
+    pixel_ref, element_ref,
 ):
-    def body(a):
-        at = span_of(a)
-        radial = merged(one_ref[a], two_ref[a], cam_count)
-        for n, pair in enumerate(pairs):
-            blocks = []
-            for h, b in enumerate(pair):
-                g = assembled(g_ref, x_ref, radial, 0, a, b, y_refs)
-                out = slice(16 * n + 8 * h, 16 * n + 8 * h + 8)
-                base = base_ref[at, out, :].reshape(64, 128)
-                half = half_ref[at, out, :].reshape(64, 128)
-                advected = base - half * g
-                advected_ref[at, out, :] = advected.reshape(8, 8, 128)
-                value = advected.astype(BF16)
-                zero = jnp.zeros_like(value)
-                blocks.append(jnp.concatenate([value, zero], axis=1))
-                blocks.append(jnp.concatenate([zero, value], axis=1))
-            turned = lax.dot_general(
-                turn_table(table_ref),
-                jnp.concatenate(blocks, axis=0),
-                (((1,), (1,)), ((), ())),
-                preferred_element_type=F32,
-            ).astype(BF16)
-            for h in range(2):
-                place = 32 * (len(pairs) * a + n) + 16 * h
-                if not isinstance(a, int):
-                    place = pl.multiple_of(place, 16)
-                for k in range(4):
-                    element_ref[pl.ds(place, 16), 128 * k : 128 * k + 128] = turned[
-                        16 * k : 16 * k + 16, 128 * h : 128 * h + 128
-                    ]
-
-    sweep(body, together)
+    inner_elements((0, 3), g_ref, x_ref, base_ref, half_ref, table_ref, element_ref)
+    for m in range(4):
+        late = pixel_values(element_ref, weight_ref, m)
+        both = jnp.concatenate([early_ref[:, 256 * m : 256 * m + 256], late], axis=0)
+        for n in range(2):
+            pixel_ref[2 * m + n] = dot(
+                pick_ref[2 * m + n, :, :384], both[:, 128 * n : 128 * n + 128]
+            )
 
 
 def render_inner_kernel(
     cam_count, g_ref, x_ref, one_ref, two_ref, base_ref, half_ref, table_ref, weight_ref, pick_ref,
-    out_hbm, pixel_ref, advected_ref, element_ref, sem,
+    pixel_in, out_hbm, pixel_ref, advected_ref, end_ref, sem,
 ):
-    advance(
-        cam_count, ((1, 2), (3, 4), (5, 6)), 2, g_ref, x_ref, one_ref, two_ref, None,
-        base_ref, half_ref, table_ref, advected_ref, element_ref,
-    )
+    end_ref[48:, :] = jnp.zeros((16, 512), F32)
+
+    def body(a):
+        packed = merged(one_ref[a], two_ref[a], cam_count)
+        for n, pair in enumerate(INNER):
+            blocks = advanced(g_ref, x_ref, packed, None, base_ref, half_ref, a, pair, 16 * n)
+            for h in range(2):
+                out = slice(16 * n + 8 * h, 16 * n + 8 * h + 8)
+                advected_ref[span_of(a), out, :] = blocks[h].reshape(8, 8, 128)
+            turned = turn(blocks, end_table(table_ref))
+            for h in range(2):
+                place = 12 * a + 4 * n + 2 * h
+                for k in range(4):
+                    end_ref[place : place + 2, 128 * k : 128 * k + 128] = turned[
+                        2 * k : 2 * k + 2, 128 * h : 128 * h + 128
+                    ]
+
+    sweep(body, 4)
     copy = pltpu.make_async_copy(advected_ref, out_hbm.at[:, pl.ds(8, 48)], sem)
     copy.start()
-    for m in range(8):
-        values = dot(element_ref[...], weight_ref[:, 128 * m : 128 * m + 128]).astype(BF16)
-        pixel_ref[m] = dot(pick_ref[m, :, :384], values)
+    ends = end_ref[...].astype(BF16)
+    for m in range(4):
+        values = dot(ends, weight_ref[:, 256 * m : 256 * m + 256]).astype(BF16)
+        for n in range(2):
+            pixel_ref[2 * m + n] = pixel_in[2 * m + n] + dot(
+                pick_ref[2 * m + n, :, 512:576], values[:, 128 * n : 128 * n + 128]
+            )
     copy.wait()
 
 
@@ -547,10 +612,14 @@
 ):
     payload_refs = rest[:cam_count]
     advected_ref, element_ref, value_ref, sems = rest[cam_count:]
-    advance(
-        cam_count, ((0, 7),), 4, g_ref, x_ref, one_ref, two_ref, (y_one_ref, y_two_ref),
-        base_ref, half_ref, table_ref, advected_ref, element_ref,
-    )
+    for a in range(4):
+        packed = merged(one_ref[a], two_ref[a], cam_count)
+        blocks = advanced(
+            g_ref, x_ref, packed, (y_one_ref, y_two_ref), base_ref, half_ref, a, (0, 7), 0
+        )
+        for h in range(2):
+            advected_ref[span_of(a), 8 * h : 8 * h + 8, :] = blocks[h].reshape(8, 8, 128)
+        store_elements(element_ref, blocks, table_ref, 32 * a)
     copies = [
         pltpu.make_async_copy(
             advected_ref.at[:, pl.ds(8 * n, 8)], out_hbm.at[:, pl.ds(56 * n, 8)], sems.at[n]
@@ -560,15 +629,17 @@
     for copy in copies:
         copy.start()
     cameras = pixel_ref.shape[0]
-    for m in range(cameras):
-        value_ref[m] = dot(element_ref[...], weight_ref[:, 128 * m : 128 * m + 128]).astype(BF16)
+    for m in range(cameras // 2):
+        values = pixel_values(element_ref, weight_ref, m)
+        value_ref[2 * m] = values[:, :128]
+        value_ref[2 * m + 1] = values[:, 128:]
     me = lax.axis_index("cam")
     share = cameras // cam_count
     sub = row_ids((16, 128))
     for d in range(cam_count):
         for n in range(share):
             m = share * (me ^ d) + n
-            values = dot(pick_ref[m, :, 384:], value_ref[m]) + pixel_ref[m]
+            values = dot(pick_ref[m, :, 384:512], value_ref[m]) + pixel_ref[m]
             payload_refs[d][n, :128, :] = values.astype(BF16)
             ids = block_ref[pl.ds(m, 1), :]
             tail = jnp.where(sub == 0, ids >> 5, jnp.where(sub == 1, ids & 31, 0))
@@ -667,7 +738,7 @@
 
     x, near = call(
         face_kernel,
-        (shape_of(2, 2, 64, 128), shape_of(*tables.shape, dtype=BF16)),
+        (shape_of(2, 2, 64, 128, dtype=BF16), shape_of(*tables.shape, dtype=BF16)),
         in_specs=[HBM] * 4,
         scratch_shapes=[
             pltpu.VMEM((2, 8, 64, 128), F32),
@@ -681,10 +752,11 @@
         scalar, velocity, mass, near
     )
     weights = call(weight_kernel, shape_of(512, 128 * cameras, dtype=BF16))(pixel_weights)
-    picks = call(pick_kernel, shape_of(cameras, 128, 512, dtype=BF16))(cut_element)
-
-    z = call(part(radial_kernel, 2), shape_of(8, 8, 128))(z, x_got)
+    picks = call(pick_kernel, shape_of(cameras, 128, 640, dtype=BF16))(cut_element)
+
+    z, x_got = call(part(radial_kernel, 2), (shape_of(8, 8, 128), shape_of(2, 2, 64, 128)))(z, x_got)
     z_got = swap_both(z, z, "cam")
+    z_got, weights, picks = lax.optimization_barrier((z_got, weights, picks))
     y = call(part(azimuth_kernel, n_cam), (shape_of(64, 128), shape_of(64, 128)))(s, x_got, *z_got)
     y_got = swap_both(*y, "ey")
     g_inner, *inner_terms, z_inner = call(
@@ -692,14 +764,26 @@
     )(s, x_got, *z_got, scalar, velocity, mass, near)
     g, x, *outer_terms, z = call(
         part(second_outer_kernel, n_cam),
-        (shape_of(*flat), shape_of(2, 1, 64, 128), shape_of(*outer), shape_of(*outer))
+        (shape_of(*flat), shape_of(2, 1, 64, 128, dtype=BF16), shape_of(*outer), shape_of(*outer))
         + (shape_of(4, 8, 128),),
         scratch_shapes=[pltpu.VMEM(outer, F32)],
     )(s, x_got, *z_got, *y_got, scalar, velocity, mass, near, g_inner, z_inner)
 
     x_got = swap_axial(x)
-    z = call(part(radial_kernel, 1), shape_of(4, 8, 128))(z, x_got)
+    early = call(
+        early_kernel,
+        shape_of(192, 128 * cameras, dtype=BF16),
+        scratch_shapes=[pltpu.VMEM((192, 512), BF16)],
+    )(g, *inner_terms, near, weights)
+    x_got, early = lax.optimization_barrier((x_got, early))
+    z, x_got = call(part(radial_kernel, 1), (shape_of(4, 8, 128), shape_of(2, 1, 64, 128)))(z, x_got)
     z_got = swap_both(z, z, "cam")
+    pixels = call(
+        middle_kernel,
+        shape_of(cameras, 128, 128),
+        scratch_shapes=[pltpu.VMEM((192, 512), BF16)],
+    )(g, x_got, *inner_terms, near, weights, picks, early)
+    z_got, pixels = lax.optimization_barrier((z_got, pixels))
     y = call(part(azimuth_kernel, n_cam), (shape_of(32, 128), shape_of(32, 128)))(g, x_got, *z_got)
     y_got = swap_both(*y, "ey")
     advected, pixels = call(
@@ -708,10 +792,10 @@
         out_specs=(HBM, VMEM),
         scratch_shapes=[
             pltpu.VMEM(inner, F32),
-            pltpu.VMEM((384, 512), BF16),
+            pltpu.VMEM((64, 512), F32),
             pltpu.SemaphoreType.DMA,
         ],
-    )(g, x_got, *z_got, *inner_terms, near, weights, picks)
+    )(g, x_got, *z_got, *inner_terms, near, weights, picks, pixels)
     payload_shape = shape_of(share, 144, 128, dtype=BF16)
     advected, *payloads = call(
         part(render_outer_kernel, n_cam),

time: 45.5 us -> 42.7 us (0.938)
  waiting for transfers between devices: 10.1 us -> 7.56 us
    ppermute x2, waiting for transfers between devices: 3.97 us -> 1.74 us  [swap_axial(): return lax.ppermute(x, 'ex', up)]
    pallas_call x1, Pallas kernels: 4.02 us -> 2.12 us  [per_device(): call(part(render_inner_kernel, n_cam), (shape_of(*flat), shape_of(cameras...]
    pallas_call x4 -> x6, Pallas kernels: 2.3 us -> 4.06 us  [the longest x1 1.79 us: per_device(): call(face_kernel, (shape_of(2, 2, 64, 128, dtype=BF16), shape_of(*tables....]
  transfers between devices with their start and end apart: 13 -> 13, of which waited for: 7 -> 6; matrix products, arithmetic and copies ran while one was open for 0% -> 0% of each run, Pallas kernels for 24% -> 26%
where the time goes in v4:
time: 42.7 us; the launch traced here: 42.6 us
  Pallas kernels  17.2 us (40%)
  starting transfers between devices  16.9 us (40%)
  waiting for transfers between devices  7.56 us (18%)
  between operations  0.83 us (2%)
    ppermute x8, starting transfers between devices, swap_both(): return (lax.ppermute(one, axis, even), lax.ppermute(two, axis, odd))  10.5 us
    ppermute x2, starting transfers between devices, swap_axial(): return lax.ppermute(x, 'ex', up)  4.51 us
    ppermute x3, waiting for transfers between devices, per_device(): lax.ppermute(payloads[d], 'cam', [(i, i ^ d) for i in range(n_cam)])  3.53 us
    pallas_call x1, Pallas kernels, per_device(): call(part(second_inner_kernel, n_cam), (shape_of(*inner),) * 3 + (shape_o...  2.77 us
    pallas_call x1, Pallas kernels, per_device(): call(first_kernel, (shape_of(64, 64, 128), shape_of(8, 8, 128)))  2.38 us
    ppermute x8, waiting for transfers between devices, swap_both(): return (lax.ppermute(one, axis, even), lax.ppermute(two, axis, odd))  2.29 us
    pallas_call x1, Pallas kernels, per_device(): call(part(render_inner_kernel, n_cam), (shape_of(*flat), shape_of(cameras...  2.12 us
    ppermute x3, starting transfers between devices, per_device(): lax.ppermute(payloads[d], 'cam', [(i, i ^ d) for i in range(n_cam)])  1.93 us
  transfers between devices with their start and end apart: 13, of which 6 were waited for; matrix products, arithmetic and copies ran while one was open for 0% of the time, Pallas kernels for 26%

profile of v4, /device:TPU:0, one launch (start us, length us, event | category | flops | bytes accessed | tf_op | source)
XLA Modules:
  0.0 42.6 jit_solution(5013679737059394632)
XLA Ops:
  0.6 0.0 copy-start
  0.6 0.0 copy-start.1
  0.6 0.0 copy-start.2
  0.7 1.8 %shard_map.86 = (bf16[2,2,64,128]{3,2,1,0:T(8,128)(2,1)S(1)}, bf16[1440,128]{1,0:T(8,128)(2,1)S(1)}) custom-call(f32[32,64,128]{2,1,0:T(8,128)} %bitcast.8, f32[3,32,64,128]{3,2,1,0:T(8,128)} %bitcast.4, f32[32,64,128]{2,1,0:T(8,128)} %bitcast.12, bf16[1440,128]{1,0:T(8,128)(2,1)} %constant.2.clone.table_hbm), custom_call_target="tpu_custom_call" | custom-call | flops 100000000 | bytes 10000000 | tf_op jit(solution)/shard_map/pallas_call | solution.py:739
  2.5 3.0 %collective-permute-start = (bf16[2,2,64,128]{3,2,1,0:T(8,128)(2,1)S(1)}, bf16[2,2,64,128]{3,2,1,0:T(8,128)(2,1)S(1)}, u32[]{:S(2)}, u32[]{:S(2)}) collective-permute-start(bf16[2,2,64,128]{3,2,1,0:T(8,128)(2,1)S(1)} %get-tuple-element.42), channel_id=1, source_target_pairs={{0,4},{4,0},{1,5},{5,1},{2,6},{6,2},{3,7},{7,3},{8,12},{12,8},{9,1... | collective-permute-start | bytes 196616 | tf_op jit(solution)/shard_map/ppermute | solution.py:716
  5.5 0.0 copy-done
  5.5 0.0 copy-done.1
  5.5 0.0 copy-done.2
  5.5 0.0 copy-start.3
  5.5 2.4 %shard_map.87 = (f32[64,64,128]{2,1,0:T(8,128)S(1)}, f32[8,8,128]{2,1,0:T(8,128)S(1)}) custom-call(f32[32,64,128]{2,1,0:T(8,128)S(1)} %bitcast.9, f32[3,32,64,128]{3,2,1,0:T(8,128)S(1)} %bitcast.5, f32[32,64,128]{2,1,0:T(8,128)S(1)} %bitcast.13, bf16[1440,128]{1,0:T(8,128)(2,1)S(1)} %get-tuple-element.39.table_ref), custom_call_target="tpu_custom_call" | custom-call | flops 100000000 | bytes 10000000 | tf_op jit(solution)/shard_map/pallas_call | solution.py:751
  7.9 0.0 copy-start.4
  7.9 0.0 collective-permute-done.x_in
  7.9 0.1 shard_map.88
  8.0 0.7 %collective-permute-start.2 = (f32[8,8,128]{2,1,0:T(8,128)S(1)}, f32[8,8,128]{2,1,0:T(8,128)S(1)}, u32[]{:S(2)}, u32[]{:S(2)}) collective-permute-start(f32[8,8,128]{2,1,0:T(8,128)S(1)} %get-tuple-element.44), channel_id=1, source_target_pairs={{0,24},{8,16},{16,8},{24,0},{1,25},{9,17},{17,9},{25,1},{2,26},{10... | collective-permute-start | bytes 98312 | tf_op jit(solution)/shard_map/ppermute | solution.py:723
  8.7 1.3 %collective-permute-start.1 = (f32[8,8,128]{2,1,0:T(8,128)S(1)}, f32[8,8,128]{2,1,0:T(8,128)S(1)}, u32[]{:S(2)}, u32[]{:S(2)}) collective-permute-start(f32[8,8,128]{2,1,0:T(8,128)S(1)} %get-tuple-element.44), channel_id=1, source_target_pairs={{0,8},{8,0},{16,24},{24,16},{1,9},{9,1},{17,25},{25,17},{2,10},{10... | collective-permute-start | bytes 98312 | tf_op jit(solution)/shard_map/ppermute | solution.py:723
  10.0 0.0 copy-done.3
  10.0 1.3 %shard_map.89.weight_ref = bf16[512,1024]{1,0:T(8,128)(2,1)S(1)} custom-call(bf16[8,512,128]{2,1,0:T(8,128)(2,1)S(1)} %copy-done.3), custom_call_target="tpu_custom_call" | custom-call | flops 100000000 | bytes 10000000 | tf_op jit(solution)/shard_map/pallas_call | solution.py:754
  11.3 0.0 copy-done.4
  11.3 0.4 shard_map.90.pick_ref
  11.7 0.0 collective-permute-done.2.two_ref
  11.7 0.0 collective-permute-done.1.one_ref
  11.7 0.2 shard_map.91
  11.9 1.9 %collective-permute-start.3 = (f32[64,128]{1,0:T(8,128)S(1)}, f32[64,128]{1,0:T(8,128)S(1)}, u32[]{:S(2)}, u32[]{:S(2)}) collective-permute-start(f32[64,128]{1,0:T(8,128)S(1)} %get-tuple-element.47), channel_id=1, source_target_pairs={{0,1},{1,0},{2,3},{3,2},{4,5},{5,4},{6,7},{7,6},{8,9},{9,8},{10,11... | collective-permute-start | bytes 98312 | tf_op jit(solution)/shard_map/ppermute | solution.py:723
  13.8 2.5 %collective-permute-start.4 = (f32[64,128]{1,0:T(8,128)S(1)}, f32[64,128]{1,0:T(8,128)S(1)}, u32[]{:S(2)}, u32[]{:S(2)}) collective-permute-start(f32[64,128]{1,0:T(8,128)S(1)} %get-tuple-element.48), channel_id=1, source_target_pairs={{0,3},{1,2},{2,1},{3,0},{4,7},{5,6},{6,5},{7,4},{8,11},{9,10},{10,... | collective-permute-start | bytes 98312 | tf_op jit(solution)/shard_map/ppermute | solution.py:723
  16.3 2.8 %shard_map.92 = (f32[32,48,128]{2,1,0:T(8,128)S(1)}, f32[32,48,128]{2,1,0:T(8,128)S(1)}, f32[32,48,128]{2,1,0:T(8,128)S(1)}, f32[4,8,128]{2,1,0:T(8,128)S(1)}) custom-call(f32[64,64,128]{2,1,0:T(8,128)S(1)} %get-tuple-element.40.s_ref, f32[2,2,64,128]{3,2,1,0:T(8,128)S(1)} %get-tuple-element.43.x_ref, f32[8,8,128]{2,1,0:T(8,128)S(1)} %collective-permute-done.1.one_ref, ...), custom_call_target="tpu_custom_call" | custom-call | flops 100000000 | bytes 10000000 | tf_op jit(solution)/shard_map/pallas_call | solution.py:762
  19.1 0.0 collective-permute-done.3.y_one_ref
  19.1 0.5 %collective-permute-done.4.y_two_ref = f32[64,128]{1,0:T(8,128)S(1)} collective-permute-done((f32[64,128]{1,0:T(8,128)S(1)}, f32[64,128]{1,0:T(8,128)S(1)}, u32[]{:S(2)}, u32[]{:S(2)}) %collective-permute-start.4) | collective-permute-done | bytes 32800 | tf_op jit(solution)/shard_map/ppermute | solution.py:723
  19.5 1.2 %shard_map.93 = (f32[32,64,128]{2,1,0:T(8,128)S(1)}, bf16[2,1,64,128]{3,2,1,0:T(8,128)(2,1)S(1)}, f32[32,16,128]{2,1,0:T(8,128)S(1)}, f32[32,16,128]{2,1,0:T(8,128)S(1)}, f32[4,8,128]{2,1,0:T(8,128)S(1)}) custom-call(f32[64,64,128]{2,1,0:T(8,128)S(1)} %get-tuple-element.40.s_ref, f32[2,2,64,128]{3,2,1,0:T(8,128)S(1)} %get-tuple-element.43.x_ref, ...), custom_call_target="tpu_custom_call" | custom-call | flops 100000000 | bytes 10000000 | tf_op jit(solution)/shard_map/pallas_call | solution.py:765
  20.7 1.5 %collective-permute-start.5 = (bf16[2,1,64,128]{3,2,1,0:T(8,128)(2,1)S(1)}, bf16[2,1,64,128]{3,2,1,0:T(8,128)(2,1)S(1)}, u32[]{:S(2)}, u32[]{:S(2)}) collective-permute-start(bf16[2,1,64,128]{3,2,1,0:T(8,128)(2,1)S(1)} %get-tuple-element.53), channel_id=1, source_target_pairs={{0,4},{4,0},{1,5},{5,1},{2,6},{6,2},{3,7},{7,3},{8,12},{12,8},{9,1... | collective-permute-start | bytes 98312 | tf_op jit(solution)/shard_map/ppermute | solution.py:716
  22.2 0.7 %shard_map.94.early_ref = bf16[192,1024]{1,0:T(8,128)(2,1)S(1)} custom-call(f32[32,64,128]{2,1,0:T(8,128)S(1)} %get-tuple-element.51.g_ref.s_ref, f32[32,48,128]{2,1,0:T(8,128)S(1)} %get-tuple-element.54.base_ref, f32[32,48,128]{2,1,0:T(8,128)S(1)} %get-tuple-element.55.half_ref, bf16[1440,128]{1,0:T(8,128)(2,1)S(1)} %get-tuple-element.39.table_ref, ...), custom_call_target="tpu_custom_call" | custom-call | flops 100000000 | bytes 10000000 | tf_op jit(solution)/shard_map/pallas_call | solution.py:773
  22.9 1.7 %collective-permute-done.5.x_in = bf16[2,1,64,128]{3,2,1,0:T(8,128)(2,1)S(1)} collective-permute-done((bf16[2,1,64,128]{3,2,1,0:T(8,128)(2,1)S(1)}, bf16[2,1,64,128]{3,2,1,0:T(8,128)(2,1)S(1)}, u32[]{:S(2)}, u32[]{:S(2)}) %collective-permute-start.5) | collective-permute-done | bytes 32800 | tf_op jit(solution)/shard_map/ppermute | solution.py:716
  24.6 0.1 shard_map.95
  24.7 0.1 collective-permute-start.7
  24.8 1.3 %collective-permute-start.6 = (f32[4,8,128]{2,1,0:T(8,128)S(1)}, f32[4,8,128]{2,1,0:T(8,128)S(1)}, u32[]{:S(2)}, u32[]{:S(2)}) collective-permute-start(f32[4,8,128]{2,1,0:T(8,128)S(1)} %get-tuple-element.59), channel_id=1, source_target_pairs={{0,8},{8,0},{16,24},{24,16},{1,9},{9,1},{17,25},{25,17},{2,10},{10... | collective-permute-start | bytes 49160 | tf_op jit(solution)/shard_map/ppermute | solution.py:723
  26.1 1.1 %shard_map.96.pixel_in = f32[8,128,128]{2,1,0:T(8,128)S(1)} custom-call(f32[32,64,128]{2,1,0:T(8,128)S(1)} %get-tuple-element.51.g_ref.s_ref, f32[2,1,64,128]{3,2,1,0:T(8,128)S(1)} %get-tuple-element.58.x_ref, f32[32,48,128]{2,1,0:T(8,128)S(1)} %get-tuple-element.54.base_ref, f32[32,48,128]{2,1,0:T(8,128)S(1)} %get-tuple-element.55.half_ref, ...), custom_call_target="tpu_custom_call" | custom-call | flops 100000000 | bytes 10000000 | tf_op jit(solution)/shard_map/pallas_call | solution.py:781
  27.2 0.7 %collective-permute-done.7.two_ref = f32[4,8,128]{2,1,0:T(8,128)S(1)} collective-permute-done((f32[4,8,128]{2,1,0:T(8,128)S(1)}, f32[4,8,128]{2,1,0:T(8,128)S(1)}, u32[]{:S(2)}, u32[]{:S(2)}) %collective-permute-start.7) | collective-permute-done | bytes 16416 | tf_op jit(solution)/shard_map/ppermute | solution.py:723
  27.9 0.0 collective-permute-done.6.one_ref
  27.9 0.2 shard_map.97
  28.1 0.3 collective-permute-start.8
  28.4 0.0 copy-start.5
  28.4 2.3 %collective-permute-start.9 = (f32[32,128]{1,0:T(8,128)S(1)}, f32[32,128]{1,0:T(8,128)S(1)}, u32[]{:S(2)}, u32[]{:S(2)}) collective-permute-start(f32[32,128]{1,0:T(8,128)S(1)} %get-tuple-element.65), channel_id=1, source_target_pairs={{0,3},{1,2},{2,1},{3,0},{4,7},{5,6},{6,5},{7,4},{8,11},{9,10},{10,... | collective-permute-start | bytes 49160 | tf_op jit(solution)/shard_map/ppermute | solution.py:723
  30.7 2.1 %shard_map.98 = (f32[32,64,128]{2,1,0:T(8,128)}, f32[8,128,128]{2,1,0:T(8,128)S(1)}) custom-call(f32[32,64,128]{2,1,0:T(8,128)S(1)} %get-tuple-element.51.g_ref.s_ref, f32[2,1,64,128]{3,2,1,0:T(8,128)S(1)} %get-tuple-element.58.x_ref, f32[4,8,128]{2,1,0:T(8,128)S(1)} %collective-permute-done.6.one_ref, f32[4,8,128]{2,1,0:T(8,128)S(1)} %collective-permute-done.7.two_ref, ...), custom_call_target="tpu_custom_call" | custom-call | flops 100000000 | bytes 10000000 | tf_op jit(solution)/shard_map/pallas_call | solution.py:789
  32.8 0.0 collective-permute-done.8.y_one_ref
  32.8 1.1 %collective-permute-done.9.y_two_ref = f32[32,128]{1,0:T(8,128)S(1)} collective-permute-done((f32[32,128]{1,0:T(8,128)S(1)}, f32[32,128]{1,0:T(8,128)S(1)}, u32[]{:S(2)}, u32[]{:S(2)}) %collective-permute-start.9) | collective-permute-done | bytes 16416 | tf_op jit(solution)/shard_map/ppermute | solution.py:723
  33.9 0.0 copy-done.5
  33.9 1.5 %shard_map.99 = (f32[32,64,128]{2,1,0:T(8,128)}, bf16[2,144,128]{2,1,0:T(8,128)(2,1)S(1)}, bf16[2,144,128]{2,1,0:T(8,128)(2,1)S(1)}, bf16[2,144,128]{2,1,0:T(8,128)(2,1)S(1)}, bf16[2,144,128]{2,1,0:T(8,128)(2,1)S(1)}) custom-call(f32[32,64,128]{2,1,0:T(8,128)S(1)} %get-tuple-element.51.g_ref.s_ref, ...), custom_call_target="tpu_custom_call", output_to_operand_aliasing={{0}: (13, {})} | custom-call | flops 100000000 | bytes 10000000 | tf_op jit(solution)/shard_map/pallas_call | solution.py:800
  35.4 0.1 collective-permute-start.10
  35.5 1.3 %collective-permute-start.11 = (bf16[2,144,128]{2,1,0:T(8,128)(2,1)S(1)}, bf16[2,144,128]{2,1,0:T(8,128)(2,1)S(1)}, u32[]{:S(2)}, u32[]{:S(2)}) collective-permute-start(bf16[2,144,128]{2,1,0:T(8,128)(2,1)S(1)} %get-tuple-element.74), channel_id=1, source_target_pairs={{0,16},{8,24},{16,0},{24,8},{1,17},{9,25},{17,1},{25,9},{2,18},{10... | collective-permute-start | bytes 221192 | tf_op jit(solution)/shard_map/ppermute | solution.py:815
  36.8 0.6 %collective-permute-start.12 = (bf16[2,144,128]{2,1,0:T(8,128)(2,1)S(1)}, bf16[2,144,128]{2,1,0:T(8,128)(2,1)S(1)}, u32[]{:S(2)}, u32[]{:S(2)}) collective-permute-start(bf16[2,144,128]{2,1,0:T(8,128)(2,1)S(1)} %get-tuple-element.75), channel_id=1, source_target_pairs={{0,24},{8,16},{16,8},{24,0},{1,25},{9,17},{17,9},{25,1},{2,26},{10... | collective-permute-start | bytes 221192 | tf_op jit(solution)/shard_map/ppermute | solution.py:815
  37.4 0.0 collective-permute-done.10.refs_1_
  37.4 0.4 shard_map.100.near_ref
  37.8 2.8 %collective-permute-done.11.refs_0_ = bf16[2,144,128]{2,1,0:T(8,128)(2,1)S(1)} collective-permute-done((bf16[2,144,128]{2,1,0:T(8,128)(2,1)S(1)}, bf16[2,144,128]{2,1,0:T(8,128)(2,1)S(1)}, u32[]{:S(2)}, u32[]{:S(2)}) %collective-permute-start.11) | collective-permute-done | bytes 73760 | tf_op jit(solution)/shard_map/ppermute | solution.py:815
  40.6 0.7 %collective-permute-done.12.refs_1_ = bf16[2,144,128]{2,1,0:T(8,128)(2,1)S(1)} collective-permute-done((bf16[2,144,128]{2,1,0:T(8,128)(2,1)S(1)}, bf16[2,144,128]{2,1,0:T(8,128)(2,1)S(1)}, u32[]{:S(2)}, u32[]{:S(2)}) %collective-permute-start.12) | collective-permute-done | bytes 73760 | tf_op jit(solution)/shard_map/ppermute | solution.py:815
  41.3 1.2 %shard_map.101 = f32[2,1024,128]{2,1,0:T(8,128)} custom-call(f32[2,1024,128]{2,1,0:T(8,128)S(1)} %shard_map.100.near_ref, bf16[2,144,128]{2,1,0:T(8,128)(2,1)S(1)} %collective-permute-done.11.refs_0_, bf16[2,144,128]{2,1,0:T(8,128)(2,1)S(1)} %collective-permute-done.12.refs_1_), custom_call_target="tpu_custom_call" | custom-call | flops 100000000 | bytes 10000000 | tf_op jit(solution)/shard_map/pallas_call | solution.py:818
Async XLA Ops:
  0.6 4.8 %copy-start = (f32[3,4,8,8,8,128]{5,4,3,2,1,0:T(8,128)S(1)}, f32[3,4,8,8,8,128]{5,4,3,2,1,0:T(8,128)}, u32[]{:S(2)}) copy-start(f32[3,4,8,8,8,128]{5,4,3,2,1,0:T(8,128)} %param.8) | copy-start | bytes 9437188
  0.6 4.8 %copy-start.1 = (f32[4,8,8,8,128]{4,3,2,1,0:T(8,128)S(1)}, f32[4,8,8,8,128]{4,3,2,1,0:T(8,128)}, u32[]{:S(2)}) copy-start(f32[4,8,8,8,128]{4,3,2,1,0:T(8,128)} %param.7) | copy-start | bytes 3145732
  0.6 4.8 %copy-start.2 = (f32[4,8,8,8,128]{4,3,2,1,0:T(8,128)S(1)}, f32[4,8,8,8,128]{4,3,2,1,0:T(8,128)}, u32[]{:S(2)}) copy-start(f32[4,8,8,8,128]{4,3,2,1,0:T(8,128)} %param.9) | copy-start | bytes 3145732
  2.5 5.4 %collective-permute-start = (bf16[2,2,64,128]{3,2,1,0:T(8,128)(2,1)S(1)}, bf16[2,2,64,128]{3,2,1,0:T(8,128)(2,1)S(1)}, u32[]{:S(2)}, u32[]{:S(2)}) collective-permute-start(bf16[2,2,64,128]{3,2,1,0:T(8,128)(2,1)S(1)} %get-tuple-element.42), channel_id=1, source_target_pairs={{0,4},{4,0},{1,5},{5,1},{2,6},{6,2},{3,7},{7,3},{8,12},{12,8},{9,1... | collective-permute-start | bytes 196616 | tf_op jit(solution)/shard_map/ppermute | solution.py:716
  5.5 4.6 %copy-start.3 = (bf16[8,512,128]{2,1,0:T(8,128)(2,1)S(1)}, bf16[8,512,128]{2,1,0:T(8,128)(2,1)}, u32[]{:S(2)}) copy-start(bf16[8,512,128]{2,1,0:T(8,128)(2,1)} %weight_ref.1) | copy-start | bytes 3145732
  7.9 3.4 %copy-start.4 = (s32[8,128]{1,0:T(8,128)S(1)}, s32[8,128]{1,0:T(8,128)}, u32[]{:S(2)}) copy-start(s32[8,128]{1,0:T(8,128)} %cut_ref.1) | copy-start | bytes 12292
  8.0 3.7 %collective-permute-start.2 = (f32[8,8,128]{2,1,0:T(8,128)S(1)}, f32[8,8,128]{2,1,0:T(8,128)S(1)}, u32[]{:S(2)}, u32[]{:S(2)}) collective-permute-start(f32[8,8,128]{2,1,0:T(8,128)S(1)} %get-tuple-element.44), channel_id=1, source_target_pairs={{0,24},{8,16},{16,8},{24,0},{1,25},{9,17},{17,9},{25,1},{2,26},{10... | collective-permute-start | bytes 98312 | tf_op jit(solution)/shard_map/ppermute | solution.py:723
  8.7 3.0 %collective-permute-start.1 = (f32[8,8,128]{2,1,0:T(8,128)S(1)}, f32[8,8,128]{2,1,0:T(8,128)S(1)}, u32[]{:S(2)}, u32[]{:S(2)}) collective-permute-start(f32[8,8,128]{2,1,0:T(8,128)S(1)} %get-tuple-element.44), channel_id=1, source_target_pairs={{0,8},{8,0},{16,24},{24,16},{1,9},{9,1},{17,25},{25,17},{2,10},{10... | collective-permute-start | bytes 98312 | tf_op jit(solution)/shard_map/ppermute | solution.py:723
  11.9 7.2 %collective-permute-start.3 = (f32[64,128]{1,0:T(8,128)S(1)}, f32[64,128]{1,0:T(8,128)S(1)}, u32[]{:S(2)}, u32[]{:S(2)}) collective-permute-start(f32[64,128]{1,0:T(8,128)S(1)} %get-tuple-element.47), channel_id=1, source_target_pairs={{0,1},{1,0},{2,3},{3,2},{4,5},{5,4},{6,7},{7,6},{8,9},{9,8},{10,11... | collective-permute-start | bytes 98312 | tf_op jit(solution)/shard_map/ppermute | solution.py:723
  13.8 5.7 %collective-permute-start.4 = (f32[64,128]{1,0:T(8,128)S(1)}, f32[64,128]{1,0:T(8,128)S(1)}, u32[]{:S(2)}, u32[]{:S(2)}) collective-permute-start(f32[64,128]{1,0:T(8,128)S(1)} %get-tuple-element.48), channel_id=1, source_target_pairs={{0,3},{1,2},{2,1},{3,0},{4,7},{5,6},{6,5},{7,4},{8,11},{9,10},{10,... | collective-permute-start | bytes 98312 | tf_op jit(solution)/shard_map/ppermute | solution.py:723
  20.7 3.9 %collective-permute-start.5 = (bf16[2,1,64,128]{3,2,1,0:T(8,128)(2,1)S(1)}, bf16[2,1,64,128]{3,2,1,0:T(8,128)(2,1)S(1)}, u32[]{:S(2)}, u32[]{:S(2)}) collective-permute-start(bf16[2,1,64,128]{3,2,1,0:T(8,128)(2,1)S(1)} %get-tuple-element.53), channel_id=1, source_target_pairs={{0,4},{4,0},{1,5},{5,1},{2,6},{6,2},{3,7},{7,3},{8,12},{12,8},{9,1... | collective-permute-start | bytes 98312 | tf_op jit(solution)/shard_map/ppermute | solution.py:716
  24.7 3.2 %collective-permute-start.7 = (f32[4,8,128]{2,1,0:T(8,128)S(1)}, f32[4,8,128]{2,1,0:T(8,128)S(1)}, u32[]{:S(2)}, u32[]{:S(2)}) collective-permute-start(f32[4,8,128]{2,1,0:T(8,128)S(1)} %get-tuple-element.59), channel_id=1, source_target_pairs={{0,24},{8,16},{16,8},{24,0},{1,25},{9,17},{17,9},{25,1},{2,26},{10... | collective-permute-start | bytes 49160 | tf_op jit(solution)/shard_map/ppermute | solution.py:723
  24.8 3.2 %collective-permute-start.6 = (f32[4,8,128]{2,1,0:T(8,128)S(1)}, f32[4,8,128]{2,1,0:T(8,128)S(1)}, u32[]{:S(2)}, u32[]{:S(2)}) collective-permute-start(f32[4,8,128]{2,1,0:T(8,128)S(1)} %get-tuple-element.59), channel_id=1, source_target_pairs={{0,8},{8,0},{16,24},{24,16},{1,9},{9,1},{17,25},{25,17},{2,10},{10... | collective-permute-start | bytes 49160 | tf_op jit(solution)/shard_map/ppermute | solution.py:723
  28.1 4.7 %collective-permute-start.8 = (f32[32,128]{1,0:T(8,128)S(1)}, f32[32,128]{1,0:T(8,128)S(1)}, u32[]{:S(2)}, u32[]{:S(2)}) collective-permute-start(f32[32,128]{1,0:T(8,128)S(1)} %get-tuple-element.64), channel_id=1, source_target_pairs={{0,1},{1,0},{2,3},{3,2},{4,5},{5,4},{6,7},{7,6},{8,9},{9,8},{10,11... | collective-permute-start | bytes 49160 | tf_op jit(solution)/shard_map/ppermute | solution.py:723
  28.4 5.5 %copy-start.5 = (s32[8,128]{1,0:T(8,128)S(1)}, s32[8,128]{1,0:T(8,128)}, u32[]{:S(2)}) copy-start(s32[8,128]{1,0:T(8,128)} %block_ref.1) | copy-start | bytes 12292
  28.4 5.5 %collective-permute-start.9 = (f32[32,128]{1,0:T(8,128)S(1)}, f32[32,128]{1,0:T(8,128)S(1)}, u32[]{:S(2)}, u32[]{:S(2)}) collective-permute-start(f32[32,128]{1,0:T(8,128)S(1)} %get-tuple-element.65), channel_id=1, source_target_pairs={{0,3},{1,2},{2,1},{3,0},{4,7},{5,6},{6,5},{7,4},{8,11},{9,10},{10,... | collective-permute-start | bytes 49160 | tf_op jit(solution)/shard_map/ppermute | solution.py:723
  35.4 1.9 %collective-permute-start.10 = (bf16[2,144,128]{2,1,0:T(8,128)(2,1)S(1)}, bf16[2,144,128]{2,1,0:T(8,128)(2,1)S(1)}, u32[]{:S(2)}, u32[]{:S(2)}) collective-permute-start(bf16[2,144,128]{2,1,0:T(8,128)(2,1)S(1)} %get-tuple-element.73), channel_id=1, source_target_pairs={{0,8},{8,0},{16,24},{24,16},{1,9},{9,1},{17,25},{25,17},{2,10},{10... | collective-permute-start | bytes 221192 | tf_op jit(solution)/shard_map/ppermute | solution.py:815
  35.5 5.1 %collective-permute-start.11 = (bf16[2,144,128]{2,1,0:T(8,128)(2,1)S(1)}, bf16[2,144,128]{2,1,0:T(8,128)(2,1)S(1)}, u32[]{:S(2)}, u32[]{:S(2)}) collective-permute-start(bf16[2,144,128]{2,1,0:T(8,128)(2,1)S(1)} %get-tuple-element.74), channel_id=1, source_target_pairs={{0,16},{8,24},{16,0},{24,8},{1,17},{9,25},{17,1},{25,9},{2,18},{10... | collective-permute-start | bytes 221192 | tf_op jit(solution)/shard_map/ppermute | solution.py:815
  36.8 4.5 %collective-permute-start.12 = (bf16[2,144,128]{2,1,0:T(8,128)(2,1)S(1)}, bf16[2,144,128]{2,1,0:T(8,128)(2,1)S(1)}, u32[]{:S(2)}, u32[]{:S(2)}) collective-permute-start(bf16[2,144,128]{2,1,0:T(8,128)(2,1)S(1)} %get-tuple-element.75), channel_id=1, source_target_pairs={{0,24},{8,16},{16,8},{24,0},{1,25},{9,17},{17,9},{25,1},{2,26},{10... | collective-permute-start | bytes 221192 | tf_op jit(solution)/shard_map/ppermute | solution.py:815

commit v5 on v4

--- a/solution.py
+++ b/solution.py
@@ -210,12 +210,12 @@
     last = scalar_hbm.shape[0] - 1
     start(scalar_hbm.at[pl.ds(last - 7, 8)], f_ref.at[0])
     start(scalar_hbm.at[pl.ds(0, 8)], f_ref.at[1])
+    start(table_hbm, table_ref)
     start(velocity_hbm.at[:, last], v_ref.at[0])
     start(velocity_hbm.at[:, 0], v_ref.at[1])
     start(mass_hbm.at[last], m_ref.at[0])
     start(mass_hbm.at[0], m_ref.at[1])
-    start(table_hbm, table_ref)
-    for copy in copies:
+    for copy in copies[:3]:
         copy.wait()
     derivative = gll_derivative()
     fields = [f_ref[0, 7], f_ref[1, 0]]
@@ -224,6 +224,8 @@
     low = jnp.concatenate([p[1] for p in pairs], axis=1)
     azimuth = dot(row_table(table_ref, 64), jnp.concatenate([high, low, high], axis=0))
     radius = by_lanes(pairs, table_ref)
+    for copy in copies[3:]:
+        copy.wait()
     values = []
     for n, node in enumerate((7, 0)):
         axial = f_ref[n, 0] * float(derivative[node, 0])
@@ -408,11 +410,13 @@
 
 
 def second_pairs(
-    cam_count, pairs, together, s_ref, x_ref, one_ref, two_ref, y_refs, scalar_ref, velocity_ref,
+    cam_count, pairs, s_ref, x_ref, one_ref, two_ref, y_refs, scalar_ref, velocity_ref,
     mass_ref, table_ref, g_ref, base_ref, half_ref, z_ref,
 ):
-    def body(a):
+    def body(a, layer=None):
         at = span_of(a)
+        layer = a if layer is None else layer
+        to = span_of(layer)
         radial_g = merged(one_ref[a], two_ref[a], cam_count)
         radial_m = merged(one_ref[a + 4], two_ref[a + 4], cam_count)
         spreads = []
@@ -426,8 +430,8 @@
                 scale = time_step / m
                 scalar = scalar_ref[at, s, :].reshape(64, 128)
                 first = scalar - scale * g
-                base_ref[at, out, :] = (0.5 * (scalar + first)).reshape(8, 8, 128)
-                half_ref[at, out, :] = (0.5 * scale).reshape(8, 8, 128)
+                base_ref[to, out, :] = (0.5 * (scalar + first)).reshape(8, 8, 128)
+                half_ref[to, out, :] = (0.5 * scale).reshape(8, 8, 128)
                 fields.append(first)
                 velocities.append(
                     [velocity_ref[d, at, s, :].reshape(64, 128) for d in range(3)]
@@ -437,32 +441,60 @@
             joined, spread = join_lanes(values, table_ref)
             for h, b in enumerate(pair):
                 out = slice(16 * n + 8 * h, 16 * n + 8 * h + 8)
-                g_ref[at, out, :] = joined[h].reshape(8, 8, 128)
+                g_ref[to, out, :] = joined[h].reshape(8, 8, 128)
                 spreads.append((b, spread[h]))
-        z_ref[a] = pick_spread(spreads)
-
-    sweep(body, together)
+        z_ref[layer] = pick_spread(spreads)
+
+    return body
 
 
 def second_inner_kernel(
     cam_count, s_ref, x_ref, one_ref, two_ref, scalar_ref, velocity_ref, mass_ref,
     table_ref, g_ref, base_ref, half_ref, z_ref,
 ):
-    second_pairs(
-        cam_count, ((1, 2), (3, 4), (5, 6)), 2, s_ref, x_ref, one_ref, two_ref, None,
+    body = second_pairs(
+        cam_count, ((1, 2), (3, 4), (5, 6)), s_ref, x_ref, one_ref, two_ref, None,
         scalar_ref, velocity_ref, mass_ref, table_ref, g_ref, base_ref, half_ref, z_ref,
     )
+    sweep(body, 2)
     join_block(g_ref)
+
+
+def second_face_kernel(
+    cam_count, s_ref, x_ref, one_ref, two_ref, y_one_ref, y_two_ref, scalar_ref, velocity_ref,
+    mass_ref, table_ref, inner_ref, x_out_ref, edge_ref, base_ref, half_ref, z_ref,
+):
+    body = second_pairs(
+        cam_count, ((0, 7),), s_ref, x_ref, one_ref, two_ref, (y_one_ref, y_two_ref),
+        scalar_ref, velocity_ref, mass_ref, table_ref, edge_ref, base_ref, half_ref, z_ref,
+    )
+    body(0, 0)
+    body(3, 1)
+    row = row_ids((64, 128))
+    for n, (layer, at) in enumerate(((15, 31), (0, 0))):
+        face = jnp.concatenate(
+            [edge_ref[layer, 0:8, :], inner_ref[at], edge_ref[layer, 8:16, :]], axis=0
+        )
+        after = jnp.where((row == 7) | (row == 55), pltpu.roll(face, 63, 0), 0.0)
+        before = jnp.where((row == 8) | (row == 56), pltpu.roll(face, 1, 0), 0.0)
+        x_out_ref[n, 0] = (face + (after + before)).astype(BF16)
 
 
 def second_outer_kernel(
     cam_count, s_ref, x_ref, one_ref, two_ref, y_one_ref, y_two_ref, scalar_ref, velocity_ref,
-    mass_ref, table_ref, inner_ref, z_in, g_ref, x_out_ref, base_ref, half_ref, z_ref, edge_ref,
+    mass_ref, table_ref, inner_ref, z_in, edge_in, base_in, half_in, z_face,
+    g_ref, base_ref, half_ref, z_ref, edge_ref,
 ):
-    second_pairs(
-        cam_count, ((0, 7),), 4, s_ref, x_ref, one_ref, two_ref, (y_one_ref, y_two_ref),
+    body = second_pairs(
+        cam_count, ((0, 7),), s_ref, x_ref, one_ref, two_ref, (y_one_ref, y_two_ref),
         scalar_ref, velocity_ref, mass_ref, table_ref, edge_ref, base_ref, half_ref, z_ref,
     )
+    body(1)
+    body(2)
+    for layer, a in ((0, 0), (1, 3)):
+        for source, target in ((edge_in, edge_ref), (base_in, base_ref), (half_in, half_ref)):
+            target[span_of(a)] = source[span_of(layer)]
+        z_ref[a] = z_face[layer]
     join_axial(edge_ref)
     g_ref[:, 0:8, :] = edge_ref[:, 0:8, :]
     g_ref[:, 8:56, :] = inner_ref[...]
@@ -471,8 +503,6 @@
         total = g_ref[:, low, :] + g_ref[:, low + 1, :]
         g_ref[:, low, :] = total
         g_ref[:, low + 1, :] = total
-    x_out_ref[0, 0] = g_ref[31].astype(BF16)
-    x_out_ref[1, 0] = g_ref[0].astype(BF16)
     for n, value in enumerate(join_packed([z_ref[a] + z_in[a] for a in range(4)])):
         z_ref[n] = value
 
@@ -605,13 +635,26 @@
     copy.wait()
 
 
-def render_outer_kernel(
+def fill_payload(payload_ref, d, cameras, cam_count, pick_ref, value_ref, pixel_ref, block_ref):
+    me = lax.axis_index("cam")
+    share = cameras // cam_count
+    sub = row_ids((16, 128))
+    for n in range(share):
+        m = share * (me ^ d) + n
+        values = dot(pick_ref[m, :, 384:512], value_ref[m]) + pixel_ref[m]
+        payload_ref[n, :128, :] = values.astype(BF16)
+        ids = block_ref[pl.ds(m, 1), :]
+        tail = jnp.where(sub == 0, ids >> 5, jnp.where(sub == 1, ids & 31, 0))
+        payload_ref[n, 128:, :] = tail.astype(F32).astype(BF16)
+
+
+def render_far_kernel(
     cam_count, g_ref, x_ref, one_ref, two_ref, y_one_ref, y_two_ref, base_ref, half_ref,
     table_ref, weight_ref, pick_ref, pixel_ref, block_ref, out_in,
-    out_hbm, *rest,
+    out_hbm, value_ref, *rest,
 ):
-    payload_refs = rest[:cam_count]
-    advected_ref, element_ref, value_ref, sems = rest[cam_count:]
+    payload_refs = rest[: cam_count - 2]
+    advected_ref, element_ref, sems = rest[cam_count - 2 :]
     for a in range(4):
         packed = merged(one_ref[a], two_ref[a], cam_count)
         blocks = advanced(
@@ -633,19 +676,21 @@
         values = pixel_values(element_ref, weight_ref, m)
         value_ref[2 * m] = values[:, :128]
         value_ref[2 * m + 1] = values[:, 128:]
-    me = lax.axis_index("cam")
-    share = cameras // cam_count
-    sub = row_ids((16, 128))
-    for d in range(cam_count):
-        for n in range(share):
-            m = share * (me ^ d) + n
-            values = dot(pick_ref[m, :, 384:512], value_ref[m]) + pixel_ref[m]
-            payload_refs[d][n, :128, :] = values.astype(BF16)
-            ids = block_ref[pl.ds(m, 1), :]
-            tail = jnp.where(sub == 0, ids >> 5, jnp.where(sub == 1, ids & 31, 0))
-            payload_refs[d][n, 128:, :] = tail.astype(F32).astype(BF16)
+    for d in range(2, cam_count):
+        fill_payload(
+            payload_refs[d - 2], d, cameras, cam_count, pick_ref, value_ref, pixel_ref, block_ref
+        )
     for copy in copies:
         copy.wait()
+
+
+def render_near_kernel(
+    cam_count, d, value_ref, pick_ref, pixel_ref, block_ref, payload_ref
+):
+    cameras = pixel_ref.shape[0]
+    fill_payload(
+        payload_ref, d, cameras, cam_count, pick_ref, value_ref, pixel_ref, block_ref
+    )
 
 
 def scatter(payload_refs, m, chunk):
@@ -660,21 +705,22 @@
     return dot(onehot, jnp.concatenate(values, axis=0))
 
 
-def near_image_kernel(*refs):
-    payload_refs, image_ref = refs[:-1], refs[-1]
+def own_image_kernel(cam_count, value_ref, pick_ref, pixel_ref, block_ref, image_ref, payload_ref):
+    cameras = pixel_ref.shape[0]
+    fill_payload(payload_ref, 0, cameras, cam_count, pick_ref, value_ref, pixel_ref, block_ref)
     for m in range(image_ref.shape[0]):
         for chunk in range(4):
             at = slice(256 * chunk, 256 * chunk + 256)
-            image_ref[m, at, :] = scatter(payload_refs, m, chunk)
-
-
-def far_image_kernel(near_ref, *refs):
+            image_ref[m, at, :] = scatter([payload_ref], m, chunk)
+
+
+def image_kernel(own_ref, *refs):
     payload_refs, (image_hbm, image_ref, sems) = refs[:-3], refs[-3:]
     copies = []
     for m in range(image_ref.shape[0]):
         for chunk in range(4):
             at = slice(256 * chunk, 256 * chunk + 256)
-            image_ref[m, at, :] = near_ref[m, at, :] + scatter(payload_refs, m, chunk)
+            image_ref[m, at, :] = own_ref[m, at, :] + scatter(payload_refs, m, chunk)
             copy = pltpu.make_async_copy(
                 image_ref.at[m, at], image_hbm.at[m, at], sems.at[4 * m + chunk]
             )
@@ -762,12 +808,17 @@
     g_inner, *inner_terms, z_inner = call(
         part(second_inner_kernel, n_cam), (shape_of(*inner),) * 3 + (shape_of(4, 8, 128),)
     )(s, x_got, *z_got, scalar, velocity, mass, near)
-    g, x, *outer_terms, z = call(
+    args = (s, x_got, *z_got, *y_got, scalar, velocity, mass, near, g_inner)
+    some = (16, 16, 128)
+    x, *faces = call(
+        part(second_face_kernel, n_cam),
+        (shape_of(2, 1, 64, 128, dtype=BF16),) + (shape_of(*some),) * 3 + (shape_of(2, 8, 128),),
+    )(*args)
+    g, *outer_terms, z = call(
         part(second_outer_kernel, n_cam),
-        (shape_of(*flat), shape_of(2, 1, 64, 128, dtype=BF16), shape_of(*outer), shape_of(*outer))
-        + (shape_of(4, 8, 128),),
+        (shape_of(*flat), shape_of(*outer), shape_of(*outer), shape_of(4, 8, 128)),
         scratch_shapes=[pltpu.VMEM(outer, F32)],
-    )(s, x_got, *z_got, *y_got, scalar, velocity, mass, near, g_inner, z_inner)
+    )(*args, z_inner, *faces)
 
     x_got = swap_axial(x)
     early = call(
@@ -797,33 +848,39 @@
         ],
     )(g, x_got, *z_got, *inner_terms, near, weights, picks, pixels)
     payload_shape = shape_of(share, 144, 128, dtype=BF16)
-    advected, *payloads = call(
-        part(render_outer_kernel, n_cam),
-        (shape_of(*flat),) + (payload_shape,) * n_cam,
+    advected, values, *far = call(
+        part(render_far_kernel, n_cam),
+        (shape_of(*flat), shape_of(cameras, 128, 128, dtype=BF16)) + (payload_shape,) * (n_cam - 2),
         in_specs=[VMEM] * 13 + [HBM],
-        out_specs=(HBM,) + (VMEM,) * n_cam,
+        out_specs=(HBM, VMEM) + (VMEM,) * (n_cam - 2),
         input_output_aliases={13: 0},
         scratch_shapes=[
             pltpu.VMEM(outer, F32),
             pltpu.VMEM((128, 512), BF16),
-            pltpu.VMEM((cameras, 128, 128), BF16),
             pltpu.SemaphoreType.DMA((2,)),
         ],
     )(g, x_got, *z_got, *y_got, *outer_terms, near, weights, picks, pixels, pixel_block, advected)
-    received = {0: payloads[0]}
-    for d in reversed(range(1, n_cam)):
-        received[d] = lax.ppermute(payloads[d], "cam", [(i, i ^ d) for i in range(n_cam)])
+    parts = (values, picks, pixels, pixel_block)
     image_shape = shape_of(share, NBLK, 128)
-    images = call(near_image_kernel, image_shape)(received[0], received[1])
     images = call(
-        far_image_kernel,
+        part(own_image_kernel, n_cam),
+        image_shape,
+        scratch_shapes=[pltpu.VMEM(payload_shape.shape, BF16)],
+    )(*parts)
+    images, parts = lax.optimization_barrier((images, parts))
+    beside = call(part(render_near_kernel, n_cam, 1), payload_shape)(*parts)
+    received = []
+    for d, payload in [(1, beside)] + [(n + 2, p) for n, p in enumerate(far)]:
+        received.append(lax.ppermute(payload, "cam", [(i, i ^ d) for i in range(n_cam)]))
+    images = call(
+        image_kernel,
         image_shape,
         out_specs=HBM,
         scratch_shapes=[
             pltpu.VMEM((share, NBLK, 128), F32),
             pltpu.SemaphoreType.DMA((4 * share,)),
         ],
-    )(images, *[received[d] for d in range(2, n_cam)])
+    )(images, *received)
     return (advected.reshape(shape), images)
 
 

time: 42.7 us -> 42.2 us (0.988)
  waiting for transfers between devices: 7.56 us -> 6.18 us
  starting transfers between devices: 16.9 us -> 17.4 us
    ppermute x2, waiting for transfers between devices: 1.74 us -> 0.91 us  [swap_axial(): return lax.ppermute(x, 'ex', up)]
    ppermute x3, waiting for transfers between devices: 3.53 us -> 2.97 us  [per_device(): lax.ppermute(payload, 'cam', [(i, i ^ d) for i in range(n_cam)])]
    pallas_call x4 -> x6, Pallas kernels: 4.31 us -> 4.82 us  [the longest x1 1.41 us: per_device(): call(part(render_far_kernel, n_cam), (shape_of(*flat), shape_of(cameras,...]
  transfers between devices with their start and end apart: 13 -> 13, of which waited for: 6 -> 6; matrix products, arithmetic and copies ran while one was open for 0% -> 0% of each run, Pallas kernels for 26% -> 29%
where the time goes in v5:
time: 42.2 us; the launch traced here: 42 us
  Pallas kernels  17.6 us (42%)
  starting transfers between devices  17.4 us (41%)
  waiting for transfers between devices  6.18 us (15%)
  between operations  0.83 us (2%)
    ppermute x8, starting transfers between devices, swap_both(): return (lax.ppermute(one, axis, even), lax.ppermute(two, axis, odd))  10.5 us
    ppermute x2, starting transfers between devices, swap_axial(): return lax.ppermute(x, 'ex', up)  4.56 us
    ppermute x3, waiting for transfers between devices, per_device(): lax.ppermute(payload, 'cam', [(i, i ^ d) for i in range(n_cam)])  2.97 us
    pallas_call x1, Pallas kernels, per_device(): call(part(second_inner_kernel, n_cam), (shape_of(*inner),) * 3 + (shape_o...  2.76 us
    pallas_call x1, Pallas kernels, per_device(): call(first_kernel, (shape_of(64, 64, 128), shape_of(8, 8, 128)))  2.32 us
    ppermute x8, waiting for transfers between devices, swap_both(): return (lax.ppermute(one, axis, even), lax.ppermute(two, axis, odd))  2.3 us
    ppermute x3, starting transfers between devices, per_device(): lax.ppermute(payload, 'cam', [(i, i ^ d) for i in range(n_cam)])  2.27 us
    pallas_call x1, Pallas kernels, per_device(): call(part(render_inner_kernel, n_cam), (shape_of(*flat), shape_of(cameras...  2.12 us
  transfers between devices with their start and end apart: 13, of which 6 were waited for; matrix products, arithmetic and copies ran while one was open for 0% of the time, Pallas kernels for 29%

profile of v5, /device:TPU:0, one launch (start us, length us, event | category | flops | bytes accessed | tf_op | source)
XLA Modules:
  0.0 42.0 jit_solution(16415503952756799085)
XLA Ops:
  0.6 0.0 copy-start
  0.6 0.0 copy-start.1
  0.6 0.0 copy-start.2
  0.7 1.8 %shard_map.86 = (bf16[2,2,64,128]{3,2,1,0:T(8,128)(2,1)S(1)}, bf16[1440,128]{1,0:T(8,128)(2,1)S(1)}) custom-call(f32[32,64,128]{2,1,0:T(8,128)} %bitcast.9, f32[3,32,64,128]{3,2,1,0:T(8,128)} %bitcast.4, f32[32,64,128]{2,1,0:T(8,128)} %bitcast.14, bf16[1440,128]{1,0:T(8,128)(2,1)} %constant.2.clone.table_hbm), custom_call_target="tpu_custom_call" | custom-call | flops 100000000 | bytes 10000000 | tf_op jit(solution)/shard_map/pallas_call | solution.py:785
  2.4 3.0 %collective-permute-start = (bf16[2,2,64,128]{3,2,1,0:T(8,128)(2,1)S(1)}, bf16[2,2,64,128]{3,2,1,0:T(8,128)(2,1)S(1)}, u32[]{:S(2)}, u32[]{:S(2)}) collective-permute-start(bf16[2,2,64,128]{3,2,1,0:T(8,128)(2,1)S(1)} %get-tuple-element.50), channel_id=1, source_target_pairs={{0,4},{4,0},{1,5},{5,1},{2,6},{6,2},{3,7},{7,3},{8,12},{12,8},{9,1... | collective-permute-start | bytes 196616 | tf_op jit(solution)/shard_map/ppermute | solution.py:762
  5.4 0.0 copy-done
  5.4 0.0 copy-done.1
  5.4 0.0 copy-done.2
  5.5 0.0 copy-start.3
  5.5 2.3 %shard_map.87 = (f32[64,64,128]{2,1,0:T(8,128)S(1)}, f32[8,8,128]{2,1,0:T(8,128)S(1)}) custom-call(f32[32,64,128]{2,1,0:T(8,128)S(1)} %bitcast.10, f32[3,32,64,128]{3,2,1,0:T(8,128)S(1)} %bitcast.5, f32[32,64,128]{2,1,0:T(8,128)S(1)} %bitcast.15, bf16[1440,128]{1,0:T(8,128)(2,1)S(1)} %get-tuple-element.47.table_ref), custom_call_target="tpu_custom_call" | custom-call | flops 100000000 | bytes 10000000 | tf_op jit(solution)/shard_map/pallas_call | solution.py:797
  7.8 0.0 copy-start.5
  7.8 0.0 collective-permute-done.x_in
  7.8 0.1 shard_map.88
  7.9 0.7 %collective-permute-start.2 = (f32[8,8,128]{2,1,0:T(8,128)S(1)}, f32[8,8,128]{2,1,0:T(8,128)S(1)}, u32[]{:S(2)}, u32[]{:S(2)}) collective-permute-start(f32[8,8,128]{2,1,0:T(8,128)S(1)} %get-tuple-element.52), channel_id=1, source_target_pairs={{0,24},{8,16},{16,8},{24,0},{1,25},{9,17},{17,9},{25,1},{2,26},{10... | collective-permute-start | bytes 98312 | tf_op jit(solution)/shard_map/ppermute | solution.py:769
  8.6 1.4 %collective-permute-start.1 = (f32[8,8,128]{2,1,0:T(8,128)S(1)}, f32[8,8,128]{2,1,0:T(8,128)S(1)}, u32[]{:S(2)}, u32[]{:S(2)}) collective-permute-start(f32[8,8,128]{2,1,0:T(8,128)S(1)} %get-tuple-element.52), channel_id=1, source_target_pairs={{0,8},{8,0},{16,24},{24,16},{1,9},{9,1},{17,25},{25,17},{2,10},{10... | collective-permute-start | bytes 98312 | tf_op jit(solution)/shard_map/ppermute | solution.py:769
  10.0 0.0 copy-done.3
  10.0 1.3 %shard_map.89.weight_ref = bf16[512,1024]{1,0:T(8,128)(2,1)S(1)} custom-call(bf16[8,512,128]{2,1,0:T(8,128)(2,1)S(1)} %copy-done.3), custom_call_target="tpu_custom_call" | custom-call | flops 100000000 | bytes 10000000 | tf_op jit(solution)/shard_map/pallas_call | solution.py:800
  11.3 0.0 copy-done.5
  11.3 0.4 shard_map.90.pick_ref
  11.7 0.0 collective-permute-done.2.two_ref
  11.7 0.0 collective-permute-done.1.one_ref
  11.7 0.2 shard_map.91
  11.9 1.9 %collective-permute-start.3 = (f32[64,128]{1,0:T(8,128)S(1)}, f32[64,128]{1,0:T(8,128)S(1)}, u32[]{:S(2)}, u32[]{:S(2)}) collective-permute-start(f32[64,128]{1,0:T(8,128)S(1)} %get-tuple-element.55), channel_id=1, source_target_pairs={{0,1},{1,0},{2,3},{3,2},{4,5},{5,4},{6,7},{7,6},{8,9},{9,8},{10,11... | collective-permute-start | bytes 98312 | tf_op jit(solution)/shard_map/ppermute | solution.py:769
  13.8 2.5 %collective-permute-start.4 = (f32[64,128]{1,0:T(8,128)S(1)}, f32[64,128]{1,0:T(8,128)S(1)}, u32[]{:S(2)}, u32[]{:S(2)}) collective-permute-start(f32[64,128]{1,0:T(8,128)S(1)} %get-tuple-element.56), channel_id=1, source_target_pairs={{0,3},{1,2},{2,1},{3,0},{4,7},{5,6},{6,5},{7,4},{8,11},{9,10},{10,... | collective-permute-start | bytes 98312 | tf_op jit(solution)/shard_map/ppermute | solution.py:769
  16.3 2.8 %shard_map.92 = (f32[32,48,128]{2,1,0:T(8,128)S(1)}, f32[32,48,128]{2,1,0:T(8,128)S(1)}, f32[32,48,128]{2,1,0:T(8,128)S(1)}, f32[4,8,128]{2,1,0:T(8,128)S(1)}) custom-call(f32[64,64,128]{2,1,0:T(8,128)S(1)} %get-tuple-element.48.s_ref, f32[2,2,64,128]{3,2,1,0:T(8,128)S(1)} %get-tuple-element.51.x_ref, f32[8,8,128]{2,1,0:T(8,128)S(1)} %collective-permute-done.1.one_ref, ...), custom_call_target="tpu_custom_call" | custom-call | flops 100000000 | bytes 10000000 | tf_op jit(solution)/shard_map/pallas_call | solution.py:808
  19.0 0.0 collective-permute-done.3.y_one_ref
  19.0 0.5 %collective-permute-done.4.y_two_ref = f32[64,128]{1,0:T(8,128)S(1)} collective-permute-done((f32[64,128]{1,0:T(8,128)S(1)}, f32[64,128]{1,0:T(8,128)S(1)}, u32[]{:S(2)}, u32[]{:S(2)}) %collective-permute-start.4) | collective-permute-done | bytes 32800 | tf_op jit(solution)/shard_map/ppermute | solution.py:769
  19.5 0.7 %shard_map.93 = (bf16[2,1,64,128]{3,2,1,0:T(8,128)(2,1)S(1)}, f32[16,16,128]{2,1,0:T(8,128)S(1)}, f32[16,16,128]{2,1,0:T(8,128)S(1)}, f32[16,16,128]{2,1,0:T(8,128)S(1)}, f32[2,8,128]{2,1,0:T(8,128)S(1)}) custom-call(f32[64,64,128]{2,1,0:T(8,128)S(1)} %get-tuple-element.48.s_ref, f32[2,2,64,128]{3,2,1,0:T(8,128)S(1)} %get-tuple-element.51.x_ref, ...), custom_call_target="tpu_custom_call" | custom-call | flops 100000000 | bytes 10000000 | tf_op jit(solution)/shard_map/pallas_call | solution.py:813
  20.2 1.6 %collective-permute-start.5 = (bf16[2,1,64,128]{3,2,1,0:T(8,128)(2,1)S(1)}, bf16[2,1,64,128]{3,2,1,0:T(8,128)(2,1)S(1)}, u32[]{:S(2)}, u32[]{:S(2)}) collective-permute-start(bf16[2,1,64,128]{3,2,1,0:T(8,128)(2,1)S(1)} %get-tuple-element.65), channel_id=1, source_target_pairs={{0,4},{4,0},{1,5},{5,1},{2,6},{6,2},{3,7},{7,3},{8,12},{12,8},{9,1... | collective-permute-start | bytes 98312 | tf_op jit(solution)/shard_map/ppermute | solution.py:762
  21.7 0.8 %shard_map.94 = (f32[32,64,128]{2,1,0:T(8,128)S(1)}, f32[32,16,128]{2,1,0:T(8,128)S(1)}, f32[32,16,128]{2,1,0:T(8,128)S(1)}, f32[4,8,128]{2,1,0:T(8,128)S(1)}) custom-call(f32[64,64,128]{2,1,0:T(8,128)S(1)} %get-tuple-element.48.s_ref, f32[2,2,64,128]{3,2,1,0:T(8,128)S(1)} %get-tuple-element.51.x_ref, f32[8,8,128]{2,1,0:T(8,128)S(1)} %collective-permute-done.1.one_ref, ...), custom_call_target="tpu_custom_call" | custom-call | flops 100000000 | bytes 10000000 | tf_op jit(solution)/shard_map/pallas_call | solution.py:817
  22.6 0.7 %shard_map.95.early_ref = bf16[192,1024]{1,0:T(8,128)(2,1)S(1)} custom-call(f32[32,64,128]{2,1,0:T(8,128)S(1)} %get-tuple-element.63.g_ref.s_ref, f32[32,48,128]{2,1,0:T(8,128)S(1)} %get-tuple-element.66.base_ref, f32[32,48,128]{2,1,0:T(8,128)S(1)} %get-tuple-element.67.half_ref, bf16[1440,128]{1,0:T(8,128)(2,1)S(1)} %get-tuple-element.47.table_ref, ...), custom_call_target="tpu_custom_call" | custom-call | flops 100000000 | bytes 10000000 | tf_op jit(solution)/shard_map/pallas_call | solution.py:824
  23.3 0.9 %collective-permute-done.5.x_in = bf16[2,1,64,128]{3,2,1,0:T(8,128)(2,1)S(1)} collective-permute-done((bf16[2,1,64,128]{3,2,1,0:T(8,128)(2,1)S(1)}, bf16[2,1,64,128]{3,2,1,0:T(8,128)(2,1)S(1)}, u32[]{:S(2)}, u32[]{:S(2)}) %collective-permute-start.5) | collective-permute-done | bytes 32800 | tf_op jit(solution)/shard_map/ppermute | solution.py:762
  24.2 0.1 shard_map.96
  24.3 0.1 collective-permute-start.7
  24.3 1.3 %collective-permute-start.6 = (f32[4,8,128]{2,1,0:T(8,128)S(1)}, f32[4,8,128]{2,1,0:T(8,128)S(1)}, u32[]{:S(2)}, u32[]{:S(2)}) collective-permute-start(f32[4,8,128]{2,1,0:T(8,128)S(1)} %get-tuple-element.71), channel_id=1, source_target_pairs={{0,8},{8,0},{16,24},{24,16},{1,9},{9,1},{17,25},{25,17},{2,10},{10... | collective-permute-start | bytes 49160 | tf_op jit(solution)/shard_map/ppermute | solution.py:769
  25.7 1.0 %shard_map.97.pixel_in = f32[8,128,128]{2,1,0:T(8,128)S(1)} custom-call(f32[32,64,128]{2,1,0:T(8,128)S(1)} %get-tuple-element.63.g_ref.s_ref, f32[2,1,64,128]{3,2,1,0:T(8,128)S(1)} %get-tuple-element.70.x_ref, f32[32,48,128]{2,1,0:T(8,128)S(1)} %get-tuple-element.66.base_ref, f32[32,48,128]{2,1,0:T(8,128)S(1)} %get-tuple-element.67.half_ref, ...), custom_call_target="tpu_custom_call" | custom-call | flops 100000000 | bytes 10000000 | tf_op jit(solution)/shard_map/pallas_call | solution.py:832
  26.7 0.7 %collective-permute-done.7.two_ref = f32[4,8,128]{2,1,0:T(8,128)S(1)} collective-permute-done((f32[4,8,128]{2,1,0:T(8,128)S(1)}, f32[4,8,128]{2,1,0:T(8,128)S(1)}, u32[]{:S(2)}, u32[]{:S(2)}) %collective-permute-start.7) | collective-permute-done | bytes 16416 | tf_op jit(solution)/shard_map/ppermute | solution.py:769
  27.5 0.0 collective-permute-done.6.one_ref
  27.5 0.2 shard_map.98
  27.6 0.3 collective-permute-start.8
  27.9 0.0 copy-start.4
  27.9 2.3 %collective-permute-start.9 = (f32[32,128]{1,0:T(8,128)S(1)}, f32[32,128]{1,0:T(8,128)S(1)}, u32[]{:S(2)}, u32[]{:S(2)}) collective-permute-start(f32[32,128]{1,0:T(8,128)S(1)} %get-tuple-element.77), channel_id=1, source_target_pairs={{0,3},{1,2},{2,1},{3,0},{4,7},{5,6},{6,5},{7,4},{8,11},{9,10},{10,... | collective-permute-start | bytes 49160 | tf_op jit(solution)/shard_map/ppermute | solution.py:769
  30.2 2.1 %shard_map.99 = (f32[32,64,128]{2,1,0:T(8,128)}, f32[8,128,128]{2,1,0:T(8,128)S(1)}) custom-call(f32[32,64,128]{2,1,0:T(8,128)S(1)} %get-tuple-element.63.g_ref.s_ref, f32[2,1,64,128]{3,2,1,0:T(8,128)S(1)} %get-tuple-element.70.x_ref, f32[4,8,128]{2,1,0:T(8,128)S(1)} %collective-permute-done.6.one_ref, f32[4,8,128]{2,1,0:T(8,128)S(1)} %collective-permute-done.7.two_ref, ...), custom_call_target="tpu_custom_call" | custom-call | flops 100000000 | bytes 10000000 | tf_op jit(solution)/shard_map/pallas_call | solution.py:840
  32.4 0.0 collective-permute-done.8.y_one_ref
  32.4 1.1 %collective-permute-done.9.y_two_ref = f32[32,128]{1,0:T(8,128)S(1)} collective-permute-done((f32[32,128]{1,0:T(8,128)S(1)}, f32[32,128]{1,0:T(8,128)S(1)}, u32[]{:S(2)}, u32[]{:S(2)}) %collective-permute-start.9) | collective-permute-done | bytes 16416 | tf_op jit(solution)/shard_map/ppermute | solution.py:769
  33.4 0.0 copy-done.4
  33.4 1.4 %shard_map.100 = (f32[32,64,128]{2,1,0:T(8,128)}, bf16[8,128,128]{2,1,0:T(8,128)(2,1)S(1)}, bf16[2,144,128]{2,1,0:T(8,128)(2,1)S(1)}, bf16[2,144,128]{2,1,0:T(8,128)(2,1)S(1)}) custom-call(f32[32,64,128]{2,1,0:T(8,128)S(1)} %get-tuple-element.63.g_ref.s_ref, f32[2,1,64,128]{3,2,1,0:T(8,128)S(1)} %get-tuple-element.70.x_ref, ...), custom_call_target="tpu_custom_call", output_to_operand_aliasing={{0}: (13, {})} | custom-call | flops 100000000 | bytes 10000000 | tf_op jit(solution)/shard_map/pallas_call | solution.py:851
  34.9 1.3 %collective-permute-start.11 = (bf16[2,144,128]{2,1,0:T(8,128)(2,1)S(1)}, bf16[2,144,128]{2,1,0:T(8,128)(2,1)S(1)}, u32[]{:S(2)}, u32[]{:S(2)}) collective-permute-start(bf16[2,144,128]{2,1,0:T(8,128)(2,1)S(1)} %get-tuple-element.90), channel_id=1, source_target_pairs={{0,16},{8,24},{16,0},{24,8},{1,17},{9,25},{17,1},{25,9},{2,18},{10... | collective-permute-start | bytes 221192 | tf_op jit(solution)/shard_map/ppermute | solution.py:874
  36.2 0.0 collective-permute-start.12
  36.2 0.4 %shard_map.101.own_ref = f32[2,1024,128]{2,1,0:T(8,128)S(1)} custom-call(bf16[8,128,128]{2,1,0:T(8,128)(2,1)S(1)} %get-tuple-element.86.value_ref, bf16[8,128,640]{2,1,0:T(8,128)(2,1)S(1)} %shard_map.90.pick_ref, f32[8,128,128]{2,1,0:T(8,128)S(1)} %get-tuple-element.88.pixel_ref, s32[8,128]{1,0:T(8,128)S(1)} %copy-done.4), custom_call_target="tpu_custom_call" | custom-call | flops 100000000 | bytes 10000000 | tf_op jit(solution)/shard_map/pallas_call | solution.py:865
  36.6 0.2 shard_map.102
  36.8 0.9 %collective-permute-start.10 = (bf16[2,144,128]{2,1,0:T(8,128)(2,1)S(1)}, bf16[2,144,128]{2,1,0:T(8,128)(2,1)S(1)}, u32[]{:S(2)}, u32[]{:S(2)}) collective-permute-start(bf16[2,144,128]{2,1,0:T(8,128)(2,1)S(1)} %shard_map.102), channel_id=1, source_target_pairs={{0,8},{8,0},{16,24},{24,16},{1,9},{9,1},{17,25},{25,17},{2,10},{10... | collective-permute-start | bytes 221192 | tf_op jit(solution)/shard_map/ppermute | solution.py:874
  37.7 1.7 %collective-permute-done.11.refs_1_ = bf16[2,144,128]{2,1,0:T(8,128)(2,1)S(1)} collective-permute-done((bf16[2,144,128]{2,1,0:T(8,128)(2,1)S(1)}, bf16[2,144,128]{2,1,0:T(8,128)(2,1)S(1)}, u32[]{:S(2)}, u32[]{:S(2)}) %collective-permute-start.11) | collective-permute-done | bytes 73760 | tf_op jit(solution)/shard_map/ppermute | solution.py:874
  39.4 1.3 %collective-permute-done.12.refs_2_ = bf16[2,144,128]{2,1,0:T(8,128)(2,1)S(1)} collective-permute-done((bf16[2,144,128]{2,1,0:T(8,128)(2,1)S(1)}, bf16[2,144,128]{2,1,0:T(8,128)(2,1)S(1)}, u32[]{:S(2)}, u32[]{:S(2)}) %collective-permute-start.12) | collective-permute-done | bytes 73760 | tf_op jit(solution)/shard_map/ppermute | solution.py:874
  40.7 0.0 collective-permute-done.10.refs_0_
  40.7 1.3 %shard_map.103 = f32[2,1024,128]{2,1,0:T(8,128)} custom-call(f32[2,1024,128]{2,1,0:T(8,128)S(1)} %shard_map.101.own_ref, bf16[2,144,128]{2,1,0:T(8,128)(2,1)S(1)} %collective-permute-done.10.refs_0_, bf16[2,144,128]{2,1,0:T(8,128)(2,1)S(1)} %collective-permute-done.11.refs_1_, bf16[2,144,128]{2,1,0:T(8,128)(2,1)S(1)} %collective-permute-done.12.refs_2_), custom_call_target="tpu_custom_call" | custom-call | flops 100000000 | bytes 10000000 | tf_op jit(solution)/shard_map/pallas_call | solution.py:875
Async XLA Ops:
  0.6 4.8 %copy-start = (f32[3,4,8,8,8,128]{5,4,3,2,1,0:T(8,128)S(1)}, f32[3,4,8,8,8,128]{5,4,3,2,1,0:T(8,128)}, u32[]{:S(2)}) copy-start(f32[3,4,8,8,8,128]{5,4,3,2,1,0:T(8,128)} %param.8) | copy-start | bytes 9437188
  0.6 4.8 %copy-start.1 = (f32[4,8,8,8,128]{4,3,2,1,0:T(8,128)S(1)}, f32[4,8,8,8,128]{4,3,2,1,0:T(8,128)}, u32[]{:S(2)}) copy-start(f32[4,8,8,8,128]{4,3,2,1,0:T(8,128)} %param.7) | copy-start | bytes 3145732
  0.6 4.8 %copy-start.2 = (f32[4,8,8,8,128]{4,3,2,1,0:T(8,128)S(1)}, f32[4,8,8,8,128]{4,3,2,1,0:T(8,128)}, u32[]{:S(2)}) copy-start(f32[4,8,8,8,128]{4,3,2,1,0:T(8,128)} %param.9) | copy-start | bytes 3145732
  2.4 5.4 %collective-permute-start = (bf16[2,2,64,128]{3,2,1,0:T(8,128)(2,1)S(1)}, bf16[2,2,64,128]{3,2,1,0:T(8,128)(2,1)S(1)}, u32[]{:S(2)}, u32[]{:S(2)}) collective-permute-start(bf16[2,2,64,128]{3,2,1,0:T(8,128)(2,1)S(1)} %get-tuple-element.50), channel_id=1, source_target_pairs={{0,4},{4,0},{1,5},{5,1},{2,6},{6,2},{3,7},{7,3},{8,12},{12,8},{9,1... | collective-permute-start | bytes 196616 | tf_op jit(solution)/shard_map/ppermute | solution.py:762
  5.5 4.6 %copy-start.3 = (bf16[8,512,128]{2,1,0:T(8,128)(2,1)S(1)}, bf16[8,512,128]{2,1,0:T(8,128)(2,1)}, u32[]{:S(2)}) copy-start(bf16[8,512,128]{2,1,0:T(8,128)(2,1)} %weight_ref.1) | copy-start | bytes 3145732
  7.8 3.5 %copy-start.5 = (s32[8,128]{1,0:T(8,128)S(1)}, s32[8,128]{1,0:T(8,128)}, u32[]{:S(2)}) copy-start(s32[8,128]{1,0:T(8,128)} %cut_ref.1) | copy-start | bytes 12292
  7.9 3.8 %collective-permute-start.2 = (f32[8,8,128]{2,1,0:T(8,128)S(1)}, f32[8,8,128]{2,1,0:T(8,128)S(1)}, u32[]{:S(2)}, u32[]{:S(2)}) collective-permute-start(f32[8,8,128]{2,1,0:T(8,128)S(1)} %get-tuple-element.52), channel_id=1, source_target_pairs={{0,24},{8,16},{16,8},{24,0},{1,25},{9,17},{17,9},{25,1},{2,26},{10... | collective-permute-start | bytes 98312 | tf_op jit(solution)/shard_map/ppermute | solution.py:769
  8.6 3.0 %collective-permute-start.1 = (f32[8,8,128]{2,1,0:T(8,128)S(1)}, f32[8,8,128]{2,1,0:T(8,128)S(1)}, u32[]{:S(2)}, u32[]{:S(2)}) collective-permute-start(f32[8,8,128]{2,1,0:T(8,128)S(1)} %get-tuple-element.52), channel_id=1, source_target_pairs={{0,8},{8,0},{16,24},{24,16},{1,9},{9,1},{17,25},{25,17},{2,10},{10... | collective-permute-start | bytes 98312 | tf_op jit(solution)/shard_map/ppermute | solution.py:769
  11.9 7.2 %collective-permute-start.3 = (f32[64,128]{1,0:T(8,128)S(1)}, f32[64,128]{1,0:T(8,128)S(1)}, u32[]{:S(2)}, u32[]{:S(2)}) collective-permute-start(f32[64,128]{1,0:T(8,128)S(1)} %get-tuple-element.55), channel_id=1, source_target_pairs={{0,1},{1,0},{2,3},{3,2},{4,5},{5,4},{6,7},{7,6},{8,9},{9,8},{10,11... | collective-permute-start | bytes 98312 | tf_op jit(solution)/shard_map/ppermute | solution.py:769
  13.8 5.7 %collective-permute-start.4 = (f32[64,128]{1,0:T(8,128)S(1)}, f32[64,128]{1,0:T(8,128)S(1)}, u32[]{:S(2)}, u32[]{:S(2)}) collective-permute-start(f32[64,128]{1,0:T(8,128)S(1)} %get-tuple-element.56), channel_id=1, source_target_pairs={{0,3},{1,2},{2,1},{3,0},{4,7},{5,6},{6,5},{7,4},{8,11},{9,10},{10,... | collective-permute-start | bytes 98312 | tf_op jit(solution)/shard_map/ppermute | solution.py:769
  20.2 4.0 %collective-permute-start.5 = (bf16[2,1,64,128]{3,2,1,0:T(8,128)(2,1)S(1)}, bf16[2,1,64,128]{3,2,1,0:T(8,128)(2,1)S(1)}, u32[]{:S(2)}, u32[]{:S(2)}) collective-permute-start(bf16[2,1,64,128]{3,2,1,0:T(8,128)(2,1)S(1)} %get-tuple-element.65), channel_id=1, source_target_pairs={{0,4},{4,0},{1,5},{5,1},{2,6},{6,2},{3,7},{7,3},{8,12},{12,8},{9,1... | collective-permute-start | bytes 98312 | tf_op jit(solution)/shard_map/ppermute | solution.py:762
  24.3 3.2 %collective-permute-start.7 = (f32[4,8,128]{2,1,0:T(8,128)S(1)}, f32[4,8,128]{2,1,0:T(8,128)S(1)}, u32[]{:S(2)}, u32[]{:S(2)}) collective-permute-start(f32[4,8,128]{2,1,0:T(8,128)S(1)} %get-tuple-element.71), channel_id=1, source_target_pairs={{0,24},{8,16},{16,8},{24,0},{1,25},{9,17},{17,9},{25,1},{2,26},{10... | collective-permute-start | bytes 49160 | tf_op jit(solution)/shard_map/ppermute | solution.py:769
  24.3 3.2 %collective-permute-start.6 = (f32[4,8,128]{2,1,0:T(8,128)S(1)}, f32[4,8,128]{2,1,0:T(8,128)S(1)}, u32[]{:S(2)}, u32[]{:S(2)}) collective-permute-start(f32[4,8,128]{2,1,0:T(8,128)S(1)} %get-tuple-element.71), channel_id=1, source_target_pairs={{0,8},{8,0},{16,24},{24,16},{1,9},{9,1},{17,25},{25,17},{2,10},{10... | collective-permute-start | bytes 49160 | tf_op jit(solution)/shard_map/ppermute | solution.py:769
  27.6 4.7 %collective-permute-start.8 = (f32[32,128]{1,0:T(8,128)S(1)}, f32[32,128]{1,0:T(8,128)S(1)}, u32[]{:S(2)}, u32[]{:S(2)}) collective-permute-start(f32[32,128]{1,0:T(8,128)S(1)} %get-tuple-element.76), channel_id=1, source_target_pairs={{0,1},{1,0},{2,3},{3,2},{4,5},{5,4},{6,7},{7,6},{8,9},{9,8},{10,11... | collective-permute-start | bytes 49160 | tf_op jit(solution)/shard_map/ppermute | solution.py:769
  27.9 5.5 %copy-start.4 = (s32[8,128]{1,0:T(8,128)S(1)}, s32[8,128]{1,0:T(8,128)}, u32[]{:S(2)}) copy-start(s32[8,128]{1,0:T(8,128)} %block_ref.4) | copy-start | bytes 12292
  27.9 5.5 %collective-permute-start.9 = (f32[32,128]{1,0:T(8,128)S(1)}, f32[32,128]{1,0:T(8,128)S(1)}, u32[]{:S(2)}, u32[]{:S(2)}) collective-permute-start(f32[32,128]{1,0:T(8,128)S(1)} %get-tuple-element.77), channel_id=1, source_target_pairs={{0,3},{1,2},{2,1},{3,0},{4,7},{5,6},{6,5},{7,4},{8,11},{9,10},{10,... | collective-permute-start | bytes 49160 | tf_op jit(solution)/shard_map/ppermute | solution.py:769
  34.9 4.6 %collective-permute-start.11 = (bf16[2,144,128]{2,1,0:T(8,128)(2,1)S(1)}, bf16[2,144,128]{2,1,0:T(8,128)(2,1)S(1)}, u32[]{:S(2)}, u32[]{:S(2)}) collective-permute-start(bf16[2,144,128]{2,1,0:T(8,128)(2,1)S(1)} %get-tuple-element.90), channel_id=1, source_target_pairs={{0,16},{8,24},{16,0},{24,8},{1,17},{9,25},{17,1},{25,9},{2,18},{10... | collective-permute-start | bytes 221192 | tf_op jit(solution)/shard_map/ppermute | solution.py:874
  36.2 4.5 %collective-permute-start.12 = (bf16[2,144,128]{2,1,0:T(8,128)(2,1)S(1)}, bf16[2,144,128]{2,1,0:T(8,128)(2,1)S(1)}, u32[]{:S(2)}, u32[]{:S(2)}) collective-permute-start(bf16[2,144,128]{2,1,0:T(8,128)(2,1)S(1)} %get-tuple-element.91), channel_id=1, source_target_pairs={{0,24},{8,16},{16,8},{24,0},{1,25},{9,17},{17,9},{25,1},{2,26},{10... | collective-permute-start | bytes 221192 | tf_op jit(solution)/shard_map/ppermute | solution.py:874
  36.8 3.9 %collective-permute-start.10 = (bf16[2,144,128]{2,1,0:T(8,128)(2,1)S(1)}, bf16[2,144,128]{2,1,0:T(8,128)(2,1)S(1)}, u32[]{:S(2)}, u32[]{:S(2)}) collective-permute-start(bf16[2,144,128]{2,1,0:T(8,128)(2,1)S(1)} %shard_map.102), channel_id=1, source_target_pairs={{0,8},{8,0},{16,24},{24,16},{1,9},{9,1},{17,25},{25,17},{2,10},{10... | collective-permute-start | bytes 221192 | tf_op jit(solution)/shard_map/ppermute | solution.py:874

commit v6 on v5

--- a/solution.py
+++ b/solution.py
@@ -319,18 +319,35 @@
             z_ref[4 * f + n] = value
 
 
-def radial_kernel(count, z_in, x_in, z_ref, x_ref):
+def radial_faces(count, z_in, x_in, x_ref):
     x_ref[...] = x_in[...].astype(F32)
+    rows = []
     for f in range(count):
         spans = [slice(8 * b, 8 * b + 8) for b in range(8)]
-        z_ref[4 * f] = z_in[4 * f] + pack_blocks(
-            [(56 + b, x_ref[0, f, s, :]) for b, s in enumerate(spans)]
-        )
-        z_ref[4 * f + 1] = z_in[4 * f + 1]
-        z_ref[4 * f + 2] = z_in[4 * f + 2]
-        z_ref[4 * f + 3] = z_in[4 * f + 3] + pack_blocks(
-            [(b, x_ref[1, f, s, :]) for b, s in enumerate(spans)]
-        )
+        low = pack_blocks([(56 + b, x_ref[0, f, s, :]) for b, s in enumerate(spans)])
+        high = pack_blocks([(b, x_ref[1, f, s, :]) for b, s in enumerate(spans)])
+        rows += [z_in[4 * f] + low, z_in[4 * f + 1], z_in[4 * f + 2], z_in[4 * f + 3] + high]
+    return jnp.concatenate(rows, axis=0).astype(BF16)
+
+
+def id_tile(block_ref):
+    ids = block_ref[...]
+    return jnp.concatenate([ids >> 5, ids & 31], axis=0).astype(F32).astype(BF16)
+
+
+def first_radial_kernel(z_in, x_in, block_ref, one_ref, two_ref, x_ref):
+    faces = radial_faces(2, z_in, x_in, x_ref)
+    one_ref[:64, :] = faces
+    one_ref[64:, :] = id_tile(block_ref)
+    two_ref[...] = faces
+
+
+def second_radial_kernel(z_in, x_in, block_ref, got_ref, one_ref, two_ref, x_ref):
+    faces = radial_faces(1, z_in, x_in, x_ref)
+    one_ref[...] = faces
+    two_ref[:32, :] = faces
+    two_ref[32:48, :] = id_tile(block_ref)
+    two_ref[48:, :] = got_ref[64:, :]
 
 
 def merged(one, two, cam_count):
@@ -349,14 +366,19 @@
     return (lane == 0) | (lane == 127)
 
 
-def azimuth_kernel(cam_count, s_ref, x_ref, one_ref, two_ref, even_ref, odd_ref):
+def azimuth_kernel(cam_count, s_ref, x_ref, one_ref, two_ref, even_ref, odd_ref, packed_ref):
     ends = end_lanes((8, 128))
     row = row_ids((8, 128))
     even = (lax.axis_index("ey") & 1) == 0
-    for q in range(one_ref.shape[0]):
-        packed = merged(one_ref[q], two_ref[q], cam_count)
+    rows = s_ref.shape[0]
+    one = one_ref[:rows, :].astype(F32)
+    two = two_ref[:rows, :].astype(F32)
+    ups, downs = [], []
+    for q in range(rows // 8):
+        at = slice(8 * q, 8 * q + 8)
+        packed = merged(one[at], two[at], cam_count)
+        packed_ref[q] = packed
         f, a = q // 4, q % 4
-        at = slice(8 * q, 8 * q + 8)
         faces = []
         for line, shift in ((0, 16), (63, 2)):
             j = line & 7
@@ -368,8 +390,10 @@
             if a == 3:
                 face = face + jnp.where(row == 7, x_ref[1, f, line : line + 1, :], 0.0)
             faces.append(face)
-        even_ref[at, :] = jnp.where(even, faces[1], faces[0])
-        odd_ref[at, :] = jnp.where(even, faces[0], faces[1])
+        ups.append(jnp.where(even, faces[1], faces[0]))
+        downs.append(jnp.where(even, faces[0], faces[1]))
+    even_ref[...] = jnp.concatenate(ups, axis=0).astype(BF16)
+    odd_ref[...] = jnp.concatenate(downs, axis=0).astype(BF16)
 
 
 def unpacked(packed, b):
@@ -400,25 +424,28 @@
     if y_refs is not None:
         one_ref, two_ref = y_refs
         even = (lax.axis_index("ey") & 1) == 0
+        at = slice(16 * (a // 2) + 32 * f, 16 * (a // 2) + 32 * f + 16)
+        one, two = one_ref[at, :].astype(F32), two_ref[at, :].astype(F32)
         if b == 0:
-            line, sublane = jnp.where(even, two_ref[at, :], one_ref[at, :]), 0
+            line, sublane = jnp.where(even, two, one), 0
         else:
-            line, sublane = jnp.where(even, one_ref[at, :], two_ref[at, :]), 7
+            line, sublane = jnp.where(even, one, two), 7
+        line = line[8 * (a % 2) : 8 * (a % 2) + 8]
         node = lax.broadcasted_iota(jnp.int32, (8, 8, 128), 1)
         block = block + jnp.where(node == sublane, line[:, None, :], 0.0)
     return block.reshape(64, 128) + jnp.concatenate(rows, axis=0)
 
 
 def second_pairs(
-    cam_count, pairs, s_ref, x_ref, one_ref, two_ref, y_refs, scalar_ref, velocity_ref,
+    pairs, s_ref, x_ref, packed_ref, y_refs, scalar_ref, velocity_ref,
     mass_ref, table_ref, g_ref, base_ref, half_ref, z_ref,
 ):
     def body(a, layer=None):
         at = span_of(a)
         layer = a if layer is None else layer
         to = span_of(layer)
-        radial_g = merged(one_ref[a], two_ref[a], cam_count)
-        radial_m = merged(one_ref[a + 4], two_ref[a + 4], cam_count)
+        radial_g = packed_ref[a]
+        radial_m = packed_ref[a + 4]
         spreads = []
         for n, pair in enumerate(pairs):
             fields, velocities, masses = [], [], []
@@ -449,11 +476,11 @@
 
 
 def second_inner_kernel(
-    cam_count, s_ref, x_ref, one_ref, two_ref, scalar_ref, velocity_ref, mass_ref,
+    s_ref, x_ref, packed_ref, scalar_ref, velocity_ref, mass_ref,
     table_ref, g_ref, base_ref, half_ref, z_ref,
 ):
     body = second_pairs(
-        cam_count, ((1, 2), (3, 4), (5, 6)), s_ref, x_ref, one_ref, two_ref, None,
+        ((1, 2), (3, 4), (5, 6)), s_ref, x_ref, packed_ref, None,
         scalar_ref, velocity_ref, mass_ref, table_ref, g_ref, base_ref, half_ref, z_ref,
     )
     sweep(body, 2)
@@ -461,11 +488,11 @@
 
 
 def second_face_kernel(
-    cam_count, s_ref, x_ref, one_ref, two_ref, y_one_ref, y_two_ref, scalar_ref, velocity_ref,
+    s_ref, x_ref, packed_ref, y_one_ref, y_two_ref, scalar_ref, velocity_ref,
     mass_ref, table_ref, inner_ref, x_out_ref, edge_ref, base_ref, half_ref, z_ref,
 ):
     body = second_pairs(
-        cam_count, ((0, 7),), s_ref, x_ref, one_ref, two_ref, (y_one_ref, y_two_ref),
+        ((0, 7),), s_ref, x_ref, packed_ref, (y_one_ref, y_two_ref),
         scalar_ref, velocity_ref, mass_ref, table_ref, edge_ref, base_ref, half_ref, z_ref,
     )
     body(0, 0)
@@ -481,12 +508,12 @@
 
 
 def second_outer_kernel(
-    cam_count, s_ref, x_ref, one_ref, two_ref, y_one_ref, y_two_ref, scalar_ref, velocity_ref,
+    s_ref, x_ref, packed_ref, y_one_ref, y_two_ref, scalar_ref, velocity_ref,
     mass_ref, table_ref, inner_ref, z_in, edge_in, base_in, half_in, z_face,
     g_ref, base_ref, half_ref, z_ref, edge_ref,
 ):
     body = second_pairs(
-        cam_count, ((0, 7),), s_ref, x_ref, one_ref, two_ref, (y_one_ref, y_two_ref),
+        ((0, 7),), s_ref, x_ref, packed_ref, (y_one_ref, y_two_ref),
         scalar_ref, velocity_ref, mass_ref, table_ref, edge_ref, base_ref, half_ref, z_ref,
     )
     body(1)
@@ -602,13 +629,13 @@
 
 
 def render_inner_kernel(
-    cam_count, g_ref, x_ref, one_ref, two_ref, base_ref, half_ref, table_ref, weight_ref, pick_ref,
+    g_ref, x_ref, packed_ref, base_ref, half_ref, table_ref, weight_ref, pick_ref,
     pixel_in, out_hbm, pixel_ref, advected_ref, end_ref, sem,
 ):
     end_ref[48:, :] = jnp.zeros((16, 512), F32)
 
     def body(a):
-        packed = merged(one_ref[a], two_ref[a], cam_count)
+        packed = packed_ref[a]
         for n, pair in enumerate(INNER):
             blocks = advanced(g_ref, x_ref, packed, None, base_ref, half_ref, a, pair, 16 * n)
             for h in range(2):
@@ -635,28 +662,24 @@
     copy.wait()
 
 
-def fill_payload(payload_ref, d, cameras, cam_count, pick_ref, value_ref, pixel_ref, block_ref):
+def fill_payload(payload_ref, d, cam_count, pick_ref, value_ref, pixel_ref):
     me = lax.axis_index("cam")
-    share = cameras // cam_count
-    sub = row_ids((16, 128))
+    share = pixel_ref.shape[0] // cam_count
     for n in range(share):
         m = share * (me ^ d) + n
         values = dot(pick_ref[m, :, 384:512], value_ref[m]) + pixel_ref[m]
-        payload_ref[n, :128, :] = values.astype(BF16)
-        ids = block_ref[pl.ds(m, 1), :]
-        tail = jnp.where(sub == 0, ids >> 5, jnp.where(sub == 1, ids & 31, 0))
-        payload_ref[n, 128:, :] = tail.astype(F32).astype(BF16)
+        payload_ref[n] = values.astype(BF16)
 
 
 def render_far_kernel(
-    cam_count, g_ref, x_ref, one_ref, two_ref, y_one_ref, y_two_ref, base_ref, half_ref,
-    table_ref, weight_ref, pick_ref, pixel_ref, block_ref, out_in,
+    cam_count, g_ref, x_ref, packed_ref, y_one_ref, y_two_ref, base_ref, half_ref,
+    table_ref, weight_ref, pick_ref, pixel_ref, out_in,
     out_hbm, value_ref, *rest,
 ):
     payload_refs = rest[: cam_count - 2]
     advected_ref, element_ref, sems = rest[cam_count - 2 :]
     for a in range(4):
-        packed = merged(one_ref[a], two_ref[a], cam_count)
+        packed = packed_ref[a]
         blocks = advanced(
             g_ref, x_ref, packed, (y_one_ref, y_two_ref), base_ref, half_ref, a, (0, 7), 0
         )
@@ -677,50 +700,46 @@
         value_ref[2 * m] = values[:, :128]
         value_ref[2 * m + 1] = values[:, 128:]
     for d in range(2, cam_count):
-        fill_payload(
-            payload_refs[d - 2], d, cameras, cam_count, pick_ref, value_ref, pixel_ref, block_ref
-        )
+        fill_payload(payload_refs[d - 2], d, cam_count, pick_ref, value_ref, pixel_ref)
     for copy in copies:
         copy.wait()
 
 
-def render_near_kernel(
-    cam_count, d, value_ref, pick_ref, pixel_ref, block_ref, payload_ref
-):
-    cameras = pixel_ref.shape[0]
-    fill_payload(
-        payload_ref, d, cameras, cam_count, pick_ref, value_ref, pixel_ref, block_ref
-    )
-
-
-def scatter(payload_refs, m, chunk):
-    ids, values = [], []
-    for payload_ref in payload_refs:
-        tail = payload_ref[m, 128:, :].astype(F32).astype(jnp.int32)
-        ids.append(tail[0:1, :] * 32 + tail[1:2, :])
-        values.append(payload_ref[m, :128, :])
-    ids = jnp.concatenate(ids, axis=1)
-    row = row_ids((256, ids.shape[1])) + 256 * chunk
-    onehot = jnp.where(row == ids, 1.0, 0.0).astype(BF16)
-    return dot(onehot, jnp.concatenate(values, axis=0))
-
-
-def own_image_kernel(cam_count, value_ref, pick_ref, pixel_ref, block_ref, image_ref, payload_ref):
-    cameras = pixel_ref.shape[0]
-    fill_payload(payload_ref, 0, cameras, cam_count, pick_ref, value_ref, pixel_ref, block_ref)
+def render_near_kernel(cam_count, d, value_ref, pick_ref, pixel_ref, payload_ref):
+    fill_payload(payload_ref, d, cam_count, pick_ref, value_ref, pixel_ref)
+
+
+def block_kernel(share, block_ref, first_ref, second_ref, onehot_ref, id_ref):
+    me = lax.axis_index("cam")
+    id_ref[0] = block_ref[...]
+    tiles = ((1, first_ref[64:80, :]), (3, second_ref[32:48, :]), (2, second_ref[48:64, :]))
+    for d, tile in tiles:
+        ids = tile.astype(F32).astype(jnp.int32)
+        id_ref[d] = ids[:8] * 32 + ids[8:]
+    for m in range(share):
+        ids = [id_ref[d, pl.ds(share * me + m, 1), :] for d in range(4)]
+        ids = jnp.concatenate(ids, axis=1)
+        for chunk in range(4):
+            row = row_ids((256, ids.shape[1])) + 256 * chunk
+            onehot_ref[m, 256 * chunk : 256 * chunk + 256, :] = jnp.where(
+                row == ids, 1.0, 0.0
+            ).astype(BF16)
+
+
+def own_image_kernel(cam_count, value_ref, pick_ref, pixel_ref, onehot_ref, image_ref, payload_ref):
+    fill_payload(payload_ref, 0, cam_count, pick_ref, value_ref, pixel_ref)
     for m in range(image_ref.shape[0]):
-        for chunk in range(4):
-            at = slice(256 * chunk, 256 * chunk + 256)
-            image_ref[m, at, :] = scatter([payload_ref], m, chunk)
-
-
-def image_kernel(own_ref, *refs):
+        image_ref[m] = dot(onehot_ref[m, :, :128], payload_ref[m])
+
+
+def image_kernel(own_ref, onehot_ref, *refs):
     payload_refs, (image_hbm, image_ref, sems) = refs[:-3], refs[-3:]
     copies = []
     for m in range(image_ref.shape[0]):
+        values = jnp.concatenate([payload_ref[m] for payload_ref in payload_refs], axis=0)
         for chunk in range(4):
             at = slice(256 * chunk, 256 * chunk + 256)
-            image_ref[m, at, :] = own_ref[m, at, :] + scatter(payload_refs, m, chunk)
+            image_ref[m, at, :] = own_ref[m, at, :] + dot(onehot_ref[m, at, 128:], values)
             copy = pltpu.make_async_copy(
                 image_ref.at[m, at], image_hbm.at[m, at], sems.at[4 * m + chunk]
             )
@@ -800,22 +819,28 @@
     weights = call(weight_kernel, shape_of(512, 128 * cameras, dtype=BF16))(pixel_weights)
     picks = call(pick_kernel, shape_of(cameras, 128, 640, dtype=BF16))(cut_element)
 
-    z, x_got = call(part(radial_kernel, 2), (shape_of(8, 8, 128), shape_of(2, 2, 64, 128)))(z, x_got)
-    z_got = swap_both(z, z, "cam")
+    half = functools.partial(shape_of, dtype=BF16)
+    *z, x_got = call(
+        first_radial_kernel, (half(80, 128), half(64, 128), shape_of(2, 2, 64, 128))
+    )(z, x_got, pixel_block)
+    z_got = swap_both(*z, "cam")
     z_got, weights, picks = lax.optimization_barrier((z_got, weights, picks))
-    y = call(part(azimuth_kernel, n_cam), (shape_of(64, 128), shape_of(64, 128)))(s, x_got, *z_got)
+    ids_got = z_got[0]
+    *y, packed = call(
+        part(azimuth_kernel, n_cam), (half(64, 128), half(64, 128), shape_of(8, 8, 128))
+    )(s, x_got, *z_got)
     y_got = swap_both(*y, "ey")
     g_inner, *inner_terms, z_inner = call(
-        part(second_inner_kernel, n_cam), (shape_of(*inner),) * 3 + (shape_of(4, 8, 128),)
-    )(s, x_got, *z_got, scalar, velocity, mass, near)
-    args = (s, x_got, *z_got, *y_got, scalar, velocity, mass, near, g_inner)
+        second_inner_kernel, (shape_of(*inner),) * 3 + (shape_of(4, 8, 128),)
+    )(s, x_got, packed, scalar, velocity, mass, near)
+    args = (s, x_got, packed, *y_got, scalar, velocity, mass, near, g_inner)
     some = (16, 16, 128)
     x, *faces = call(
-        part(second_face_kernel, n_cam),
+        second_face_kernel,
         (shape_of(2, 1, 64, 128, dtype=BF16),) + (shape_of(*some),) * 3 + (shape_of(2, 8, 128),),
     )(*args)
     g, *outer_terms, z = call(
-        part(second_outer_kernel, n_cam),
+        second_outer_kernel,
         (shape_of(*flat), shape_of(*outer), shape_of(*outer), shape_of(4, 8, 128)),
         scratch_shapes=[pltpu.VMEM(outer, F32)],
     )(*args, z_inner, *faces)
@@ -827,18 +852,28 @@
         scratch_shapes=[pltpu.VMEM((192, 512), BF16)],
     )(g, *inner_terms, near, weights)
     x_got, early = lax.optimization_barrier((x_got, early))
-    z, x_got = call(part(radial_kernel, 1), (shape_of(4, 8, 128), shape_of(2, 1, 64, 128)))(z, x_got)
-    z_got = swap_both(z, z, "cam")
+    *z, x_got = call(
+        second_radial_kernel, (half(32, 128), half(64, 128), shape_of(2, 1, 64, 128))
+    )(z, x_got, pixel_block, ids_got)
+    z_got = swap_both(*z, "cam")
     pixels = call(
         middle_kernel,
         shape_of(cameras, 128, 128),
         scratch_shapes=[pltpu.VMEM((192, 512), BF16)],
     )(g, x_got, *inner_terms, near, weights, picks, early)
     z_got, pixels = lax.optimization_barrier((z_got, pixels))
-    y = call(part(azimuth_kernel, n_cam), (shape_of(32, 128), shape_of(32, 128)))(g, x_got, *z_got)
+    *y, packed = call(
+        part(azimuth_kernel, n_cam), (half(32, 128), half(32, 128), shape_of(4, 8, 128))
+    )(g, x_got, *z_got)
     y_got = swap_both(*y, "ey")
+    packed, ids = lax.optimization_barrier((packed, (ids_got, z_got[1])))
+    onehot = call(
+        part(block_kernel, share),
+        half(share, NBLK, 128 * n_cam),
+        scratch_shapes=[pltpu.VMEM((n_cam, cameras, 128), jnp.int32)],
+    )(pixel_block, *ids)
     advected, pixels = call(
-        part(render_inner_kernel, n_cam),
+        render_inner_kernel,
         (shape_of(*flat), shape_of(cameras, 128, 128)),
         out_specs=(HBM, VMEM),
         scratch_shapes=[
@@ -846,27 +881,28 @@
             pltpu.VMEM((64, 512), F32),
             pltpu.SemaphoreType.DMA,
         ],
-    )(g, x_got, *z_got, *inner_terms, near, weights, picks, pixels)
-    payload_shape = shape_of(share, 144, 128, dtype=BF16)
+    )(g, x_got, packed, *inner_terms, near, weights, picks, pixels)
+    y_got, onehot = lax.optimization_barrier((y_got, onehot))
+    payload_shape = half(share, 128, 128)
     advected, values, *far = call(
         part(render_far_kernel, n_cam),
         (shape_of(*flat), shape_of(cameras, 128, 128, dtype=BF16)) + (payload_shape,) * (n_cam - 2),
-        in_specs=[VMEM] * 13 + [HBM],
+        in_specs=[VMEM] * 11 + [HBM],
         out_specs=(HBM, VMEM) + (VMEM,) * (n_cam - 2),
-        input_output_aliases={13: 0},
+        input_output_aliases={11: 0},
         scratch_shapes=[
             pltpu.VMEM(outer, F32),
             pltpu.VMEM((128, 512), BF16),
             pltpu.SemaphoreType.DMA((2,)),
         ],
-    )(g, x_got, *z_got, *y_got, *outer_terms, near, weights, picks, pixels, pixel_block, advected)
-    parts = (values, picks, pixels, pixel_block)
+    )(g, x_got, packed, *y_got, *outer_terms, near, weights, picks, pixels, advected)
+    parts = (values, picks, pixels)
     image_shape = shape_of(share, NBLK, 128)
     images = call(
         part(own_image_kernel, n_cam),
         image_shape,
         scratch_shapes=[pltpu.VMEM(payload_shape.shape, BF16)],
-    )(*parts)
+    )(*parts, onehot)
     images, parts = lax.optimization_barrier((images, parts))
     beside = call(part(render_near_kernel, n_cam, 1), payload_shape)(*parts)
     received = []
@@ -880,7 +916,7 @@
             pltpu.VMEM((share, NBLK, 128), F32),
             pltpu.SemaphoreType.DMA((4 * share,)),
         ],
-    )(images, *received)
+    )(images, onehot, *received)
     return (advected.reshape(shape), images)
 
 

time: 42.2 us -> 41.5 us (0.983)
  waiting for transfers between devices: 6.18 us -> 5.52 us
    ppermute x8, waiting for transfers between devices: 2.3 us -> 1.72 us  [swap_both(): return (lax.ppermute(one, axis, even), lax.ppermute(two, axis, odd))]
    pallas_call x8 -> x9, Pallas kernels: 6.85 us -> 7.01 us  [the longest x1 2.6 us: per_device(): call(second_inner_kernel, (shape_of(*inner),) * 3 + (shape_of(4, 8, 128),))]
  transfers between devices with their start and end apart: 13 -> 13, of which waited for: 6 -> 6; matrix products, arithmetic and copies ran while one was open for 0% -> 0% of each run, Pallas kernels for 29% -> 30%
where the time goes in v6:
time: 41.5 us; the launch traced here: 41.4 us
  Pallas kernels  17.8 us (43%)
  starting transfers between devices  17.1 us (41%)
  waiting for transfers between devices  5.52 us (13%)
  between operations  0.86 us (2%)
    ppermute x8, starting transfers between devices, swap_both(): return (lax.ppermute(one, axis, even), lax.ppermute(two, axis, odd))  10.3 us
    ppermute x2, starting transfers between devices, swap_axial(): return lax.ppermute(x, 'ex', up)  4.56 us
    ppermute x3, waiting for transfers between devices, per_device(): lax.ppermute(payload, 'cam', [(i, i ^ d) for i in range(n_cam)])  2.81 us
    pallas_call x1, Pallas kernels, per_device(): call(second_inner_kernel, (shape_of(*inner),) * 3 + (shape_of(4, 8, 128),))  2.6 us
    pallas_call x1, Pallas kernels, per_device(): call(first_kernel, (shape_of(64, 64, 128), shape_of(8, 8, 128)))  2.43 us
    ppermute x3, starting transfers between devices, per_device(): lax.ppermute(payload, 'cam', [(i, i ^ d) for i in range(n_cam)])  2.27 us
    pallas_call x1, Pallas kernels, per_device(): call(render_inner_kernel, (shape_of(*flat), shape_of(cameras, 128, 128)),...  2.02 us
    pallas_call x1, Pallas kernels, per_device(): call(face_kernel, (shape_of(2, 2, 64, 128, dtype=BF16), shape_of(*tables....  1.77 us
  transfers between devices with their start and end apart: 13, of which 6 were waited for; matrix products, arithmetic and copies ran while one was open for 0% of the time, Pallas kernels for 30%

profile of v6, /device:TPU:0, one launch (start us, length us, event | category | flops | bytes accessed | tf_op | source)
XLA Modules:
  0.0 41.4 jit_solution(4275582989094752353)
XLA Ops:
  0.6 0.0 copy-start
  0.6 0.0 copy-start.1
  0.6 0.0 copy-start.2
  0.7 1.8 %shard_map.86 = (bf16[2,2,64,128]{3,2,1,0:T(8,128)(2,1)S(1)}, bf16[1440,128]{1,0:T(8,128)(2,1)S(1)}) custom-call(f32[32,64,128]{2,1,0:T(8,128)} %bitcast.9, f32[3,32,64,128]{3,2,1,0:T(8,128)} %bitcast.4, f32[32,64,128]{2,1,0:T(8,128)} %bitcast.14, bf16[1440,128]{1,0:T(8,128)(2,1)} %constant.2.clone.table_hbm), custom_call_target="tpu_custom_call" | custom-call | flops 100000000 | bytes 10000000 | tf_op jit(solution)/shard_map/pallas_call | solution.py:804
  2.4 3.0 %collective-permute-start = (bf16[2,2,64,128]{3,2,1,0:T(8,128)(2,1)S(1)}, bf16[2,2,64,128]{3,2,1,0:T(8,128)(2,1)S(1)}, u32[]{:S(2)}, u32[]{:S(2)}) collective-permute-start(bf16[2,2,64,128]{3,2,1,0:T(8,128)(2,1)S(1)} %get-tuple-element.59), channel_id=1, source_target_pairs={{0,4},{4,0},{1,5},{5,1},{2,6},{6,2},{3,7},{7,3},{8,12},{12,8},{9,1... | collective-permute-start | bytes 196616 | tf_op jit(solution)/shard_map/ppermute | solution.py:781
  5.4 0.0 copy-done
  5.4 0.0 copy-done.1
  5.4 0.0 copy-done.2
  5.5 0.0 copy-start.5
  5.5 0.0 copy-start.3
  5.5 2.4 %shard_map.87 = (f32[64,64,128]{2,1,0:T(8,128)S(1)}, f32[8,8,128]{2,1,0:T(8,128)S(1)}) custom-call(f32[32,64,128]{2,1,0:T(8,128)S(1)} %bitcast.10, f32[3,32,64,128]{3,2,1,0:T(8,128)S(1)} %bitcast.5, f32[32,64,128]{2,1,0:T(8,128)S(1)} %bitcast.15, bf16[1440,128]{1,0:T(8,128)(2,1)S(1)} %get-tuple-element.56.table_ref), custom_call_target="tpu_custom_call" | custom-call | flops 100000000 | bytes 10000000 | tf_op jit(solution)/shard_map/pallas_call | solution.py:816
  7.9 0.0 copy-start.4
  7.9 0.0 collective-permute-done.x_in
  7.9 0.0 copy-done.5
  7.9 0.1 shard_map.88
  8.0 0.1 collective-permute-start.1
  8.1 1.9 %collective-permute-start.2 = (bf16[64,128]{1,0:T(8,128)(2,1)S(1)}, bf16[64,128]{1,0:T(8,128)(2,1)S(1)}, u32[]{:S(2)}, u32[]{:S(2)}) collective-permute-start(bf16[64,128]{1,0:T(8,128)(2,1)S(1)} %get-tuple-element.62), channel_id=1, source_target_pairs={{0,24},{8,16},{16,8},{24,0},{1,25},{9,17},{17,9},{25,1},{2,26},{10... | collective-permute-start | bytes 49160 | tf_op jit(solution)/shard_map/ppermute | solution.py:788
  10.0 0.0 copy-done.3
  10.0 1.3 %shard_map.89.weight_ref = bf16[512,1024]{1,0:T(8,128)(2,1)S(1)} custom-call(bf16[8,512,128]{2,1,0:T(8,128)(2,1)S(1)} %copy-done.3), custom_call_target="tpu_custom_call" | custom-call | flops 100000000 | bytes 10000000 | tf_op jit(solution)/shard_map/pallas_call | solution.py:819
  11.3 0.0 copy-done.4
  11.3 0.4 shard_map.90.pick_ref
  11.7 0.0 collective-permute-done.2.two_ref
  11.7 0.0 collective-permute-done.1.one_ref.got_ref.first_ref
  11.7 0.2 shard_map.91
  11.9 1.7 %collective-permute-start.3 = (bf16[64,128]{1,0:T(8,128)(2,1)S(1)}, bf16[64,128]{1,0:T(8,128)(2,1)S(1)}, u32[]{:S(2)}, u32[]{:S(2)}) collective-permute-start(bf16[64,128]{1,0:T(8,128)(2,1)S(1)} %get-tuple-element.66), channel_id=1, source_target_pairs={{0,1},{1,0},{2,3},{3,2},{4,5},{5,4},{6,7},{7,6},{8,9},{9,8},{10,11... | collective-permute-start | bytes 49160 | tf_op jit(solution)/shard_map/ppermute | solution.py:788
  13.5 2.5 %collective-permute-start.4 = (bf16[64,128]{1,0:T(8,128)(2,1)S(1)}, bf16[64,128]{1,0:T(8,128)(2,1)S(1)}, u32[]{:S(2)}, u32[]{:S(2)}) collective-permute-start(bf16[64,128]{1,0:T(8,128)(2,1)S(1)} %get-tuple-element.67), channel_id=1, source_target_pairs={{0,3},{1,2},{2,1},{3,0},{4,7},{5,6},{6,5},{7,4},{8,11},{9,10},{10,... | collective-permute-start | bytes 49160 | tf_op jit(solution)/shard_map/ppermute | solution.py:788
  16.0 2.6 %shard_map.92 = (f32[32,48,128]{2,1,0:T(8,128)S(1)}, f32[32,48,128]{2,1,0:T(8,128)S(1)}, f32[32,48,128]{2,1,0:T(8,128)S(1)}, f32[4,8,128]{2,1,0:T(8,128)S(1)}) custom-call(f32[64,64,128]{2,1,0:T(8,128)S(1)} %get-tuple-element.57.s_ref, f32[2,2,64,128]{3,2,1,0:T(8,128)S(1)} %get-tuple-element.60.x_ref, f32[8,8,128]{2,1,0:T(8,128)S(1)} %get-tuple-element.65.packed_ref, ...), custom_call_target="tpu_custom_call" | custom-call | flops 100000000 | bytes 10000000 | tf_op jit(solution)/shard_map/pallas_call | solution.py:833
  18.6 0.0 collective-permute-done.3.y_one_ref
  18.6 0.4 %collective-permute-done.4.y_two_ref = bf16[64,128]{1,0:T(8,128)(2,1)S(1)} collective-permute-done((bf16[64,128]{1,0:T(8,128)(2,1)S(1)}, bf16[64,128]{1,0:T(8,128)(2,1)S(1)}, u32[]{:S(2)}, u32[]{:S(2)}) %collective-permute-start.4) | collective-permute-done | bytes 16416 | tf_op jit(solution)/shard_map/ppermute | solution.py:788
  19.1 0.6 %shard_map.93 = (bf16[2,1,64,128]{3,2,1,0:T(8,128)(2,1)S(1)}, f32[16,16,128]{2,1,0:T(8,128)S(1)}, f32[16,16,128]{2,1,0:T(8,128)S(1)}, f32[16,16,128]{2,1,0:T(8,128)S(1)}, f32[2,8,128]{2,1,0:T(8,128)S(1)}) custom-call(f32[64,64,128]{2,1,0:T(8,128)S(1)} %get-tuple-element.57.s_ref, f32[2,2,64,128]{3,2,1,0:T(8,128)S(1)} %get-tuple-element.60.x_ref, ...), custom_call_target="tpu_custom_call" | custom-call | flops 100000000 | bytes 10000000 | tf_op jit(solution)/shard_map/pallas_call | solution.py:838
  19.7 1.6 %collective-permute-start.5 = (bf16[2,1,64,128]{3,2,1,0:T(8,128)(2,1)S(1)}, bf16[2,1,64,128]{3,2,1,0:T(8,128)(2,1)S(1)}, u32[]{:S(2)}, u32[]{:S(2)}) collective-permute-start(bf16[2,1,64,128]{3,2,1,0:T(8,128)(2,1)S(1)} %get-tuple-element.76), channel_id=1, source_target_pairs={{0,4},{4,0},{1,5},{5,1},{2,6},{6,2},{3,7},{7,3},{8,12},{12,8},{9,1... | collective-permute-start | bytes 98312 | tf_op jit(solution)/shard_map/ppermute | solution.py:781
  21.2 0.7 %shard_map.94 = (f32[32,64,128]{2,1,0:T(8,128)S(1)}, f32[32,16,128]{2,1,0:T(8,128)S(1)}, f32[32,16,128]{2,1,0:T(8,128)S(1)}, f32[4,8,128]{2,1,0:T(8,128)S(1)}) custom-call(f32[64,64,128]{2,1,0:T(8,128)S(1)} %get-tuple-element.57.s_ref, f32[2,2,64,128]{3,2,1,0:T(8,128)S(1)} %get-tuple-element.60.x_ref, f32[8,8,128]{2,1,0:T(8,128)S(1)} %get-tuple-element.65.packed_ref, ...), custom_call_target="tpu_custom_call" | custom-call | flops 100000000 | bytes 10000000 | tf_op jit(solution)/shard_map/pallas_call | solution.py:842
  22.0 0.7 %shard_map.95.early_ref = bf16[192,1024]{1,0:T(8,128)(2,1)S(1)} custom-call(f32[32,64,128]{2,1,0:T(8,128)S(1)} %get-tuple-element.74.g_ref.s_ref, f32[32,48,128]{2,1,0:T(8,128)S(1)} %get-tuple-element.77.base_ref, f32[32,48,128]{2,1,0:T(8,128)S(1)} %get-tuple-element.78.half_ref, bf16[1440,128]{1,0:T(8,128)(2,1)S(1)} %get-tuple-element.56.table_ref, ...), custom_call_target="tpu_custom_call" | custom-call | flops 100000000 | bytes 10000000 | tf_op jit(solution)/shard_map/pallas_call | solution.py:849
  22.7 1.0 %collective-permute-done.5.x_in = bf16[2,1,64,128]{3,2,1,0:T(8,128)(2,1)S(1)} collective-permute-done((bf16[2,1,64,128]{3,2,1,0:T(8,128)(2,1)S(1)}, bf16[2,1,64,128]{3,2,1,0:T(8,128)(2,1)S(1)}, u32[]{:S(2)}, u32[]{:S(2)}) %collective-permute-start.5) | collective-permute-done | bytes 32800 | tf_op jit(solution)/shard_map/ppermute | solution.py:781
  23.6 0.1 shard_map.96
  23.7 0.1 collective-permute-start.7
  23.8 1.5 %collective-permute-start.6 = (bf16[32,128]{1,0:T(8,128)(2,1)S(1)}, bf16[32,128]{1,0:T(8,128)(2,1)S(1)}, u32[]{:S(2)}, u32[]{:S(2)}) collective-permute-start(bf16[32,128]{1,0:T(8,128)(2,1)S(1)} %get-tuple-element.82), channel_id=1, source_target_pairs={{0,8},{8,0},{16,24},{24,16},{1,9},{9,1},{17,25},{25,17},{2,10},{10... | collective-permute-start | bytes 24584 | tf_op jit(solution)/shard_map/ppermute | solution.py:788
  25.3 1.0 %shard_map.97.pixel_in = f32[8,128,128]{2,1,0:T(8,128)S(1)} custom-call(f32[32,64,128]{2,1,0:T(8,128)S(1)} %get-tuple-element.74.g_ref.s_ref, f32[2,1,64,128]{3,2,1,0:T(8,128)S(1)} %get-tuple-element.81.x_ref, f32[32,48,128]{2,1,0:T(8,128)S(1)} %get-tuple-element.77.base_ref, f32[32,48,128]{2,1,0:T(8,128)S(1)} %get-tuple-element.78.half_ref, ...), custom_call_target="tpu_custom_call" | custom-call | flops 100000000 | bytes 10000000 | tf_op jit(solution)/shard_map/pallas_call | solution.py:859
  26.4 0.0 collective-permute-done.6.one_ref
  26.4 0.7 %collective-permute-done.7.two_ref.second_ref = bf16[64,128]{1,0:T(8,128)(2,1)S(1)} collective-permute-done((bf16[64,128]{1,0:T(8,128)(2,1)S(1)}, bf16[64,128]{1,0:T(8,128)(2,1)S(1)}, u32[]{:S(2)}, u32[]{:S(2)}) %collective-permute-start.7) | collective-permute-done | bytes 16416 | tf_op jit(solution)/shard_map/ppermute | solution.py:788
  27.1 0.2 shard_map.98
  27.3 0.3 collective-permute-start.8
  27.6 2.3 %collective-permute-start.9 = (bf16[32,128]{1,0:T(8,128)(2,1)S(1)}, bf16[32,128]{1,0:T(8,128)(2,1)S(1)}, u32[]{:S(2)}, u32[]{:S(2)}) collective-permute-start(bf16[32,128]{1,0:T(8,128)(2,1)S(1)} %get-tuple-element.91), channel_id=1, source_target_pairs={{0,3},{1,2},{2,1},{3,0},{4,7},{5,6},{6,5},{7,4},{8,11},{9,10},{10,... | collective-permute-start | bytes 24584 | tf_op jit(solution)/shard_map/ppermute | solution.py:788
  29.9 2.0 %shard_map.100 = (f32[32,64,128]{2,1,0:T(8,128)}, f32[8,128,128]{2,1,0:T(8,128)S(1)}) custom-call(f32[32,64,128]{2,1,0:T(8,128)S(1)} %get-tuple-element.74.g_ref.s_ref, f32[2,1,64,128]{3,2,1,0:T(8,128)S(1)} %get-tuple-element.81.x_ref, f32[4,8,128]{2,1,0:T(8,128)S(1)} %get-tuple-element.89.packed_ref, f32[32,48,128]{2,1,0:T(8,128)S(1)} %get-tuple-element.77.base_ref, ...), custom_call_target="tpu_custom_call" | custom-call | flops 100000000 | bytes 10000000 | tf_op jit(solution)/shard_map/pallas_call | solution.py:875
  31.9 0.5 %shard_map.99.onehot_ref = bf16[2,1024,512]{2,1,0:T(8,128)(2,1)S(1)} custom-call(s32[8,128]{1,0:T(8,128)S(1)} %copy-done.5, bf16[80,128]{1,0:T(8,128)(2,1)S(1)} %collective-permute-done.1.one_ref.got_ref.first_ref, bf16[64,128]{1,0:T(8,128)(2,1)S(1)} %collective-permute-done.7.two_ref.second_ref), custom_call_target="tpu_custom_call" | custom-call | flops 100000000 | bytes 10000000 | tf_op jit(solution)/shard_map/pallas_call | solution.py:870
  32.5 0.0 collective-permute-done.8.y_one_ref
  32.5 0.6 %collective-permute-done.9.y_two_ref = bf16[32,128]{1,0:T(8,128)(2,1)S(1)} collective-permute-done((bf16[32,128]{1,0:T(8,128)(2,1)S(1)}, bf16[32,128]{1,0:T(8,128)(2,1)S(1)}, u32[]{:S(2)}, u32[]{:S(2)}) %collective-permute-start.9) | collective-permute-done | bytes 8224 | tf_op jit(solution)/shard_map/ppermute | solution.py:788
  33.0 1.3 %shard_map.101 = (f32[32,64,128]{2,1,0:T(8,128)}, bf16[8,128,128]{2,1,0:T(8,128)(2,1)S(1)}, bf16[2,128,128]{2,1,0:T(8,128)(2,1)S(1)}, bf16[2,128,128]{2,1,0:T(8,128)(2,1)S(1)}) custom-call(f32[32,64,128]{2,1,0:T(8,128)S(1)} %get-tuple-element.74.g_ref.s_ref, f32[2,1,64,128]{3,2,1,0:T(8,128)S(1)} %get-tuple-element.81.x_ref, ...), custom_call_target="tpu_custom_call", output_to_operand_aliasing={{0}: (11, {})} | custom-call | flops 100000000 | bytes 10000000 | tf_op jit(solution)/shard_map/pallas_call | solution.py:887
  34.4 1.3 %collective-permute-start.11 = (bf16[2,128,128]{2,1,0:T(8,128)(2,1)S(1)}, bf16[2,128,128]{2,1,0:T(8,128)(2,1)S(1)}, u32[]{:S(2)}, u32[]{:S(2)}) collective-permute-start(bf16[2,128,128]{2,1,0:T(8,128)(2,1)S(1)} %get-tuple-element.108), channel_id=1, source_target_pairs={{0,16},{8,24},{16,0},{24,8},{1,17},{9,25},{17,1},{25,9},{2,18},{10... | collective-permute-start | bytes 196616 | tf_op jit(solution)/shard_map/ppermute | solution.py:910
  35.7 0.0 collective-permute-start.12
  35.7 0.4 %shard_map.102.own_ref = f32[2,1024,128]{2,1,0:T(8,128)S(1)} custom-call(bf16[8,128,128]{2,1,0:T(8,128)(2,1)S(1)} %get-tuple-element.105.value_ref, bf16[8,128,640]{2,1,0:T(8,128)(2,1)S(1)} %shard_map.90.pick_ref, f32[8,128,128]{2,1,0:T(8,128)S(1)} %get-tuple-element.107.pixel_ref, bf16[2,1024,512]{2,1,0:T(8,128)(2,1)S(1)} %shard_map.99.onehot_ref), custom_call_target="tpu_custom_call" | custom-call | flops 100000000 | bytes 10000000 | tf_op jit(solution)/shard_map/pallas_call | solution.py:901
  36.2 0.2 shard_map.103
  36.3 0.9 %collective-permute-start.10 = (bf16[2,128,128]{2,1,0:T(8,128)(2,1)S(1)}, bf16[2,128,128]{2,1,0:T(8,128)(2,1)S(1)}, u32[]{:S(2)}, u32[]{:S(2)}) collective-permute-start(bf16[2,128,128]{2,1,0:T(8,128)(2,1)S(1)} %shard_map.103), channel_id=1, source_target_pairs={{0,8},{8,0},{16,24},{24,16},{1,9},{9,1},{17,25},{25,17},{2,10},{10... | collective-permute-start | bytes 196616 | tf_op jit(solution)/shard_map/ppermute | solution.py:910
  37.2 1.5 %collective-permute-done.11.refs_1_ = bf16[2,128,128]{2,1,0:T(8,128)(2,1)S(1)} collective-permute-done((bf16[2,128,128]{2,1,0:T(8,128)(2,1)S(1)}, bf16[2,128,128]{2,1,0:T(8,128)(2,1)S(1)}, u32[]{:S(2)}, u32[]{:S(2)}) %collective-permute-start.11) | collective-permute-done | bytes 65568 | tf_op jit(solution)/shard_map/ppermute | solution.py:910
  38.7 1.4 %collective-permute-done.12.refs_2_ = bf16[2,128,128]{2,1,0:T(8,128)(2,1)S(1)} collective-permute-done((bf16[2,128,128]{2,1,0:T(8,128)(2,1)S(1)}, bf16[2,128,128]{2,1,0:T(8,128)(2,1)S(1)}, u32[]{:S(2)}, u32[]{:S(2)}) %collective-permute-start.12) | collective-permute-done | bytes 65568 | tf_op jit(solution)/shard_map/ppermute | solution.py:910
  40.1 0.0 collective-permute-done.10.refs_0_
  40.1 1.3 %shard_map.104 = f32[2,1024,128]{2,1,0:T(8,128)} custom-call(f32[2,1024,128]{2,1,0:T(8,128)S(1)} %shard_map.102.own_ref, bf16[2,1024,512]{2,1,0:T(8,128)(2,1)S(1)} %shard_map.99.onehot_ref, bf16[2,128,128]{2,1,0:T(8,128)(2,1)S(1)} %collective-permute-done.10.refs_0_, bf16[2,128,128]{2,1,0:T(8,128)(2,1)S(1)} %collective-permute-done.11.refs_1_, ...), custom_call_target="tpu_custom_call" | custom-call | flops 100000000 | bytes 10000000 | tf_op jit(solution)/shard_map/pallas_call | solution.py:911
Async XLA Ops:
  0.6 4.8 %copy-start = (f32[3,4,8,8,8,128]{5,4,3,2,1,0:T(8,128)S(1)}, f32[3,4,8,8,8,128]{5,4,3,2,1,0:T(8,128)}, u32[]{:S(2)}) copy-start(f32[3,4,8,8,8,128]{5,4,3,2,1,0:T(8,128)} %param.8) | copy-start | bytes 9437188
  0.6 4.8 %copy-start.1 = (f32[4,8,8,8,128]{4,3,2,1,0:T(8,128)S(1)}, f32[4,8,8,8,128]{4,3,2,1,0:T(8,128)}, u32[]{:S(2)}) copy-start(f32[4,8,8,8,128]{4,3,2,1,0:T(8,128)} %param.7) | copy-start | bytes 3145732
  0.6 4.8 %copy-start.2 = (f32[4,8,8,8,128]{4,3,2,1,0:T(8,128)S(1)}, f32[4,8,8,8,128]{4,3,2,1,0:T(8,128)}, u32[]{:S(2)}) copy-start(f32[4,8,8,8,128]{4,3,2,1,0:T(8,128)} %param.9) | copy-start | bytes 3145732
  2.4 5.5 %collective-permute-start = (bf16[2,2,64,128]{3,2,1,0:T(8,128)(2,1)S(1)}, bf16[2,2,64,128]{3,2,1,0:T(8,128)(2,1)S(1)}, u32[]{:S(2)}, u32[]{:S(2)}) collective-permute-start(bf16[2,2,64,128]{3,2,1,0:T(8,128)(2,1)S(1)} %get-tuple-element.59), channel_id=1, source_target_pairs={{0,4},{4,0},{1,5},{5,1},{2,6},{6,2},{3,7},{7,3},{8,12},{12,8},{9,1... | collective-permute-start | bytes 196616 | tf_op jit(solution)/shard_map/ppermute | solution.py:781
  5.5 2.5 %copy-start.5 = (s32[8,128]{1,0:T(8,128)S(1)}, s32[8,128]{1,0:T(8,128)}, u32[]{:S(2)}) copy-start(s32[8,128]{1,0:T(8,128)} %block_ref.5) | copy-start | bytes 12292
  5.5 4.6 %copy-start.3 = (bf16[8,512,128]{2,1,0:T(8,128)(2,1)S(1)}, bf16[8,512,128]{2,1,0:T(8,128)(2,1)}, u32[]{:S(2)}) copy-start(bf16[8,512,128]{2,1,0:T(8,128)(2,1)} %weight_ref.1) | copy-start | bytes 3145732
  7.9 3.4 %copy-start.4 = (s32[8,128]{1,0:T(8,128)S(1)}, s32[8,128]{1,0:T(8,128)}, u32[]{:S(2)}) copy-start(s32[8,128]{1,0:T(8,128)} %cut_ref.1) | copy-start | bytes 12292
  8.0 3.7 %collective-permute-start.1 = (bf16[80,128]{1,0:T(8,128)(2,1)S(1)}, bf16[80,128]{1,0:T(8,128)(2,1)S(1)}, u32[]{:S(2)}, u32[]{:S(2)}) collective-permute-start(bf16[80,128]{1,0:T(8,128)(2,1)S(1)} %get-tuple-element.61), channel_id=1, source_target_pairs={{0,8},{8,0},{16,24},{24,16},{1,9},{9,1},{17,25},{25,17},{2,10},{10... | collective-permute-start | bytes 61448 | tf_op jit(solution)/shard_map/ppermute | solution.py:788
  8.1 3.6 %collective-permute-start.2 = (bf16[64,128]{1,0:T(8,128)(2,1)S(1)}, bf16[64,128]{1,0:T(8,128)(2,1)S(1)}, u32[]{:S(2)}, u32[]{:S(2)}) collective-permute-start(bf16[64,128]{1,0:T(8,128)(2,1)S(1)} %get-tuple-element.62), channel_id=1, source_target_pairs={{0,24},{8,16},{16,8},{24,0},{1,25},{9,17},{17,9},{25,1},{2,26},{10... | collective-permute-start | bytes 49160 | tf_op jit(solution)/shard_map/ppermute | solution.py:788
  11.9 6.7 %collective-permute-start.3 = (bf16[64,128]{1,0:T(8,128)(2,1)S(1)}, bf16[64,128]{1,0:T(8,128)(2,1)S(1)}, u32[]{:S(2)}, u32[]{:S(2)}) collective-permute-start(bf16[64,128]{1,0:T(8,128)(2,1)S(1)} %get-tuple-element.66), channel_id=1, source_target_pairs={{0,1},{1,0},{2,3},{3,2},{4,5},{5,4},{6,7},{7,6},{8,9},{9,8},{10,11... | collective-permute-start | bytes 49160 | tf_op jit(solution)/shard_map/ppermute | solution.py:788
  13.5 5.5 %collective-permute-start.4 = (bf16[64,128]{1,0:T(8,128)(2,1)S(1)}, bf16[64,128]{1,0:T(8,128)(2,1)S(1)}, u32[]{:S(2)}, u32[]{:S(2)}) collective-permute-start(bf16[64,128]{1,0:T(8,128)(2,1)S(1)} %get-tuple-element.67), channel_id=1, source_target_pairs={{0,3},{1,2},{2,1},{3,0},{4,7},{5,6},{6,5},{7,4},{8,11},{9,10},{10,... | collective-permute-start | bytes 49160 | tf_op jit(solution)/shard_map/ppermute | solution.py:788
  19.7 4.0 %collective-permute-start.5 = (bf16[2,1,64,128]{3,2,1,0:T(8,128)(2,1)S(1)}, bf16[2,1,64,128]{3,2,1,0:T(8,128)(2,1)S(1)}, u32[]{:S(2)}, u32[]{:S(2)}) collective-permute-start(bf16[2,1,64,128]{3,2,1,0:T(8,128)(2,1)S(1)} %get-tuple-element.76), channel_id=1, source_target_pairs={{0,4},{4,0},{1,5},{5,1},{2,6},{6,2},{3,7},{7,3},{8,12},{12,8},{9,1... | collective-permute-start | bytes 98312 | tf_op jit(solution)/shard_map/ppermute | solution.py:781
  23.7 3.4 %collective-permute-start.7 = (bf16[64,128]{1,0:T(8,128)(2,1)S(1)}, bf16[64,128]{1,0:T(8,128)(2,1)S(1)}, u32[]{:S(2)}, u32[]{:S(2)}) collective-permute-start(bf16[64,128]{1,0:T(8,128)(2,1)S(1)} %get-tuple-element.83), channel_id=1, source_target_pairs={{0,24},{8,16},{16,8},{24,0},{1,25},{9,17},{17,9},{25,1},{2,26},{10... | collective-permute-start | bytes 49160 | tf_op jit(solution)/shard_map/ppermute | solution.py:788
  23.8 2.6 %collective-permute-start.6 = (bf16[32,128]{1,0:T(8,128)(2,1)S(1)}, bf16[32,128]{1,0:T(8,128)(2,1)S(1)}, u32[]{:S(2)}, u32[]{:S(2)}) collective-permute-start(bf16[32,128]{1,0:T(8,128)(2,1)S(1)} %get-tuple-element.82), channel_id=1, source_target_pairs={{0,8},{8,0},{16,24},{24,16},{1,9},{9,1},{17,25},{25,17},{2,10},{10... | collective-permute-start | bytes 24584 | tf_op jit(solution)/shard_map/ppermute | solution.py:788
  27.3 5.2 %collective-permute-start.8 = (bf16[32,128]{1,0:T(8,128)(2,1)S(1)}, bf16[32,128]{1,0:T(8,128)(2,1)S(1)}, u32[]{:S(2)}, u32[]{:S(2)}) collective-permute-start(bf16[32,128]{1,0:T(8,128)(2,1)S(1)} %get-tuple-element.90), channel_id=1, source_target_pairs={{0,1},{1,0},{2,3},{3,2},{4,5},{5,4},{6,7},{7,6},{8,9},{9,8},{10,11... | collective-permute-start | bytes 24584 | tf_op jit(solution)/shard_map/ppermute | solution.py:788
  27.6 5.4 %collective-permute-start.9 = (bf16[32,128]{1,0:T(8,128)(2,1)S(1)}, bf16[32,128]{1,0:T(8,128)(2,1)S(1)}, u32[]{:S(2)}, u32[]{:S(2)}) collective-permute-start(bf16[32,128]{1,0:T(8,128)(2,1)S(1)} %get-tuple-element.91), channel_id=1, source_target_pairs={{0,3},{1,2},{2,1},{3,0},{4,7},{5,6},{6,5},{7,4},{8,11},{9,10},{10,... | collective-permute-start | bytes 24584 | tf_op jit(solution)/shard_map/ppermute | solution.py:788
  34.4 4.3 %collective-permute-start.11 = (bf16[2,128,128]{2,1,0:T(8,128)(2,1)S(1)}, bf16[2,128,128]{2,1,0:T(8,128)(2,1)S(1)}, u32[]{:S(2)}, u32[]{:S(2)}) collective-permute-start(bf16[2,128,128]{2,1,0:T(8,128)(2,1)S(1)} %get-tuple-element.108), channel_id=1, source_target_pairs={{0,16},{8,24},{16,0},{24,8},{1,17},{9,25},{17,1},{25,9},{2,18},{10... | collective-permute-start | bytes 196616 | tf_op jit(solution)/shard_map/ppermute | solution.py:910
  35.7 4.3 %collective-permute-start.12 = (bf16[2,128,128]{2,1,0:T(8,128)(2,1)S(1)}, bf16[2,128,128]{2,1,0:T(8,128)(2,1)S(1)}, u32[]{:S(2)}, u32[]{:S(2)}) collective-permute-start(bf16[2,128,128]{2,1,0:T(8,128)(2,1)S(1)} %get-tuple-element.109), channel_id=1, source_target_pairs={{0,24},{8,16},{16,8},{24,0},{1,25},{9,17},{17,9},{25,1},{2,26},{10... | collective-permute-start | bytes 196616 | tf_op jit(solution)/shard_map/ppermute | solution.py:910
  36.3 3.7 %collective-permute-start.10 = (bf16[2,128,128]{2,1,0:T(8,128)(2,1)S(1)}, bf16[2,128,128]{2,1,0:T(8,128)(2,1)S(1)}, u32[]{:S(2)}, u32[]{:S(2)}) collective-permute-start(bf16[2,128,128]{2,1,0:T(8,128)(2,1)S(1)} %shard_map.103), channel_id=1, source_target_pairs={{0,8},{8,0},{16,24},{24,16},{1,9},{9,1},{17,25},{25,17},{2,10},{10... | collective-permute-start | bytes 196616 | tf_op jit(solution)/shard_map/ppermute | solution.py:910

commit v7 on v6

--- a/solution.py
+++ b/solution.py
@@ -88,10 +88,17 @@
             turn[16 * k + c, 128 + 8 * c + 2 * k + 1] = 1.0
     ends = turn.reshape(4, 16, 256)[:, ::15].reshape(8, 256)
     ends = np.concatenate([ends, np.zeros_like(ends)], axis=0)
+    partial = np.zeros((16, 64))
+    for i in range(8):
+        partial[i, 8 * i + 1 : 8 * i + 8] = derivative[0, 1:]
+        partial[8 + i, 8 * i : 8 * i + 7] = derivative[7, :7]
+    high, low = split_two(partial)
+    partial = np.concatenate([high, high, low, np.zeros_like(high)], axis=1)
     exact = [spread, spread, turn[:, :128], turn[:, 128:], ends[:, :128], ends[:, 128:]]
     exact = np.concatenate(exact, axis=0)
     split = [row_table[:, :128], row_table[:, 128:], lane_table[:, :128], lane_table[:, 128:]]
     split += [join_table, exact.astype(np.float32).astype(BF16)]
+    split += [partial[:, :128], partial[:, 128:]]
     return jnp.asarray(np.concatenate(split, axis=0))
 
 
@@ -114,6 +121,10 @@
 
 def end_table(table_ref):
     return jnp.concatenate([table_ref[1408:1424], table_ref[1424:1440]], axis=1)
+
+
+def partial_table(table_ref):
+    return jnp.concatenate([table_ref[1440:1456], table_ref[1456:1472][:, :64]], axis=1)
 
 
 def span_of(a, offset=0):
@@ -366,21 +377,23 @@
     return (lane == 0) | (lane == 127)
 
 
-def azimuth_kernel(cam_count, s_ref, x_ref, one_ref, two_ref, even_ref, odd_ref, packed_ref):
+def azimuth_kernel(
+    cam_count, s_ref, x_ref, one_ref, two_ref, scalar_ref, velocity_ref, mass_ref, table_ref,
+    even_ref, odd_ref, packed_ref,
+):
     ends = end_lanes((8, 128))
     row = row_ids((8, 128))
     even = (lax.axis_index("ey") & 1) == 0
-    rows = s_ref.shape[0]
-    one = one_ref[:rows, :].astype(F32)
-    two = two_ref[:rows, :].astype(F32)
-    ups, downs = [], []
-    for q in range(rows // 8):
+    count = s_ref.shape[0]
+    one = one_ref[:count, :].astype(F32)
+    two = two_ref[:count, :].astype(F32)
+    low, high = [], []
+    for q in range(count // 8):
         at = slice(8 * q, 8 * q + 8)
         packed = merged(one[at], two[at], cam_count)
         packed_ref[q] = packed
         f, a = q // 4, q % 4
-        faces = []
-        for line, shift in ((0, 16), (63, 2)):
+        for line, shift, faces in ((0, 16, low), (63, 2, high)):
             j = line & 7
             spread = jnp.broadcast_to(packed[j : j + 1, :], (8, 128))
             moved = pltpu.roll(spread, shift, 1, stride=16, stride_axis=0)
@@ -390,10 +403,27 @@
             if a == 3:
                 face = face + jnp.where(row == 7, x_ref[1, f, line : line + 1, :], 0.0)
             faces.append(face)
-        ups.append(jnp.where(even, faces[1], faces[0]))
-        downs.append(jnp.where(even, faces[0], faces[1]))
-    even_ref[...] = jnp.concatenate(ups, axis=0).astype(BF16)
-    odd_ref[...] = jnp.concatenate(downs, axis=0).astype(BF16)
+    slopes = [[], []]
+    for a in range(4):
+        pairs = []
+        for b in (0, 7):
+            g = assembled(s_ref, x_ref, packed_ref[a], 0, a, b)
+            m = assembled(s_ref, x_ref, packed_ref[a + 4], 1, a, b)
+            scalar = scalar_ref[span_of(a), 8 * b : 8 * b + 8, :].reshape(64, 128)
+            pairs.append(halves(scalar - (time_step / m) * g))
+        tops = jnp.concatenate([p[0] for p in pairs], axis=1)
+        rests = jnp.concatenate([p[1] for p in pairs], axis=1)
+        both = dot(partial_table(table_ref), jnp.concatenate([tops, rests, tops], axis=0))
+        slopes[0].append(both[:8, :128])
+        slopes[1].append(both[8:, 128:])
+    messages = []
+    for faces, line, slope in ((low, 0, slopes[0]), (high, 63, slopes[1])):
+        flow = [mass_ref[:, line, :] * velocity_ref[d, :, line, :] for d in range(3)]
+        share = flow[1] * jnp.concatenate(slope, axis=0)
+        rows = faces + [share] + flow + [scalar_ref[:, line, :]]
+        messages.append(jnp.concatenate(rows, axis=0))
+    even_ref[...] = jnp.where(even, messages[1], messages[0]).astype(BF16)
+    odd_ref[...] = jnp.where(even, messages[0], messages[1]).astype(BF16)
 
 
 def unpacked(packed, b):
@@ -438,7 +468,7 @@
 
 def second_pairs(
     pairs, s_ref, x_ref, packed_ref, y_refs, scalar_ref, velocity_ref,
-    mass_ref, table_ref, g_ref, base_ref, half_ref, z_ref,
+    mass_ref, table_ref, g_ref, base_ref, half_ref, z_ref, first_ref=None,
 ):
     def body(a, layer=None):
         at = span_of(a)
@@ -460,6 +490,8 @@
                 base_ref[to, out, :] = (0.5 * (scalar + first)).reshape(8, 8, 128)
                 half_ref[to, out, :] = (0.5 * scale).reshape(8, 8, 128)
                 fields.append(first)
+                if first_ref is not None:
+                    first_ref[to, out, :] = first.reshape(8, 8, 128)
                 velocities.append(
                     [velocity_ref[d, at, s, :].reshape(64, 128) for d in range(3)]
                 )
@@ -487,16 +519,51 @@
     join_block(g_ref)
 
 
+def add_beyond(layers, y_one_ref, y_two_ref, first_ref, scalar_ref, table_ref, g_ref, z_ref):
+    even = (lax.axis_index("ey") & 1) == 0
+    one, two = y_one_ref[64:, :].astype(F32), y_two_ref[64:, :].astype(F32)
+    sides = (jnp.where(even, two, one), jnp.where(even, one, two))
+    rows = []
+    for h, (line, outer) in enumerate(((0, 0), (15, 63))):
+        for a, n in layers:
+            change = first_ref[span_of(n), line, :] - scalar_ref[span_of(a), outer, :]
+            rows.append(sides[h][128 + 8 * a : 136 + 8 * a] + change)
+    count = len(layers)
+    field = jnp.concatenate(rows + [jnp.zeros((64 - 16 * count, 128), F32)], axis=0)
+    high, low = halves(field)
+    axial = dot(row_table(table_ref, 64), jnp.concatenate([high, low, high], axis=0))
+    radius = by_lanes([(high, low)], table_ref)
+    corner = float(gll_derivative()[7, 7])
+    values = []
+    for h, sign in ((0, corner), (1, -corner)):
+        for k, (a, _) in enumerate(layers):
+            at = slice(8 * (count * h + k), 8 * (count * h + k) + 8)
+            share, *flow = [sides[h][32 * n + 8 * a : 32 * n + 8 * a + 8] for n in range(4)]
+            azimuth = sign * field[at]
+            values.append(share + flow[0] * axial[at] + flow[1] * azimuth + flow[2] * radius[at])
+    (joined,), (spread,) = join_lanes([jnp.concatenate(values, axis=0)], table_ref)
+    slot = ((lane_ids((8, 128)) + 1) >> 1) & 63
+    row = row_ids((8, 128))
+    for h, line in ((0, 0), (1, 15)):
+        for k, (_, n) in enumerate(layers):
+            at = slice(8 * (count * h + k), 8 * (count * h + k) + 8)
+            g_ref[span_of(n), line, :] = g_ref[span_of(n), line, :] + joined[at]
+            mine = jnp.where(slot == 56 - 8 * row + 7 * h, spread[at], 0.0)
+            total = jnp.sum(mine, axis=0, keepdims=True)
+            z_ref[n] = z_ref[n] + jnp.where(row == 7 * h, total, 0.0)
+
+
 def second_face_kernel(
     s_ref, x_ref, packed_ref, y_one_ref, y_two_ref, scalar_ref, velocity_ref,
-    mass_ref, table_ref, inner_ref, x_out_ref, edge_ref, base_ref, half_ref, z_ref,
+    mass_ref, table_ref, inner_ref, x_out_ref, edge_ref, base_ref, half_ref, z_ref, first_ref,
 ):
     body = second_pairs(
-        ((0, 7),), s_ref, x_ref, packed_ref, (y_one_ref, y_two_ref),
-        scalar_ref, velocity_ref, mass_ref, table_ref, edge_ref, base_ref, half_ref, z_ref,
+        ((0, 7),), s_ref, x_ref, packed_ref, (y_one_ref, y_two_ref), scalar_ref, velocity_ref,
+        mass_ref, table_ref, edge_ref, base_ref, half_ref, z_ref, first_ref,
     )
     body(0, 0)
     body(3, 1)
+    add_beyond(((0, 0), (3, 1)), y_one_ref, y_two_ref, first_ref, scalar_ref, table_ref, edge_ref, z_ref)
     row = row_ids((64, 128))
     for n, (layer, at) in enumerate(((15, 31), (0, 0))):
         face = jnp.concatenate(
@@ -510,14 +577,15 @@
 def second_outer_kernel(
     s_ref, x_ref, packed_ref, y_one_ref, y_two_ref, scalar_ref, velocity_ref,
     mass_ref, table_ref, inner_ref, z_in, edge_in, base_in, half_in, z_face,
-    g_ref, base_ref, half_ref, z_ref, edge_ref,
+    g_ref, base_ref, half_ref, z_ref, edge_ref, first_ref,
 ):
     body = second_pairs(
-        ((0, 7),), s_ref, x_ref, packed_ref, (y_one_ref, y_two_ref),
-        scalar_ref, velocity_ref, mass_ref, table_ref, edge_ref, base_ref, half_ref, z_ref,
+        ((0, 7),), s_ref, x_ref, packed_ref, (y_one_ref, y_two_ref), scalar_ref, velocity_ref,
+        mass_ref, table_ref, edge_ref, base_ref, half_ref, z_ref, first_ref,
     )
     body(1)
     body(2)
+    add_beyond(((1, 1), (2, 2)), y_one_ref, y_two_ref, first_ref, scalar_ref, table_ref, edge_ref, z_ref)
     for layer, a in ((0, 0), (1, 3)):
         for source, target in ((edge_in, edge_ref), (base_in, base_ref), (half_in, half_ref)):
             target[span_of(a)] = source[span_of(layer)]
@@ -546,11 +614,9 @@
     cut = cut_ref[...]
     a, b, c = cut >> 7, (cut >> 4) & 7, cut & 15
     order = jnp.where(a == 0, 2, jnp.where(a == 3, 3, a - 1))
-    inner = 96 * order + 16 * (b - 1) + c
-    ends = 512 + 12 * a + 2 * (b - 1) + (c >> 3)
-    outer = 384 + 32 * a + jnp.where(b == 7, 16, 0) + c
+    inner = 128 * order + 16 * b + c
+    ends = 512 + 16 * a + 2 * b + (c >> 3)
     place = jnp.where((c == 0) | (c == 15), ends, inner)
-    place = jnp.where((b == 0) | (b == 7), outer, place)
     turned = place.astype(F32).T.astype(jnp.int32)
     lane = lane_ids((128, 640))
     for m in range(8):
@@ -572,14 +638,22 @@
     )
 
 
-def advanced(g_ref, x_ref, packed, y_refs, base_ref, half_ref, a, pair, place):
+PAIRS = ((0, 1), (2, 3), (4, 5), (6, 7))
+
+
+def term(refs, a, b):
+    inner_ref, outer_ref = refs
+    at = span_of(a)
+    if b in (0, 7):
+        return outer_ref[at, 8 * (b // 7) : 8 * (b // 7) + 8, :].reshape(64, 128)
+    return inner_ref[at, 8 * b - 8 : 8 * b, :].reshape(64, 128)
+
+
+def advanced(g_ref, x_ref, packed, bases, halfs, a, pair):
     blocks = []
-    for h, b in enumerate(pair):
-        g = assembled(g_ref, x_ref, packed, 0, a, b, y_refs)
-        out = slice(place + 8 * h, place + 8 * h + 8)
-        base = base_ref[span_of(a), out, :].reshape(64, 128)
-        half = half_ref[span_of(a), out, :].reshape(64, 128)
-        blocks.append(base - half * g)
+    for b in pair:
+        g = assembled(g_ref, x_ref, packed, 0, a, b)
+        blocks.append(term(bases, a, b) - term(halfs, a, b) * g)
     return blocks
 
 
@@ -596,70 +670,37 @@
     return dot(element_ref[...], weight_ref[:, 256 * m : 256 * m + 256]).astype(BF16)
 
 
-INNER = ((1, 2), (3, 4), (5, 6))
-
-
-def inner_elements(layers, g_ref, x_ref, base_ref, half_ref, table_ref, element_ref):
+def layer_elements(layers, g_ref, x_ref, bases, halfs, table_ref, element_ref):
     place = 0
     for a in layers:
-        for n, pair in enumerate(INNER):
-            blocks = advanced(g_ref, x_ref, None, None, base_ref, half_ref, a, pair, 16 * n)
+        for pair in PAIRS:
+            blocks = advanced(g_ref, x_ref, None, bases, halfs, a, pair)
             store_elements(element_ref, blocks, table_ref, place)
             place += 32
 
 
-def early_kernel(g_ref, base_ref, half_ref, table_ref, weight_ref, value_ref, element_ref):
-    inner_elements((1, 2), g_ref, None, base_ref, half_ref, table_ref, element_ref)
+def early_kernel(
+    g_ref, base_one, half_one, base_two, half_two, table_ref, weight_ref, value_ref, element_ref
+):
+    bases, halfs = (base_one, base_two), (half_one, half_two)
+    layer_elements((1, 2), g_ref, None, bases, halfs, table_ref, element_ref)
     for m in range(4):
         value_ref[:, 256 * m : 256 * m + 256] = pixel_values(element_ref, weight_ref, m)
 
 
 def middle_kernel(
-    g_ref, x_ref, base_ref, half_ref, table_ref, weight_ref, pick_ref, early_ref,
-    pixel_ref, element_ref,
+    g_ref, x_ref, base_one, half_one, base_two, half_two, table_ref, weight_ref, pick_ref,
+    early_ref, pixel_ref, element_ref,
 ):
-    inner_elements((0, 3), g_ref, x_ref, base_ref, half_ref, table_ref, element_ref)
+    bases, halfs = (base_one, base_two), (half_one, half_two)
+    layer_elements((0, 3), g_ref, x_ref, bases, halfs, table_ref, element_ref)
     for m in range(4):
         late = pixel_values(element_ref, weight_ref, m)
         both = jnp.concatenate([early_ref[:, 256 * m : 256 * m + 256], late], axis=0)
         for n in range(2):
             pixel_ref[2 * m + n] = dot(
-                pick_ref[2 * m + n, :, :384], both[:, 128 * n : 128 * n + 128]
+                pick_ref[2 * m + n, :, :512], both[:, 128 * n : 128 * n + 128]
             )
-
-
-def render_inner_kernel(
-    g_ref, x_ref, packed_ref, base_ref, half_ref, table_ref, weight_ref, pick_ref,
-    pixel_in, out_hbm, pixel_ref, advected_ref, end_ref, sem,
-):
-    end_ref[48:, :] = jnp.zeros((16, 512), F32)
-
-    def body(a):
-        packed = packed_ref[a]
-        for n, pair in enumerate(INNER):
-            blocks = advanced(g_ref, x_ref, packed, None, base_ref, half_ref, a, pair, 16 * n)
-            for h in range(2):
-                out = slice(16 * n + 8 * h, 16 * n + 8 * h + 8)
-                advected_ref[span_of(a), out, :] = blocks[h].reshape(8, 8, 128)
-            turned = turn(blocks, end_table(table_ref))
-            for h in range(2):
-                place = 12 * a + 4 * n + 2 * h
-                for k in range(4):
-                    end_ref[place : place + 2, 128 * k : 128 * k + 128] = turned[
-                        2 * k : 2 * k + 2, 128 * h : 128 * h + 128
-                    ]
-
-    sweep(body, 4)
-    copy = pltpu.make_async_copy(advected_ref, out_hbm.at[:, pl.ds(8, 48)], sem)
-    copy.start()
-    ends = end_ref[...].astype(BF16)
-    for m in range(4):
-        values = dot(ends, weight_ref[:, 256 * m : 256 * m + 256]).astype(BF16)
-        for n in range(2):
-            pixel_ref[2 * m + n] = pixel_in[2 * m + n] + dot(
-                pick_ref[2 * m + n, :, 512:576], values[:, 128 * n : 128 * n + 128]
-            )
-    copy.wait()
 
 
 def fill_payload(payload_ref, d, cam_count, pick_ref, value_ref, pixel_ref):
@@ -667,69 +708,67 @@
     share = pixel_ref.shape[0] // cam_count
     for n in range(share):
         m = share * (me ^ d) + n
-        values = dot(pick_ref[m, :, 384:512], value_ref[m]) + pixel_ref[m]
+        values = dot(pick_ref[m, :, 512:576], value_ref[m]) + pixel_ref[m]
         payload_ref[n] = values.astype(BF16)
 
 
 def render_far_kernel(
-    cam_count, g_ref, x_ref, packed_ref, y_one_ref, y_two_ref, base_ref, half_ref,
-    table_ref, weight_ref, pick_ref, pixel_ref, out_in,
-    out_hbm, value_ref, *rest,
+    cam_count, g_ref, x_ref, one_ref, two_ref, base_one, half_one, base_two, half_two,
+    table_ref, weight_ref, pick_ref, pixel_ref, out_hbm, value_ref, *rest,
 ):
     payload_refs = rest[: cam_count - 2]
-    advected_ref, element_ref, sems = rest[cam_count - 2 :]
+    advected_ref, end_ref, sem = rest[cam_count - 2 :]
+    bases, halfs = (base_one, base_two), (half_one, half_two)
+    one, two = one_ref[:32, :].astype(F32), two_ref[:32, :].astype(F32)
     for a in range(4):
-        packed = packed_ref[a]
-        blocks = advanced(
-            g_ref, x_ref, packed, (y_one_ref, y_two_ref), base_ref, half_ref, a, (0, 7), 0
-        )
-        for h in range(2):
-            advected_ref[span_of(a), 8 * h : 8 * h + 8, :] = blocks[h].reshape(8, 8, 128)
-        store_elements(element_ref, blocks, table_ref, 32 * a)
-    copies = [
-        pltpu.make_async_copy(
-            advected_ref.at[:, pl.ds(8 * n, 8)], out_hbm.at[:, pl.ds(56 * n, 8)], sems.at[n]
-        )
-        for n in range(2)
-    ]
-    for copy in copies:
-        copy.start()
-    cameras = pixel_ref.shape[0]
-    for m in range(cameras // 2):
-        values = pixel_values(element_ref, weight_ref, m)
+        packed = merged(one[8 * a : 8 * a + 8], two[8 * a : 8 * a + 8], cam_count)
+        for n, pair in enumerate(PAIRS):
+            blocks = advanced(g_ref, x_ref, packed, bases, halfs, a, pair)
+            turned = turn(blocks, end_table(table_ref))
+            for h, b in enumerate(pair):
+                advected_ref[span_of(a), 8 * b : 8 * b + 8, :] = blocks[h].reshape(8, 8, 128)
+                place = 16 * a + 2 * b
+                for k in range(4):
+                    end_ref[place : place + 2, 128 * k : 128 * k + 128] = turned[
+                        2 * k : 2 * k + 2, 128 * h : 128 * h + 128
+                    ]
+    copy = pltpu.make_async_copy(advected_ref, out_hbm, sem)
+    copy.start()
+    ends = end_ref[...].astype(BF16)
+    for m in range(pixel_ref.shape[0] // 2):
+        values = dot(ends, weight_ref[:, 256 * m : 256 * m + 256]).astype(BF16)
         value_ref[2 * m] = values[:, :128]
         value_ref[2 * m + 1] = values[:, 128:]
     for d in range(2, cam_count):
         fill_payload(payload_refs[d - 2], d, cam_count, pick_ref, value_ref, pixel_ref)
-    for copy in copies:
-        copy.wait()
+    copy.wait()
 
 
 def render_near_kernel(cam_count, d, value_ref, pick_ref, pixel_ref, payload_ref):
     fill_payload(payload_ref, d, cam_count, pick_ref, value_ref, pixel_ref)
 
 
-def block_kernel(share, block_ref, first_ref, second_ref, onehot_ref, id_ref):
+def own_image_kernel(
+    cam_count, value_ref, pick_ref, pixel_ref, block_ref, first_ref, second_ref,
+    image_ref, onehot_ref, payload_ref, id_ref,
+):
     me = lax.axis_index("cam")
+    share = image_ref.shape[0]
     id_ref[0] = block_ref[...]
     tiles = ((1, first_ref[64:80, :]), (3, second_ref[32:48, :]), (2, second_ref[48:64, :]))
     for d, tile in tiles:
         ids = tile.astype(F32).astype(jnp.int32)
         id_ref[d] = ids[:8] * 32 + ids[8:]
+    fill_payload(payload_ref, 0, cam_count, pick_ref, value_ref, pixel_ref)
     for m in range(share):
         ids = [id_ref[d, pl.ds(share * me + m, 1), :] for d in range(4)]
         ids = jnp.concatenate(ids, axis=1)
         for chunk in range(4):
+            at = slice(256 * chunk, 256 * chunk + 256)
             row = row_ids((256, ids.shape[1])) + 256 * chunk
-            onehot_ref[m, 256 * chunk : 256 * chunk + 256, :] = jnp.where(
-                row == ids, 1.0, 0.0
-            ).astype(BF16)
-
-
-def own_image_kernel(cam_count, value_ref, pick_ref, pixel_ref, onehot_ref, image_ref, payload_ref):
-    fill_payload(payload_ref, 0, cam_count, pick_ref, value_ref, pixel_ref)
-    for m in range(image_ref.shape[0]):
-        image_ref[m] = dot(onehot_ref[m, :, :128], payload_ref[m])
+            onehot = jnp.where(row == ids, 1.0, 0.0).astype(BF16)
+            onehot_ref[m, at, :] = onehot
+            image_ref[m, at, :] = dot(onehot[:, :128], payload_ref[m])
 
 
 def image_kernel(own_ref, onehot_ref, *refs):
@@ -827,8 +866,8 @@
     z_got, weights, picks = lax.optimization_barrier((z_got, weights, picks))
     ids_got = z_got[0]
     *y, packed = call(
-        part(azimuth_kernel, n_cam), (half(64, 128), half(64, 128), shape_of(8, 8, 128))
-    )(s, x_got, *z_got)
+        part(azimuth_kernel, n_cam), (half(224, 128), half(224, 128), shape_of(8, 8, 128))
+    )(s, x_got, *z_got, scalar, velocity, mass, near)
     y_got = swap_both(*y, "ey")
     g_inner, *inner_terms, z_inner = call(
         second_inner_kernel, (shape_of(*inner),) * 3 + (shape_of(4, 8, 128),)
@@ -838,19 +877,21 @@
     x, *faces = call(
         second_face_kernel,
         (shape_of(2, 1, 64, 128, dtype=BF16),) + (shape_of(*some),) * 3 + (shape_of(2, 8, 128),),
+        scratch_shapes=[pltpu.VMEM(some, F32)],
     )(*args)
     g, *outer_terms, z = call(
         second_outer_kernel,
         (shape_of(*flat), shape_of(*outer), shape_of(*outer), shape_of(4, 8, 128)),
-        scratch_shapes=[pltpu.VMEM(outer, F32)],
+        scratch_shapes=[pltpu.VMEM(outer, F32), pltpu.VMEM(outer, F32)],
     )(*args, z_inner, *faces)
 
+    terms = (*inner_terms, *outer_terms)
     x_got = swap_axial(x)
     early = call(
         early_kernel,
-        shape_of(192, 128 * cameras, dtype=BF16),
-        scratch_shapes=[pltpu.VMEM((192, 512), BF16)],
-    )(g, *inner_terms, near, weights)
+        shape_of(256, 128 * cameras, dtype=BF16),
+        scratch_shapes=[pltpu.VMEM((256, 512), BF16)],
+    )(g, *terms, near, weights)
     x_got, early = lax.optimization_barrier((x_got, early))
     *z, x_got = call(
         second_radial_kernel, (half(32, 128), half(64, 128), shape_of(2, 1, 64, 128))
@@ -859,50 +900,30 @@
     pixels = call(
         middle_kernel,
         shape_of(cameras, 128, 128),
-        scratch_shapes=[pltpu.VMEM((192, 512), BF16)],
-    )(g, x_got, *inner_terms, near, weights, picks, early)
+        scratch_shapes=[pltpu.VMEM((256, 512), BF16)],
+    )(g, x_got, *terms, near, weights, picks, early)
     z_got, pixels = lax.optimization_barrier((z_got, pixels))
-    *y, packed = call(
-        part(azimuth_kernel, n_cam), (half(32, 128), half(32, 128), shape_of(4, 8, 128))
-    )(g, x_got, *z_got)
-    y_got = swap_both(*y, "ey")
-    packed, ids = lax.optimization_barrier((packed, (ids_got, z_got[1])))
-    onehot = call(
-        part(block_kernel, share),
-        half(share, NBLK, 128 * n_cam),
-        scratch_shapes=[pltpu.VMEM((n_cam, cameras, 128), jnp.int32)],
-    )(pixel_block, *ids)
-    advected, pixels = call(
-        render_inner_kernel,
-        (shape_of(*flat), shape_of(cameras, 128, 128)),
-        out_specs=(HBM, VMEM),
+    payload_shape = half(share, 128, 128)
+    advected, values, *far = call(
+        part(render_far_kernel, n_cam),
+        (shape_of(*flat), half(cameras, 64, 128)) + (payload_shape,) * (n_cam - 2),
+        out_specs=(HBM, VMEM) + (VMEM,) * (n_cam - 2),
         scratch_shapes=[
-            pltpu.VMEM(inner, F32),
+            pltpu.VMEM(flat, F32),
             pltpu.VMEM((64, 512), F32),
             pltpu.SemaphoreType.DMA,
         ],
-    )(g, x_got, packed, *inner_terms, near, weights, picks, pixels)
-    y_got, onehot = lax.optimization_barrier((y_got, onehot))
-    payload_shape = half(share, 128, 128)
-    advected, values, *far = call(
-        part(render_far_kernel, n_cam),
-        (shape_of(*flat), shape_of(cameras, 128, 128, dtype=BF16)) + (payload_shape,) * (n_cam - 2),
-        in_specs=[VMEM] * 11 + [HBM],
-        out_specs=(HBM, VMEM) + (VMEM,) * (n_cam - 2),
-        input_output_aliases={11: 0},
-        scratch_shapes=[
-            pltpu.VMEM(outer, F32),
-            pltpu.VMEM((128, 512), BF16),
-            pltpu.SemaphoreType.DMA((2,)),
-        ],
-    )(g, x_got, packed, *y_got, *outer_terms, near, weights, picks, pixels, advected)
+    )(g, x_got, *z_got, *terms, near, weights, picks, pixels)
     parts = (values, picks, pixels)
     image_shape = shape_of(share, NBLK, 128)
-    images = call(
+    images, onehot = call(
         part(own_image_kernel, n_cam),
-        image_shape,
-        scratch_shapes=[pltpu.VMEM(payload_shape.shape, BF16)],
-    )(*parts, onehot)
+        (image_shape, half(share, NBLK, 128 * n_cam)),
+        scratch_shapes=[
+            pltpu.VMEM(payload_shape.shape, BF16),
+            pltpu.VMEM((n_cam, cameras, 128), jnp.int32),
+        ],
+    )(*parts, pixel_block, ids_got, z_got[1])
     images, parts = lax.optimization_barrier((images, parts))
     beside = call(part(render_near_kernel, n_cam, 1), payload_shape)(*parts)
     received = []

time: 41.5 us -> 37.2 us (0.90)
  starting transfers between devices: 17.1 us -> 14.7 us
  waiting for transfers between devices: 5.52 us -> 4.51 us
  Pallas kernels: 17.8 us -> 17 us
    ppermute x8 -> x6, starting transfers between devices: 10.3 us -> 7.85 us  [swap_both(): return (lax.ppermute(one, axis, even), lax.ppermute(two, axis, odd))]
    pallas_call x7 -> x4, Pallas kernels: 5.36 us -> 3.89 us  [the longest x1 2.04 us: per_device(): call(part(render_far_kernel, n_cam), (shape_of(*flat), half(cameras, 64,...]
    ppermute x8 -> x6, waiting for transfers between devices: 1.72 us -> 1.09 us  [swap_both(): return (lax.ppermute(one, axis, even), lax.ppermute(two, axis, odd))]
    pallas_call x1, Pallas kernels: 1.05 us -> 1.49 us  [per_device(): call(middle_kernel, shape_of(cameras, 128, 128), scratch_shapes=[pltpu.VM...]
  transfers between devices with their start and end apart: 13 -> 11, of which waited for: 6 -> 5; matrix products, arithmetic and copies ran while one was open for 0% -> 0% of each run, Pallas kernels for 30% -> 28%
where the time goes in v7:
time: 37.2 us; the launch traced here: 37 us
  Pallas kernels  17 us (46%)
  starting transfers between devices  14.7 us (40%)
  waiting for transfers between devices  4.51 us (12%)
  between operations  0.84 us (2%)
    ppermute x6, starting transfers between devices, swap_both(): return (lax.ppermute(one, axis, even), lax.ppermute(two, axis, odd))  7.85 us
    ppermute x2, starting transfers between devices, swap_axial(): return lax.ppermute(x, 'ex', up)  4.56 us
    ppermute x3, waiting for transfers between devices, per_device(): lax.ppermute(payload, 'cam', [(i, i ^ d) for i in range(n_cam)])  2.69 us
    pallas_call x1, Pallas kernels, per_device(): call(second_inner_kernel, (shape_of(*inner),) * 3 + (shape_of(4, 8, 128),))  2.6 us
    pallas_call x1, Pallas kernels, per_device(): call(first_kernel, (shape_of(64, 64, 128), shape_of(8, 8, 128)))  2.35 us
    ppermute x3, starting transfers between devices, per_device(): lax.ppermute(payload, 'cam', [(i, i ^ d) for i in range(n_cam)])  2.27 us
    pallas_call x1, Pallas kernels, per_device(): call(part(render_far_kernel, n_cam), (shape_of(*flat), half(cameras, 64,...  2.04 us
    pallas_call x1, Pallas kernels, per_device(): call(face_kernel, (shape_of(2, 2, 64, 128, dtype=BF16), shape_of(*tables....  1.77 us
  transfers between devices with their start and end apart: 11, of which 5 were waited for; matrix products, arithmetic and copies ran while one was open for 0% of the time, Pallas kernels for 28%

profile of v7, /device:TPU:0, one launch (start us, length us, event | category | flops | bytes accessed | tf_op | source)
XLA Modules:
  0.0 37.0 jit_solution(18416343711747627459)
XLA Ops:
  0.6 0.0 copy-start
  0.6 0.0 copy-start.1
  0.6 0.0 copy-start.2
  0.7 1.8 %shard_map.86 = (bf16[2,2,64,128]{3,2,1,0:T(8,128)(2,1)S(1)}, bf16[1472,128]{1,0:T(8,128)(2,1)S(1)}) custom-call(f32[32,64,128]{2,1,0:T(8,128)} %bitcast.10, f32[3,32,64,128]{3,2,1,0:T(8,128)} %bitcast.4, f32[32,64,128]{2,1,0:T(8,128)} %bitcast.16, bf16[1472,128]{1,0:T(8,128)(2,1)} %constant.2.clone.table_hbm), custom_call_target="tpu_custom_call" | custom-call | flops 100000000 | bytes 10000000 | tf_op jit(solution)/shard_map/pallas_call | solution.py:843
  2.4 3.0 %collective-permute-start = (bf16[2,2,64,128]{3,2,1,0:T(8,128)(2,1)S(1)}, bf16[2,2,64,128]{3,2,1,0:T(8,128)(2,1)S(1)}, u32[]{:S(2)}, u32[]{:S(2)}) collective-permute-start(bf16[2,2,64,128]{3,2,1,0:T(8,128)(2,1)S(1)} %get-tuple-element.50), channel_id=1, source_target_pairs={{0,4},{4,0},{1,5},{5,1},{2,6},{6,2},{3,7},{7,3},{8,12},{12,8},{9,1... | collective-permute-start | bytes 196616 | tf_op jit(solution)/shard_map/ppermute | solution.py:820
  5.4 0.0 copy-done
  5.4 0.0 copy-done.1
  5.4 0.0 copy-done.2
  5.5 0.0 copy-start.5
  5.5 0.0 copy-start.3
  5.5 2.3 %shard_map.87 = (f32[64,64,128]{2,1,0:T(8,128)S(1)}, f32[8,8,128]{2,1,0:T(8,128)S(1)}) custom-call(f32[32,64,128]{2,1,0:T(8,128)S(1)} %bitcast.11, f32[3,32,64,128]{3,2,1,0:T(8,128)S(1)} %bitcast.5, f32[32,64,128]{2,1,0:T(8,128)S(1)} %bitcast.17, bf16[1472,128]{1,0:T(8,128)(2,1)S(1)} %get-tuple-element.47.table_ref), custom_call_target="tpu_custom_call" | custom-call | flops 100000000 | bytes 10000000 | tf_op jit(solution)/shard_map/pallas_call | solution.py:855
  7.8 0.0 copy-start.4
  7.8 0.0 collective-permute-done.x_in
  7.8 0.0 copy-done.5
  7.9 0.1 shard_map.88
  8.0 0.1 collective-permute-start.1
  8.0 2.0 %collective-permute-start.2 = (bf16[64,128]{1,0:T(8,128)(2,1)S(1)}, bf16[64,128]{1,0:T(8,128)(2,1)S(1)}, u32[]{:S(2)}, u32[]{:S(2)}) collective-permute-start(bf16[64,128]{1,0:T(8,128)(2,1)S(1)} %get-tuple-element.53), channel_id=1, source_target_pairs={{0,24},{8,16},{16,8},{24,0},{1,25},{9,17},{17,9},{25,1},{2,26},{10... | collective-permute-start | bytes 49160 | tf_op jit(solution)/shard_map/ppermute | solution.py:827
  10.0 0.0 copy-done.3
  10.0 1.3 %shard_map.89.weight_ref = bf16[512,1024]{1,0:T(8,128)(2,1)S(1)} custom-call(bf16[8,512,128]{2,1,0:T(8,128)(2,1)S(1)} %copy-done.3), custom_call_target="tpu_custom_call" | custom-call | flops 100000000 | bytes 10000000 | tf_op jit(solution)/shard_map/pallas_call | solution.py:858
  11.3 0.0 copy-done.4
  11.3 0.4 shard_map.90.pick_ref
  11.7 0.0 collective-permute-done.2.two_ref
  11.7 0.0 collective-permute-done.1.one_ref.got_ref.first_ref
  11.7 0.5 %shard_map.91 = (bf16[224,128]{1,0:T(8,128)(2,1)S(1)}, bf16[224,128]{1,0:T(8,128)(2,1)S(1)}, f32[8,8,128]{2,1,0:T(8,128)S(1)}) custom-call(f32[64,64,128]{2,1,0:T(8,128)S(1)} %get-tuple-element.48.s_ref, f32[2,2,64,128]{3,2,1,0:T(8,128)S(1)} %get-tuple-element.51.x_ref, bf16[80,128]{1,0:T(8,128)(2,1)S(1)} %collective-permute-done.1.one_ref.got_ref.first_ref, ...), custom_call_target="tpu_custom_call" | custom-call | flops 100000000 | bytes 10000000 | tf_op jit(solution)/shard_map/pallas_call | solution.py:868
  12.2 1.7 %collective-permute-start.3 = (bf16[224,128]{1,0:T(8,128)(2,1)S(1)}, bf16[224,128]{1,0:T(8,128)(2,1)S(1)}, u32[]{:S(2)}, u32[]{:S(2)}) collective-permute-start(bf16[224,128]{1,0:T(8,128)(2,1)S(1)} %get-tuple-element.57), channel_id=1, source_target_pairs={{0,1},{1,0},{2,3},{3,2},{4,5},{5,4},{6,7},{7,6},{8,9},{9,8},{10,11... | collective-permute-start | bytes 172040 | tf_op jit(solution)/shard_map/ppermute | solution.py:827
  13.8 2.5 %collective-permute-start.4 = (bf16[224,128]{1,0:T(8,128)(2,1)S(1)}, bf16[224,128]{1,0:T(8,128)(2,1)S(1)}, u32[]{:S(2)}, u32[]{:S(2)}) collective-permute-start(bf16[224,128]{1,0:T(8,128)(2,1)S(1)} %get-tuple-element.58), channel_id=1, source_target_pairs={{0,3},{1,2},{2,1},{3,0},{4,7},{5,6},{6,5},{7,4},{8,11},{9,10},{10,... | collective-permute-start | bytes 172040 | tf_op jit(solution)/shard_map/ppermute | solution.py:827
  16.3 2.6 %shard_map.92 = (f32[32,48,128]{2,1,0:T(8,128)S(1)}, f32[32,48,128]{2,1,0:T(8,128)S(1)}, f32[32,48,128]{2,1,0:T(8,128)S(1)}, f32[4,8,128]{2,1,0:T(8,128)S(1)}) custom-call(f32[64,64,128]{2,1,0:T(8,128)S(1)} %get-tuple-element.48.s_ref, f32[2,2,64,128]{3,2,1,0:T(8,128)S(1)} %get-tuple-element.51.x_ref, f32[8,8,128]{2,1,0:T(8,128)S(1)} %get-tuple-element.56.packed_ref, ...), custom_call_target="tpu_custom_call" | custom-call | flops 100000000 | bytes 10000000 | tf_op jit(solution)/shard_map/pallas_call | solution.py:872
  18.9 0.0 collective-permute-done.3.y_one_ref
  18.9 0.9 %collective-permute-done.4.y_two_ref = bf16[224,128]{1,0:T(8,128)(2,1)S(1)} collective-permute-done((bf16[224,128]{1,0:T(8,128)(2,1)S(1)}, bf16[224,128]{1,0:T(8,128)(2,1)S(1)}, u32[]{:S(2)}, u32[]{:S(2)}) %collective-permute-start.4) | collective-permute-done | bytes 57376 | tf_op jit(solution)/shard_map/ppermute | solution.py:827
  19.8 0.7 %shard_map.93 = (bf16[2,1,64,128]{3,2,1,0:T(8,128)(2,1)S(1)}, f32[16,16,128]{2,1,0:T(8,128)S(1)}, f32[16,16,128]{2,1,0:T(8,128)S(1)}, f32[16,16,128]{2,1,0:T(8,128)S(1)}, f32[2,8,128]{2,1,0:T(8,128)S(1)}) custom-call(f32[64,64,128]{2,1,0:T(8,128)S(1)} %get-tuple-element.48.s_ref, f32[2,2,64,128]{3,2,1,0:T(8,128)S(1)} %get-tuple-element.51.x_ref, ...), custom_call_target="tpu_custom_call" | custom-call | flops 100000000 | bytes 10000000 | tf_op jit(solution)/shard_map/pallas_call | solution.py:877
  20.5 1.6 %collective-permute-start.5 = (bf16[2,1,64,128]{3,2,1,0:T(8,128)(2,1)S(1)}, bf16[2,1,64,128]{3,2,1,0:T(8,128)(2,1)S(1)}, u32[]{:S(2)}, u32[]{:S(2)}) collective-permute-start(bf16[2,1,64,128]{3,2,1,0:T(8,128)(2,1)S(1)} %get-tuple-element.67), channel_id=1, source_target_pairs={{0,4},{4,0},{1,5},{5,1},{2,6},{6,2},{3,7},{7,3},{8,12},{12,8},{9,1... | collective-permute-start | bytes 98312 | tf_op jit(solution)/shard_map/ppermute | solution.py:820
  22.1 0.9 %shard_map.94 = (f32[32,64,128]{2,1,0:T(8,128)S(1)}, f32[32,16,128]{2,1,0:T(8,128)S(1)}, f32[32,16,128]{2,1,0:T(8,128)S(1)}, f32[4,8,128]{2,1,0:T(8,128)S(1)}) custom-call(f32[64,64,128]{2,1,0:T(8,128)S(1)} %get-tuple-element.48.s_ref, f32[2,2,64,128]{3,2,1,0:T(8,128)S(1)} %get-tuple-element.51.x_ref, f32[8,8,128]{2,1,0:T(8,128)S(1)} %get-tuple-element.56.packed_ref, ...), custom_call_target="tpu_custom_call" | custom-call | flops 100000000 | bytes 10000000 | tf_op jit(solution)/shard_map/pallas_call | solution.py:882
  23.0 0.8 %shard_map.95.early_ref = bf16[256,1024]{1,0:T(8,128)(2,1)S(1)} custom-call(f32[32,64,128]{2,1,0:T(8,128)S(1)} %get-tuple-element.65.g_ref, f32[32,48,128]{2,1,0:T(8,128)S(1)} %get-tuple-element.68.base_one, f32[32,48,128]{2,1,0:T(8,128)S(1)} %get-tuple-element.69.half_one, f32[32,16,128]{2,1,0:T(8,128)S(1)} %get-tuple-element.70.base_two, ...), custom_call_target="tpu_custom_call" | custom-call | flops 100000000 | bytes 10000000 | tf_op jit(solution)/shard_map/pallas_call | solution.py:890
  23.8 0.7 %collective-permute-done.5.x_in = bf16[2,1,64,128]{3,2,1,0:T(8,128)(2,1)S(1)} collective-permute-done((bf16[2,1,64,128]{3,2,1,0:T(8,128)(2,1)S(1)}, bf16[2,1,64,128]{3,2,1,0:T(8,128)(2,1)S(1)}, u32[]{:S(2)}, u32[]{:S(2)}) %collective-permute-start.5) | collective-permute-done | bytes 32800 | tf_op jit(solution)/shard_map/ppermute | solution.py:820
  24.5 0.1 shard_map.96
  24.6 0.1 collective-permute-start.7
  24.7 1.6 %collective-permute-start.6 = (bf16[32,128]{1,0:T(8,128)(2,1)S(1)}, bf16[32,128]{1,0:T(8,128)(2,1)S(1)}, u32[]{:S(2)}, u32[]{:S(2)}) collective-permute-start(bf16[32,128]{1,0:T(8,128)(2,1)S(1)} %get-tuple-element.75), channel_id=1, source_target_pairs={{0,8},{8,0},{16,24},{24,16},{1,9},{9,1},{17,25},{25,17},{2,10},{10... | collective-permute-start | bytes 24584 | tf_op jit(solution)/shard_map/ppermute | solution.py:827
  26.3 1.5 %shard_map.97.pixel_ref = f32[8,128,128]{2,1,0:T(8,128)S(1)} custom-call(f32[32,64,128]{2,1,0:T(8,128)S(1)} %get-tuple-element.65.g_ref, f32[2,1,64,128]{3,2,1,0:T(8,128)S(1)} %get-tuple-element.74.x_ref, f32[32,48,128]{2,1,0:T(8,128)S(1)} %get-tuple-element.68.base_one, f32[32,48,128]{2,1,0:T(8,128)S(1)} %get-tuple-element.69.half_one, ...), custom_call_target="tpu_custom_call" | custom-call | flops 100000000 | bytes 10000000 | tf_op jit(solution)/shard_map/pallas_call | solution.py:900
  27.8 0.0 collective-permute-done.6.one_ref
  27.8 0.2 collective-permute-done.7.two_ref.second_ref
  28.0 2.0 %shard_map.98 = (f32[32,64,128]{2,1,0:T(8,128)}, bf16[8,64,128]{2,1,0:T(8,128)(2,1)S(1)}, bf16[2,128,128]{2,1,0:T(8,128)(2,1)S(1)}, bf16[2,128,128]{2,1,0:T(8,128)(2,1)S(1)}) custom-call(f32[32,64,128]{2,1,0:T(8,128)S(1)} %get-tuple-element.65.g_ref, f32[2,1,64,128]{3,2,1,0:T(8,128)S(1)} %get-tuple-element.74.x_ref, ...), custom_call_target="tpu_custom_call" | custom-call | flops 100000000 | bytes 10000000 | tf_op jit(solution)/shard_map/pallas_call | solution.py:907
  30.0 1.4 %collective-permute-start.9 = (bf16[2,128,128]{2,1,0:T(8,128)(2,1)S(1)}, bf16[2,128,128]{2,1,0:T(8,128)(2,1)S(1)}, u32[]{:S(2)}, u32[]{:S(2)}) collective-permute-start(bf16[2,128,128]{2,1,0:T(8,128)(2,1)S(1)} %get-tuple-element.90), channel_id=1, source_target_pairs={{0,16},{8,24},{16,0},{24,8},{1,17},{9,25},{17,1},{25,9},{2,18},{10... | collective-permute-start | bytes 196616 | tf_op jit(solution)/shard_map/ppermute | solution.py:931
  31.4 0.1 collective-permute-start.10
  31.5 0.6 %shard_map.99 = (f32[2,1024,128]{2,1,0:T(8,128)S(1)}, bf16[2,1024,512]{2,1,0:T(8,128)(2,1)S(1)}) custom-call(bf16[8,64,128]{2,1,0:T(8,128)(2,1)S(1)} %get-tuple-element.87.value_ref, bf16[8,128,640]{2,1,0:T(8,128)(2,1)S(1)} %shard_map.90.pick_ref, f32[8,128,128]{2,1,0:T(8,128)S(1)} %shard_map.97.pixel_ref, s32[8,128]{1,0:T(8,128)S(1)} %copy-done.5, ...), custom_call_target="tpu_custom_call" | custom-call | flops 100000000 | bytes 10000000 | tf_op jit(solution)/shard_map/pallas_call | solution.py:919
  32.2 0.2 shard_map.100
  32.3 0.7 %collective-permute-start.8 = (bf16[2,128,128]{2,1,0:T(8,128)(2,1)S(1)}, bf16[2,128,128]{2,1,0:T(8,128)(2,1)S(1)}, u32[]{:S(2)}, u32[]{:S(2)}) collective-permute-start(bf16[2,128,128]{2,1,0:T(8,128)(2,1)S(1)} %shard_map.100), channel_id=1, source_target_pairs={{0,8},{8,0},{16,24},{24,16},{1,9},{9,1},{17,25},{25,17},{2,10},{10... | collective-permute-start | bytes 196616 | tf_op jit(solution)/shard_map/ppermute | solution.py:931
  33.1 1.3 %collective-permute-done.9.refs_1_ = bf16[2,128,128]{2,1,0:T(8,128)(2,1)S(1)} collective-permute-done((bf16[2,128,128]{2,1,0:T(8,128)(2,1)S(1)}, bf16[2,128,128]{2,1,0:T(8,128)(2,1)S(1)}, u32[]{:S(2)}, u32[]{:S(2)}) %collective-permute-start.9) | collective-permute-done | bytes 65568 | tf_op jit(solution)/shard_map/ppermute | solution.py:931
  34.3 1.4 %collective-permute-done.10.refs_2_ = bf16[2,128,128]{2,1,0:T(8,128)(2,1)S(1)} collective-permute-done((bf16[2,128,128]{2,1,0:T(8,128)(2,1)S(1)}, bf16[2,128,128]{2,1,0:T(8,128)(2,1)S(1)}, u32[]{:S(2)}, u32[]{:S(2)}) %collective-permute-start.10) | collective-permute-done | bytes 65568 | tf_op jit(solution)/shard_map/ppermute | solution.py:931
  35.7 0.0 collective-permute-done.8.refs_0_
  35.7 1.3 %shard_map.101 = f32[2,1024,128]{2,1,0:T(8,128)} custom-call(f32[2,1024,128]{2,1,0:T(8,128)S(1)} %get-tuple-element.85.own_ref, bf16[2,1024,512]{2,1,0:T(8,128)(2,1)S(1)} %get-tuple-element.86.onehot_ref, bf16[2,128,128]{2,1,0:T(8,128)(2,1)S(1)} %collective-permute-done.8.refs_0_, bf16[2,128,128]{2,1,0:T(8,128)(2,1)S(1)} %collective-permute-done.9.refs_1_, ...), custom_call_target="tpu_custom_call" | custom-call | flops 100000000 | bytes 10000000 | tf_op jit(solution)/shard_map/pallas_call | solution.py:932
Async XLA Ops:
  0.6 4.8 %copy-start = (f32[3,4,8,8,8,128]{5,4,3,2,1,0:T(8,128)S(1)}, f32[3,4,8,8,8,128]{5,4,3,2,1,0:T(8,128)}, u32[]{:S(2)}) copy-start(f32[3,4,8,8,8,128]{5,4,3,2,1,0:T(8,128)} %param.8) | copy-start | bytes 9437188
  0.6 4.8 %copy-start.1 = (f32[4,8,8,8,128]{4,3,2,1,0:T(8,128)S(1)}, f32[4,8,8,8,128]{4,3,2,1,0:T(8,128)}, u32[]{:S(2)}) copy-start(f32[4,8,8,8,128]{4,3,2,1,0:T(8,128)} %param.7) | copy-start | bytes 3145732
  0.6 4.8 %copy-start.2 = (f32[4,8,8,8,128]{4,3,2,1,0:T(8,128)S(1)}, f32[4,8,8,8,128]{4,3,2,1,0:T(8,128)}, u32[]{:S(2)}) copy-start(f32[4,8,8,8,128]{4,3,2,1,0:T(8,128)} %param.9) | copy-start | bytes 3145732
  2.4 5.4 %collective-permute-start = (bf16[2,2,64,128]{3,2,1,0:T(8,128)(2,1)S(1)}, bf16[2,2,64,128]{3,2,1,0:T(8,128)(2,1)S(1)}, u32[]{:S(2)}, u32[]{:S(2)}) collective-permute-start(bf16[2,2,64,128]{3,2,1,0:T(8,128)(2,1)S(1)} %get-tuple-element.50), channel_id=1, source_target_pairs={{0,4},{4,0},{1,5},{5,1},{2,6},{6,2},{3,7},{7,3},{8,12},{12,8},{9,1... | collective-permute-start | bytes 196616 | tf_op jit(solution)/shard_map/ppermute | solution.py:820
  5.5 2.4 %copy-start.5 = (s32[8,128]{1,0:T(8,128)S(1)}, s32[8,128]{1,0:T(8,128)}, u32[]{:S(2)}) copy-start(s32[8,128]{1,0:T(8,128)} %block_ref.5) | copy-start | bytes 12292
  5.5 4.6 %copy-start.3 = (bf16[8,512,128]{2,1,0:T(8,128)(2,1)S(1)}, bf16[8,512,128]{2,1,0:T(8,128)(2,1)}, u32[]{:S(2)}) copy-start(bf16[8,512,128]{2,1,0:T(8,128)(2,1)} %weight_ref.1) | copy-start | bytes 3145732
  7.8 3.5 %copy-start.4 = (s32[8,128]{1,0:T(8,128)S(1)}, s32[8,128]{1,0:T(8,128)}, u32[]{:S(2)}) copy-start(s32[8,128]{1,0:T(8,128)} %cut_ref.1) | copy-start | bytes 12292
  8.0 3.7 %collective-permute-start.1 = (bf16[80,128]{1,0:T(8,128)(2,1)S(1)}, bf16[80,128]{1,0:T(8,128)(2,1)S(1)}, u32[]{:S(2)}, u32[]{:S(2)}) collective-permute-start(bf16[80,128]{1,0:T(8,128)(2,1)S(1)} %get-tuple-element.52), channel_id=1, source_target_pairs={{0,8},{8,0},{16,24},{24,16},{1,9},{9,1},{17,25},{25,17},{2,10},{10... | collective-permute-start | bytes 61448 | tf_op jit(solution)/shard_map/ppermute | solution.py:827
  8.0 3.6 %collective-permute-start.2 = (bf16[64,128]{1,0:T(8,128)(2,1)S(1)}, bf16[64,128]{1,0:T(8,128)(2,1)S(1)}, u32[]{:S(2)}, u32[]{:S(2)}) collective-permute-start(bf16[64,128]{1,0:T(8,128)(2,1)S(1)} %get-tuple-element.53), channel_id=1, source_target_pairs={{0,24},{8,16},{16,8},{24,0},{1,25},{9,17},{17,9},{25,1},{2,26},{10... | collective-permute-start | bytes 49160 | tf_op jit(solution)/shard_map/ppermute | solution.py:827
  12.2 6.7 %collective-permute-start.3 = (bf16[224,128]{1,0:T(8,128)(2,1)S(1)}, bf16[224,128]{1,0:T(8,128)(2,1)S(1)}, u32[]{:S(2)}, u32[]{:S(2)}) collective-permute-start(bf16[224,128]{1,0:T(8,128)(2,1)S(1)} %get-tuple-element.57), channel_id=1, source_target_pairs={{0,1},{1,0},{2,3},{3,2},{4,5},{5,4},{6,7},{7,6},{8,9},{9,8},{10,11... | collective-permute-start | bytes 172040 | tf_op jit(solution)/shard_map/ppermute | solution.py:827
  13.8 6.0 %collective-permute-start.4 = (bf16[224,128]{1,0:T(8,128)(2,1)S(1)}, bf16[224,128]{1,0:T(8,128)(2,1)S(1)}, u32[]{:S(2)}, u32[]{:S(2)}) collective-permute-start(bf16[224,128]{1,0:T(8,128)(2,1)S(1)} %get-tuple-element.58), channel_id=1, source_target_pairs={{0,3},{1,2},{2,1},{3,0},{4,7},{5,6},{6,5},{7,4},{8,11},{9,10},{10,... | collective-permute-start | bytes 172040 | tf_op jit(solution)/shard_map/ppermute | solution.py:827
  20.5 4.0 %collective-permute-start.5 = (bf16[2,1,64,128]{3,2,1,0:T(8,128)(2,1)S(1)}, bf16[2,1,64,128]{3,2,1,0:T(8,128)(2,1)S(1)}, u32[]{:S(2)}, u32[]{:S(2)}) collective-permute-start(bf16[2,1,64,128]{3,2,1,0:T(8,128)(2,1)S(1)} %get-tuple-element.67), channel_id=1, source_target_pairs={{0,4},{4,0},{1,5},{5,1},{2,6},{6,2},{3,7},{7,3},{8,12},{12,8},{9,1... | collective-permute-start | bytes 98312 | tf_op jit(solution)/shard_map/ppermute | solution.py:820
  24.6 3.4 %collective-permute-start.7 = (bf16[64,128]{1,0:T(8,128)(2,1)S(1)}, bf16[64,128]{1,0:T(8,128)(2,1)S(1)}, u32[]{:S(2)}, u32[]{:S(2)}) collective-permute-start(bf16[64,128]{1,0:T(8,128)(2,1)S(1)} %get-tuple-element.76), channel_id=1, source_target_pairs={{0,24},{8,16},{16,8},{24,0},{1,25},{9,17},{17,9},{25,1},{2,26},{10... | collective-permute-start | bytes 49160 | tf_op jit(solution)/shard_map/ppermute | solution.py:827
  24.7 3.1 %collective-permute-start.6 = (bf16[32,128]{1,0:T(8,128)(2,1)S(1)}, bf16[32,128]{1,0:T(8,128)(2,1)S(1)}, u32[]{:S(2)}, u32[]{:S(2)}) collective-permute-start(bf16[32,128]{1,0:T(8,128)(2,1)S(1)} %get-tuple-element.75), channel_id=1, source_target_pairs={{0,8},{8,0},{16,24},{24,16},{1,9},{9,1},{17,25},{25,17},{2,10},{10... | collective-permute-start | bytes 24584 | tf_op jit(solution)/shard_map/ppermute | solution.py:827
  30.0 4.3 %collective-permute-start.9 = (bf16[2,128,128]{2,1,0:T(8,128)(2,1)S(1)}, bf16[2,128,128]{2,1,0:T(8,128)(2,1)S(1)}, u32[]{:S(2)}, u32[]{:S(2)}) collective-permute-start(bf16[2,128,128]{2,1,0:T(8,128)(2,1)S(1)} %get-tuple-element.90), channel_id=1, source_target_pairs={{0,16},{8,24},{16,0},{24,8},{1,17},{9,25},{17,1},{25,9},{2,18},{10... | collective-permute-start | bytes 196616 | tf_op jit(solution)/shard_map/ppermute | solution.py:931
  31.4 4.3 %collective-permute-start.10 = (bf16[2,128,128]{2,1,0:T(8,128)(2,1)S(1)}, bf16[2,128,128]{2,1,0:T(8,128)(2,1)S(1)}, u32[]{:S(2)}, u32[]{:S(2)}) collective-permute-start(bf16[2,128,128]{2,1,0:T(8,128)(2,1)S(1)} %get-tuple-element.91), channel_id=1, source_target_pairs={{0,24},{8,16},{16,8},{24,0},{1,25},{9,17},{17,9},{25,1},{2,26},{10... | collective-permute-start | bytes 196616 | tf_op jit(solution)/shard_map/ppermute | solution.py:931
  32.3 3.4 %collective-permute-start.8 = (bf16[2,128,128]{2,1,0:T(8,128)(2,1)S(1)}, bf16[2,128,128]{2,1,0:T(8,128)(2,1)S(1)}, u32[]{:S(2)}, u32[]{:S(2)}) collective-permute-start(bf16[2,128,128]{2,1,0:T(8,128)(2,1)S(1)} %shard_map.100), channel_id=1, source_target_pairs={{0,8},{8,0},{16,24},{24,16},{1,9},{9,1},{17,25},{25,17},{2,10},{10... | collective-permute-start | bytes 196616 | tf_op jit(solution)/shard_map/ppermute | solution.py:931

commit v8 on v7

--- a/solution.py
+++ b/solution.py
@@ -712,28 +712,33 @@
         payload_ref[n] = values.astype(BF16)
 
 
-def render_far_kernel(
-    cam_count, g_ref, x_ref, one_ref, two_ref, base_one, half_one, base_two, half_two,
-    table_ref, weight_ref, pick_ref, pixel_ref, out_hbm, value_ref, *rest,
-):
-    payload_refs = rest[: cam_count - 2]
-    advected_ref, end_ref, sem = rest[cam_count - 2 :]
+def final_layers(cam_count, g_ref, x_ref, one_ref, two_ref, terms, use):
+    base_one, half_one, base_two, half_two = terms
     bases, halfs = (base_one, base_two), (half_one, half_two)
     one, two = one_ref[:32, :].astype(F32), two_ref[:32, :].astype(F32)
     for a in range(4):
         packed = merged(one[8 * a : 8 * a + 8], two[8 * a : 8 * a + 8], cam_count)
-        for n, pair in enumerate(PAIRS):
-            blocks = advanced(g_ref, x_ref, packed, bases, halfs, a, pair)
-            turned = turn(blocks, end_table(table_ref))
-            for h, b in enumerate(pair):
-                advected_ref[span_of(a), 8 * b : 8 * b + 8, :] = blocks[h].reshape(8, 8, 128)
-                place = 16 * a + 2 * b
-                for k in range(4):
-                    end_ref[place : place + 2, 128 * k : 128 * k + 128] = turned[
-                        2 * k : 2 * k + 2, 128 * h : 128 * h + 128
-                    ]
-    copy = pltpu.make_async_copy(advected_ref, out_hbm, sem)
-    copy.start()
+        for pair in PAIRS:
+            use(a, pair, advanced(g_ref, x_ref, packed, bases, halfs, a, pair))
+
+
+def render_far_kernel(
+    cam_count, g_ref, x_ref, one_ref, two_ref, base_one, half_one, base_two, half_two,
+    table_ref, weight_ref, pick_ref, pixel_ref, value_ref, *rest,
+):
+    payload_refs, end_ref = rest[:-1], rest[-1]
+
+    def use(a, pair, blocks):
+        turned = turn(blocks, end_table(table_ref))
+        for h, b in enumerate(pair):
+            place = 16 * a + 2 * b
+            for k in range(4):
+                end_ref[place : place + 2, 128 * k : 128 * k + 128] = turned[
+                    2 * k : 2 * k + 2, 128 * h : 128 * h + 128
+                ]
+
+    terms = (base_one, half_one, base_two, half_two)
+    final_layers(cam_count, g_ref, x_ref, one_ref, two_ref, terms, use)
     ends = end_ref[...].astype(BF16)
     for m in range(pixel_ref.shape[0] // 2):
         values = dot(ends, weight_ref[:, 256 * m : 256 * m + 256]).astype(BF16)
@@ -741,7 +746,27 @@
         value_ref[2 * m + 1] = values[:, 128:]
     for d in range(2, cam_count):
         fill_payload(payload_refs[d - 2], d, cam_count, pick_ref, value_ref, pixel_ref)
-    copy.wait()
+
+
+def advected_kernel(
+    cam_count, g_ref, x_ref, one_ref, two_ref, base_one, half_one, base_two, half_two,
+    out_hbm, advected_ref, sems,
+):
+    copies = []
+
+    def use(a, pair, blocks):
+        for h, b in enumerate(pair):
+            advected_ref[span_of(a), 8 * b : 8 * b + 8, :] = blocks[h].reshape(8, 8, 128)
+        if pair == PAIRS[-1]:
+            at = span_of(a)
+            copy = pltpu.make_async_copy(advected_ref.at[at], out_hbm.at[at], sems.at[a])
+            copy.start()
+            copies.append(copy)
+
+    terms = (base_one, half_one, base_two, half_two)
+    final_layers(cam_count, g_ref, x_ref, one_ref, two_ref, terms, use)
+    for copy in copies:
+        copy.wait()
 
 
 def render_near_kernel(cam_count, d, value_ref, pick_ref, pixel_ref, payload_ref):
@@ -904,15 +929,10 @@
     )(g, x_got, *terms, near, weights, picks, early)
     z_got, pixels = lax.optimization_barrier((z_got, pixels))
     payload_shape = half(share, 128, 128)
-    advected, values, *far = call(
+    values, *far = call(
         part(render_far_kernel, n_cam),
-        (shape_of(*flat), half(cameras, 64, 128)) + (payload_shape,) * (n_cam - 2),
-        out_specs=(HBM, VMEM) + (VMEM,) * (n_cam - 2),
-        scratch_shapes=[
-            pltpu.VMEM(flat, F32),
-            pltpu.VMEM((64, 512), F32),
-            pltpu.SemaphoreType.DMA,
-        ],
+        (half(cameras, 64, 128),) + (payload_shape,) * (n_cam - 2),
+        scratch_shapes=[pltpu.VMEM((64, 512), F32)],
     )(g, x_got, *z_got, *terms, near, weights, picks, pixels)
     parts = (values, picks, pixels)
     image_shape = shape_of(share, NBLK, 128)
@@ -926,6 +946,15 @@
     )(*parts, pixel_block, ids_got, z_got[1])
     images, parts = lax.optimization_barrier((images, parts))
     beside = call(part(render_near_kernel, n_cam, 1), payload_shape)(*parts)
+    final = (g, x_got, *z_got, *terms)
+    final, beside = lax.optimization_barrier((final, beside))
+    advected = call(
+        part(advected_kernel, n_cam),
+        shape_of(*flat),
+        out_specs=HBM,
+        scratch_shapes=[pltpu.VMEM(flat, F32), pltpu.SemaphoreType.DMA((4,))],
+    )(*final)
+    images, advected = lax.optimization_barrier((images, advected))
     received = []
     for d, payload in [(1, beside)] + [(n + 2, p) for n, p in enumerate(far)]:
         received.append(lax.ppermute(payload, "cam", [(i, i ^ d) for i in range(n_cam)]))

time: 37.2 us -> 36.4 us (0.978)
  waiting for transfers between devices: 4.51 us -> 3.28 us
  Pallas kernels: 17 us -> 17.4 us
    ppermute x3, waiting for transfers between devices: 2.69 us -> 1.45 us  [per_device(): lax.ppermute(payload, 'cam', [(i, i ^ d) for i in range(n_cam)])]
    pallas_call x1 -> x2, Pallas kernels: 2.04 us -> 2.45 us  [the longest x1 1.23 us: per_device(): call(part(advected_kernel, n_cam), shape_of(*flat), out_specs=HBM, scratc...]
  transfers between devices with their start and end apart: 11 -> 11, of which waited for: 5 -> 4; matrix products, arithmetic and copies ran while one was open for 0% -> 0% of each run, Pallas kernels for 28% -> 32%
where the time goes in v8:
time: 36.4 us; the launch traced here: 36.2 us
  Pallas kernels  17.4 us (48%)
  starting transfers between devices  14.7 us (40%)
  waiting for transfers between devices  3.28 us (9%)
  between operations  0.85 us (2%)
    ppermute x6, starting transfers between devices, swap_both(): return (lax.ppermute(one, axis, even), lax.ppermute(two, axis, odd))  7.85 us
    ppermute x2, starting transfers between devices, swap_axial(): return lax.ppermute(x, 'ex', up)  4.56 us
    pallas_call x1, Pallas kernels, per_device(): call(second_inner_kernel, (shape_of(*inner),) * 3 + (shape_of(4, 8, 128),))  2.6 us
    pallas_call x1, Pallas kernels, per_device(): call(first_kernel, (shape_of(64, 64, 128), shape_of(8, 8, 128)))  2.35 us
    ppermute x3, starting transfers between devices, per_device(): lax.ppermute(payload, 'cam', [(i, i ^ d) for i in range(n_cam)])  2.27 us
    pallas_call x1, Pallas kernels, per_device(): call(face_kernel, (shape_of(2, 2, 64, 128, dtype=BF16), shape_of(*tables....  1.77 us
    pallas_call x1, Pallas kernels, per_device(): call(middle_kernel, shape_of(cameras, 128, 128), scratch_shapes=[pltpu.VM...  1.49 us
    ppermute x3, waiting for transfers between devices, per_device(): lax.ppermute(payload, 'cam', [(i, i ^ d) for i in range(n_cam)])  1.45 us
  transfers between devices with their start and end apart: 11, of which 4 were waited for; matrix products, arithmetic and copies ran while one was open for 0% of the time, Pallas kernels for 32%

profile of v8, /device:TPU:0, one launch (start us, length us, event | category | flops | bytes accessed | tf_op | source)
XLA Modules:
  0.0 36.2 jit_solution(3650005977315230341)
XLA Ops:
  0.6 0.0 copy-start
  0.6 0.0 copy-start.1
  0.6 0.0 copy-start.2
  0.7 1.8 %shard_map.86 = (bf16[2,2,64,128]{3,2,1,0:T(8,128)(2,1)S(1)}, bf16[1472,128]{1,0:T(8,128)(2,1)S(1)}) custom-call(f32[32,64,128]{2,1,0:T(8,128)} %bitcast.10, f32[3,32,64,128]{3,2,1,0:T(8,128)} %bitcast.4, f32[32,64,128]{2,1,0:T(8,128)} %bitcast.16, bf16[1472,128]{1,0:T(8,128)(2,1)} %constant.2.clone.table_hbm), custom_call_target="tpu_custom_call" | custom-call | flops 100000000 | bytes 10000000 | tf_op jit(solution)/shard_map/pallas_call | solution.py:868
  2.4 3.0 %collective-permute-start = (bf16[2,2,64,128]{3,2,1,0:T(8,128)(2,1)S(1)}, bf16[2,2,64,128]{3,2,1,0:T(8,128)(2,1)S(1)}, u32[]{:S(2)}, u32[]{:S(2)}) collective-permute-start(bf16[2,2,64,128]{3,2,1,0:T(8,128)(2,1)S(1)} %get-tuple-element.60), channel_id=1, source_target_pairs={{0,4},{4,0},{1,5},{5,1},{2,6},{6,2},{3,7},{7,3},{8,12},{12,8},{9,1... | collective-permute-start | bytes 196616 | tf_op jit(solution)/shard_map/ppermute | solution.py:845
  5.4 0.0 copy-done
  5.4 0.0 copy-done.1
  5.4 0.0 copy-done.2
  5.5 0.0 copy-start.5
  5.5 0.0 copy-start.3
  5.5 2.3 %shard_map.87 = (f32[64,64,128]{2,1,0:T(8,128)S(1)}, f32[8,8,128]{2,1,0:T(8,128)S(1)}) custom-call(f32[32,64,128]{2,1,0:T(8,128)S(1)} %bitcast.11, f32[3,32,64,128]{3,2,1,0:T(8,128)S(1)} %bitcast.5, f32[32,64,128]{2,1,0:T(8,128)S(1)} %bitcast.17, bf16[1472,128]{1,0:T(8,128)(2,1)S(1)} %get-tuple-element.57.table_ref), custom_call_target="tpu_custom_call" | custom-call | flops 100000000 | bytes 10000000 | tf_op jit(solution)/shard_map/pallas_call | solution.py:880
  7.8 0.0 copy-start.4
  7.8 0.0 collective-permute-done.x_in
  7.9 0.0 copy-done.5
  7.9 0.1 shard_map.88
  8.0 0.1 collective-permute-start.1
  8.0 2.0 %collective-permute-start.2 = (bf16[64,128]{1,0:T(8,128)(2,1)S(1)}, bf16[64,128]{1,0:T(8,128)(2,1)S(1)}, u32[]{:S(2)}, u32[]{:S(2)}) collective-permute-start(bf16[64,128]{1,0:T(8,128)(2,1)S(1)} %get-tuple-element.63), channel_id=1, source_target_pairs={{0,24},{8,16},{16,8},{24,0},{1,25},{9,17},{17,9},{25,1},{2,26},{10... | collective-permute-start | bytes 49160 | tf_op jit(solution)/shard_map/ppermute | solution.py:852
  10.0 0.0 copy-done.3
  10.0 1.3 %shard_map.89.weight_ref = bf16[512,1024]{1,0:T(8,128)(2,1)S(1)} custom-call(bf16[8,512,128]{2,1,0:T(8,128)(2,1)S(1)} %copy-done.3), custom_call_target="tpu_custom_call" | custom-call | flops 100000000 | bytes 10000000 | tf_op jit(solution)/shard_map/pallas_call | solution.py:883
  11.3 0.0 copy-done.4
  11.3 0.4 %shard_map.90.pick_ref = bf16[8,128,640]{2,1,0:T(8,128)(2,1)S(1)} custom-call(s32[8,128]{1,0:T(8,128)S(1)} %copy-done.4), custom_call_target="tpu_custom_call" | custom-call | flops 100000000 | bytes 10000000 | tf_op jit(solution)/shard_map/pallas_call | solution.py:884
  11.7 0.0 collective-permute-done.2.two_ref
  11.7 0.0 collective-permute-done.1.one_ref.got_ref.first_ref
  11.7 0.5 %shard_map.91 = (bf16[224,128]{1,0:T(8,128)(2,1)S(1)}, bf16[224,128]{1,0:T(8,128)(2,1)S(1)}, f32[8,8,128]{2,1,0:T(8,128)S(1)}) custom-call(f32[64,64,128]{2,1,0:T(8,128)S(1)} %get-tuple-element.58.s_ref, f32[2,2,64,128]{3,2,1,0:T(8,128)S(1)} %get-tuple-element.61.x_ref, bf16[80,128]{1,0:T(8,128)(2,1)S(1)} %collective-permute-done.1.one_ref.got_ref.first_ref, ...), custom_call_target="tpu_custom_call" | custom-call | flops 100000000 | bytes 10000000 | tf_op jit(solution)/shard_map/pallas_call | solution.py:893
  12.2 1.7 %collective-permute-start.3 = (bf16[224,128]{1,0:T(8,128)(2,1)S(1)}, bf16[224,128]{1,0:T(8,128)(2,1)S(1)}, u32[]{:S(2)}, u32[]{:S(2)}) collective-permute-start(bf16[224,128]{1,0:T(8,128)(2,1)S(1)} %get-tuple-element.67), channel_id=1, source_target_pairs={{0,1},{1,0},{2,3},{3,2},{4,5},{5,4},{6,7},{7,6},{8,9},{9,8},{10,11... | collective-permute-start | bytes 172040 | tf_op jit(solution)/shard_map/ppermute | solution.py:852
  13.8 2.5 %collective-permute-start.4 = (bf16[224,128]{1,0:T(8,128)(2,1)S(1)}, bf16[224,128]{1,0:T(8,128)(2,1)S(1)}, u32[]{:S(2)}, u32[]{:S(2)}) collective-permute-start(bf16[224,128]{1,0:T(8,128)(2,1)S(1)} %get-tuple-element.68), channel_id=1, source_target_pairs={{0,3},{1,2},{2,1},{3,0},{4,7},{5,6},{6,5},{7,4},{8,11},{9,10},{10,... | collective-permute-start | bytes 172040 | tf_op jit(solution)/shard_map/ppermute | solution.py:852
  16.3 2.6 %shard_map.92 = (f32[32,48,128]{2,1,0:T(8,128)S(1)}, f32[32,48,128]{2,1,0:T(8,128)S(1)}, f32[32,48,128]{2,1,0:T(8,128)S(1)}, f32[4,8,128]{2,1,0:T(8,128)S(1)}) custom-call(f32[64,64,128]{2,1,0:T(8,128)S(1)} %get-tuple-element.58.s_ref, f32[2,2,64,128]{3,2,1,0:T(8,128)S(1)} %get-tuple-element.61.x_ref, f32[8,8,128]{2,1,0:T(8,128)S(1)} %get-tuple-element.66.packed_ref, ...), custom_call_target="tpu_custom_call" | custom-call | flops 100000000 | bytes 10000000 | tf_op jit(solution)/shard_map/pallas_call | solution.py:897
  18.9 0.0 collective-permute-done.3.y_one_ref
  18.9 0.9 %collective-permute-done.4.y_two_ref = bf16[224,128]{1,0:T(8,128)(2,1)S(1)} collective-permute-done((bf16[224,128]{1,0:T(8,128)(2,1)S(1)}, bf16[224,128]{1,0:T(8,128)(2,1)S(1)}, u32[]{:S(2)}, u32[]{:S(2)}) %collective-permute-start.4) | collective-permute-done | bytes 57376 | tf_op jit(solution)/shard_map/ppermute | solution.py:852
  19.8 0.7 %shard_map.93 = (bf16[2,1,64,128]{3,2,1,0:T(8,128)(2,1)S(1)}, f32[16,16,128]{2,1,0:T(8,128)S(1)}, f32[16,16,128]{2,1,0:T(8,128)S(1)}, f32[16,16,128]{2,1,0:T(8,128)S(1)}, f32[2,8,128]{2,1,0:T(8,128)S(1)}) custom-call(f32[64,64,128]{2,1,0:T(8,128)S(1)} %get-tuple-element.58.s_ref, f32[2,2,64,128]{3,2,1,0:T(8,128)S(1)} %get-tuple-element.61.x_ref, ...), custom_call_target="tpu_custom_call" | custom-call | flops 100000000 | bytes 10000000 | tf_op jit(solution)/shard_map/pallas_call | solution.py:902
  20.5 1.6 %collective-permute-start.5 = (bf16[2,1,64,128]{3,2,1,0:T(8,128)(2,1)S(1)}, bf16[2,1,64,128]{3,2,1,0:T(8,128)(2,1)S(1)}, u32[]{:S(2)}, u32[]{:S(2)}) collective-permute-start(bf16[2,1,64,128]{3,2,1,0:T(8,128)(2,1)S(1)} %get-tuple-element.77), channel_id=1, source_target_pairs={{0,4},{4,0},{1,5},{5,1},{2,6},{6,2},{3,7},{7,3},{8,12},{12,8},{9,1... | collective-permute-start | bytes 98312 | tf_op jit(solution)/shard_map/ppermute | solution.py:845
  22.1 0.9 %shard_map.94 = (f32[32,64,128]{2,1,0:T(8,128)S(1)}, f32[32,16,128]{2,1,0:T(8,128)S(1)}, f32[32,16,128]{2,1,0:T(8,128)S(1)}, f32[4,8,128]{2,1,0:T(8,128)S(1)}) custom-call(f32[64,64,128]{2,1,0:T(8,128)S(1)} %get-tuple-element.58.s_ref, f32[2,2,64,128]{3,2,1,0:T(8,128)S(1)} %get-tuple-element.61.x_ref, f32[8,8,128]{2,1,0:T(8,128)S(1)} %get-tuple-element.66.packed_ref, ...), custom_call_target="tpu_custom_call" | custom-call | flops 100000000 | bytes 10000000 | tf_op jit(solution)/shard_map/pallas_call | solution.py:907
  23.0 0.8 %shard_map.95.early_ref = bf16[256,1024]{1,0:T(8,128)(2,1)S(1)} custom-call(f32[32,64,128]{2,1,0:T(8,128)S(1)} %get-tuple-element.98.g_ref, f32[32,48,128]{2,1,0:T(8,128)S(1)} %get-tuple-element.102.base_one, f32[32,48,128]{2,1,0:T(8,128)S(1)} %get-tuple-element.103.half_one, f32[32,16,128]{2,1,0:T(8,128)S(1)} %get-tuple-element.104.base_two, ...), custom_call_target="tpu_custom_call" | custom-call | flops 100000000 | bytes 10000000 | tf_op jit(solution)/shard_map/pallas_call | solution.py:915
  23.8 0.7 %collective-permute-done.5.x_in = bf16[2,1,64,128]{3,2,1,0:T(8,128)(2,1)S(1)} collective-permute-done((bf16[2,1,64,128]{3,2,1,0:T(8,128)(2,1)S(1)}, bf16[2,1,64,128]{3,2,1,0:T(8,128)(2,1)S(1)}, u32[]{:S(2)}, u32[]{:S(2)}) %collective-permute-start.5) | collective-permute-done | bytes 32800 | tf_op jit(solution)/shard_map/ppermute | solution.py:845
  24.5 0.1 shard_map.96
  24.6 0.1 collective-permute-start.7
  24.7 1.6 %collective-permute-start.6 = (bf16[32,128]{1,0:T(8,128)(2,1)S(1)}, bf16[32,128]{1,0:T(8,128)(2,1)S(1)}, u32[]{:S(2)}, u32[]{:S(2)}) collective-permute-start(bf16[32,128]{1,0:T(8,128)(2,1)S(1)} %get-tuple-element.85), channel_id=1, source_target_pairs={{0,8},{8,0},{16,24},{24,16},{1,9},{9,1},{17,25},{25,17},{2,10},{10... | collective-permute-start | bytes 24584 | tf_op jit(solution)/shard_map/ppermute | solution.py:852
  26.3 1.5 %shard_map.97.pixel_ref = f32[8,128,128]{2,1,0:T(8,128)S(1)} custom-call(f32[32,64,128]{2,1,0:T(8,128)S(1)} %get-tuple-element.98.g_ref, f32[2,1,64,128]{3,2,1,0:T(8,128)S(1)} %get-tuple-element.99.x_ref, f32[32,48,128]{2,1,0:T(8,128)S(1)} %get-tuple-element.102.base_one, f32[32,48,128]{2,1,0:T(8,128)S(1)} %get-tuple-element.103.half_one, ...), custom_call_target="tpu_custom_call" | custom-call | flops 100000000 | bytes 10000000 | tf_op jit(solution)/shard_map/pallas_call | solution.py:925
  27.8 0.0 collective-permute-done.6.one_ref
  27.8 0.2 collective-permute-done.7.two_ref.second_ref
  28.0 1.2 %shard_map.98 = (bf16[8,64,128]{2,1,0:T(8,128)(2,1)S(1)}, bf16[2,128,128]{2,1,0:T(8,128)(2,1)S(1)}, bf16[2,128,128]{2,1,0:T(8,128)(2,1)S(1)}) custom-call(f32[32,64,128]{2,1,0:T(8,128)S(1)} %get-tuple-element.98.g_ref, f32[2,1,64,128]{3,2,1,0:T(8,128)S(1)} %get-tuple-element.99.x_ref, bf16[32,128]{1,0:T(8,128)(2,1)S(1)} %collective-permute-done.6.one_ref, ...), custom_call_target="tpu_custom_call" | custom-call | flops 100000000 | bytes 10000000 | tf_op jit(solution)/shard_map/pallas_call | solution.py:932
  29.2 1.4 %collective-permute-start.9 = (bf16[2,128,128]{2,1,0:T(8,128)(2,1)S(1)}, bf16[2,128,128]{2,1,0:T(8,128)(2,1)S(1)}, u32[]{:S(2)}, u32[]{:S(2)}) collective-permute-start(bf16[2,128,128]{2,1,0:T(8,128)(2,1)S(1)} %get-tuple-element.110), channel_id=1, source_target_pairs={{0,16},{8,24},{16,0},{24,8},{1,17},{9,25},{17,1},{25,9},{2,18},{10... | collective-permute-start | bytes 196616 | tf_op jit(solution)/shard_map/ppermute | solution.py:960
  30.6 0.1 collective-permute-start.10
  30.7 0.6 %shard_map.99 = (f32[2,1024,128]{2,1,0:T(8,128)S(1)}, bf16[2,1024,512]{2,1,0:T(8,128)(2,1)S(1)}) custom-call(bf16[8,64,128]{2,1,0:T(8,128)(2,1)S(1)} %get-tuple-element.95.value_ref, bf16[8,128,640]{2,1,0:T(8,128)(2,1)S(1)} %shard_map.90.pick_ref, f32[8,128,128]{2,1,0:T(8,128)S(1)} %shard_map.97.pixel_ref, s32[8,128]{1,0:T(8,128)S(1)} %copy-done.5, ...), custom_call_target="tpu_custom_call" | custom-call | flops 100000000 | bytes 10000000 | tf_op jit(solution)/shard_map/pallas_call | solution.py:939
  31.3 0.2 shard_map.100
  31.5 0.7 %collective-permute-start.8 = (bf16[2,128,128]{2,1,0:T(8,128)(2,1)S(1)}, bf16[2,128,128]{2,1,0:T(8,128)(2,1)S(1)}, u32[]{:S(2)}, u32[]{:S(2)}) collective-permute-start(bf16[2,128,128]{2,1,0:T(8,128)(2,1)S(1)} %shard_map.100), channel_id=1, source_target_pairs={{0,8},{8,0},{16,24},{24,16},{1,9},{9,1},{17,25},{25,17},{2,10},{10... | collective-permute-start | bytes 196616 | tf_op jit(solution)/shard_map/ppermute | solution.py:960
  32.2 1.2 %shard_map.101 = f32[32,64,128]{2,1,0:T(8,128)} custom-call(f32[32,64,128]{2,1,0:T(8,128)S(1)} %get-tuple-element.98.g_ref, f32[2,1,64,128]{3,2,1,0:T(8,128)S(1)} %get-tuple-element.99.x_ref, bf16[32,128]{1,0:T(8,128)(2,1)S(1)} %collective-permute-done.6.one_ref, bf16[64,128]{1,0:T(8,128)(2,1)S(1)} %collective-permute-done.7.two_ref.second_ref, ...), custom_call_target="tpu_custom_call" | custom-call | flops 100000000 | bytes 10000000 | tf_op jit(solution)/shard_map/pallas_call | solution.py:951
  33.5 0.0 collective-permute-done.9.refs_1_
  33.5 1.4 %collective-permute-done.10.refs_2_ = bf16[2,128,128]{2,1,0:T(8,128)(2,1)S(1)} collective-permute-done((bf16[2,128,128]{2,1,0:T(8,128)(2,1)S(1)}, bf16[2,128,128]{2,1,0:T(8,128)(2,1)S(1)}, u32[]{:S(2)}, u32[]{:S(2)}) %collective-permute-start.10) | collective-permute-done | bytes 65568 | tf_op jit(solution)/shard_map/ppermute | solution.py:960
  34.9 0.0 collective-permute-done.8.refs_0_
  34.9 1.3 %shard_map.102 = f32[2,1024,128]{2,1,0:T(8,128)} custom-call(f32[2,1024,128]{2,1,0:T(8,128)S(1)} %get-tuple-element.107.own_ref, bf16[2,1024,512]{2,1,0:T(8,128)(2,1)S(1)} %get-tuple-element.108.onehot_ref, bf16[2,128,128]{2,1,0:T(8,128)(2,1)S(1)} %collective-permute-done.8.refs_0_, bf16[2,128,128]{2,1,0:T(8,128)(2,1)S(1)} %collective-permute-done.9.refs_1_, ...), custom_call_target="tpu_custom_call" | custom-call | flops 100000000 | bytes 10000000 | tf_op jit(solution)/shard_map/pallas_call | solution.py:961
Async XLA Ops:
  0.6 4.8 %copy-start = (f32[3,4,8,8,8,128]{5,4,3,2,1,0:T(8,128)S(1)}, f32[3,4,8,8,8,128]{5,4,3,2,1,0:T(8,128)}, u32[]{:S(2)}) copy-start(f32[3,4,8,8,8,128]{5,4,3,2,1,0:T(8,128)} %param.8) | copy-start | bytes 9437188
  0.6 4.8 %copy-start.1 = (f32[4,8,8,8,128]{4,3,2,1,0:T(8,128)S(1)}, f32[4,8,8,8,128]{4,3,2,1,0:T(8,128)}, u32[]{:S(2)}) copy-start(f32[4,8,8,8,128]{4,3,2,1,0:T(8,128)} %param.7) | copy-start | bytes 3145732
  0.6 4.8 %copy-start.2 = (f32[4,8,8,8,128]{4,3,2,1,0:T(8,128)S(1)}, f32[4,8,8,8,128]{4,3,2,1,0:T(8,128)}, u32[]{:S(2)}) copy-start(f32[4,8,8,8,128]{4,3,2,1,0:T(8,128)} %param.9) | copy-start | bytes 3145732
  2.4 5.4 %collective-permute-start = (bf16[2,2,64,128]{3,2,1,0:T(8,128)(2,1)S(1)}, bf16[2,2,64,128]{3,2,1,0:T(8,128)(2,1)S(1)}, u32[]{:S(2)}, u32[]{:S(2)}) collective-permute-start(bf16[2,2,64,128]{3,2,1,0:T(8,128)(2,1)S(1)} %get-tuple-element.60), channel_id=1, source_target_pairs={{0,4},{4,0},{1,5},{5,1},{2,6},{6,2},{3,7},{7,3},{8,12},{12,8},{9,1... | collective-permute-start | bytes 196616 | tf_op jit(solution)/shard_map/ppermute | solution.py:845
  5.5 2.4 %copy-start.5 = (s32[8,128]{1,0:T(8,128)S(1)}, s32[8,128]{1,0:T(8,128)}, u32[]{:S(2)}) copy-start(s32[8,128]{1,0:T(8,128)} %block_ref.5) | copy-start | bytes 12292
  5.5 4.6 %copy-start.3 = (bf16[8,512,128]{2,1,0:T(8,128)(2,1)S(1)}, bf16[8,512,128]{2,1,0:T(8,128)(2,1)}, u32[]{:S(2)}) copy-start(bf16[8,512,128]{2,1,0:T(8,128)(2,1)} %weight_ref.1) | copy-start | bytes 3145732
  7.8 3.5 %copy-start.4 = (s32[8,128]{1,0:T(8,128)S(1)}, s32[8,128]{1,0:T(8,128)}, u32[]{:S(2)}) copy-start(s32[8,128]{1,0:T(8,128)} %cut_ref.1) | copy-start | bytes 12292
  8.0 3.7 %collective-permute-start.1 = (bf16[80,128]{1,0:T(8,128)(2,1)S(1)}, bf16[80,128]{1,0:T(8,128)(2,1)S(1)}, u32[]{:S(2)}, u32[]{:S(2)}) collective-permute-start(bf16[80,128]{1,0:T(8,128)(2,1)S(1)} %get-tuple-element.62), channel_id=1, source_target_pairs={{0,8},{8,0},{16,24},{24,16},{1,9},{9,1},{17,25},{25,17},{2,10},{10... | collective-permute-start | bytes 61448 | tf_op jit(solution)/shard_map/ppermute | solution.py:852
  8.0 3.6 %collective-permute-start.2 = (bf16[64,128]{1,0:T(8,128)(2,1)S(1)}, bf16[64,128]{1,0:T(8,128)(2,1)S(1)}, u32[]{:S(2)}, u32[]{:S(2)}) collective-permute-start(bf16[64,128]{1,0:T(8,128)(2,1)S(1)} %get-tuple-element.63), channel_id=1, source_target_pairs={{0,24},{8,16},{16,8},{24,0},{1,25},{9,17},{17,9},{25,1},{2,26},{10... | collective-permute-start | bytes 49160 | tf_op jit(solution)/shard_map/ppermute | solution.py:852
  12.2 6.7 %collective-permute-start.3 = (bf16[224,128]{1,0:T(8,128)(2,1)S(1)}, bf16[224,128]{1,0:T(8,128)(2,1)S(1)}, u32[]{:S(2)}, u32[]{:S(2)}) collective-permute-start(bf16[224,128]{1,0:T(8,128)(2,1)S(1)} %get-tuple-element.67), channel_id=1, source_target_pairs={{0,1},{1,0},{2,3},{3,2},{4,5},{5,4},{6,7},{7,6},{8,9},{9,8},{10,11... | collective-permute-start | bytes 172040 | tf_op jit(solution)/shard_map/ppermute | solution.py:852
  13.8 6.0 %collective-permute-start.4 = (bf16[224,128]{1,0:T(8,128)(2,1)S(1)}, bf16[224,128]{1,0:T(8,128)(2,1)S(1)}, u32[]{:S(2)}, u32[]{:S(2)}) collective-permute-start(bf16[224,128]{1,0:T(8,128)(2,1)S(1)} %get-tuple-element.68), channel_id=1, source_target_pairs={{0,3},{1,2},{2,1},{3,0},{4,7},{5,6},{6,5},{7,4},{8,11},{9,10},{10,... | collective-permute-start | bytes 172040 | tf_op jit(solution)/shard_map/ppermute | solution.py:852
  20.5 4.0 %collective-permute-start.5 = (bf16[2,1,64,128]{3,2,1,0:T(8,128)(2,1)S(1)}, bf16[2,1,64,128]{3,2,1,0:T(8,128)(2,1)S(1)}, u32[]{:S(2)}, u32[]{:S(2)}) collective-permute-start(bf16[2,1,64,128]{3,2,1,0:T(8,128)(2,1)S(1)} %get-tuple-element.77), channel_id=1, source_target_pairs={{0,4},{4,0},{1,5},{5,1},{2,6},{6,2},{3,7},{7,3},{8,12},{12,8},{9,1... | collective-permute-start | bytes 98312 | tf_op jit(solution)/shard_map/ppermute | solution.py:845
  24.6 3.4 %collective-permute-start.7 = (bf16[64,128]{1,0:T(8,128)(2,1)S(1)}, bf16[64,128]{1,0:T(8,128)(2,1)S(1)}, u32[]{:S(2)}, u32[]{:S(2)}) collective-permute-start(bf16[64,128]{1,0:T(8,128)(2,1)S(1)} %get-tuple-element.86), channel_id=1, source_target_pairs={{0,24},{8,16},{16,8},{24,0},{1,25},{9,17},{17,9},{25,1},{2,26},{10... | collective-permute-start | bytes 49160 | tf_op jit(solution)/shard_map/ppermute | solution.py:852
  24.7 3.1 %collective-permute-start.6 = (bf16[32,128]{1,0:T(8,128)(2,1)S(1)}, bf16[32,128]{1,0:T(8,128)(2,1)S(1)}, u32[]{:S(2)}, u32[]{:S(2)}) collective-permute-start(bf16[32,128]{1,0:T(8,128)(2,1)S(1)} %get-tuple-element.85), channel_id=1, source_target_pairs={{0,8},{8,0},{16,24},{24,16},{1,9},{9,1},{17,25},{25,17},{2,10},{10... | collective-permute-start | bytes 24584 | tf_op jit(solution)/shard_map/ppermute | solution.py:852
  29.2 4.3 %collective-permute-start.9 = (bf16[2,128,128]{2,1,0:T(8,128)(2,1)S(1)}, bf16[2,128,128]{2,1,0:T(8,128)(2,1)S(1)}, u32[]{:S(2)}, u32[]{:S(2)}) collective-permute-start(bf16[2,128,128]{2,1,0:T(8,128)(2,1)S(1)} %get-tuple-element.110), channel_id=1, source_target_pairs={{0,16},{8,24},{16,0},{24,8},{1,17},{9,25},{17,1},{25,9},{2,18},{10... | collective-permute-start | bytes 196616 | tf_op jit(solution)/shard_map/ppermute | solution.py:960
  30.6 4.3 %collective-permute-start.10 = (bf16[2,128,128]{2,1,0:T(8,128)(2,1)S(1)}, bf16[2,128,128]{2,1,0:T(8,128)(2,1)S(1)}, u32[]{:S(2)}, u32[]{:S(2)}) collective-permute-start(bf16[2,128,128]{2,1,0:T(8,128)(2,1)S(1)} %get-tuple-element.111), channel_id=1, source_target_pairs={{0,24},{8,16},{16,8},{24,0},{1,25},{9,17},{17,9},{25,1},{2,26},{10... | collective-permute-start | bytes 196616 | tf_op jit(solution)/shard_map/ppermute | solution.py:960
  31.5 3.4 %collective-permute-start.8 = (bf16[2,128,128]{2,1,0:T(8,128)(2,1)S(1)}, bf16[2,128,128]{2,1,0:T(8,128)(2,1)S(1)}, u32[]{:S(2)}, u32[]{:S(2)}) collective-permute-start(bf16[2,128,128]{2,1,0:T(8,128)(2,1)S(1)} %shard_map.100), channel_id=1, source_target_pairs={{0,8},{8,0},{16,24},{24,16},{1,9},{9,1},{17,25},{25,17},{2,10},{10... | collective-permute-start | bytes 196616 | tf_op jit(solution)/shard_map/ppermute | solution.py:960

commit v9 on v8

--- a/solution.py
+++ b/solution.py
@@ -680,12 +680,17 @@
 
 
 def early_kernel(
-    g_ref, base_one, half_one, base_two, half_two, table_ref, weight_ref, value_ref, element_ref
+    g_ref, base_one, half_one, base_two, half_two, table_ref, weight_ref, pick_ref,
+    pixel_ref, element_ref,
 ):
     bases, halfs = (base_one, base_two), (half_one, half_two)
     layer_elements((1, 2), g_ref, None, bases, halfs, table_ref, element_ref)
     for m in range(4):
-        value_ref[:, 256 * m : 256 * m + 256] = pixel_values(element_ref, weight_ref, m)
+        values = pixel_values(element_ref, weight_ref, m)
+        for n in range(2):
+            pixel_ref[2 * m + n] = dot(
+                pick_ref[2 * m + n, :, :256], values[:, 128 * n : 128 * n + 128]
+            )
 
 
 def middle_kernel(
@@ -695,21 +700,23 @@
     bases, halfs = (base_one, base_two), (half_one, half_two)
     layer_elements((0, 3), g_ref, x_ref, bases, halfs, table_ref, element_ref)
     for m in range(4):
-        late = pixel_values(element_ref, weight_ref, m)
-        both = jnp.concatenate([early_ref[:, 256 * m : 256 * m + 256], late], axis=0)
+        values = pixel_values(element_ref, weight_ref, m)
         for n in range(2):
-            pixel_ref[2 * m + n] = dot(
-                pick_ref[2 * m + n, :, :512], both[:, 128 * n : 128 * n + 128]
+            pixel_ref[2 * m + n] = early_ref[2 * m + n] + dot(
+                pick_ref[2 * m + n, :, 256:512], values[:, 128 * n : 128 * n + 128]
             )
 
 
-def fill_payload(payload_ref, d, cam_count, pick_ref, value_ref, pixel_ref):
-    me = lax.axis_index("cam")
+def fill_payload(payload_ref, d, cam_count, ends, weight_ref, pick_ref, pixel_ref):
+    owner = lax.axis_index("cam") ^ d
     share = pixel_ref.shape[0] // cam_count
+    width = 128 * share
+    block = weight_ref[:, pl.ds(pl.multiple_of(owner * width, 128), width)]
+    values = dot(ends, block).astype(BF16)
     for n in range(share):
-        m = share * (me ^ d) + n
-        values = dot(pick_ref[m, :, 512:576], value_ref[m]) + pixel_ref[m]
-        payload_ref[n] = values.astype(BF16)
+        m = share * owner + n
+        picked = dot(pick_ref[m, :, 512:576], values[:, 128 * n : 128 * n + 128])
+        payload_ref[n] = (picked + pixel_ref[m]).astype(BF16)
 
 
 def final_layers(cam_count, g_ref, x_ref, one_ref, two_ref, terms, use):
@@ -724,7 +731,7 @@
 
 def render_far_kernel(
     cam_count, g_ref, x_ref, one_ref, two_ref, base_one, half_one, base_two, half_two,
-    table_ref, weight_ref, pick_ref, pixel_ref, value_ref, *rest,
+    table_ref, weight_ref, pick_ref, pixel_ref, out_ref, *rest,
 ):
     payload_refs, end_ref = rest[:-1], rest[-1]
 
@@ -740,12 +747,9 @@
     terms = (base_one, half_one, base_two, half_two)
     final_layers(cam_count, g_ref, x_ref, one_ref, two_ref, terms, use)
     ends = end_ref[...].astype(BF16)
-    for m in range(pixel_ref.shape[0] // 2):
-        values = dot(ends, weight_ref[:, 256 * m : 256 * m + 256]).astype(BF16)
-        value_ref[2 * m] = values[:, :128]
-        value_ref[2 * m + 1] = values[:, 128:]
+    out_ref[...] = ends
     for d in range(2, cam_count):
-        fill_payload(payload_refs[d - 2], d, cam_count, pick_ref, value_ref, pixel_ref)
+        fill_payload(payload_refs[d - 2], d, cam_count, ends, weight_ref, pick_ref, pixel_ref)
 
 
 def advected_kernel(
@@ -769,12 +773,12 @@
         copy.wait()
 
 
-def render_near_kernel(cam_count, d, value_ref, pick_ref, pixel_ref, payload_ref):
-    fill_payload(payload_ref, d, cam_count, pick_ref, value_ref, pixel_ref)
+def render_near_kernel(cam_count, d, end_ref, weight_ref, pick_ref, pixel_ref, payload_ref):
+    fill_payload(payload_ref, d, cam_count, end_ref[...], weight_ref, pick_ref, pixel_ref)
 
 
 def own_image_kernel(
-    cam_count, value_ref, pick_ref, pixel_ref, block_ref, first_ref, second_ref,
+    cam_count, end_ref, weight_ref, pick_ref, pixel_ref, block_ref, first_ref, second_ref,
     image_ref, onehot_ref, payload_ref, id_ref,
 ):
     me = lax.axis_index("cam")
@@ -784,7 +788,7 @@
     for d, tile in tiles:
         ids = tile.astype(F32).astype(jnp.int32)
         id_ref[d] = ids[:8] * 32 + ids[8:]
-    fill_payload(payload_ref, 0, cam_count, pick_ref, value_ref, pixel_ref)
+    fill_payload(payload_ref, 0, cam_count, end_ref[...], weight_ref, pick_ref, pixel_ref)
     for m in range(share):
         ids = [id_ref[d, pl.ds(share * me + m, 1), :] for d in range(4)]
         ids = jnp.concatenate(ids, axis=1)
@@ -914,9 +918,9 @@
     x_got = swap_axial(x)
     early = call(
         early_kernel,
-        shape_of(256, 128 * cameras, dtype=BF16),
+        shape_of(cameras, 128, 128),
         scratch_shapes=[pltpu.VMEM((256, 512), BF16)],
-    )(g, *terms, near, weights)
+    )(g, *terms, near, weights, picks)
     x_got, early = lax.optimization_barrier((x_got, early))
     *z, x_got = call(
         second_radial_kernel, (half(32, 128), half(64, 128), shape_of(2, 1, 64, 128))
@@ -929,12 +933,12 @@
     )(g, x_got, *terms, near, weights, picks, early)
     z_got, pixels = lax.optimization_barrier((z_got, pixels))
     payload_shape = half(share, 128, 128)
-    values, *far = call(
+    ends, *far = call(
         part(render_far_kernel, n_cam),
-        (half(cameras, 64, 128),) + (payload_shape,) * (n_cam - 2),
+        (half(64, 512),) + (payload_shape,) * (n_cam - 2),
         scratch_shapes=[pltpu.VMEM((64, 512), F32)],
     )(g, x_got, *z_got, *terms, near, weights, picks, pixels)
-    parts = (values, picks, pixels)
+    parts = (ends, weights, picks, pixels)
     image_shape = shape_of(share, NBLK, 128)
     images, onehot = call(
         part(own_image_kernel, n_cam),

time: 36.4 us -> 36.6 us (level)
  Pallas kernels: 17.4 us -> 18.8 us
  waiting for transfers between devices: 3.28 us -> 2.02 us
    pallas_call x2, Pallas kernels: 2.01 us -> 2.93 us  [the longest x1 1.6 us: per_device(): call(early_kernel, shape_of(cameras, 128, 128), scratch_shapes=[pltpu.VME...]
    ppermute x2, waiting for transfers between devices: 0.73 us -> 0.01 us  [swap_axial(): return lax.ppermute(x, 'ex', up)]
    ppermute x3, waiting for transfers between devices: 1.45 us -> 1.02 us  [per_device(): lax.ppermute(payload, 'cam', [(i, i ^ d) for i in range(n_cam)])]
  transfers between devices with their start and end apart: 11 -> 11, of which waited for: 4 -> 3; matrix products, arithmetic and copies ran while one was open for 0% -> 0% of each run, Pallas kernels for 32% -> 36%
where the time goes in v9:
time: 36.6 us; the launch traced here: 36.4 us
  Pallas kernels  18.8 us (51%)
  starting transfers between devices  14.7 us (40%)
  waiting for transfers between devices  2.02 us (6%)
  between operations  0.87 us (2%)
    ppermute x6, starting transfers between devices, swap_both(): return (lax.ppermute(one, axis, even), lax.ppermute(two, axis, odd))  7.85 us
    ppermute x2, starting transfers between devices, swap_axial(): return lax.ppermute(x, 'ex', up)  4.56 us
    pallas_call x1, Pallas kernels, per_device(): call(second_inner_kernel, (shape_of(*inner),) * 3 + (shape_of(4, 8, 128),))  2.59 us
    pallas_call x1, Pallas kernels, per_device(): call(first_kernel, (shape_of(64, 64, 128), shape_of(8, 8, 128)))  2.35 us
    ppermute x3, starting transfers between devices, per_device(): lax.ppermute(payload, 'cam', [(i, i ^ d) for i in range(n_cam)])  2.28 us
    pallas_call x1, Pallas kernels, per_device(): call(face_kernel, (shape_of(2, 2, 64, 128, dtype=BF16), shape_of(*tables....  1.77 us
    pallas_call x1, Pallas kernels, per_device(): call(early_kernel, shape_of(cameras, 128, 128), scratch_shapes=[pltpu.VME...  1.6 us
    pallas_call x1, Pallas kernels, per_device(): call(middle_kernel, shape_of(cameras, 128, 128), scratch_shapes=[pltpu.VM...  1.6 us
  transfers between devices with their start and end apart: 11, of which 3 were waited for; matrix products, arithmetic and copies ran while one was open for 0% of the time, Pallas kernels for 36%

profile of v9, /device:TPU:0, one launch (start us, length us, event | category | flops | bytes accessed | tf_op | source)
XLA Modules:
  0.0 36.4 jit_solution(13505823818438231209)
XLA Ops:
  0.6 0.0 copy-start
  0.6 0.0 copy-start.1
  0.6 0.0 copy-start.2
  0.7 1.8 %shard_map.86 = (bf16[2,2,64,128]{3,2,1,0:T(8,128)(2,1)S(1)}, bf16[1472,128]{1,0:T(8,128)(2,1)S(1)}) custom-call(f32[32,64,128]{2,1,0:T(8,128)} %bitcast.10, f32[3,32,64,128]{3,2,1,0:T(8,128)} %bitcast.4, f32[32,64,128]{2,1,0:T(8,128)} %bitcast.16, bf16[1472,128]{1,0:T(8,128)(2,1)} %constant.2.clone.table_hbm), custom_call_target="tpu_custom_call" | custom-call | flops 100000000 | bytes 10000000 | tf_op jit(solution)/shard_map/pallas_call | solution.py:872
  2.4 3.0 %collective-permute-start = (bf16[2,2,64,128]{3,2,1,0:T(8,128)(2,1)S(1)}, bf16[2,2,64,128]{3,2,1,0:T(8,128)(2,1)S(1)}, u32[]{:S(2)}, u32[]{:S(2)}) collective-permute-start(bf16[2,2,64,128]{3,2,1,0:T(8,128)(2,1)S(1)} %get-tuple-element.61), channel_id=1, source_target_pairs={{0,4},{4,0},{1,5},{5,1},{2,6},{6,2},{3,7},{7,3},{8,12},{12,8},{9,1... | collective-permute-start | bytes 196616 | tf_op jit(solution)/shard_map/ppermute | solution.py:849
  5.4 0.0 copy-done
  5.4 0.0 copy-done.1
  5.4 0.0 copy-done.2
  5.5 0.0 copy-start.5
  5.5 0.0 copy-start.3
  5.5 2.3 %shard_map.87 = (f32[64,64,128]{2,1,0:T(8,128)S(1)}, f32[8,8,128]{2,1,0:T(8,128)S(1)}) custom-call(f32[32,64,128]{2,1,0:T(8,128)S(1)} %bitcast.11, f32[3,32,64,128]{3,2,1,0:T(8,128)S(1)} %bitcast.5, f32[32,64,128]{2,1,0:T(8,128)S(1)} %bitcast.17, bf16[1472,128]{1,0:T(8,128)(2,1)S(1)} %get-tuple-element.58.table_ref), custom_call_target="tpu_custom_call" | custom-call | flops 100000000 | bytes 10000000 | tf_op jit(solution)/shard_map/pallas_call | solution.py:884
  7.8 0.0 copy-start.4
  7.8 0.0 collective-permute-done.x_in
  7.8 0.0 copy-done.5
  7.9 0.1 shard_map.88
  8.0 0.1 collective-permute-start.1
  8.0 2.0 %collective-permute-start.2 = (bf16[64,128]{1,0:T(8,128)(2,1)S(1)}, bf16[64,128]{1,0:T(8,128)(2,1)S(1)}, u32[]{:S(2)}, u32[]{:S(2)}) collective-permute-start(bf16[64,128]{1,0:T(8,128)(2,1)S(1)} %get-tuple-element.64), channel_id=1, source_target_pairs={{0,24},{8,16},{16,8},{24,0},{1,25},{9,17},{17,9},{25,1},{2,26},{10... | collective-permute-start | bytes 49160 | tf_op jit(solution)/shard_map/ppermute | solution.py:856
  10.0 0.0 copy-done.3
  10.0 1.3 %shard_map.89.weight_ref = bf16[512,1024]{1,0:T(8,128)(2,1)S(1)} custom-call(bf16[8,512,128]{2,1,0:T(8,128)(2,1)S(1)} %copy-done.3), custom_call_target="tpu_custom_call" | custom-call | flops 100000000 | bytes 10000000 | tf_op jit(solution)/shard_map/pallas_call | solution.py:887
  11.3 0.0 copy-done.4
  11.3 0.4 shard_map.90.pick_ref
  11.7 0.0 collective-permute-done.2.two_ref
  11.7 0.0 collective-permute-done.1.one_ref.got_ref.first_ref
  11.7 0.4 %shard_map.91 = (bf16[224,128]{1,0:T(8,128)(2,1)S(1)}, bf16[224,128]{1,0:T(8,128)(2,1)S(1)}, f32[8,8,128]{2,1,0:T(8,128)S(1)}) custom-call(f32[64,64,128]{2,1,0:T(8,128)S(1)} %get-tuple-element.59.s_ref, f32[2,2,64,128]{3,2,1,0:T(8,128)S(1)} %get-tuple-element.62.x_ref, bf16[80,128]{1,0:T(8,128)(2,1)S(1)} %collective-permute-done.1.one_ref.got_ref.first_ref, ...), custom_call_target="tpu_custom_call" | custom-call | flops 100000000 | bytes 10000000 | tf_op jit(solution)/shard_map/pallas_call | solution.py:897
  12.2 1.7 %collective-permute-start.3 = (bf16[224,128]{1,0:T(8,128)(2,1)S(1)}, bf16[224,128]{1,0:T(8,128)(2,1)S(1)}, u32[]{:S(2)}, u32[]{:S(2)}) collective-permute-start(bf16[224,128]{1,0:T(8,128)(2,1)S(1)} %get-tuple-element.68), channel_id=1, source_target_pairs={{0,1},{1,0},{2,3},{3,2},{4,5},{5,4},{6,7},{7,6},{8,9},{9,8},{10,11... | collective-permute-start | bytes 172040 | tf_op jit(solution)/shard_map/ppermute | solution.py:856
  13.8 2.5 %collective-permute-start.4 = (bf16[224,128]{1,0:T(8,128)(2,1)S(1)}, bf16[224,128]{1,0:T(8,128)(2,1)S(1)}, u32[]{:S(2)}, u32[]{:S(2)}) collective-permute-start(bf16[224,128]{1,0:T(8,128)(2,1)S(1)} %get-tuple-element.69), channel_id=1, source_target_pairs={{0,3},{1,2},{2,1},{3,0},{4,7},{5,6},{6,5},{7,4},{8,11},{9,10},{10,... | collective-permute-start | bytes 172040 | tf_op jit(solution)/shard_map/ppermute | solution.py:856
  16.3 2.6 %shard_map.92 = (f32[32,48,128]{2,1,0:T(8,128)S(1)}, f32[32,48,128]{2,1,0:T(8,128)S(1)}, f32[32,48,128]{2,1,0:T(8,128)S(1)}, f32[4,8,128]{2,1,0:T(8,128)S(1)}) custom-call(f32[64,64,128]{2,1,0:T(8,128)S(1)} %get-tuple-element.59.s_ref, f32[2,2,64,128]{3,2,1,0:T(8,128)S(1)} %get-tuple-element.62.x_ref, f32[8,8,128]{2,1,0:T(8,128)S(1)} %get-tuple-element.67.packed_ref, ...), custom_call_target="tpu_custom_call" | custom-call | flops 100000000 | bytes 10000000 | tf_op jit(solution)/shard_map/pallas_call | solution.py:901
  18.9 0.0 collective-permute-done.3.y_one_ref
  18.9 0.9 %collective-permute-done.4.y_two_ref = bf16[224,128]{1,0:T(8,128)(2,1)S(1)} collective-permute-done((bf16[224,128]{1,0:T(8,128)(2,1)S(1)}, bf16[224,128]{1,0:T(8,128)(2,1)S(1)}, u32[]{:S(2)}, u32[]{:S(2)}) %collective-permute-start.4) | collective-permute-done | bytes 57376 | tf_op jit(solution)/shard_map/ppermute | solution.py:856
  19.8 0.7 %shard_map.93 = (bf16[2,1,64,128]{3,2,1,0:T(8,128)(2,1)S(1)}, f32[16,16,128]{2,1,0:T(8,128)S(1)}, f32[16,16,128]{2,1,0:T(8,128)S(1)}, f32[16,16,128]{2,1,0:T(8,128)S(1)}, f32[2,8,128]{2,1,0:T(8,128)S(1)}) custom-call(f32[64,64,128]{2,1,0:T(8,128)S(1)} %get-tuple-element.59.s_ref, f32[2,2,64,128]{3,2,1,0:T(8,128)S(1)} %get-tuple-element.62.x_ref, ...), custom_call_target="tpu_custom_call" | custom-call | flops 100000000 | bytes 10000000 | tf_op jit(solution)/shard_map/pallas_call | solution.py:906
  20.5 1.6 %collective-permute-start.5 = (bf16[2,1,64,128]{3,2,1,0:T(8,128)(2,1)S(1)}, bf16[2,1,64,128]{3,2,1,0:T(8,128)(2,1)S(1)}, u32[]{:S(2)}, u32[]{:S(2)}) collective-permute-start(bf16[2,1,64,128]{3,2,1,0:T(8,128)(2,1)S(1)} %get-tuple-element.78), channel_id=1, source_target_pairs={{0,4},{4,0},{1,5},{5,1},{2,6},{6,2},{3,7},{7,3},{8,12},{12,8},{9,1... | collective-permute-start | bytes 98312 | tf_op jit(solution)/shard_map/ppermute | solution.py:849
  22.1 0.9 %shard_map.94 = (f32[32,64,128]{2,1,0:T(8,128)S(1)}, f32[32,16,128]{2,1,0:T(8,128)S(1)}, f32[32,16,128]{2,1,0:T(8,128)S(1)}, f32[4,8,128]{2,1,0:T(8,128)S(1)}) custom-call(f32[64,64,128]{2,1,0:T(8,128)S(1)} %get-tuple-element.59.s_ref, f32[2,2,64,128]{3,2,1,0:T(8,128)S(1)} %get-tuple-element.62.x_ref, f32[8,8,128]{2,1,0:T(8,128)S(1)} %get-tuple-element.67.packed_ref, ...), custom_call_target="tpu_custom_call" | custom-call | flops 100000000 | bytes 10000000 | tf_op jit(solution)/shard_map/pallas_call | solution.py:911
  23.0 1.6 %shard_map.95.early_ref = f32[8,128,128]{2,1,0:T(8,128)S(1)} custom-call(f32[32,64,128]{2,1,0:T(8,128)S(1)} %get-tuple-element.100.g_ref, f32[32,48,128]{2,1,0:T(8,128)S(1)} %get-tuple-element.104.base_one, f32[32,48,128]{2,1,0:T(8,128)S(1)} %get-tuple-element.105.half_one, f32[32,16,128]{2,1,0:T(8,128)S(1)} %get-tuple-element.106.base_two, ...), custom_call_target="tpu_custom_call" | custom-call | flops 100000000 | bytes 10000000 | tf_op jit(solution)/shard_map/pallas_call | solution.py:919
  24.6 0.0 collective-permute-done.5.x_in
  24.6 0.1 shard_map.96
  24.7 0.1 collective-permute-start.7
  24.8 1.6 %collective-permute-start.6 = (bf16[32,128]{1,0:T(8,128)(2,1)S(1)}, bf16[32,128]{1,0:T(8,128)(2,1)S(1)}, u32[]{:S(2)}, u32[]{:S(2)}) collective-permute-start(bf16[32,128]{1,0:T(8,128)(2,1)S(1)} %get-tuple-element.87), channel_id=1, source_target_pairs={{0,8},{8,0},{16,24},{24,16},{1,9},{9,1},{17,25},{25,17},{2,10},{10... | collective-permute-start | bytes 24584 | tf_op jit(solution)/shard_map/ppermute | solution.py:856
  26.4 1.6 %shard_map.97.pixel_ref = f32[8,128,128]{2,1,0:T(8,128)S(1)} custom-call(f32[32,64,128]{2,1,0:T(8,128)S(1)} %get-tuple-element.100.g_ref, f32[2,1,64,128]{3,2,1,0:T(8,128)S(1)} %get-tuple-element.101.x_ref, f32[32,48,128]{2,1,0:T(8,128)S(1)} %get-tuple-element.104.base_one, f32[32,48,128]{2,1,0:T(8,128)S(1)} %get-tuple-element.105.half_one, ...), custom_call_target="tpu_custom_call" | custom-call | flops 100000000 | bytes 10000000 | tf_op jit(solution)/shard_map/pallas_call | solution.py:929
  28.0 0.0 collective-permute-done.6.one_ref
  28.0 0.1 collective-permute-done.7.two_ref.second_ref
  28.1 1.3 %shard_map.98 = (bf16[64,512]{1,0:T(8,128)(2,1)S(1)}, bf16[2,128,128]{2,1,0:T(8,128)(2,1)S(1)}, bf16[2,128,128]{2,1,0:T(8,128)(2,1)S(1)}) custom-call(f32[32,64,128]{2,1,0:T(8,128)S(1)} %get-tuple-element.100.g_ref, f32[2,1,64,128]{3,2,1,0:T(8,128)S(1)} %get-tuple-element.101.x_ref, bf16[32,128]{1,0:T(8,128)(2,1)S(1)} %collective-permute-done.6.one_ref, ...), custom_call_target="tpu_custom_call" | custom-call | flops 100000000 | bytes 10000000 | tf_op jit(solution)/shard_map/pallas_call | solution.py:936
  29.4 1.4 %collective-permute-start.9 = (bf16[2,128,128]{2,1,0:T(8,128)(2,1)S(1)}, bf16[2,128,128]{2,1,0:T(8,128)(2,1)S(1)}, u32[]{:S(2)}, u32[]{:S(2)}) collective-permute-start(bf16[2,128,128]{2,1,0:T(8,128)(2,1)S(1)} %get-tuple-element.112), channel_id=1, source_target_pairs={{0,16},{8,24},{16,0},{24,8},{1,17},{9,25},{17,1},{25,9},{2,18},{10... | collective-permute-start | bytes 196616 | tf_op jit(solution)/shard_map/ppermute | solution.py:964
  30.8 0.1 collective-permute-start.10
  30.9 0.8 %shard_map.99 = (f32[2,1024,128]{2,1,0:T(8,128)S(1)}, bf16[2,1024,512]{2,1,0:T(8,128)(2,1)S(1)}) custom-call(bf16[64,512]{1,0:T(8,128)(2,1)S(1)} %get-tuple-element.96.end_ref, bf16[512,1024]{1,0:T(8,128)(2,1)S(1)} %shard_map.89.weight_ref, bf16[8,128,640]{2,1,0:T(8,128)(2,1)S(1)} %shard_map.90.pick_ref, f32[8,128,128]{2,1,0:T(8,128)S(1)} %shard_map.97.pixel_ref, ...), custom_call_target="tpu_custom_call" | custom-call | flops 100000000 | bytes 10000000 | tf_op jit(solution)/shard_map/pallas_call | solution.py:943
  31.8 0.4 %shard_map.100 = bf16[2,128,128]{2,1,0:T(8,128)(2,1)S(1)} custom-call(bf16[64,512]{1,0:T(8,128)(2,1)S(1)} %get-tuple-element.96.end_ref, bf16[512,1024]{1,0:T(8,128)(2,1)S(1)} %shard_map.89.weight_ref, bf16[8,128,640]{2,1,0:T(8,128)(2,1)S(1)} %shard_map.90.pick_ref, f32[8,128,128]{2,1,0:T(8,128)S(1)} %shard_map.97.pixel_ref), custom_call_target="tpu_custom_call" | custom-call | flops 100000000 | bytes 10000000 | tf_op jit(solution)/shard_map/pallas_call | solution.py:952
  32.1 0.7 %collective-permute-start.8 = (bf16[2,128,128]{2,1,0:T(8,128)(2,1)S(1)}, bf16[2,128,128]{2,1,0:T(8,128)(2,1)S(1)}, u32[]{:S(2)}, u32[]{:S(2)}) collective-permute-start(bf16[2,128,128]{2,1,0:T(8,128)(2,1)S(1)} %shard_map.100), channel_id=1, source_target_pairs={{0,8},{8,0},{16,24},{24,16},{1,9},{9,1},{17,25},{25,17},{2,10},{10... | collective-permute-start | bytes 196616 | tf_op jit(solution)/shard_map/ppermute | solution.py:964
  32.9 1.2 %shard_map.101 = f32[32,64,128]{2,1,0:T(8,128)} custom-call(f32[32,64,128]{2,1,0:T(8,128)S(1)} %get-tuple-element.100.g_ref, f32[2,1,64,128]{3,2,1,0:T(8,128)S(1)} %get-tuple-element.101.x_ref, bf16[32,128]{1,0:T(8,128)(2,1)S(1)} %collective-permute-done.6.one_ref, bf16[64,128]{1,0:T(8,128)(2,1)S(1)} %collective-permute-done.7.two_ref.second_ref, ...), custom_call_target="tpu_custom_call" | custom-call | flops 100000000 | bytes 10000000 | tf_op jit(solution)/shard_map/pallas_call | solution.py:955
  34.1 0.0 collective-permute-done.9.refs_1_
  34.1 1.0 %collective-permute-done.10.refs_2_ = bf16[2,128,128]{2,1,0:T(8,128)(2,1)S(1)} collective-permute-done((bf16[2,128,128]{2,1,0:T(8,128)(2,1)S(1)}, bf16[2,128,128]{2,1,0:T(8,128)(2,1)S(1)}, u32[]{:S(2)}, u32[]{:S(2)}) %collective-permute-start.10) | collective-permute-done | bytes 65568 | tf_op jit(solution)/shard_map/ppermute | solution.py:964
  35.1 0.0 collective-permute-done.8.refs_0_
  35.1 1.3 %shard_map.102 = f32[2,1024,128]{2,1,0:T(8,128)} custom-call(f32[2,1024,128]{2,1,0:T(8,128)S(1)} %get-tuple-element.109.own_ref, bf16[2,1024,512]{2,1,0:T(8,128)(2,1)S(1)} %get-tuple-element.110.onehot_ref, bf16[2,128,128]{2,1,0:T(8,128)(2,1)S(1)} %collective-permute-done.8.refs_0_, bf16[2,128,128]{2,1,0:T(8,128)(2,1)S(1)} %collective-permute-done.9.refs_1_, ...), custom_call_target="tpu_custom_call" | custom-call | flops 100000000 | bytes 10000000 | tf_op jit(solution)/shard_map/pallas_call | solution.py:965
Async XLA Ops:
  0.6 4.8 %copy-start = (f32[3,4,8,8,8,128]{5,4,3,2,1,0:T(8,128)S(1)}, f32[3,4,8,8,8,128]{5,4,3,2,1,0:T(8,128)}, u32[]{:S(2)}) copy-start(f32[3,4,8,8,8,128]{5,4,3,2,1,0:T(8,128)} %param.8) | copy-start | bytes 9437188
  0.6 4.8 %copy-start.1 = (f32[4,8,8,8,128]{4,3,2,1,0:T(8,128)S(1)}, f32[4,8,8,8,128]{4,3,2,1,0:T(8,128)}, u32[]{:S(2)}) copy-start(f32[4,8,8,8,128]{4,3,2,1,0:T(8,128)} %param.7) | copy-start | bytes 3145732
  0.6 4.8 %copy-start.2 = (f32[4,8,8,8,128]{4,3,2,1,0:T(8,128)S(1)}, f32[4,8,8,8,128]{4,3,2,1,0:T(8,128)}, u32[]{:S(2)}) copy-start(f32[4,8,8,8,128]{4,3,2,1,0:T(8,128)} %param.9) | copy-start | bytes 3145732
  2.4 5.4 %collective-permute-start = (bf16[2,2,64,128]{3,2,1,0:T(8,128)(2,1)S(1)}, bf16[2,2,64,128]{3,2,1,0:T(8,128)(2,1)S(1)}, u32[]{:S(2)}, u32[]{:S(2)}) collective-permute-start(bf16[2,2,64,128]{3,2,1,0:T(8,128)(2,1)S(1)} %get-tuple-element.61), channel_id=1, source_target_pairs={{0,4},{4,0},{1,5},{5,1},{2,6},{6,2},{3,7},{7,3},{8,12},{12,8},{9,1... | collective-permute-start | bytes 196616 | tf_op jit(solution)/shard_map/ppermute | solution.py:849
  5.5 2.4 %copy-start.5 = (s32[8,128]{1,0:T(8,128)S(1)}, s32[8,128]{1,0:T(8,128)}, u32[]{:S(2)}) copy-start(s32[8,128]{1,0:T(8,128)} %block_ref.5) | copy-start | bytes 12292
  5.5 4.6 %copy-start.3 = (bf16[8,512,128]{2,1,0:T(8,128)(2,1)S(1)}, bf16[8,512,128]{2,1,0:T(8,128)(2,1)}, u32[]{:S(2)}) copy-start(bf16[8,512,128]{2,1,0:T(8,128)(2,1)} %weight_ref.1) | copy-start | bytes 3145732
  7.8 3.5 %copy-start.4 = (s32[8,128]{1,0:T(8,128)S(1)}, s32[8,128]{1,0:T(8,128)}, u32[]{:S(2)}) copy-start(s32[8,128]{1,0:T(8,128)} %cut_ref.1) | copy-start | bytes 12292
  8.0 3.7 %collective-permute-start.1 = (bf16[80,128]{1,0:T(8,128)(2,1)S(1)}, bf16[80,128]{1,0:T(8,128)(2,1)S(1)}, u32[]{:S(2)}, u32[]{:S(2)}) collective-permute-start(bf16[80,128]{1,0:T(8,128)(2,1)S(1)} %get-tuple-element.63), channel_id=1, source_target_pairs={{0,8},{8,0},{16,24},{24,16},{1,9},{9,1},{17,25},{25,17},{2,10},{10... | collective-permute-start | bytes 61448 | tf_op jit(solution)/shard_map/ppermute | solution.py:856
  8.0 3.6 %collective-permute-start.2 = (bf16[64,128]{1,0:T(8,128)(2,1)S(1)}, bf16[64,128]{1,0:T(8,128)(2,1)S(1)}, u32[]{:S(2)}, u32[]{:S(2)}) collective-permute-start(bf16[64,128]{1,0:T(8,128)(2,1)S(1)} %get-tuple-element.64), channel_id=1, source_target_pairs={{0,24},{8,16},{16,8},{24,0},{1,25},{9,17},{17,9},{25,1},{2,26},{10... | collective-permute-start | bytes 49160 | tf_op jit(solution)/shard_map/ppermute | solution.py:856
  12.2 6.7 %collective-permute-start.3 = (bf16[224,128]{1,0:T(8,128)(2,1)S(1)}, bf16[224,128]{1,0:T(8,128)(2,1)S(1)}, u32[]{:S(2)}, u32[]{:S(2)}) collective-permute-start(bf16[224,128]{1,0:T(8,128)(2,1)S(1)} %get-tuple-element.68), channel_id=1, source_target_pairs={{0,1},{1,0},{2,3},{3,2},{4,5},{5,4},{6,7},{7,6},{8,9},{9,8},{10,11... | collective-permute-start | bytes 172040 | tf_op jit(solution)/shard_map/ppermute | solution.py:856
  13.8 6.0 %collective-permute-start.4 = (bf16[224,128]{1,0:T(8,128)(2,1)S(1)}, bf16[224,128]{1,0:T(8,128)(2,1)S(1)}, u32[]{:S(2)}, u32[]{:S(2)}) collective-permute-start(bf16[224,128]{1,0:T(8,128)(2,1)S(1)} %get-tuple-element.69), channel_id=1, source_target_pairs={{0,3},{1,2},{2,1},{3,0},{4,7},{5,6},{6,5},{7,4},{8,11},{9,10},{10,... | collective-permute-start | bytes 172040 | tf_op jit(solution)/shard_map/ppermute | solution.py:856
  20.5 4.1 %collective-permute-start.5 = (bf16[2,1,64,128]{3,2,1,0:T(8,128)(2,1)S(1)}, bf16[2,1,64,128]{3,2,1,0:T(8,128)(2,1)S(1)}, u32[]{:S(2)}, u32[]{:S(2)}) collective-permute-start(bf16[2,1,64,128]{3,2,1,0:T(8,128)(2,1)S(1)} %get-tuple-element.78), channel_id=1, source_target_pairs={{0,4},{4,0},{1,5},{5,1},{2,6},{6,2},{3,7},{7,3},{8,12},{12,8},{9,1... | collective-permute-start | bytes 98312 | tf_op jit(solution)/shard_map/ppermute | solution.py:849
  24.7 3.4 %collective-permute-start.7 = (bf16[64,128]{1,0:T(8,128)(2,1)S(1)}, bf16[64,128]{1,0:T(8,128)(2,1)S(1)}, u32[]{:S(2)}, u32[]{:S(2)}) collective-permute-start(bf16[64,128]{1,0:T(8,128)(2,1)S(1)} %get-tuple-element.88), channel_id=1, source_target_pairs={{0,24},{8,16},{16,8},{24,0},{1,25},{9,17},{17,9},{25,1},{2,26},{10... | collective-permute-start | bytes 49160 | tf_op jit(solution)/shard_map/ppermute | solution.py:856
  24.8 3.2 %collective-permute-start.6 = (bf16[32,128]{1,0:T(8,128)(2,1)S(1)}, bf16[32,128]{1,0:T(8,128)(2,1)S(1)}, u32[]{:S(2)}, u32[]{:S(2)}) collective-permute-start(bf16[32,128]{1,0:T(8,128)(2,1)S(1)} %get-tuple-element.87), channel_id=1, source_target_pairs={{0,8},{8,0},{16,24},{24,16},{1,9},{9,1},{17,25},{25,17},{2,10},{10... | collective-permute-start | bytes 24584 | tf_op jit(solution)/shard_map/ppermute | solution.py:856
  29.4 4.7 %collective-permute-start.9 = (bf16[2,128,128]{2,1,0:T(8,128)(2,1)S(1)}, bf16[2,128,128]{2,1,0:T(8,128)(2,1)S(1)}, u32[]{:S(2)}, u32[]{:S(2)}) collective-permute-start(bf16[2,128,128]{2,1,0:T(8,128)(2,1)S(1)} %get-tuple-element.112), channel_id=1, source_target_pairs={{0,16},{8,24},{16,0},{24,8},{1,17},{9,25},{17,1},{25,9},{2,18},{10... | collective-permute-start | bytes 196616 | tf_op jit(solution)/shard_map/ppermute | solution.py:964
  30.8 4.3 %collective-permute-start.10 = (bf16[2,128,128]{2,1,0:T(8,128)(2,1)S(1)}, bf16[2,128,128]{2,1,0:T(8,128)(2,1)S(1)}, u32[]{:S(2)}, u32[]{:S(2)}) collective-permute-start(bf16[2,128,128]{2,1,0:T(8,128)(2,1)S(1)} %get-tuple-element.113), channel_id=1, source_target_pairs={{0,24},{8,16},{16,8},{24,0},{1,25},{9,17},{17,9},{25,1},{2,26},{10... | collective-permute-start | bytes 196616 | tf_op jit(solution)/shard_map/ppermute | solution.py:964
  32.1 3.0 %collective-permute-start.8 = (bf16[2,128,128]{2,1,0:T(8,128)(2,1)S(1)}, bf16[2,128,128]{2,1,0:T(8,128)(2,1)S(1)}, u32[]{:S(2)}, u32[]{:S(2)}) collective-permute-start(bf16[2,128,128]{2,1,0:T(8,128)(2,1)S(1)} %shard_map.100), channel_id=1, source_target_pairs={{0,8},{8,0},{16,24},{24,16},{1,9},{9,1},{17,25},{25,17},{2,10},{10... | collective-permute-start | bytes 196616 | tf_op jit(solution)/shard_map/ppermute | solution.py:964

commit v10 on v8

--- a/solution.py
+++ b/solution.py
@@ -379,7 +379,7 @@
 
 def azimuth_kernel(
     cam_count, s_ref, x_ref, one_ref, two_ref, scalar_ref, velocity_ref, mass_ref, table_ref,
-    even_ref, odd_ref, packed_ref,
+    odd_ref, even_ref, packed_ref,
 ):
     ends = end_lanes((8, 128))
     row = row_ids((8, 128))
@@ -457,9 +457,9 @@
         at = slice(16 * (a // 2) + 32 * f, 16 * (a // 2) + 32 * f + 16)
         one, two = one_ref[at, :].astype(F32), two_ref[at, :].astype(F32)
         if b == 0:
-            line, sublane = jnp.where(even, two, one), 0
+            line, sublane = jnp.where(even, one, two), 0
         else:
-            line, sublane = jnp.where(even, one, two), 7
+            line, sublane = jnp.where(even, two, one), 7
         line = line[8 * (a % 2) : 8 * (a % 2) + 8]
         node = lax.broadcasted_iota(jnp.int32, (8, 8, 128), 1)
         block = block + jnp.where(node == sublane, line[:, None, :], 0.0)
@@ -522,7 +522,7 @@
 def add_beyond(layers, y_one_ref, y_two_ref, first_ref, scalar_ref, table_ref, g_ref, z_ref):
     even = (lax.axis_index("ey") & 1) == 0
     one, two = y_one_ref[64:, :].astype(F32), y_two_ref[64:, :].astype(F32)
-    sides = (jnp.where(even, two, one), jnp.where(even, one, two))
+    sides = (jnp.where(even, one, two), jnp.where(even, two, one))
     rows = []
     for h, (line, outer) in enumerate(((0, 0), (15, 63))):
         for a, n in layers:
@@ -893,7 +893,8 @@
     *y, packed = call(
         part(azimuth_kernel, n_cam), (half(224, 128), half(224, 128), shape_of(8, 8, 128))
     )(s, x_got, *z_got, scalar, velocity, mass, near)
-    y_got = swap_both(*y, "ey")
+    near_swap, wrap_swap = swaps("ey")
+    y_got = (lax.ppermute(y[0], "ey", wrap_swap), lax.ppermute(y[1], "ey", near_swap))
     g_inner, *inner_terms, z_inner = call(
         second_inner_kernel, (shape_of(*inner),) * 3 + (shape_of(4, 8, 128),)
     )(s, x_got, packed, scalar, velocity, mass, near)

time: 36.4 us -> 36.6 us (level)
  waiting for transfers between devices: 3.28 us -> 3.97 us
  starting transfers between devices: 14.7 us -> 14.2 us
    ppermute x6 -> x4, starting transfers between devices: 7.85 us -> 3.66 us  [swap_both(): return (lax.ppermute(one, axis, even), lax.ppermute(two, axis, odd))]
    ppermute x0 -> x2, starting transfers between devices: none -> 3.69 us  [the longest x1 3.68 us: per_device(): lax.ppermute(y[0], 'ey', wrap_swap)]
    ppermute x0 -> x2, waiting for transfers between devices: none -> 1.57 us  [the longest x1 1.27 us: per_device(): lax.ppermute(y[1], 'ey', near_swap)]
    ppermute x6 -> x4, waiting for transfers between devices: 1.09 us -> 0.28 us  [swap_both(): return (lax.ppermute(one, axis, even), lax.ppermute(two, axis, odd))]
  transfers between devices with their start and end apart: 11 -> 11, of which waited for: 4 -> 6; matrix products, arithmetic and copies ran while one was open for 0% -> 0% of each run, Pallas kernels for 32% -> 32%
where the time goes in v10:
time: 36.6 us; the launch traced here: 36.4 us
  Pallas kernels  17.4 us (48%)
  starting transfers between devices  14.2 us (39%)
  waiting for transfers between devices  3.97 us (11%)
  between operations  0.84 us (2%)
    ppermute x2, starting transfers between devices, swap_axial(): return lax.ppermute(x, 'ex', up)  4.56 us
    ppermute x1, starting transfers between devices, per_device(): lax.ppermute(y[0], 'ey', wrap_swap)  3.68 us
    ppermute x4, starting transfers between devices, swap_both(): return (lax.ppermute(one, axis, even), lax.ppermute(two, axis, odd))  3.66 us
    pallas_call x1, Pallas kernels, per_device(): call(second_inner_kernel, (shape_of(*inner),) * 3 + (shape_of(4, 8, 128),))  2.6 us
    pallas_call x1, Pallas kernels, per_device(): call(first_kernel, (shape_of(64, 64, 128), shape_of(8, 8, 128)))  2.35 us
    ppermute x3, starting transfers between devices, per_device(): lax.ppermute(payload, 'cam', [(i, i ^ d) for i in range(n_cam)])  2.27 us
    pallas_call x1, Pallas kernels, per_device(): call(face_kernel, (shape_of(2, 2, 64, 128, dtype=BF16), shape_of(*tables....  1.77 us
    pallas_call x1, Pallas kernels, per_device(): call(middle_kernel, shape_of(cameras, 128, 128), scratch_shapes=[pltpu.VM...  1.49 us
  transfers between devices with their start and end apart: 11, of which 6 were waited for; matrix products, arithmetic and copies ran while one was open for 0% of the time, Pallas kernels for 32%

profile of v10, /device:TPU:0, one launch (start us, length us, event | category | flops | bytes accessed | tf_op | source)
XLA Modules:
  0.0 36.4 jit_solution(2801163231691121209)
XLA Ops:
  0.6 0.0 copy-start
  0.6 0.0 copy-start.1
  0.6 0.0 copy-start.2
  0.7 1.8 %shard_map.86 = (bf16[2,2,64,128]{3,2,1,0:T(8,128)(2,1)S(1)}, bf16[1472,128]{1,0:T(8,128)(2,1)S(1)}) custom-call(f32[32,64,128]{2,1,0:T(8,128)} %bitcast.10, f32[3,32,64,128]{3,2,1,0:T(8,128)} %bitcast.4, f32[32,64,128]{2,1,0:T(8,128)} %bitcast.16, bf16[1472,128]{1,0:T(8,128)(2,1)} %constant.2.clone.table_hbm), custom_call_target="tpu_custom_call" | custom-call | flops 100000000 | bytes 10000000 | tf_op jit(solution)/shard_map/pallas_call | solution.py:868
  2.4 3.0 %collective-permute-start = (bf16[2,2,64,128]{3,2,1,0:T(8,128)(2,1)S(1)}, bf16[2,2,64,128]{3,2,1,0:T(8,128)(2,1)S(1)}, u32[]{:S(2)}, u32[]{:S(2)}) collective-permute-start(bf16[2,2,64,128]{3,2,1,0:T(8,128)(2,1)S(1)} %get-tuple-element.60), channel_id=1, source_target_pairs={{0,4},{4,0},{1,5},{5,1},{2,6},{6,2},{3,7},{7,3},{8,12},{12,8},{9,1... | collective-permute-start | bytes 196616 | tf_op jit(solution)/shard_map/ppermute | solution.py:845
  5.4 0.0 copy-done
  5.4 0.0 copy-done.1
  5.4 0.0 copy-done.2
  5.5 0.0 copy-start.5
  5.5 0.0 copy-start.3
  5.5 2.3 %shard_map.87 = (f32[64,64,128]{2,1,0:T(8,128)S(1)}, f32[8,8,128]{2,1,0:T(8,128)S(1)}) custom-call(f32[32,64,128]{2,1,0:T(8,128)S(1)} %bitcast.11, f32[3,32,64,128]{3,2,1,0:T(8,128)S(1)} %bitcast.5, f32[32,64,128]{2,1,0:T(8,128)S(1)} %bitcast.17, bf16[1472,128]{1,0:T(8,128)(2,1)S(1)} %get-tuple-element.57.table_ref), custom_call_target="tpu_custom_call" | custom-call | flops 100000000 | bytes 10000000 | tf_op jit(solution)/shard_map/pallas_call | solution.py:880
  7.8 0.0 copy-start.4
  7.8 0.0 collective-permute-done.x_in
  7.9 0.0 copy-done.5
  7.9 0.1 shard_map.88
  8.0 0.1 collective-permute-start.1
  8.0 2.0 %collective-permute-start.2 = (bf16[64,128]{1,0:T(8,128)(2,1)S(1)}, bf16[64,128]{1,0:T(8,128)(2,1)S(1)}, u32[]{:S(2)}, u32[]{:S(2)}) collective-permute-start(bf16[64,128]{1,0:T(8,128)(2,1)S(1)} %get-tuple-element.63), channel_id=1, source_target_pairs={{0,24},{8,16},{16,8},{24,0},{1,25},{9,17},{17,9},{25,1},{2,26},{10... | collective-permute-start | bytes 49160 | tf_op jit(solution)/shard_map/ppermute | solution.py:852
  10.0 0.0 copy-done.3
  10.0 1.3 %shard_map.89.weight_ref = bf16[512,1024]{1,0:T(8,128)(2,1)S(1)} custom-call(bf16[8,512,128]{2,1,0:T(8,128)(2,1)S(1)} %copy-done.3), custom_call_target="tpu_custom_call" | custom-call | flops 100000000 | bytes 10000000 | tf_op jit(solution)/shard_map/pallas_call | solution.py:883
  11.3 0.0 copy-done.4
  11.3 0.4 shard_map.90.pick_ref
  11.7 0.0 collective-permute-done.2.two_ref
  11.7 0.0 collective-permute-done.1.one_ref.got_ref.first_ref
  11.7 0.5 %shard_map.91 = (bf16[224,128]{1,0:T(8,128)(2,1)S(1)}, bf16[224,128]{1,0:T(8,128)(2,1)S(1)}, f32[8,8,128]{2,1,0:T(8,128)S(1)}) custom-call(f32[64,64,128]{2,1,0:T(8,128)S(1)} %get-tuple-element.58.s_ref, f32[2,2,64,128]{3,2,1,0:T(8,128)S(1)} %get-tuple-element.61.x_ref, bf16[80,128]{1,0:T(8,128)(2,1)S(1)} %collective-permute-done.1.one_ref.got_ref.first_ref, ...), custom_call_target="tpu_custom_call" | custom-call | flops 100000000 | bytes 10000000 | tf_op jit(solution)/shard_map/pallas_call | solution.py:893
  12.2 3.7 %collective-permute-start.3 = (bf16[224,128]{1,0:T(8,128)(2,1)S(1)}, bf16[224,128]{1,0:T(8,128)(2,1)S(1)}, u32[]{:S(2)}, u32[]{:S(2)}) collective-permute-start(bf16[224,128]{1,0:T(8,128)(2,1)S(1)} %get-tuple-element.67), channel_id=1, source_target_pairs={{0,3},{1,2},{2,1},{3,0},{4,7},{5,6},{6,5},{7,4},{8,11},{9,10},{10,... | collective-permute-start | bytes 172040 | tf_op jit(solution)/shard_map/ppermute | solution.py:897
  15.8 0.0 collective-permute-start.4
  15.8 2.6 %shard_map.92 = (f32[32,48,128]{2,1,0:T(8,128)S(1)}, f32[32,48,128]{2,1,0:T(8,128)S(1)}, f32[32,48,128]{2,1,0:T(8,128)S(1)}, f32[4,8,128]{2,1,0:T(8,128)S(1)}) custom-call(f32[64,64,128]{2,1,0:T(8,128)S(1)} %get-tuple-element.58.s_ref, f32[2,2,64,128]{3,2,1,0:T(8,128)S(1)} %get-tuple-element.61.x_ref, f32[8,8,128]{2,1,0:T(8,128)S(1)} %get-tuple-element.66.packed_ref, ...), custom_call_target="tpu_custom_call" | custom-call | flops 100000000 | bytes 10000000 | tf_op jit(solution)/shard_map/pallas_call | solution.py:898
  18.5 0.3 collective-permute-done.3.y_one_ref
  18.8 1.3 %collective-permute-done.4.y_two_ref = bf16[224,128]{1,0:T(8,128)(2,1)S(1)} collective-permute-done((bf16[224,128]{1,0:T(8,128)(2,1)S(1)}, bf16[224,128]{1,0:T(8,128)(2,1)S(1)}, u32[]{:S(2)}, u32[]{:S(2)}) %collective-permute-start.4) | collective-permute-done | bytes 57376 | tf_op jit(solution)/shard_map/ppermute | solution.py:897
  20.0 0.7 %shard_map.93 = (bf16[2,1,64,128]{3,2,1,0:T(8,128)(2,1)S(1)}, f32[16,16,128]{2,1,0:T(8,128)S(1)}, f32[16,16,128]{2,1,0:T(8,128)S(1)}, f32[16,16,128]{2,1,0:T(8,128)S(1)}, f32[2,8,128]{2,1,0:T(8,128)S(1)}) custom-call(f32[64,64,128]{2,1,0:T(8,128)S(1)} %get-tuple-element.58.s_ref, f32[2,2,64,128]{3,2,1,0:T(8,128)S(1)} %get-tuple-element.61.x_ref, ...), custom_call_target="tpu_custom_call" | custom-call | flops 100000000 | bytes 10000000 | tf_op jit(solution)/shard_map/pallas_call | solution.py:903
  20.8 1.6 %collective-permute-start.5 = (bf16[2,1,64,128]{3,2,1,0:T(8,128)(2,1)S(1)}, bf16[2,1,64,128]{3,2,1,0:T(8,128)(2,1)S(1)}, u32[]{:S(2)}, u32[]{:S(2)}) collective-permute-start(bf16[2,1,64,128]{3,2,1,0:T(8,128)(2,1)S(1)} %get-tuple-element.77), channel_id=1, source_target_pairs={{0,4},{4,0},{1,5},{5,1},{2,6},{6,2},{3,7},{7,3},{8,12},{12,8},{9,1... | collective-permute-start | bytes 98312 | tf_op jit(solution)/shard_map/ppermute | solution.py:845
  22.3 0.9 %shard_map.94 = (f32[32,64,128]{2,1,0:T(8,128)S(1)}, f32[32,16,128]{2,1,0:T(8,128)S(1)}, f32[32,16,128]{2,1,0:T(8,128)S(1)}, f32[4,8,128]{2,1,0:T(8,128)S(1)}) custom-call(f32[64,64,128]{2,1,0:T(8,128)S(1)} %get-tuple-element.58.s_ref, f32[2,2,64,128]{3,2,1,0:T(8,128)S(1)} %get-tuple-element.61.x_ref, f32[8,8,128]{2,1,0:T(8,128)S(1)} %get-tuple-element.66.packed_ref, ...), custom_call_target="tpu_custom_call" | custom-call | flops 100000000 | bytes 10000000 | tf_op jit(solution)/shard_map/pallas_call | solution.py:908
  23.2 0.8 %shard_map.95.early_ref = bf16[256,1024]{1,0:T(8,128)(2,1)S(1)} custom-call(f32[32,64,128]{2,1,0:T(8,128)S(1)} %get-tuple-element.98.g_ref, f32[32,48,128]{2,1,0:T(8,128)S(1)} %get-tuple-element.102.base_one, f32[32,48,128]{2,1,0:T(8,128)S(1)} %get-tuple-element.103.half_one, f32[32,16,128]{2,1,0:T(8,128)S(1)} %get-tuple-element.104.base_two, ...), custom_call_target="tpu_custom_call" | custom-call | flops 100000000 | bytes 10000000 | tf_op jit(solution)/shard_map/pallas_call | solution.py:916
  24.0 0.7 %collective-permute-done.5.x_in = bf16[2,1,64,128]{3,2,1,0:T(8,128)(2,1)S(1)} collective-permute-done((bf16[2,1,64,128]{3,2,1,0:T(8,128)(2,1)S(1)}, bf16[2,1,64,128]{3,2,1,0:T(8,128)(2,1)S(1)}, u32[]{:S(2)}, u32[]{:S(2)}) %collective-permute-start.5) | collective-permute-done | bytes 32800 | tf_op jit(solution)/shard_map/ppermute | solution.py:845
  24.7 0.1 shard_map.96
  24.8 0.1 collective-permute-start.7
  24.9 1.5 %collective-permute-start.6 = (bf16[32,128]{1,0:T(8,128)(2,1)S(1)}, bf16[32,128]{1,0:T(8,128)(2,1)S(1)}, u32[]{:S(2)}, u32[]{:S(2)}) collective-permute-start(bf16[32,128]{1,0:T(8,128)(2,1)S(1)} %get-tuple-element.85), channel_id=1, source_target_pairs={{0,8},{8,0},{16,24},{24,16},{1,9},{9,1},{17,25},{25,17},{2,10},{10... | collective-permute-start | bytes 24584 | tf_op jit(solution)/shard_map/ppermute | solution.py:852
  26.4 1.5 %shard_map.97.pixel_ref = f32[8,128,128]{2,1,0:T(8,128)S(1)} custom-call(f32[32,64,128]{2,1,0:T(8,128)S(1)} %get-tuple-element.98.g_ref, f32[2,1,64,128]{3,2,1,0:T(8,128)S(1)} %get-tuple-element.99.x_ref, f32[32,48,128]{2,1,0:T(8,128)S(1)} %get-tuple-element.102.base_one, f32[32,48,128]{2,1,0:T(8,128)S(1)} %get-tuple-element.103.half_one, ...), custom_call_target="tpu_custom_call" | custom-call | flops 100000000 | bytes 10000000 | tf_op jit(solution)/shard_map/pallas_call | solution.py:926
  27.9 0.0 collective-permute-done.6.one_ref
  27.9 0.3 collective-permute-done.7.two_ref.second_ref
  28.2 1.2 %shard_map.98 = (bf16[8,64,128]{2,1,0:T(8,128)(2,1)S(1)}, bf16[2,128,128]{2,1,0:T(8,128)(2,1)S(1)}, bf16[2,128,128]{2,1,0:T(8,128)(2,1)S(1)}) custom-call(f32[32,64,128]{2,1,0:T(8,128)S(1)} %get-tuple-element.98.g_ref, f32[2,1,64,128]{3,2,1,0:T(8,128)S(1)} %get-tuple-element.99.x_ref, bf16[32,128]{1,0:T(8,128)(2,1)S(1)} %collective-permute-done.6.one_ref, ...), custom_call_target="tpu_custom_call" | custom-call | flops 100000000 | bytes 10000000 | tf_op jit(solution)/shard_map/pallas_call | solution.py:933
  29.4 1.3 %collective-permute-start.9 = (bf16[2,128,128]{2,1,0:T(8,128)(2,1)S(1)}, bf16[2,128,128]{2,1,0:T(8,128)(2,1)S(1)}, u32[]{:S(2)}, u32[]{:S(2)}) collective-permute-start(bf16[2,128,128]{2,1,0:T(8,128)(2,1)S(1)} %get-tuple-element.110), channel_id=1, source_target_pairs={{0,16},{8,24},{16,0},{24,8},{1,17},{9,25},{17,1},{25,9},{2,18},{10... | collective-permute-start | bytes 196616 | tf_op jit(solution)/shard_map/ppermute | solution.py:961
  30.8 0.2 collective-permute-start.10
  30.9 0.6 %shard_map.99 = (f32[2,1024,128]{2,1,0:T(8,128)S(1)}, bf16[2,1024,512]{2,1,0:T(8,128)(2,1)S(1)}) custom-call(bf16[8,64,128]{2,1,0:T(8,128)(2,1)S(1)} %get-tuple-element.95.value_ref, bf16[8,128,640]{2,1,0:T(8,128)(2,1)S(1)} %shard_map.90.pick_ref, f32[8,128,128]{2,1,0:T(8,128)S(1)} %shard_map.97.pixel_ref, s32[8,128]{1,0:T(8,128)S(1)} %copy-done.5, ...), custom_call_target="tpu_custom_call" | custom-call | flops 100000000 | bytes 10000000 | tf_op jit(solution)/shard_map/pallas_call | solution.py:940
  31.6 0.2 shard_map.100
  31.7 0.8 %collective-permute-start.8 = (bf16[2,128,128]{2,1,0:T(8,128)(2,1)S(1)}, bf16[2,128,128]{2,1,0:T(8,128)(2,1)S(1)}, u32[]{:S(2)}, u32[]{:S(2)}) collective-permute-start(bf16[2,128,128]{2,1,0:T(8,128)(2,1)S(1)} %shard_map.100), channel_id=1, source_target_pairs={{0,8},{8,0},{16,24},{24,16},{1,9},{9,1},{17,25},{25,17},{2,10},{10... | collective-permute-start | bytes 196616 | tf_op jit(solution)/shard_map/ppermute | solution.py:961
  32.5 1.2 %shard_map.101 = f32[32,64,128]{2,1,0:T(8,128)} custom-call(f32[32,64,128]{2,1,0:T(8,128)S(1)} %get-tuple-element.98.g_ref, f32[2,1,64,128]{3,2,1,0:T(8,128)S(1)} %get-tuple-element.99.x_ref, bf16[32,128]{1,0:T(8,128)(2,1)S(1)} %collective-permute-done.6.one_ref, bf16[64,128]{1,0:T(8,128)(2,1)S(1)} %collective-permute-done.7.two_ref.second_ref, ...), custom_call_target="tpu_custom_call" | custom-call | flops 100000000 | bytes 10000000 | tf_op jit(solution)/shard_map/pallas_call | solution.py:952
  33.7 0.1 collective-permute-done.9.refs_1_
  33.8 1.3 %collective-permute-done.10.refs_2_ = bf16[2,128,128]{2,1,0:T(8,128)(2,1)S(1)} collective-permute-done((bf16[2,128,128]{2,1,0:T(8,128)(2,1)S(1)}, bf16[2,128,128]{2,1,0:T(8,128)(2,1)S(1)}, u32[]{:S(2)}, u32[]{:S(2)}) %collective-permute-start.10) | collective-permute-done | bytes 65568 | tf_op jit(solution)/shard_map/ppermute | solution.py:961
  35.1 0.0 collective-permute-done.8.refs_0_
  35.1 1.3 %shard_map.102 = f32[2,1024,128]{2,1,0:T(8,128)} custom-call(f32[2,1024,128]{2,1,0:T(8,128)S(1)} %get-tuple-element.107.own_ref, bf16[2,1024,512]{2,1,0:T(8,128)(2,1)S(1)} %get-tuple-element.108.onehot_ref, bf16[2,128,128]{2,1,0:T(8,128)(2,1)S(1)} %collective-permute-done.8.refs_0_, bf16[2,128,128]{2,1,0:T(8,128)(2,1)S(1)} %collective-permute-done.9.refs_1_, ...), custom_call_target="tpu_custom_call" | custom-call | flops 100000000 | bytes 10000000 | tf_op jit(solution)/shard_map/pallas_call | solution.py:962
Async XLA Ops:
  0.6 4.8 %copy-start = (f32[3,4,8,8,8,128]{5,4,3,2,1,0:T(8,128)S(1)}, f32[3,4,8,8,8,128]{5,4,3,2,1,0:T(8,128)}, u32[]{:S(2)}) copy-start(f32[3,4,8,8,8,128]{5,4,3,2,1,0:T(8,128)} %param.8) | copy-start | bytes 9437188
  0.6 4.8 %copy-start.1 = (f32[4,8,8,8,128]{4,3,2,1,0:T(8,128)S(1)}, f32[4,8,8,8,128]{4,3,2,1,0:T(8,128)}, u32[]{:S(2)}) copy-start(f32[4,8,8,8,128]{4,3,2,1,0:T(8,128)} %param.7) | copy-start | bytes 3145732
  0.6 4.8 %copy-start.2 = (f32[4,8,8,8,128]{4,3,2,1,0:T(8,128)S(1)}, f32[4,8,8,8,128]{4,3,2,1,0:T(8,128)}, u32[]{:S(2)}) copy-start(f32[4,8,8,8,128]{4,3,2,1,0:T(8,128)} %param.9) | copy-start | bytes 3145732
  2.4 5.4 %collective-permute-start = (bf16[2,2,64,128]{3,2,1,0:T(8,128)(2,1)S(1)}, bf16[2,2,64,128]{3,2,1,0:T(8,128)(2,1)S(1)}, u32[]{:S(2)}, u32[]{:S(2)}) collective-permute-start(bf16[2,2,64,128]{3,2,1,0:T(8,128)(2,1)S(1)} %get-tuple-element.60), channel_id=1, source_target_pairs={{0,4},{4,0},{1,5},{5,1},{2,6},{6,2},{3,7},{7,3},{8,12},{12,8},{9,1... | collective-permute-start | bytes 196616 | tf_op jit(solution)/shard_map/ppermute | solution.py:845
  5.5 2.4 %copy-start.5 = (s32[8,128]{1,0:T(8,128)S(1)}, s32[8,128]{1,0:T(8,128)}, u32[]{:S(2)}) copy-start(s32[8,128]{1,0:T(8,128)} %block_ref.5) | copy-start | bytes 12292
  5.5 4.6 %copy-start.3 = (bf16[8,512,128]{2,1,0:T(8,128)(2,1)S(1)}, bf16[8,512,128]{2,1,0:T(8,128)(2,1)}, u32[]{:S(2)}) copy-start(bf16[8,512,128]{2,1,0:T(8,128)(2,1)} %weight_ref.1) | copy-start | bytes 3145732
  7.8 3.5 %copy-start.4 = (s32[8,128]{1,0:T(8,128)S(1)}, s32[8,128]{1,0:T(8,128)}, u32[]{:S(2)}) copy-start(s32[8,128]{1,0:T(8,128)} %cut_ref.1) | copy-start | bytes 12292
  8.0 3.7 %collective-permute-start.1 = (bf16[80,128]{1,0:T(8,128)(2,1)S(1)}, bf16[80,128]{1,0:T(8,128)(2,1)S(1)}, u32[]{:S(2)}, u32[]{:S(2)}) collective-permute-start(bf16[80,128]{1,0:T(8,128)(2,1)S(1)} %get-tuple-element.62), channel_id=1, source_target_pairs={{0,8},{8,0},{16,24},{24,16},{1,9},{9,1},{17,25},{25,17},{2,10},{10... | collective-permute-start | bytes 61448 | tf_op jit(solution)/shard_map/ppermute | solution.py:852
  8.0 3.6 %collective-permute-start.2 = (bf16[64,128]{1,0:T(8,128)(2,1)S(1)}, bf16[64,128]{1,0:T(8,128)(2,1)S(1)}, u32[]{:S(2)}, u32[]{:S(2)}) collective-permute-start(bf16[64,128]{1,0:T(8,128)(2,1)S(1)} %get-tuple-element.63), channel_id=1, source_target_pairs={{0,24},{8,16},{16,8},{24,0},{1,25},{9,17},{17,9},{25,1},{2,26},{10... | collective-permute-start | bytes 49160 | tf_op jit(solution)/shard_map/ppermute | solution.py:852
  12.2 6.6 %collective-permute-start.3 = (bf16[224,128]{1,0:T(8,128)(2,1)S(1)}, bf16[224,128]{1,0:T(8,128)(2,1)S(1)}, u32[]{:S(2)}, u32[]{:S(2)}) collective-permute-start(bf16[224,128]{1,0:T(8,128)(2,1)S(1)} %get-tuple-element.67), channel_id=1, source_target_pairs={{0,3},{1,2},{2,1},{3,0},{4,7},{5,6},{6,5},{7,4},{8,11},{9,10},{10,... | collective-permute-start | bytes 172040 | tf_op jit(solution)/shard_map/ppermute | solution.py:897
  15.8 4.2 %collective-permute-start.4 = (bf16[224,128]{1,0:T(8,128)(2,1)S(1)}, bf16[224,128]{1,0:T(8,128)(2,1)S(1)}, u32[]{:S(2)}, u32[]{:S(2)}) collective-permute-start(bf16[224,128]{1,0:T(8,128)(2,1)S(1)} %get-tuple-element.68), channel_id=1, source_target_pairs={{0,1},{1,0},{2,3},{3,2},{4,5},{5,4},{6,7},{7,6},{8,9},{9,8},{10,11... | collective-permute-start | bytes 172040 | tf_op jit(solution)/shard_map/ppermute | solution.py:897
  20.8 4.0 %collective-permute-start.5 = (bf16[2,1,64,128]{3,2,1,0:T(8,128)(2,1)S(1)}, bf16[2,1,64,128]{3,2,1,0:T(8,128)(2,1)S(1)}, u32[]{:S(2)}, u32[]{:S(2)}) collective-permute-start(bf16[2,1,64,128]{3,2,1,0:T(8,128)(2,1)S(1)} %get-tuple-element.77), channel_id=1, source_target_pairs={{0,4},{4,0},{1,5},{5,1},{2,6},{6,2},{3,7},{7,3},{8,12},{12,8},{9,1... | collective-permute-start | bytes 98312 | tf_op jit(solution)/shard_map/ppermute | solution.py:845
  24.8 3.4 %collective-permute-start.7 = (bf16[64,128]{1,0:T(8,128)(2,1)S(1)}, bf16[64,128]{1,0:T(8,128)(2,1)S(1)}, u32[]{:S(2)}, u32[]{:S(2)}) collective-permute-start(bf16[64,128]{1,0:T(8,128)(2,1)S(1)} %get-tuple-element.86), channel_id=1, source_target_pairs={{0,24},{8,16},{16,8},{24,0},{1,25},{9,17},{17,9},{25,1},{2,26},{10... | collective-permute-start | bytes 49160 | tf_op jit(solution)/shard_map/ppermute | solution.py:852
  24.9 3.0 %collective-permute-start.6 = (bf16[32,128]{1,0:T(8,128)(2,1)S(1)}, bf16[32,128]{1,0:T(8,128)(2,1)S(1)}, u32[]{:S(2)}, u32[]{:S(2)}) collective-permute-start(bf16[32,128]{1,0:T(8,128)(2,1)S(1)} %get-tuple-element.85), channel_id=1, source_target_pairs={{0,8},{8,0},{16,24},{24,16},{1,9},{9,1},{17,25},{25,17},{2,10},{10... | collective-permute-start | bytes 24584 | tf_op jit(solution)/shard_map/ppermute | solution.py:852
  29.4 4.4 %collective-permute-start.9 = (bf16[2,128,128]{2,1,0:T(8,128)(2,1)S(1)}, bf16[2,128,128]{2,1,0:T(8,128)(2,1)S(1)}, u32[]{:S(2)}, u32[]{:S(2)}) collective-permute-start(bf16[2,128,128]{2,1,0:T(8,128)(2,1)S(1)} %get-tuple-element.110), channel_id=1, source_target_pairs={{0,16},{8,24},{16,0},{24,8},{1,17},{9,25},{17,1},{25,9},{2,18},{10... | collective-permute-start | bytes 196616 | tf_op jit(solution)/shard_map/ppermute | solution.py:961
  30.8 4.3 %collective-permute-start.10 = (bf16[2,128,128]{2,1,0:T(8,128)(2,1)S(1)}, bf16[2,128,128]{2,1,0:T(8,128)(2,1)S(1)}, u32[]{:S(2)}, u32[]{:S(2)}) collective-permute-start(bf16[2,128,128]{2,1,0:T(8,128)(2,1)S(1)} %get-tuple-element.111), channel_id=1, source_target_pairs={{0,24},{8,16},{16,8},{24,0},{1,25},{9,17},{17,9},{25,1},{2,26},{10... | collective-permute-start | bytes 196616 | tf_op jit(solution)/shard_map/ppermute | solution.py:961
  31.7 3.4 %collective-permute-start.8 = (bf16[2,128,128]{2,1,0:T(8,128)(2,1)S(1)}, bf16[2,128,128]{2,1,0:T(8,128)(2,1)S(1)}, u32[]{:S(2)}, u32[]{:S(2)}) collective-permute-start(bf16[2,128,128]{2,1,0:T(8,128)(2,1)S(1)} %shard_map.100), channel_id=1, source_target_pairs={{0,8},{8,0},{16,24},{24,16},{1,9},{9,1},{17,25},{25,17},{2,10},{10... | collective-permute-start | bytes 196616 | tf_op jit(solution)/shard_map/ppermute | solution.py:961

commit v11 on v8

--- a/solution.py
+++ b/solution.py
@@ -436,6 +436,25 @@
     return rows
 
 
+def spread_back(packed, pair, table_ref):
+    slot = ((lane_ids((8, 128)) + 1) >> 1) & 63
+    high, low = halves(packed)
+    high, low = high.astype(F32), low.astype(F32)
+    rows = []
+    for b in pair:
+        for i in range(8):
+            here = slot == 56 - 8 * i + b
+            both = [jnp.where(here, high, 0.0), jnp.where(here, low, 0.0)]
+            rows.append(jnp.concatenate(both, axis=1))
+    spread = table_ref[1024:1152]
+    return lax.dot_general(
+        jnp.concatenate(rows, axis=0).astype(BF16),
+        jnp.concatenate([spread, spread], axis=1),
+        (((1,), (1,)), ((), ())),
+        preferred_element_type=F32,
+    )
+
+
 def assembled(s_ref, x_ref, packed, f, a, b, y_refs=None):
     span = slice(8 * b, 8 * b + 8)
     at = span_of(a, 32 * f)
@@ -712,14 +731,22 @@
         payload_ref[n] = values.astype(BF16)
 
 
-def final_layers(cam_count, g_ref, x_ref, one_ref, two_ref, terms, use):
+def final_layers(cam_count, g_ref, x_ref, one_ref, two_ref, terms, use, table_ref=None):
     base_one, half_one, base_two, half_two = terms
     bases, halfs = (base_one, base_two), (half_one, half_two)
     one, two = one_ref[:32, :].astype(F32), two_ref[:32, :].astype(F32)
     for a in range(4):
         packed = merged(one[8 * a : 8 * a + 8], two[8 * a : 8 * a + 8], cam_count)
         for pair in PAIRS:
-            use(a, pair, advanced(g_ref, x_ref, packed, bases, halfs, a, pair))
+            if table_ref is None:
+                use(a, pair, advanced(g_ref, x_ref, packed, bases, halfs, a, pair))
+                continue
+            ends = spread_back(packed, pair, table_ref)
+            blocks = []
+            for h, b in enumerate(pair):
+                g = assembled(g_ref, x_ref, None, 0, a, b) + ends[64 * h : 64 * h + 64]
+                blocks.append(term(bases, a, b) - term(halfs, a, b) * g)
+            use(a, pair, blocks)
 
 
 def render_far_kernel(
@@ -738,7 +765,7 @@
                 ]
 
     terms = (base_one, half_one, base_two, half_two)
-    final_layers(cam_count, g_ref, x_ref, one_ref, two_ref, terms, use)
+    final_layers(cam_count, g_ref, x_ref, one_ref, two_ref, terms, use, table_ref)
     ends = end_ref[...].astype(BF16)
     for m in range(pixel_ref.shape[0] // 2):
         values = dot(ends, weight_ref[:, 256 * m : 256 * m + 256]).astype(BF16)

time: 36.4 us -> 37.6 us (1.033)
  Pallas kernels: 17.4 us -> 18.6 us
    pallas_call x1, Pallas kernels: 1.22 us -> 2.44 us  [per_device(): call(part(render_far_kernel, n_cam), (half(cameras, 64, 128),) + (payload...]
  transfers between devices with their start and end apart: 11 -> 11, of which waited for: 4 -> 4; matrix products, arithmetic and copies ran while one was open for 0% -> 0% of each run, Pallas kernels for 32% -> 31%
where the time goes in v11:
time: 37.6 us; the launch traced here: 37.5 us
  Pallas kernels  18.6 us (49%)
  starting transfers between devices  14.7 us (39%)
  waiting for transfers between devices  3.28 us (9%)
  between operations  0.85 us (2%)
    ppermute x6, starting transfers between devices, swap_both(): return (lax.ppermute(one, axis, even), lax.ppermute(two, axis, odd))  7.85 us
    ppermute x2, starting transfers between devices, swap_axial(): return lax.ppermute(x, 'ex', up)  4.56 us
    pallas_call x1, Pallas kernels, per_device(): call(second_inner_kernel, (shape_of(*inner),) * 3 + (shape_of(4, 8, 128),))  2.6 us
    pallas_call x1, Pallas kernels, per_device(): call(part(render_far_kernel, n_cam), (half(cameras, 64, 128),) + (payload...  2.44 us
    pallas_call x1, Pallas kernels, per_device(): call(first_kernel, (shape_of(64, 64, 128), shape_of(8, 8, 128)))  2.35 us
    ppermute x3, starting transfers between devices, per_device(): lax.ppermute(payload, 'cam', [(i, i ^ d) for i in range(n_cam)])  2.27 us
    pallas_call x1, Pallas kernels, per_device(): call(face_kernel, (shape_of(2, 2, 64, 128, dtype=BF16), shape_of(*tables....  1.77 us
    pallas_call x1, Pallas kernels, per_device(): call(middle_kernel, shape_of(cameras, 128, 128), scratch_shapes=[pltpu.VM...  1.49 us
  transfers between devices with their start and end apart: 11, of which 4 were waited for; matrix products, arithmetic and copies ran while one was open for 0% of the time, Pallas kernels for 31%

profile of v11, /device:TPU:0, one launch (start us, length us, event | category | flops | bytes accessed | tf_op | source)
XLA Modules:
  0.0 37.5 jit_solution(14365217284571470842)
XLA Ops:
  0.6 0.0 copy-start
  0.6 0.0 copy-start.1
  0.6 0.0 copy-start.2
  0.7 1.8 %shard_map.86 = (bf16[2,2,64,128]{3,2,1,0:T(8,128)(2,1)S(1)}, bf16[1472,128]{1,0:T(8,128)(2,1)S(1)}) custom-call(f32[32,64,128]{2,1,0:T(8,128)} %bitcast.10, f32[3,32,64,128]{3,2,1,0:T(8,128)} %bitcast.4, f32[32,64,128]{2,1,0:T(8,128)} %bitcast.16, bf16[1472,128]{1,0:T(8,128)(2,1)} %constant.2.clone.table_hbm), custom_call_target="tpu_custom_call" | custom-call | flops 100000000 | bytes 10000000 | tf_op jit(solution)/shard_map/pallas_call | solution.py:895
  2.4 3.0 %collective-permute-start = (bf16[2,2,64,128]{3,2,1,0:T(8,128)(2,1)S(1)}, bf16[2,2,64,128]{3,2,1,0:T(8,128)(2,1)S(1)}, u32[]{:S(2)}, u32[]{:S(2)}) collective-permute-start(bf16[2,2,64,128]{3,2,1,0:T(8,128)(2,1)S(1)} %get-tuple-element.60), channel_id=1, source_target_pairs={{0,4},{4,0},{1,5},{5,1},{2,6},{6,2},{3,7},{7,3},{8,12},{12,8},{9,1... | collective-permute-start | bytes 196616 | tf_op jit(solution)/shard_map/ppermute | solution.py:872
  5.4 0.0 copy-done
  5.4 0.0 copy-done.1
  5.4 0.0 copy-done.2
  5.5 0.0 copy-start.5
  5.5 0.0 copy-start.3
  5.5 2.3 %shard_map.87 = (f32[64,64,128]{2,1,0:T(8,128)S(1)}, f32[8,8,128]{2,1,0:T(8,128)S(1)}) custom-call(f32[32,64,128]{2,1,0:T(8,128)S(1)} %bitcast.11, f32[3,32,64,128]{3,2,1,0:T(8,128)S(1)} %bitcast.5, f32[32,64,128]{2,1,0:T(8,128)S(1)} %bitcast.17, bf16[1472,128]{1,0:T(8,128)(2,1)S(1)} %get-tuple-element.57.table_ref), custom_call_target="tpu_custom_call" | custom-call | flops 100000000 | bytes 10000000 | tf_op jit(solution)/shard_map/pallas_call | solution.py:907
  7.8 0.0 copy-start.4
  7.8 0.0 collective-permute-done.x_in
  7.9 0.0 copy-done.5
  7.9 0.1 shard_map.88
  8.0 0.1 collective-permute-start.1
  8.0 2.0 %collective-permute-start.2 = (bf16[64,128]{1,0:T(8,128)(2,1)S(1)}, bf16[64,128]{1,0:T(8,128)(2,1)S(1)}, u32[]{:S(2)}, u32[]{:S(2)}) collective-permute-start(bf16[64,128]{1,0:T(8,128)(2,1)S(1)} %get-tuple-element.63), channel_id=1, source_target_pairs={{0,24},{8,16},{16,8},{24,0},{1,25},{9,17},{17,9},{25,1},{2,26},{10... | collective-permute-start | bytes 49160 | tf_op jit(solution)/shard_map/ppermute | solution.py:879
  10.0 0.0 copy-done.3
  10.0 1.3 %shard_map.89.weight_ref = bf16[512,1024]{1,0:T(8,128)(2,1)S(1)} custom-call(bf16[8,512,128]{2,1,0:T(8,128)(2,1)S(1)} %copy-done.3), custom_call_target="tpu_custom_call" | custom-call | flops 100000000 | bytes 10000000 | tf_op jit(solution)/shard_map/pallas_call | solution.py:910
  11.3 0.0 copy-done.4
  11.3 0.4 shard_map.90.pick_ref
  11.7 0.0 collective-permute-done.2.two_ref
  11.7 0.0 collective-permute-done.1.one_ref.got_ref.first_ref
  11.7 0.5 %shard_map.91 = (bf16[224,128]{1,0:T(8,128)(2,1)S(1)}, bf16[224,128]{1,0:T(8,128)(2,1)S(1)}, f32[8,8,128]{2,1,0:T(8,128)S(1)}) custom-call(f32[64,64,128]{2,1,0:T(8,128)S(1)} %get-tuple-element.58.s_ref, f32[2,2,64,128]{3,2,1,0:T(8,128)S(1)} %get-tuple-element.61.x_ref, bf16[80,128]{1,0:T(8,128)(2,1)S(1)} %collective-permute-done.1.one_ref.got_ref.first_ref, ...), custom_call_target="tpu_custom_call" | custom-call | flops 100000000 | bytes 10000000 | tf_op jit(solution)/shard_map/pallas_call | solution.py:920
  12.2 1.7 %collective-permute-start.3 = (bf16[224,128]{1,0:T(8,128)(2,1)S(1)}, bf16[224,128]{1,0:T(8,128)(2,1)S(1)}, u32[]{:S(2)}, u32[]{:S(2)}) collective-permute-start(bf16[224,128]{1,0:T(8,128)(2,1)S(1)} %get-tuple-element.67), channel_id=1, source_target_pairs={{0,1},{1,0},{2,3},{3,2},{4,5},{5,4},{6,7},{7,6},{8,9},{9,8},{10,11... | collective-permute-start | bytes 172040 | tf_op jit(solution)/shard_map/ppermute | solution.py:879
  13.8 2.5 %collective-permute-start.4 = (bf16[224,128]{1,0:T(8,128)(2,1)S(1)}, bf16[224,128]{1,0:T(8,128)(2,1)S(1)}, u32[]{:S(2)}, u32[]{:S(2)}) collective-permute-start(bf16[224,128]{1,0:T(8,128)(2,1)S(1)} %get-tuple-element.68), channel_id=1, source_target_pairs={{0,3},{1,2},{2,1},{3,0},{4,7},{5,6},{6,5},{7,4},{8,11},{9,10},{10,... | collective-permute-start | bytes 172040 | tf_op jit(solution)/shard_map/ppermute | solution.py:879
  16.3 2.6 %shard_map.92 = (f32[32,48,128]{2,1,0:T(8,128)S(1)}, f32[32,48,128]{2,1,0:T(8,128)S(1)}, f32[32,48,128]{2,1,0:T(8,128)S(1)}, f32[4,8,128]{2,1,0:T(8,128)S(1)}) custom-call(f32[64,64,128]{2,1,0:T(8,128)S(1)} %get-tuple-element.58.s_ref, f32[2,2,64,128]{3,2,1,0:T(8,128)S(1)} %get-tuple-element.61.x_ref, f32[8,8,128]{2,1,0:T(8,128)S(1)} %get-tuple-element.66.packed_ref, ...), custom_call_target="tpu_custom_call" | custom-call | flops 100000000 | bytes 10000000 | tf_op jit(solution)/shard_map/pallas_call | solution.py:924
  18.9 0.0 collective-permute-done.3.y_one_ref
  18.9 0.9 %collective-permute-done.4.y_two_ref = bf16[224,128]{1,0:T(8,128)(2,1)S(1)} collective-permute-done((bf16[224,128]{1,0:T(8,128)(2,1)S(1)}, bf16[224,128]{1,0:T(8,128)(2,1)S(1)}, u32[]{:S(2)}, u32[]{:S(2)}) %collective-permute-start.4) | collective-permute-done | bytes 57376 | tf_op jit(solution)/shard_map/ppermute | solution.py:879
  19.8 0.7 %shard_map.93 = (bf16[2,1,64,128]{3,2,1,0:T(8,128)(2,1)S(1)}, f32[16,16,128]{2,1,0:T(8,128)S(1)}, f32[16,16,128]{2,1,0:T(8,128)S(1)}, f32[16,16,128]{2,1,0:T(8,128)S(1)}, f32[2,8,128]{2,1,0:T(8,128)S(1)}) custom-call(f32[64,64,128]{2,1,0:T(8,128)S(1)} %get-tuple-element.58.s_ref, f32[2,2,64,128]{3,2,1,0:T(8,128)S(1)} %get-tuple-element.61.x_ref, ...), custom_call_target="tpu_custom_call" | custom-call | flops 100000000 | bytes 10000000 | tf_op jit(solution)/shard_map/pallas_call | solution.py:929
  20.5 1.6 %collective-permute-start.5 = (bf16[2,1,64,128]{3,2,1,0:T(8,128)(2,1)S(1)}, bf16[2,1,64,128]{3,2,1,0:T(8,128)(2,1)S(1)}, u32[]{:S(2)}, u32[]{:S(2)}) collective-permute-start(bf16[2,1,64,128]{3,2,1,0:T(8,128)(2,1)S(1)} %get-tuple-element.77), channel_id=1, source_target_pairs={{0,4},{4,0},{1,5},{5,1},{2,6},{6,2},{3,7},{7,3},{8,12},{12,8},{9,1... | collective-permute-start | bytes 98312 | tf_op jit(solution)/shard_map/ppermute | solution.py:872
  22.1 0.9 %shard_map.94 = (f32[32,64,128]{2,1,0:T(8,128)S(1)}, f32[32,16,128]{2,1,0:T(8,128)S(1)}, f32[32,16,128]{2,1,0:T(8,128)S(1)}, f32[4,8,128]{2,1,0:T(8,128)S(1)}) custom-call(f32[64,64,128]{2,1,0:T(8,128)S(1)} %get-tuple-element.58.s_ref, f32[2,2,64,128]{3,2,1,0:T(8,128)S(1)} %get-tuple-element.61.x_ref, f32[8,8,128]{2,1,0:T(8,128)S(1)} %get-tuple-element.66.packed_ref, ...), custom_call_target="tpu_custom_call" | custom-call | flops 100000000 | bytes 10000000 | tf_op jit(solution)/shard_map/pallas_call | solution.py:934
  23.0 0.8 %shard_map.95.early_ref = bf16[256,1024]{1,0:T(8,128)(2,1)S(1)} custom-call(f32[32,64,128]{2,1,0:T(8,128)S(1)} %get-tuple-element.98.g_ref, f32[32,48,128]{2,1,0:T(8,128)S(1)} %get-tuple-element.102.base_one, f32[32,48,128]{2,1,0:T(8,128)S(1)} %get-tuple-element.103.half_one, f32[32,16,128]{2,1,0:T(8,128)S(1)} %get-tuple-element.104.base_two, ...), custom_call_target="tpu_custom_call" | custom-call | flops 100000000 | bytes 10000000 | tf_op jit(solution)/shard_map/pallas_call | solution.py:942
  23.8 0.7 %collective-permute-done.5.x_in = bf16[2,1,64,128]{3,2,1,0:T(8,128)(2,1)S(1)} collective-permute-done((bf16[2,1,64,128]{3,2,1,0:T(8,128)(2,1)S(1)}, bf16[2,1,64,128]{3,2,1,0:T(8,128)(2,1)S(1)}, u32[]{:S(2)}, u32[]{:S(2)}) %collective-permute-start.5) | collective-permute-done | bytes 32800 | tf_op jit(solution)/shard_map/ppermute | solution.py:872
  24.5 0.1 shard_map.96
  24.6 0.1 collective-permute-start.7
  24.7 1.6 %collective-permute-start.6 = (bf16[32,128]{1,0:T(8,128)(2,1)S(1)}, bf16[32,128]{1,0:T(8,128)(2,1)S(1)}, u32[]{:S(2)}, u32[]{:S(2)}) collective-permute-start(bf16[32,128]{1,0:T(8,128)(2,1)S(1)} %get-tuple-element.85), channel_id=1, source_target_pairs={{0,8},{8,0},{16,24},{24,16},{1,9},{9,1},{17,25},{25,17},{2,10},{10... | collective-permute-start | bytes 24584 | tf_op jit(solution)/shard_map/ppermute | solution.py:879
  26.3 1.5 %shard_map.97.pixel_ref = f32[8,128,128]{2,1,0:T(8,128)S(1)} custom-call(f32[32,64,128]{2,1,0:T(8,128)S(1)} %get-tuple-element.98.g_ref, f32[2,1,64,128]{3,2,1,0:T(8,128)S(1)} %get-tuple-element.99.x_ref, f32[32,48,128]{2,1,0:T(8,128)S(1)} %get-tuple-element.102.base_one, f32[32,48,128]{2,1,0:T(8,128)S(1)} %get-tuple-element.103.half_one, ...), custom_call_target="tpu_custom_call" | custom-call | flops 100000000 | bytes 10000000 | tf_op jit(solution)/shard_map/pallas_call | solution.py:952
  27.8 0.0 collective-permute-done.6.one_ref
  27.8 0.2 collective-permute-done.7.two_ref.second_ref
  28.0 2.4 %shard_map.98 = (bf16[8,64,128]{2,1,0:T(8,128)(2,1)S(1)}, bf16[2,128,128]{2,1,0:T(8,128)(2,1)S(1)}, bf16[2,128,128]{2,1,0:T(8,128)(2,1)S(1)}) custom-call(f32[32,64,128]{2,1,0:T(8,128)S(1)} %get-tuple-element.98.g_ref, f32[2,1,64,128]{3,2,1,0:T(8,128)S(1)} %get-tuple-element.99.x_ref, bf16[32,128]{1,0:T(8,128)(2,1)S(1)} %collective-permute-done.6.one_ref, ...), custom_call_target="tpu_custom_call" | custom-call | flops 100000000 | bytes 10000000 | tf_op jit(solution)/shard_map/pallas_call | solution.py:959
  30.4 1.4 %collective-permute-start.9 = (bf16[2,128,128]{2,1,0:T(8,128)(2,1)S(1)}, bf16[2,128,128]{2,1,0:T(8,128)(2,1)S(1)}, u32[]{:S(2)}, u32[]{:S(2)}) collective-permute-start(bf16[2,128,128]{2,1,0:T(8,128)(2,1)S(1)} %get-tuple-element.110), channel_id=1, source_target_pairs={{0,16},{8,24},{16,0},{24,8},{1,17},{9,25},{17,1},{25,9},{2,18},{10... | collective-permute-start | bytes 196616 | tf_op jit(solution)/shard_map/ppermute | solution.py:987
  31.8 0.1 collective-permute-start.10
  31.9 0.6 %shard_map.99 = (f32[2,1024,128]{2,1,0:T(8,128)S(1)}, bf16[2,1024,512]{2,1,0:T(8,128)(2,1)S(1)}) custom-call(bf16[8,64,128]{2,1,0:T(8,128)(2,1)S(1)} %get-tuple-element.95.value_ref, bf16[8,128,640]{2,1,0:T(8,128)(2,1)S(1)} %shard_map.90.pick_ref, f32[8,128,128]{2,1,0:T(8,128)S(1)} %shard_map.97.pixel_ref, s32[8,128]{1,0:T(8,128)S(1)} %copy-done.5, ...), custom_call_target="tpu_custom_call" | custom-call | flops 100000000 | bytes 10000000 | tf_op jit(solution)/shard_map/pallas_call | solution.py:966
  32.6 0.2 shard_map.100
  32.7 0.7 %collective-permute-start.8 = (bf16[2,128,128]{2,1,0:T(8,128)(2,1)S(1)}, bf16[2,128,128]{2,1,0:T(8,128)(2,1)S(1)}, u32[]{:S(2)}, u32[]{:S(2)}) collective-permute-start(bf16[2,128,128]{2,1,0:T(8,128)(2,1)S(1)} %shard_map.100), channel_id=1, source_target_pairs={{0,8},{8,0},{16,24},{24,16},{1,9},{9,1},{17,25},{25,17},{2,10},{10... | collective-permute-start | bytes 196616 | tf_op jit(solution)/shard_map/ppermute | solution.py:987
  33.5 1.2 %shard_map.101 = f32[32,64,128]{2,1,0:T(8,128)} custom-call(f32[32,64,128]{2,1,0:T(8,128)S(1)} %get-tuple-element.98.g_ref, f32[2,1,64,128]{3,2,1,0:T(8,128)S(1)} %get-tuple-element.99.x_ref, bf16[32,128]{1,0:T(8,128)(2,1)S(1)} %collective-permute-done.6.one_ref, bf16[64,128]{1,0:T(8,128)(2,1)S(1)} %collective-permute-done.7.two_ref.second_ref, ...), custom_call_target="tpu_custom_call" | custom-call | flops 100000000 | bytes 10000000 | tf_op jit(solution)/shard_map/pallas_call | solution.py:978
  34.7 0.0 collective-permute-done.9.refs_1_
  34.7 1.4 %collective-permute-done.10.refs_2_ = bf16[2,128,128]{2,1,0:T(8,128)(2,1)S(1)} collective-permute-done((bf16[2,128,128]{2,1,0:T(8,128)(2,1)S(1)}, bf16[2,128,128]{2,1,0:T(8,128)(2,1)S(1)}, u32[]{:S(2)}, u32[]{:S(2)}) %collective-permute-start.10) | collective-permute-done | bytes 65568 | tf_op jit(solution)/shard_map/ppermute | solution.py:987
  36.2 0.0 collective-permute-done.8.refs_0_
  36.2 1.3 %shard_map.102 = f32[2,1024,128]{2,1,0:T(8,128)} custom-call(f32[2,1024,128]{2,1,0:T(8,128)S(1)} %get-tuple-element.107.own_ref, bf16[2,1024,512]{2,1,0:T(8,128)(2,1)S(1)} %get-tuple-element.108.onehot_ref, bf16[2,128,128]{2,1,0:T(8,128)(2,1)S(1)} %collective-permute-done.8.refs_0_, bf16[2,128,128]{2,1,0:T(8,128)(2,1)S(1)} %collective-permute-done.9.refs_1_, ...), custom_call_target="tpu_custom_call" | custom-call | flops 100000000 | bytes 10000000 | tf_op jit(solution)/shard_map/pallas_call | solution.py:988
Async XLA Ops:
  0.6 4.8 %copy-start = (f32[3,4,8,8,8,128]{5,4,3,2,1,0:T(8,128)S(1)}, f32[3,4,8,8,8,128]{5,4,3,2,1,0:T(8,128)}, u32[]{:S(2)}) copy-start(f32[3,4,8,8,8,128]{5,4,3,2,1,0:T(8,128)} %param.8) | copy-start | bytes 9437188
  0.6 4.8 %copy-start.1 = (f32[4,8,8,8,128]{4,3,2,1,0:T(8,128)S(1)}, f32[4,8,8,8,128]{4,3,2,1,0:T(8,128)}, u32[]{:S(2)}) copy-start(f32[4,8,8,8,128]{4,3,2,1,0:T(8,128)} %param.7) | copy-start | bytes 3145732
  0.6 4.8 %copy-start.2 = (f32[4,8,8,8,128]{4,3,2,1,0:T(8,128)S(1)}, f32[4,8,8,8,128]{4,3,2,1,0:T(8,128)}, u32[]{:S(2)}) copy-start(f32[4,8,8,8,128]{4,3,2,1,0:T(8,128)} %param.9) | copy-start | bytes 3145732
  2.4 5.4 %collective-permute-start = (bf16[2,2,64,128]{3,2,1,0:T(8,128)(2,1)S(1)}, bf16[2,2,64,128]{3,2,1,0:T(8,128)(2,1)S(1)}, u32[]{:S(2)}, u32[]{:S(2)}) collective-permute-start(bf16[2,2,64,128]{3,2,1,0:T(8,128)(2,1)S(1)} %get-tuple-element.60), channel_id=1, source_target_pairs={{0,4},{4,0},{1,5},{5,1},{2,6},{6,2},{3,7},{7,3},{8,12},{12,8},{9,1... | collective-permute-start | bytes 196616 | tf_op jit(solution)/shard_map/ppermute | solution.py:872
  5.5 2.4 %copy-start.5 = (s32[8,128]{1,0:T(8,128)S(1)}, s32[8,128]{1,0:T(8,128)}, u32[]{:S(2)}) copy-start(s32[8,128]{1,0:T(8,128)} %block_ref.5) | copy-start | bytes 12292
  5.5 4.6 %copy-start.3 = (bf16[8,512,128]{2,1,0:T(8,128)(2,1)S(1)}, bf16[8,512,128]{2,1,0:T(8,128)(2,1)}, u32[]{:S(2)}) copy-start(bf16[8,512,128]{2,1,0:T(8,128)(2,1)} %weight_ref.1) | copy-start | bytes 3145732
  7.8 3.5 %copy-start.4 = (s32[8,128]{1,0:T(8,128)S(1)}, s32[8,128]{1,0:T(8,128)}, u32[]{:S(2)}) copy-start(s32[8,128]{1,0:T(8,128)} %cut_ref.1) | copy-start | bytes 12292
  8.0 3.7 %collective-permute-start.1 = (bf16[80,128]{1,0:T(8,128)(2,1)S(1)}, bf16[80,128]{1,0:T(8,128)(2,1)S(1)}, u32[]{:S(2)}, u32[]{:S(2)}) collective-permute-start(bf16[80,128]{1,0:T(8,128)(2,1)S(1)} %get-tuple-element.62), channel_id=1, source_target_pairs={{0,8},{8,0},{16,24},{24,16},{1,9},{9,1},{17,25},{25,17},{2,10},{10... | collective-permute-start | bytes 61448 | tf_op jit(solution)/shard_map/ppermute | solution.py:879
  8.0 3.6 %collective-permute-start.2 = (bf16[64,128]{1,0:T(8,128)(2,1)S(1)}, bf16[64,128]{1,0:T(8,128)(2,1)S(1)}, u32[]{:S(2)}, u32[]{:S(2)}) collective-permute-start(bf16[64,128]{1,0:T(8,128)(2,1)S(1)} %get-tuple-element.63), channel_id=1, source_target_pairs={{0,24},{8,16},{16,8},{24,0},{1,25},{9,17},{17,9},{25,1},{2,26},{10... | collective-permute-start | bytes 49160 | tf_op jit(solution)/shard_map/ppermute | solution.py:879
  12.2 6.7 %collective-permute-start.3 = (bf16[224,128]{1,0:T(8,128)(2,1)S(1)}, bf16[224,128]{1,0:T(8,128)(2,1)S(1)}, u32[]{:S(2)}, u32[]{:S(2)}) collective-permute-start(bf16[224,128]{1,0:T(8,128)(2,1)S(1)} %get-tuple-element.67), channel_id=1, source_target_pairs={{0,1},{1,0},{2,3},{3,2},{4,5},{5,4},{6,7},{7,6},{8,9},{9,8},{10,11... | collective-permute-start | bytes 172040 | tf_op jit(solution)/shard_map/ppermute | solution.py:879
  13.8 6.0 %collective-permute-start.4 = (bf16[224,128]{1,0:T(8,128)(2,1)S(1)}, bf16[224,128]{1,0:T(8,128)(2,1)S(1)}, u32[]{:S(2)}, u32[]{:S(2)}) collective-permute-start(bf16[224,128]{1,0:T(8,128)(2,1)S(1)} %get-tuple-element.68), channel_id=1, source_target_pairs={{0,3},{1,2},{2,1},{3,0},{4,7},{5,6},{6,5},{7,4},{8,11},{9,10},{10,... | collective-permute-start | bytes 172040 | tf_op jit(solution)/shard_map/ppermute | solution.py:879
  20.5 4.0 %collective-permute-start.5 = (bf16[2,1,64,128]{3,2,1,0:T(8,128)(2,1)S(1)}, bf16[2,1,64,128]{3,2,1,0:T(8,128)(2,1)S(1)}, u32[]{:S(2)}, u32[]{:S(2)}) collective-permute-start(bf16[2,1,64,128]{3,2,1,0:T(8,128)(2,1)S(1)} %get-tuple-element.77), channel_id=1, source_target_pairs={{0,4},{4,0},{1,5},{5,1},{2,6},{6,2},{3,7},{7,3},{8,12},{12,8},{9,1... | collective-permute-start | bytes 98312 | tf_op jit(solution)/shard_map/ppermute | solution.py:872
  24.6 3.4 %collective-permute-start.7 = (bf16[64,128]{1,0:T(8,128)(2,1)S(1)}, bf16[64,128]{1,0:T(8,128)(2,1)S(1)}, u32[]{:S(2)}, u32[]{:S(2)}) collective-permute-start(bf16[64,128]{1,0:T(8,128)(2,1)S(1)} %get-tuple-element.86), channel_id=1, source_target_pairs={{0,24},{8,16},{16,8},{24,0},{1,25},{9,17},{17,9},{25,1},{2,26},{10... | collective-permute-start | bytes 49160 | tf_op jit(solution)/shard_map/ppermute | solution.py:879
  24.7 3.1 %collective-permute-start.6 = (bf16[32,128]{1,0:T(8,128)(2,1)S(1)}, bf16[32,128]{1,0:T(8,128)(2,1)S(1)}, u32[]{:S(2)}, u32[]{:S(2)}) collective-permute-start(bf16[32,128]{1,0:T(8,128)(2,1)S(1)} %get-tuple-element.85), channel_id=1, source_target_pairs={{0,8},{8,0},{16,24},{24,16},{1,9},{9,1},{17,25},{25,17},{2,10},{10... | collective-permute-start | bytes 24584 | tf_op jit(solution)/shard_map/ppermute | solution.py:879
  30.4 4.3 %collective-permute-start.9 = (bf16[2,128,128]{2,1,0:T(8,128)(2,1)S(1)}, bf16[2,128,128]{2,1,0:T(8,128)(2,1)S(1)}, u32[]{:S(2)}, u32[]{:S(2)}) collective-permute-start(bf16[2,128,128]{2,1,0:T(8,128)(2,1)S(1)} %get-tuple-element.110), channel_id=1, source_target_pairs={{0,16},{8,24},{16,0},{24,8},{1,17},{9,25},{17,1},{25,9},{2,18},{10... | collective-permute-start | bytes 196616 | tf_op jit(solution)/shard_map/ppermute | solution.py:987
  31.8 4.3 %collective-permute-start.10 = (bf16[2,128,128]{2,1,0:T(8,128)(2,1)S(1)}, bf16[2,128,128]{2,1,0:T(8,128)(2,1)S(1)}, u32[]{:S(2)}, u32[]{:S(2)}) collective-permute-start(bf16[2,128,128]{2,1,0:T(8,128)(2,1)S(1)} %get-tuple-element.111), channel_id=1, source_target_pairs={{0,24},{8,16},{16,8},{24,0},{1,25},{9,17},{17,9},{25,1},{2,26},{10... | collective-permute-start | bytes 196616 | tf_op jit(solution)/shard_map/ppermute | solution.py:987
  32.7 3.4 %collective-permute-start.8 = (bf16[2,128,128]{2,1,0:T(8,128)(2,1)S(1)}, bf16[2,128,128]{2,1,0:T(8,128)(2,1)S(1)}, u32[]{:S(2)}, u32[]{:S(2)}) collective-permute-start(bf16[2,128,128]{2,1,0:T(8,128)(2,1)S(1)} %shard_map.100), channel_id=1, source_target_pairs={{0,8},{8,0},{16,24},{24,16},{1,9},{9,1},{17,25},{25,17},{2,10},{10... | collective-permute-start | bytes 196616 | tf_op jit(solution)/shard_map/ppermute | solution.py:987

commit v12 on v8

--- a/solution.py
+++ b/solution.py
@@ -801,11 +801,11 @@
     copies = []
     for m in range(image_ref.shape[0]):
         values = jnp.concatenate([payload_ref[m] for payload_ref in payload_refs], axis=0)
-        for chunk in range(4):
-            at = slice(256 * chunk, 256 * chunk + 256)
+        for chunk in range(2):
+            at = slice(512 * chunk, 512 * chunk + 512)
             image_ref[m, at, :] = own_ref[m, at, :] + dot(onehot_ref[m, at, 128:], values)
             copy = pltpu.make_async_copy(
-                image_ref.at[m, at], image_hbm.at[m, at], sems.at[4 * m + chunk]
+                image_ref.at[m, at], image_hbm.at[m, at], sems.at[2 * m + chunk]
             )
             copy.start()
             copies.append(copy)

time: 36.4 us -> 36.4 us (level)
  no operation moved by 1% of the time
where the time goes in v12:
time: 36.4 us; the launch traced here: 36.3 us
  Pallas kernels  17.5 us (48%)
  starting transfers between devices  14.7 us (40%)
  waiting for transfers between devices  3.28 us (9%)
  between operations  0.85 us (2%)
    ppermute x6, starting transfers between devices, swap_both(): return (lax.ppermute(one, axis, even), lax.ppermute(two, axis, odd))  7.85 us
    ppermute x2, starting transfers between devices, swap_axial(): return lax.ppermute(x, 'ex', up)  4.56 us
    pallas_call x1, Pallas kernels, per_device(): call(second_inner_kernel, (shape_of(*inner),) * 3 + (shape_of(4, 8, 128),))  2.6 us
    pallas_call x1, Pallas kernels, per_device(): call(first_kernel, (shape_of(64, 64, 128), shape_of(8, 8, 128)))  2.35 us
    ppermute x3, starting transfers between devices, per_device(): lax.ppermute(payload, 'cam', [(i, i ^ d) for i in range(n_cam)])  2.27 us
    pallas_call x1, Pallas kernels, per_device(): call(face_kernel, (shape_of(2, 2, 64, 128, dtype=BF16), shape_of(*tables....  1.77 us
    pallas_call x1, Pallas kernels, per_device(): call(middle_kernel, shape_of(cameras, 128, 128), scratch_shapes=[pltpu.VM...  1.49 us
    ppermute x3, waiting for transfers between devices, per_device(): lax.ppermute(payload, 'cam', [(i, i ^ d) for i in range(n_cam)])  1.45 us
  transfers between devices with their start and end apart: 11, of which 4 were waited for; matrix products, arithmetic and copies ran while one was open for 0% of the time, Pallas kernels for 32%

profile of v12, /device:TPU:0, one launch (start us, length us, event | category | flops | bytes accessed | tf_op | source)
XLA Modules:
  0.0 36.3 jit_solution(13555070521581727416)
XLA Ops:
  0.6 0.0 copy-start
  0.6 0.0 copy-start.1
  0.6 0.0 copy-start.2
  0.7 1.8 %shard_map.86 = (bf16[2,2,64,128]{3,2,1,0:T(8,128)(2,1)S(1)}, bf16[1472,128]{1,0:T(8,128)(2,1)S(1)}) custom-call(f32[32,64,128]{2,1,0:T(8,128)} %bitcast.10, f32[3,32,64,128]{3,2,1,0:T(8,128)} %bitcast.4, f32[32,64,128]{2,1,0:T(8,128)} %bitcast.16, bf16[1472,128]{1,0:T(8,128)(2,1)} %constant.2.clone.table_hbm), custom_call_target="tpu_custom_call" | custom-call | flops 100000000 | bytes 10000000 | tf_op jit(solution)/shard_map/pallas_call | solution.py:868
  2.4 3.0 %collective-permute-start = (bf16[2,2,64,128]{3,2,1,0:T(8,128)(2,1)S(1)}, bf16[2,2,64,128]{3,2,1,0:T(8,128)(2,1)S(1)}, u32[]{:S(2)}, u32[]{:S(2)}) collective-permute-start(bf16[2,2,64,128]{3,2,1,0:T(8,128)(2,1)S(1)} %get-tuple-element.60), channel_id=1, source_target_pairs={{0,4},{4,0},{1,5},{5,1},{2,6},{6,2},{3,7},{7,3},{8,12},{12,8},{9,1... | collective-permute-start | bytes 196616 | tf_op jit(solution)/shard_map/ppermute | solution.py:845
  5.4 0.0 copy-done
  5.4 0.0 copy-done.1
  5.4 0.0 copy-done.2
  5.5 0.0 copy-start.5
  5.5 0.0 copy-start.3
  5.5 2.3 %shard_map.87 = (f32[64,64,128]{2,1,0:T(8,128)S(1)}, f32[8,8,128]{2,1,0:T(8,128)S(1)}) custom-call(f32[32,64,128]{2,1,0:T(8,128)S(1)} %bitcast.11, f32[3,32,64,128]{3,2,1,0:T(8,128)S(1)} %bitcast.5, f32[32,64,128]{2,1,0:T(8,128)S(1)} %bitcast.17, bf16[1472,128]{1,0:T(8,128)(2,1)S(1)} %get-tuple-element.57.table_ref), custom_call_target="tpu_custom_call" | custom-call | flops 100000000 | bytes 10000000 | tf_op jit(solution)/shard_map/pallas_call | solution.py:880
  7.8 0.0 copy-start.4
  7.8 0.0 collective-permute-done.x_in
  7.9 0.0 copy-done.5
  7.9 0.1 shard_map.88
  8.0 0.1 collective-permute-start.1
  8.0 2.0 %collective-permute-start.2 = (bf16[64,128]{1,0:T(8,128)(2,1)S(1)}, bf16[64,128]{1,0:T(8,128)(2,1)S(1)}, u32[]{:S(2)}, u32[]{:S(2)}) collective-permute-start(bf16[64,128]{1,0:T(8,128)(2,1)S(1)} %get-tuple-element.63), channel_id=1, source_target_pairs={{0,24},{8,16},{16,8},{24,0},{1,25},{9,17},{17,9},{25,1},{2,26},{10... | collective-permute-start | bytes 49160 | tf_op jit(solution)/shard_map/ppermute | solution.py:852
  10.0 0.0 copy-done.3
  10.0 1.3 %shard_map.89.weight_ref = bf16[512,1024]{1,0:T(8,128)(2,1)S(1)} custom-call(bf16[8,512,128]{2,1,0:T(8,128)(2,1)S(1)} %copy-done.3), custom_call_target="tpu_custom_call" | custom-call | flops 100000000 | bytes 10000000 | tf_op jit(solution)/shard_map/pallas_call | solution.py:883
  11.3 0.0 copy-done.4
  11.3 0.4 %shard_map.90.pick_ref = bf16[8,128,640]{2,1,0:T(8,128)(2,1)S(1)} custom-call(s32[8,128]{1,0:T(8,128)S(1)} %copy-done.4), custom_call_target="tpu_custom_call" | custom-call | flops 100000000 | bytes 10000000 | tf_op jit(solution)/shard_map/pallas_call | solution.py:884
  11.7 0.0 collective-permute-done.2.two_ref
  11.7 0.0 collective-permute-done.1.one_ref.got_ref.first_ref
  11.7 0.5 %shard_map.91 = (bf16[224,128]{1,0:T(8,128)(2,1)S(1)}, bf16[224,128]{1,0:T(8,128)(2,1)S(1)}, f32[8,8,128]{2,1,0:T(8,128)S(1)}) custom-call(f32[64,64,128]{2,1,0:T(8,128)S(1)} %get-tuple-element.58.s_ref, f32[2,2,64,128]{3,2,1,0:T(8,128)S(1)} %get-tuple-element.61.x_ref, bf16[80,128]{1,0:T(8,128)(2,1)S(1)} %collective-permute-done.1.one_ref.got_ref.first_ref, ...), custom_call_target="tpu_custom_call" | custom-call | flops 100000000 | bytes 10000000 | tf_op jit(solution)/shard_map/pallas_call | solution.py:893
  12.2 1.7 %collective-permute-start.3 = (bf16[224,128]{1,0:T(8,128)(2,1)S(1)}, bf16[224,128]{1,0:T(8,128)(2,1)S(1)}, u32[]{:S(2)}, u32[]{:S(2)}) collective-permute-start(bf16[224,128]{1,0:T(8,128)(2,1)S(1)} %get-tuple-element.67), channel_id=1, source_target_pairs={{0,1},{1,0},{2,3},{3,2},{4,5},{5,4},{6,7},{7,6},{8,9},{9,8},{10,11... | collective-permute-start | bytes 172040 | tf_op jit(solution)/shard_map/ppermute | solution.py:852
  13.8 2.5 %collective-permute-start.4 = (bf16[224,128]{1,0:T(8,128)(2,1)S(1)}, bf16[224,128]{1,0:T(8,128)(2,1)S(1)}, u32[]{:S(2)}, u32[]{:S(2)}) collective-permute-start(bf16[224,128]{1,0:T(8,128)(2,1)S(1)} %get-tuple-element.68), channel_id=1, source_target_pairs={{0,3},{1,2},{2,1},{3,0},{4,7},{5,6},{6,5},{7,4},{8,11},{9,10},{10,... | collective-permute-start | bytes 172040 | tf_op jit(solution)/shard_map/ppermute | solution.py:852
  16.3 2.6 %shard_map.92 = (f32[32,48,128]{2,1,0:T(8,128)S(1)}, f32[32,48,128]{2,1,0:T(8,128)S(1)}, f32[32,48,128]{2,1,0:T(8,128)S(1)}, f32[4,8,128]{2,1,0:T(8,128)S(1)}) custom-call(f32[64,64,128]{2,1,0:T(8,128)S(1)} %get-tuple-element.58.s_ref, f32[2,2,64,128]{3,2,1,0:T(8,128)S(1)} %get-tuple-element.61.x_ref, f32[8,8,128]{2,1,0:T(8,128)S(1)} %get-tuple-element.66.packed_ref, ...), custom_call_target="tpu_custom_call" | custom-call | flops 100000000 | bytes 10000000 | tf_op jit(solution)/shard_map/pallas_call | solution.py:897
  18.9 0.0 collective-permute-done.3.y_one_ref
  18.9 0.9 %collective-permute-done.4.y_two_ref = bf16[224,128]{1,0:T(8,128)(2,1)S(1)} collective-permute-done((bf16[224,128]{1,0:T(8,128)(2,1)S(1)}, bf16[224,128]{1,0:T(8,128)(2,1)S(1)}, u32[]{:S(2)}, u32[]{:S(2)}) %collective-permute-start.4) | collective-permute-done | bytes 57376 | tf_op jit(solution)/shard_map/ppermute | solution.py:852
  19.8 0.7 %shard_map.93 = (bf16[2,1,64,128]{3,2,1,0:T(8,128)(2,1)S(1)}, f32[16,16,128]{2,1,0:T(8,128)S(1)}, f32[16,16,128]{2,1,0:T(8,128)S(1)}, f32[16,16,128]{2,1,0:T(8,128)S(1)}, f32[2,8,128]{2,1,0:T(8,128)S(1)}) custom-call(f32[64,64,128]{2,1,0:T(8,128)S(1)} %get-tuple-element.58.s_ref, f32[2,2,64,128]{3,2,1,0:T(8,128)S(1)} %get-tuple-element.61.x_ref, ...), custom_call_target="tpu_custom_call" | custom-call | flops 100000000 | bytes 10000000 | tf_op jit(solution)/shard_map/pallas_call | solution.py:902
  20.5 1.6 %collective-permute-start.5 = (bf16[2,1,64,128]{3,2,1,0:T(8,128)(2,1)S(1)}, bf16[2,1,64,128]{3,2,1,0:T(8,128)(2,1)S(1)}, u32[]{:S(2)}, u32[]{:S(2)}) collective-permute-start(bf16[2,1,64,128]{3,2,1,0:T(8,128)(2,1)S(1)} %get-tuple-element.77), channel_id=1, source_target_pairs={{0,4},{4,0},{1,5},{5,1},{2,6},{6,2},{3,7},{7,3},{8,12},{12,8},{9,1... | collective-permute-start | bytes 98312 | tf_op jit(solution)/shard_map/ppermute | solution.py:845
  22.1 0.9 %shard_map.94 = (f32[32,64,128]{2,1,0:T(8,128)S(1)}, f32[32,16,128]{2,1,0:T(8,128)S(1)}, f32[32,16,128]{2,1,0:T(8,128)S(1)}, f32[4,8,128]{2,1,0:T(8,128)S(1)}) custom-call(f32[64,64,128]{2,1,0:T(8,128)S(1)} %get-tuple-element.58.s_ref, f32[2,2,64,128]{3,2,1,0:T(8,128)S(1)} %get-tuple-element.61.x_ref, f32[8,8,128]{2,1,0:T(8,128)S(1)} %get-tuple-element.66.packed_ref, ...), custom_call_target="tpu_custom_call" | custom-call | flops 100000000 | bytes 10000000 | tf_op jit(solution)/shard_map/pallas_call | solution.py:907
  23.0 0.8 %shard_map.95.early_ref = bf16[256,1024]{1,0:T(8,128)(2,1)S(1)} custom-call(f32[32,64,128]{2,1,0:T(8,128)S(1)} %get-tuple-element.98.g_ref, f32[32,48,128]{2,1,0:T(8,128)S(1)} %get-tuple-element.102.base_one, f32[32,48,128]{2,1,0:T(8,128)S(1)} %get-tuple-element.103.half_one, f32[32,16,128]{2,1,0:T(8,128)S(1)} %get-tuple-element.104.base_two, ...), custom_call_target="tpu_custom_call" | custom-call | flops 100000000 | bytes 10000000 | tf_op jit(solution)/shard_map/pallas_call | solution.py:915
  23.8 0.7 %collective-permute-done.5.x_in = bf16[2,1,64,128]{3,2,1,0:T(8,128)(2,1)S(1)} collective-permute-done((bf16[2,1,64,128]{3,2,1,0:T(8,128)(2,1)S(1)}, bf16[2,1,64,128]{3,2,1,0:T(8,128)(2,1)S(1)}, u32[]{:S(2)}, u32[]{:S(2)}) %collective-permute-start.5) | collective-permute-done | bytes 32800 | tf_op jit(solution)/shard_map/ppermute | solution.py:845
  24.5 0.1 shard_map.96
  24.6 0.1 collective-permute-start.7
  24.7 1.6 %collective-permute-start.6 = (bf16[32,128]{1,0:T(8,128)(2,1)S(1)}, bf16[32,128]{1,0:T(8,128)(2,1)S(1)}, u32[]{:S(2)}, u32[]{:S(2)}) collective-permute-start(bf16[32,128]{1,0:T(8,128)(2,1)S(1)} %get-tuple-element.85), channel_id=1, source_target_pairs={{0,8},{8,0},{16,24},{24,16},{1,9},{9,1},{17,25},{25,17},{2,10},{10... | collective-permute-start | bytes 24584 | tf_op jit(solution)/shard_map/ppermute | solution.py:852
  26.3 1.5 %shard_map.97.pixel_ref = f32[8,128,128]{2,1,0:T(8,128)S(1)} custom-call(f32[32,64,128]{2,1,0:T(8,128)S(1)} %get-tuple-element.98.g_ref, f32[2,1,64,128]{3,2,1,0:T(8,128)S(1)} %get-tuple-element.99.x_ref, f32[32,48,128]{2,1,0:T(8,128)S(1)} %get-tuple-element.102.base_one, f32[32,48,128]{2,1,0:T(8,128)S(1)} %get-tuple-element.103.half_one, ...), custom_call_target="tpu_custom_call" | custom-call | flops 100000000 | bytes 10000000 | tf_op jit(solution)/shard_map/pallas_call | solution.py:925
  27.8 0.0 collective-permute-done.6.one_ref
  27.8 0.2 collective-permute-done.7.two_ref.second_ref
  28.0 1.2 %shard_map.98 = (bf16[8,64,128]{2,1,0:T(8,128)(2,1)S(1)}, bf16[2,128,128]{2,1,0:T(8,128)(2,1)S(1)}, bf16[2,128,128]{2,1,0:T(8,128)(2,1)S(1)}) custom-call(f32[32,64,128]{2,1,0:T(8,128)S(1)} %get-tuple-element.98.g_ref, f32[2,1,64,128]{3,2,1,0:T(8,128)S(1)} %get-tuple-element.99.x_ref, bf16[32,128]{1,0:T(8,128)(2,1)S(1)} %collective-permute-done.6.one_ref, ...), custom_call_target="tpu_custom_call" | custom-call | flops 100000000 | bytes 10000000 | tf_op jit(solution)/shard_map/pallas_call | solution.py:932
  29.2 1.4 %collective-permute-start.9 = (bf16[2,128,128]{2,1,0:T(8,128)(2,1)S(1)}, bf16[2,128,128]{2,1,0:T(8,128)(2,1)S(1)}, u32[]{:S(2)}, u32[]{:S(2)}) collective-permute-start(bf16[2,128,128]{2,1,0:T(8,128)(2,1)S(1)} %get-tuple-element.110), channel_id=1, source_target_pairs={{0,16},{8,24},{16,0},{24,8},{1,17},{9,25},{17,1},{25,9},{2,18},{10... | collective-permute-start | bytes 196616 | tf_op jit(solution)/shard_map/ppermute | solution.py:960
  30.6 0.1 collective-permute-start.10
  30.7 0.6 %shard_map.99 = (f32[2,1024,128]{2,1,0:T(8,128)S(1)}, bf16[2,1024,512]{2,1,0:T(8,128)(2,1)S(1)}) custom-call(bf16[8,64,128]{2,1,0:T(8,128)(2,1)S(1)} %get-tuple-element.95.value_ref, bf16[8,128,640]{2,1,0:T(8,128)(2,1)S(1)} %shard_map.90.pick_ref, f32[8,128,128]{2,1,0:T(8,128)S(1)} %shard_map.97.pixel_ref, s32[8,128]{1,0:T(8,128)S(1)} %copy-done.5, ...), custom_call_target="tpu_custom_call" | custom-call | flops 100000000 | bytes 10000000 | tf_op jit(solution)/shard_map/pallas_call | solution.py:939
  31.3 0.2 shard_map.100
  31.5 0.7 %collective-permute-start.8 = (bf16[2,128,128]{2,1,0:T(8,128)(2,1)S(1)}, bf16[2,128,128]{2,1,0:T(8,128)(2,1)S(1)}, u32[]{:S(2)}, u32[]{:S(2)}) collective-permute-start(bf16[2,128,128]{2,1,0:T(8,128)(2,1)S(1)} %shard_map.100), channel_id=1, source_target_pairs={{0,8},{8,0},{16,24},{24,16},{1,9},{9,1},{17,25},{25,17},{2,10},{10... | collective-permute-start | bytes 196616 | tf_op jit(solution)/shard_map/ppermute | solution.py:960
  32.2 1.2 %shard_map.101 = f32[32,64,128]{2,1,0:T(8,128)} custom-call(f32[32,64,128]{2,1,0:T(8,128)S(1)} %get-tuple-element.98.g_ref, f32[2,1,64,128]{3,2,1,0:T(8,128)S(1)} %get-tuple-element.99.x_ref, bf16[32,128]{1,0:T(8,128)(2,1)S(1)} %collective-permute-done.6.one_ref, bf16[64,128]{1,0:T(8,128)(2,1)S(1)} %collective-permute-done.7.two_ref.second_ref, ...), custom_call_target="tpu_custom_call" | custom-call | flops 100000000 | bytes 10000000 | tf_op jit(solution)/shard_map/pallas_call | solution.py:951
  33.5 0.0 collective-permute-done.9.refs_1_
  33.5 1.4 %collective-permute-done.10.refs_2_ = bf16[2,128,128]{2,1,0:T(8,128)(2,1)S(1)} collective-permute-done((bf16[2,128,128]{2,1,0:T(8,128)(2,1)S(1)}, bf16[2,128,128]{2,1,0:T(8,128)(2,1)S(1)}, u32[]{:S(2)}, u32[]{:S(2)}) %collective-permute-start.10) | collective-permute-done | bytes 65568 | tf_op jit(solution)/shard_map/ppermute | solution.py:960
  34.9 0.0 collective-permute-done.8.refs_0_
  34.9 1.3 %shard_map.102 = f32[2,1024,128]{2,1,0:T(8,128)} custom-call(f32[2,1024,128]{2,1,0:T(8,128)S(1)} %get-tuple-element.107.own_ref, bf16[2,1024,512]{2,1,0:T(8,128)(2,1)S(1)} %get-tuple-element.108.onehot_ref, bf16[2,128,128]{2,1,0:T(8,128)(2,1)S(1)} %collective-permute-done.8.refs_0_, bf16[2,128,128]{2,1,0:T(8,128)(2,1)S(1)} %collective-permute-done.9.refs_1_, ...), custom_call_target="tpu_custom_call" | custom-call | flops 100000000 | bytes 10000000 | tf_op jit(solution)/shard_map/pallas_call | solution.py:961
Async XLA Ops:
  0.6 4.8 %copy-start = (f32[3,4,8,8,8,128]{5,4,3,2,1,0:T(8,128)S(1)}, f32[3,4,8,8,8,128]{5,4,3,2,1,0:T(8,128)}, u32[]{:S(2)}) copy-start(f32[3,4,8,8,8,128]{5,4,3,2,1,0:T(8,128)} %param.8) | copy-start | bytes 9437188
  0.6 4.8 %copy-start.1 = (f32[4,8,8,8,128]{4,3,2,1,0:T(8,128)S(1)}, f32[4,8,8,8,128]{4,3,2,1,0:T(8,128)}, u32[]{:S(2)}) copy-start(f32[4,8,8,8,128]{4,3,2,1,0:T(8,128)} %param.7) | copy-start | bytes 3145732
  0.6 4.8 %copy-start.2 = (f32[4,8,8,8,128]{4,3,2,1,0:T(8,128)S(1)}, f32[4,8,8,8,128]{4,3,2,1,0:T(8,128)}, u32[]{:S(2)}) copy-start(f32[4,8,8,8,128]{4,3,2,1,0:T(8,128)} %param.9) | copy-start | bytes 3145732
  2.4 5.4 %collective-permute-start = (bf16[2,2,64,128]{3,2,1,0:T(8,128)(2,1)S(1)}, bf16[2,2,64,128]{3,2,1,0:T(8,128)(2,1)S(1)}, u32[]{:S(2)}, u32[]{:S(2)}) collective-permute-start(bf16[2,2,64,128]{3,2,1,0:T(8,128)(2,1)S(1)} %get-tuple-element.60), channel_id=1, source_target_pairs={{0,4},{4,0},{1,5},{5,1},{2,6},{6,2},{3,7},{7,3},{8,12},{12,8},{9,1... | collective-permute-start | bytes 196616 | tf_op jit(solution)/shard_map/ppermute | solution.py:845
  5.5 2.4 %copy-start.5 = (s32[8,128]{1,0:T(8,128)S(1)}, s32[8,128]{1,0:T(8,128)}, u32[]{:S(2)}) copy-start(s32[8,128]{1,0:T(8,128)} %block_ref.5) | copy-start | bytes 12292
  5.5 4.6 %copy-start.3 = (bf16[8,512,128]{2,1,0:T(8,128)(2,1)S(1)}, bf16[8,512,128]{2,1,0:T(8,128)(2,1)}, u32[]{:S(2)}) copy-start(bf16[8,512,128]{2,1,0:T(8,128)(2,1)} %weight_ref.1) | copy-start | bytes 3145732
  7.8 3.5 %copy-start.4 = (s32[8,128]{1,0:T(8,128)S(1)}, s32[8,128]{1,0:T(8,128)}, u32[]{:S(2)}) copy-start(s32[8,128]{1,0:T(8,128)} %cut_ref.1) | copy-start | bytes 12292
  8.0 3.7 %collective-permute-start.1 = (bf16[80,128]{1,0:T(8,128)(2,1)S(1)}, bf16[80,128]{1,0:T(8,128)(2,1)S(1)}, u32[]{:S(2)}, u32[]{:S(2)}) collective-permute-start(bf16[80,128]{1,0:T(8,128)(2,1)S(1)} %get-tuple-element.62), channel_id=1, source_target_pairs={{0,8},{8,0},{16,24},{24,16},{1,9},{9,1},{17,25},{25,17},{2,10},{10... | collective-permute-start | bytes 61448 | tf_op jit(solution)/shard_map/ppermute | solution.py:852
  8.0 3.6 %collective-permute-start.2 = (bf16[64,128]{1,0:T(8,128)(2,1)S(1)}, bf16[64,128]{1,0:T(8,128)(2,1)S(1)}, u32[]{:S(2)}, u32[]{:S(2)}) collective-permute-start(bf16[64,128]{1,0:T(8,128)(2,1)S(1)} %get-tuple-element.63), channel_id=1, source_target_pairs={{0,24},{8,16},{16,8},{24,0},{1,25},{9,17},{17,9},{25,1},{2,26},{10... | collective-permute-start | bytes 49160 | tf_op jit(solution)/shard_map/ppermute | solution.py:852
  12.2 6.7 %collective-permute-start.3 = (bf16[224,128]{1,0:T(8,128)(2,1)S(1)}, bf16[224,128]{1,0:T(8,128)(2,1)S(1)}, u32[]{:S(2)}, u32[]{:S(2)}) collective-permute-start(bf16[224,128]{1,0:T(8,128)(2,1)S(1)} %get-tuple-element.67), channel_id=1, source_target_pairs={{0,1},{1,0},{2,3},{3,2},{4,5},{5,4},{6,7},{7,6},{8,9},{9,8},{10,11... | collective-permute-start | bytes 172040 | tf_op jit(solution)/shard_map/ppermute | solution.py:852
  13.8 6.0 %collective-permute-start.4 = (bf16[224,128]{1,0:T(8,128)(2,1)S(1)}, bf16[224,128]{1,0:T(8,128)(2,1)S(1)}, u32[]{:S(2)}, u32[]{:S(2)}) collective-permute-start(bf16[224,128]{1,0:T(8,128)(2,1)S(1)} %get-tuple-element.68), channel_id=1, source_target_pairs={{0,3},{1,2},{2,1},{3,0},{4,7},{5,6},{6,5},{7,4},{8,11},{9,10},{10,... | collective-permute-start | bytes 172040 | tf_op jit(solution)/shard_map/ppermute | solution.py:852
  20.5 4.0 %collective-permute-start.5 = (bf16[2,1,64,128]{3,2,1,0:T(8,128)(2,1)S(1)}, bf16[2,1,64,128]{3,2,1,0:T(8,128)(2,1)S(1)}, u32[]{:S(2)}, u32[]{:S(2)}) collective-permute-start(bf16[2,1,64,128]{3,2,1,0:T(8,128)(2,1)S(1)} %get-tuple-element.77), channel_id=1, source_target_pairs={{0,4},{4,0},{1,5},{5,1},{2,6},{6,2},{3,7},{7,3},{8,12},{12,8},{9,1... | collective-permute-start | bytes 98312 | tf_op jit(solution)/shard_map/ppermute | solution.py:845
  24.6 3.4 %collective-permute-start.7 = (bf16[64,128]{1,0:T(8,128)(2,1)S(1)}, bf16[64,128]{1,0:T(8,128)(2,1)S(1)}, u32[]{:S(2)}, u32[]{:S(2)}) collective-permute-start(bf16[64,128]{1,0:T(8,128)(2,1)S(1)} %get-tuple-element.86), channel_id=1, source_target_pairs={{0,24},{8,16},{16,8},{24,0},{1,25},{9,17},{17,9},{25,1},{2,26},{10... | collective-permute-start | bytes 49160 | tf_op jit(solution)/shard_map/ppermute | solution.py:852
  24.7 3.1 %collective-permute-start.6 = (bf16[32,128]{1,0:T(8,128)(2,1)S(1)}, bf16[32,128]{1,0:T(8,128)(2,1)S(1)}, u32[]{:S(2)}, u32[]{:S(2)}) collective-permute-start(bf16[32,128]{1,0:T(8,128)(2,1)S(1)} %get-tuple-element.85), channel_id=1, source_target_pairs={{0,8},{8,0},{16,24},{24,16},{1,9},{9,1},{17,25},{25,17},{2,10},{10... | collective-permute-start | bytes 24584 | tf_op jit(solution)/shard_map/ppermute | solution.py:852
  29.2 4.3 %collective-permute-start.9 = (bf16[2,128,128]{2,1,0:T(8,128)(2,1)S(1)}, bf16[2,128,128]{2,1,0:T(8,128)(2,1)S(1)}, u32[]{:S(2)}, u32[]{:S(2)}) collective-permute-start(bf16[2,128,128]{2,1,0:T(8,128)(2,1)S(1)} %get-tuple-element.110), channel_id=1, source_target_pairs={{0,16},{8,24},{16,0},{24,8},{1,17},{9,25},{17,1},{25,9},{2,18},{10... | collective-permute-start | bytes 196616 | tf_op jit(solution)/shard_map/ppermute | solution.py:960
  30.6 4.3 %collective-permute-start.10 = (bf16[2,128,128]{2,1,0:T(8,128)(2,1)S(1)}, bf16[2,128,128]{2,1,0:T(8,128)(2,1)S(1)}, u32[]{:S(2)}, u32[]{:S(2)}) collective-permute-start(bf16[2,128,128]{2,1,0:T(8,128)(2,1)S(1)} %get-tuple-element.111), channel_id=1, source_target_pairs={{0,24},{8,16},{16,8},{24,0},{1,25},{9,17},{17,9},{25,1},{2,26},{10... | collective-permute-start | bytes 196616 | tf_op jit(solution)/shard_map/ppermute | solution.py:960
  31.5 3.4 %collective-permute-start.8 = (bf16[2,128,128]{2,1,0:T(8,128)(2,1)S(1)}, bf16[2,128,128]{2,1,0:T(8,128)(2,1)S(1)}, u32[]{:S(2)}, u32[]{:S(2)}) collective-permute-start(bf16[2,128,128]{2,1,0:T(8,128)(2,1)S(1)} %shard_map.100), channel_id=1, source_target_pairs={{0,8},{8,0},{16,24},{24,16},{1,9},{9,1},{17,25},{25,17},{2,10},{10... | collective-permute-start | bytes 196616 | tf_op jit(solution)/shard_map/ppermute | solution.py:960
